TPU v7x, 32 devices: a whole 2x2x4 slice. The times are simulated.
32 devices in a mesh: fsdp: 8 (over z, core), dp: 4 (over y, x).
Axes of the slice: x: 2, y: 2, z: 4, core: 2. Of those that a mesh axis runs over, the one named last changes fastest.
Arguments:
- latents: bfloat16 [8, 60, 256, 320], P('fsdp', 'dp'), may hold values from -6 to 6
- target_noise: bfloat16 [8, 60, 256, 320], P('fsdp', 'dp'), may hold values from -6 to 6
- counts: int32 [8, 4], P('fsdp'), may hold values from 1 to 15, 32 in all within a row
- timesteps: int32 [8, 60], P('fsdp', 'dp'), may hold values from 0 to 999
- conv_master: float32 [2880, 320], P('fsdp'), may hold values from -0.109375 to 0.109375
- temb_master: float32 [1280, 320], P('fsdp'), may hold values from -0.15625 to 0.15625
Outputs:
- prediction: bfloat16 [8, 60, 256, 320], P('fsdp', 'dp')
- conv_grad: float32 [2880, 320], P('fsdp')
- temb_grad: float32 [1280, 320], P('fsdp')
Inputs may be any that keep to these rules, and one draw needn't show every extreme that they name: In each row (one slide group) the 4 owners' live counts sum to exactly 32; 15 is reached in every row; an owner's live tiles are its first slots.
All inputs are finite; a program needn't handle non-finite values.
Results may differ from a plain program's by a relative error of at most 0.0085.
Values may be sent and summed in bfloat16 or wider, within the bound.
No kernel may reach another device: no remote copies, remote signals or barrier semaphores. Data moves between devices by JAX's collectives and lax.ppermute only.
A program may use at most 128 MiB of HBM per device.

v0:
```python
import math

import jax
import jax.numpy as jnp
from jax import lax
from jax.sharding import PartitionSpec as P

EMB = 1280
GROUPS = 32
SIDE = 16
BAL = 8


def time_features(timestep_list):
    half_width = EMB // 2
    frequency = jnp.exp(-math.log(10000.0) * jnp.arange(half_width, dtype=jnp.float32) / half_width)
    angles = timestep_list.astype(jnp.float32)[:, None] * frequency[None, :]
    return jax.nn.silu(jnp.concatenate([jnp.cos(angles), jnp.sin(angles)], axis=1)).astype(
        jnp.bfloat16
    )


def normed(tile_block):
    number, pixels, channels = tile_block.shape
    grouped = tile_block.astype(jnp.float32).reshape(number, pixels, GROUPS, channels // GROUPS)
    group_mean = jnp.mean(grouped, axis=(1, 3), keepdims=True)
    centred = grouped - group_mean
    variance = jnp.mean(centred * centred, axis=(1, 3), keepdims=True)
    return (
        jax.nn.silu(centred / jnp.sqrt(variance + 1e-05))
        .reshape(number, pixels, channels)
        .astype(jnp.bfloat16)
    )


def unfold(values):
    number, pixels, channels = values.shape
    spatial = values.reshape(number, SIDE, SIDE, channels)
    padded = jnp.pad(spatial, ((0, 0), (1, 1), (1, 1), (0, 0)))
    shifted = [padded[:, a : a + SIDE, b : b + SIDE] for a in range(3) for b in range(3)]
    return jnp.concatenate(shifted, axis=-1).reshape(number * pixels, 9 * channels)


def predict(tile_block, time_act, conv_master, temb_master):
    number, pixels, channels = tile_block.shape
    columns = unfold(normed(tile_block))
    time_weight = lax.all_gather(temb_master.astype(jnp.bfloat16), "fsdp", axis=0, tiled=True)
    time_bias = jnp.dot(time_act, time_weight, preferred_element_type=jnp.float32)
    conv_out = jnp.dot(
        columns,
        lax.all_gather(conv_master.astype(jnp.bfloat16), "fsdp", axis=0, tiled=True),
        preferred_element_type=jnp.float32,
    )
    pred32 = (
        tile_block.astype(jnp.float32)
        + conv_out.reshape(number, pixels, channels)
        + time_bias[:, None, :]
    )
    return (columns, pred32)


def finish(pred32, target_block, time_act, live_mask):
    number, pixels, channels = pred32.shape
    keep = live_mask[:, None, None]
    predicted = jnp.where(keep, pred32, 0.0).astype(jnp.bfloat16)
    error_grad = jnp.where(keep, (pred32 - target_block.astype(jnp.float32)) / pixels, 0.0).astype(
        jnp.bfloat16
    )
    error_sums = jnp.sum(error_grad.astype(jnp.float32), axis=1)
    temb_term = lax.dot_general(
        time_act.astype(jnp.float32),
        error_sums,
        (((0,), (0,)), ((), ())),
        precision=lax.Precision.HIGHEST,
        preferred_element_type=jnp.float32,
    )
    return (predicted, error_grad.reshape(number * pixels, channels), temb_term)


def per_device(latents, target_noise, counts, timesteps, conv_master, temb_master):
    tiles_here = latents[0]
    targets_here = target_noise[0]
    live_counts = counts[0]
    own_slots, pixels, channels = tiles_here.shape
    time_here = time_features(timesteps[0])
    peers = lax.axis_size("dp")
    my_index = lax.axis_index("dp")
    positions = jnp.arange(peers, dtype=jnp.int32)
    count_ends = jnp.cumsum(live_counts)
    count_starts = count_ends - live_counts
    my_start = jnp.sum(jnp.where(positions == my_index, count_starts, 0))
    my_count = jnp.sum(jnp.where(positions == my_index, live_counts, 0))
    slot_ids = jnp.arange(own_slots, dtype=jnp.int32)
    own_live = slot_ids < my_count
    depth = -(-own_slots // peers)
    layers = jnp.arange(depth, dtype=jnp.int32)[None, :]
    local_ids = layers * peers + (positions[:, None] - my_start) % peers
    safe_ids = jnp.clip(local_ids, 0, own_slots - 1).reshape(-1)
    wanted = jnp.arange(BAL, dtype=jnp.int32) * peers + my_index
    owner_index = jnp.sum((count_ends[None, :] <= wanted[:, None]).astype(jnp.int32), axis=1)
    owner_start = jnp.sum(
        jnp.where(owner_index[:, None] == positions[None, :], count_starts[None, :], 0), axis=1
    )
    flat_ids = owner_index * depth + (wanted - owner_start) // peers
    source_ids = layers * peers + (my_index - count_starts[:, None]) % peers
    compact_ids = jnp.clip((count_starts[:, None] + source_ids) // peers, 0, BAL - 1).reshape(-1)
    home_ids = (my_start + slot_ids) % peers * depth + slot_ids // peers
    out_tiles = jnp.take(tiles_here, safe_ids, axis=0).reshape(peers, depth, pixels, channels)
    out_targets = jnp.take(targets_here, safe_ids, axis=0).reshape(peers, depth, pixels, channels)
    out_times = jnp.take(time_here, safe_ids, axis=0).reshape(peers, depth, EMB)
    got_tiles, got_targets, got_times = (
        lax.all_to_all(out_tiles, "dp", split_axis=0, concat_axis=0, tiled=True),
        lax.all_to_all(out_targets, "dp", split_axis=0, concat_axis=0, tiled=True),
        lax.all_to_all(out_times, "dp", split_axis=0, concat_axis=0, tiled=True),
    )
    packed_tiles = jnp.take(got_tiles.reshape(peers * depth, pixels, channels), flat_ids, axis=0)
    packed_targets = jnp.take(
        got_targets.reshape(peers * depth, pixels, channels), flat_ids, axis=0
    )
    packed_times = jnp.take(got_times.reshape(peers * depth, EMB), flat_ids, axis=0)
    columns, pred32 = predict(packed_tiles, packed_times, conv_master, temb_master)
    predicted, error_rows, temb_term = finish(
        pred32, packed_targets, packed_times, jnp.ones((BAL,), dtype=bool)
    )
    back_tiles = jnp.take(predicted, compact_ids, axis=0).reshape(peers, depth, pixels, channels)
    home_tiles = lax.all_to_all(back_tiles, "dp", split_axis=0, concat_axis=0, tiled=True).reshape(
        peers * depth, pixels, channels
    )
    picked = jnp.take(home_tiles, home_ids, axis=0)
    returned = jnp.where(own_live[:, None, None], picked, jnp.zeros((), jnp.bfloat16))
    conv_part = lax.psum_scatter(
        lax.dot_general(
            columns, error_rows, (((0,), (0,)), ((), ())), preferred_element_type=jnp.float32
        ).astype(jnp.bfloat16),
        "fsdp",
        scatter_dimension=0,
        tiled=True,
    )
    time_part = lax.psum_scatter(
        temb_term.astype(jnp.bfloat16), "fsdp", scatter_dimension=0, tiled=True
    )
    conv_grad, temb_grad = (
        lax.psum(conv_part, "dp").astype(jnp.float32),
        lax.psum(time_part, "dp").astype(jnp.float32),
    )
    return (returned[None], conv_grad, temb_grad)


def solution(mesh):
    placed = (
        P("fsdp", "dp", None, None),
        P("fsdp", "dp", None, None),
        P("fsdp", None),
        P("fsdp", "dp"),
        P("fsdp", None),
        P("fsdp", None),
    )
    return jax.shard_map(
        per_device,
        mesh=mesh,
        in_specs=placed,
        out_specs=(P("fsdp", "dp", None, None), P("fsdp", None), P("fsdp", None)),
        check_vma=False,
    )
```

profile of v0, /device:TPU:0, one launch (start us, length us, event | category | flops | bytes accessed | tf_op | source)
XLA Modules:
  0.0 346.5 jit_solution(10692876846711080838)
XLA Ops:
  8.2 1.3 and_select_fusion.6
  13.3 5.2 %all-to-all-start.1 = ((bf16[4,4,1280]{2,1,0:T(4,128)(2,1)}), bf16[4,4,1280]{2,1,0:T(4,128)(2,1)S(1)}, u32[]{:S(2)}, u32[]{:S(2)}) async-start(bf16[4,4,1280]{2,1,0:T(4,128)(2,1)} %broadcast_select_fusion.4), calls=%async_computation.1 | async-start | bytes 81920 | tf_op jit(solution)/shard_map/all_to_all | solution.py:114
  18.6 2.2 gather_fusion.6
  20.8 4.0 %gather_fusion.4 = bf16[16,256,320]{1,2,0:T(8,128)(2,1)} fusion(bf16[15,256,320]{1,2,0:T(8,128)(2,1)} %bitcast.100, s32[1024]{0:T(1024)S(1)} %pad_clamp_fusion.5), kind=kCustom, calls=%fused_computation.clone | custom fusion | bytes 5242944 | tf_op jit(solution)/shard_map/jit(_take)/gather | solution.py:108
  24.9 4.6 %broadcast_select_fusion = (bf16[16,256,320]{1,2,0:T(8,128)(2,1)}, bf16[16,256,320]{1,2,0:T(8,128)(2,1)}) fusion(bf16[16,256,320]{1,2,0:T(8,128)(2,1)S(1)} %copy-done.2, pred[16]{0:T(512)(128)(4,1)S(1)} %compare_and_fusion.1, bf16[16,256,320]{1,2,0:T(8,128)(2,1)} %gather_fusion.4), kind=kLoop, calls=%fused_computation.28 | loop fusion | flops 2621440 | bytes 10485776 | tf_op jit(solution)/shard_map/jit(_take)/select_n | solution.py:109
  29.4 35.5 %all_to_all.20 = bf16[4,4,256,320]{2,3,1,0:T(8,128)(2,1)} all-to-all(bf16[4,4,256,320]{2,3,1,0:T(8,128)(2,1)} %bitcast.97), channel_id=1, replica_groups=mesh['fsdp'=8,'dp'=4] {'dp'}, dimensions={0} | all-to-all | bytes 5242880 | tf_op jit(solution)/shard_map/all_to_all | solution.py:113
  64.9 3.8 %all-to-all-start = ((bf16[4,4,256,320]{2,3,1,0:T(8,128)(2,1)}), bf16[4,4,256,320]{2,3,1,0:T(8,128)(2,1)S(1)}, u32[]{:S(2)}, u32[]{:S(2)}) async-start(bf16[4,4,256,320]{2,3,1,0:T(8,128)(2,1)} %bitcast.6), calls=%async_computation | async-start | bytes 5242880 | tf_op jit(solution)/shard_map/all_to_all | solution.py:112
  70.0 19.3 %all_gather.7 = bf16[1280,320]{1,0:T(8,128)(2,1)} all-gather(bf16[160,320]{1,0:T(8,128)(2,1)S(1)} %convert_element_type.63), channel_id=1, replica_groups=mesh['fsdp'=8,'dp'=4] {'fsdp'}, dimensions={0}, use_global_device_ids=true | all-gather | bytes 921600 | tf_op jit(solution)/shard_map/all_gather | solution.py:47
  89.8 1.5 fusion.6
  91.3 3.5 %gather_fusion.7 = bf16[8,256,320]{1,2,0:T(8,128)(2,1)} fusion(bf16[16,256,320]{1,2,0:T(8,128)(2,1)} %bitcast.99, s32[1024]{0:T(1024)S(1)} %pad_clamp_fusion.4), kind=kCustom, calls=%fused_computation.3.clone | custom fusion | bytes 2621472 | tf_op jit(solution)/shard_map/jit(_take)/gather | solution.py:117
  94.8 3.1 all-to-all-done
  97.9 1.5 copy-done.3
  99.4 2.4 gather_fusion.5
  104.5 2.0 multiply_convert_fusion.1
  106.5 1.8 copy.36
  108.4 5.9 %pad_slice_fusion = (bf16[8,16,16,320]{3,2,1,0:T(8,128)(2,1)}, bf16[8,16,16,320]{3,2,1,0:T(8,128)(2,1)}, bf16[8,16,16,320]{3,2,1,0:T(8,128)(2,1)}, bf16[8,16,16,...) fusion(bf16[8,16,16,320]{3,2,1,0:T(8,128)(2,1)S(1)} %bitcast.78), kind=kLoop, calls=%fused_computation.8 | loop fusion | bytes 11796480 | tf_op jit(solution)/shard_map/slice | solution.py:40
  114.3 2.6 copy.37
  116.8 2.6 copy.38
  119.4 2.5 copy.39
  121.9 2.5 copy.40
  124.5 2.5 copy.41
  127.0 2.5 copy.42
  129.6 2.6 copy.43
  132.1 2.5 copy.44
  134.6 19.3 %concatenate.63 = bf16[2048,2880]{1,0:T(8,128)(2,1)} concatenate(bf16[2048,320]{1,0:T(8,128)(2,1)} %bitcast.95, bf16[2048,320]{1,0:T(8,128)(2,1)} %bitcast.83, bf16[2048,320]{1,0:T(8,128)(2,1)} %bitcast.85, bf16[2048,320]{1,0:T(8,128)(2,1)} %bitcast.87, bf16[2048,320]{1,0:T(8,128)(2,1)S(1)} %bitcast.79, bf16[2048,320]{1,0:T(8,128)(2,1)} %bitcast.89, bf16[2048,320]{1,0:T(8,128)(2,1)} %bitcast.91, ...), dimensions={1} | concatenate | bytes 23592960 | tf_op jit(solution)/shard_map/concatenate | solution.py:41
  153.9 2.6 constant_dynamic-update-slice_fusion.8
  156.5 1.2 constant_dynamic-update-slice_fusion.7
  157.7 1.2 constant_dynamic-update-slice_fusion.6
  158.9 1.2 constant_dynamic-update-slice_fusion.5
  160.1 2.0 constant_dynamic-update-slice_fusion.4
  164.4 1.2 constant_dynamic-update-slice_fusion.1
  165.6 1.2 constant_dynamic-update-slice_fusion
  166.7 2.7 copy.45
  169.4 2.7 reshape.617
  172.1 10.6 %convert_reduce_fusion.1 = (f32[8,320]{1,0:T(8,128)S(1)}, bf16[8,256,320]{1,2,0:T(8,128)(2,1)S(1)}, bf16[8,256,320]{1,2,0:T(8,128)(2,1)}) fusion(bf16[8,256,320]{1,2,0:T(8,128)(2,1)} %gather_fusion.7, f32[8,320]{1,0:T(8,128)S(1)} %fusion.6, bf16[8,256,320]{1,2,0:T(8,128)(2,1)S(1)} %gather_fusion.5, pred[8]{0:T(512)(128)(4,1)S(1)} %get-tuple-element.11, ...), kind=kOutput, calls=%fused_computation.25 | convolution fusion | flops 3782735360 | bytes 18903048 | tf_op jit(solution)/shard_map/dot_general | solution.py:49
  182.8 9.8 %convolution_convert_fusion = bf16[2880,320]{0,1:T(8,128)(2,1)} fusion(bf16[2048,320]{0,1:T(8,128)(2,1)S(1)} %bitcast.102, bf16[2048,2880]{1,0:T(8,128)(2,1)} %concatenate.63), kind=kOutput, calls=%fused_computation.16 | convolution fusion | flops 3775795200 | bytes 14950400 | tf_op jit(solution)/shard_map/dot_general | solution.py:132
  192.7 2.0 gather_fusion.2
  194.8 1.8 broadcast_select_fusion.2
  196.6 4.7 %all-to-all-start.2 = ((bf16[4,4,256,320]{2,3,1,0:T(8,128)(2,1)}), bf16[4,4,256,320]{2,3,1,0:T(8,128)(2,1)}, u32[]{:S(2)}, u32[]{:S(2)}) async-start(bf16[4,4,256,320]{2,3,1,0:T(8,128)(2,1)} %broadcast_select_fusion.2), calls=%async_computation.2 | async-start | bytes 5242880 | tf_op jit(solution)/shard_map/all_to_all | solution.py:126
  201.3 2.0 convolution_convert_fusion.1
  206.6 50.0 %all-reduce.6.cloned.1.call-done = bf16[2880,320]{0,1:T(8,128)(2,1)} async-done(((bf16[2880,320]{0,1:T(8,128)(2,1)}), bf16[2880,320]{0,1:T(8,128)(2,1)}) %all-reduce.6.cloned.1.call-update) | async-done | bytes 1843216
  256.6 1.8 constant_dynamic-slice_fusion
  258.4 32.3 %reduce-scatter.3.cloned.1.call-done = bf16[160,320]{1,0:T(8,128)(2,1)} async-done(((bf16[1280,320]{1,0:T(8,128)(2,1)}), bf16[160,320]{1,0:T(8,128)(2,1)}) %reduce-scatter.3.cloned.1.call-update) | async-done | bytes 102416 | tf_op jit(solution)/shard_map/reduce_scatter | solution.py:139
  290.7 4.0 %gather_fusion.3 = bf16[15,256,320]{1,2,0:T(8,128)(2,1)} fusion(bf16[16,256,320]{1,2,0:T(8,128)(2,1)} %bitcast.25, s32[1024]{0:T(1024)S(1)} %pad_clamp_fusion), kind=kCustom, calls=%fused_computation.7 | custom fusion | bytes 4915260 | tf_op jit(solution)/shard_map/jit(_take)/gather | solution.py:129
  294.8 3.5 %fusion.4 = bf16[1,15,256,320]{2,3,1,0:T(8,128)(2,1)} fusion(bf16[15,256,320]{1,2,0:T(8,128)(2,1)} %gather_fusion.3, pred[15]{0:T(512)(128)(4,1)S(1)} %compare_and_fusion.4, pred[15]{0:T(512)(128)(4,1)S(1)} %iota_compare_fusion.1), kind=kLoop, calls=%fused_computation.32 | loop fusion | flops 2457600 | bytes 4915230 | tf_op jit(solution)/shard_map/jit(_where)/select_n | solution.py:130
  298.2 38.4 %all-reduce.8.cloned.1.call-done = (bf16[360,320]{0,1:T(8,128)(2,1)}, bf16[160,320]{1,0:T(8,128)(2,1)}) async-done(((bf16[360,320]{0,1:T(8,128)(2,1)}, bf16[160,320]{1,0:T(8,128)(2,1)}), (bf16[360,320]{0,1:T(8,128)(2,1)}, bf16[160,320]{1,0:T(8,128)(2,1)})) %all-reduce.8.cloned.1.call-update) | async-done | bytes 332816 | tf_op jit(solution)/shard_map/psum | solution.py:143
  336.6 1.8 convert_element_type.68
  338.4 1.6 convert_element_type.71
  (94 shorter events, 14.4 us)
Async XLA Ops:
  7.2 11.4 %copy-start = (bf16[1,15,256,320]{2,3,1,0:T(8,128)(2,1)S(1)}, bf16[1,15,256,320]{2,3,1,0:T(8,128)(2,1)}, u32[]{:S(2)}) copy-start(bf16[1,15,256,320]{2,3,1,0:T(8,128)(2,1)} %param.11) | copy-start | bytes 7372804
  13.3 16.1 %all-to-all-start.1 = ((bf16[4,4,1280]{2,1,0:T(4,128)(2,1)}), bf16[4,4,1280]{2,1,0:T(4,128)(2,1)S(1)}, u32[]{:S(2)}, u32[]{:S(2)}) async-start(bf16[4,4,1280]{2,1,0:T(4,128)(2,1)} %broadcast_select_fusion.4), calls=%async_computation.1 | async-start | bytes 81920 | tf_op jit(solution)/shard_map/all_to_all | solution.py:114
  20.8 4.1 %copy-start.2 = (bf16[16,256,320]{1,2,0:T(8,128)(2,1)S(1)}, bf16[16,256,320]{1,2,0:T(8,128)(2,1)}, u32[]{:S(2)}) copy-start(bf16[16,256,320]{1,2,0:T(8,128)(2,1)} %gather_fusion.6) | copy-start | bytes 7864324
  64.9 3.9 %copy-start.11 = (f32[360,320]{0,1:T(8,128)S(1)}, f32[360,320]{0,1:T(8,128)}, u32[]{:S(2)}) copy-start(f32[360,320]{0,1:T(8,128)} %param.14) | copy-start | bytes 1382404
  64.9 4.7 %copy-start.12 = (f32[160,320]{1,0:T(8,128)S(1)}, f32[160,320]{1,0:T(8,128)}, u32[]{:S(2)}) copy-start(f32[160,320]{1,0:T(8,128)} %param.15) | copy-start | bytes 614404
  64.9 4.9 %copy-start.13 = (s32[1,4]{1,0:T(1,128)S(1)}, s32[1,4]{1,0:T(1,128)}, u32[]{:S(2)}) copy-start(s32[1,4]{1,0:T(1,128)} %param.12) | copy-start | bytes 52
  64.9 33.0 %all-to-all-start = ((bf16[4,4,256,320]{2,3,1,0:T(8,128)(2,1)}), bf16[4,4,256,320]{2,3,1,0:T(8,128)(2,1)S(1)}, u32[]{:S(2)}, u32[]{:S(2)}) async-start(bf16[4,4,256,320]{2,3,1,0:T(8,128)(2,1)} %bitcast.6), calls=%async_computation | async-start | bytes 5242880 | tf_op jit(solution)/shard_map/all_to_all | solution.py:112
  68.7 98.0 %all-gather.3.cloned.1.call-start = ((), (), s32[]{:S(2)}) async-start(), calls=%async_computation.6 | async-start | bytes 2211840 | tf_op jit(solution)/shard_map/all_gather | solution.py:51
  69.5 187.1 %all-reduce.6.cloned.1.call-start = ((), (), s32[]{:S(2)}) async-start(), calls=%async_computation.7 | async-start | bytes 3768320
  97.9 1.5 copy-start.3
  153.9 2.6 copy-start.10
  153.9 3.8 %copy-start.9 = (bf16[8,256,320]{1,2,0:T(8,128)(2,1)S(1)}, bf16[8,256,320]{1,2,0:T(8,128)(2,1)}, u32[]{:S(2)}) copy-start(bf16[8,256,320]{1,2,0:T(8,128)(2,1)} %copy.39) | copy-start | bytes 3932164
  156.5 2.3 copy-start.8
  158.9 3.2 copy-start.7
  160.1 3.2 copy-start.6
  162.1 2.3 copy-start.5
  163.2 2.3 copy-start.4
  196.6 6.8 %copy-start.14 = (u32[32]{0:T(128)S(1)}, u32[32]{0:T(128)}, u32[]{:S(2)}) copy-start(u32[32]{0:T(128)} %constant.185) | copy-start | bytes 388
  196.6 94.1 %all-to-all-start.2 = ((bf16[4,4,256,320]{2,3,1,0:T(8,128)(2,1)}), bf16[4,4,256,320]{2,3,1,0:T(8,128)(2,1)}, u32[]{:S(2)}, u32[]{:S(2)}) async-start(bf16[4,4,256,320]{2,3,1,0:T(8,128)(2,1)} %broadcast_select_fusion.2), calls=%async_computation.2 | async-start | bytes 5242880 | tf_op jit(solution)/shard_map/all_to_all | solution.py:126
  201.3 89.4 %reduce-scatter.3.cloned.1.call-start = ((), (), s32[]{:S(2)}) async-start(), calls=%async_computation.5 | async-start | bytes 1105920 | tf_op jit(solution)/shard_map/reduce_scatter | solution.py:139
  203.4 133.2 %all-reduce.8.cloned.1.call-start = ((), (), s32[]{:S(2)}) async-start(), calls=%async_computation.8 | async-start | bytes 737280 | tf_op jit(solution)/shard_map/psum | solution.py:143
  290.7 49.3 %copy-start.1 = (bf16[1,15,256,320]{2,3,1,0:T(8,128)(2,1)S(1)}, bf16[1,15,256,320]{2,3,1,0:T(8,128)(2,1)}, u32[]{:S(2)}) copy-start(bf16[1,15,256,320]{2,3,1,0:T(8,128)(2,1)} %param.11) | copy-start | bytes 7372804
Sparse Core Ops, SparseCore 0:
  71.8 31.5 all-gather.2
  192.8 63.7 all-reduce.5
  259.0 31.6 reduce-scatter.2
  294.2 42.3 all-reduce.7
where the time goes:
time: 349 us; the launch traced here: 347 us
  waiting for transfers between devices  124 us (36%)
  local copies, waits for them, and re-layouts  88 us (25%)
  blocking collectives  54.8 us (16%)
  other arithmetic  27.5 us (8%)
  matrix products  23.9 us (7%)
  between operations  14.8 us (4%)
  starting transfers between devices  13.8 us (4%)
    unnamed x5, waiting for transfers between devices  50.1 us
    concatenate x10, local copies, waits for them, and re-layouts, unfold(): jnp.concatenate(shifted, axis=-1).reshape(number * pixels, 9 * channels)  40.8 us
    psum x1, waiting for transfers between devices, per_device(): lax.psum(conv_part, 'dp').astype(jnp.float32)  38.4 us
    all_to_all x1, blocking collectives, per_device(): lax.all_to_all(out_targets, 'dp', split_axis=0, concat_axis=0, tiled=True)  35.5 us
    reduce_scatter x1, waiting for transfers between devices, per_device(): lax.psum_scatter(temb_term.astype(jnp.bfloat16), 'fsdp', scatter_dimensio...  32.3 us
    all_gather x1, blocking collectives, predict(): lax.all_gather(temb_master.astype(jnp.bfloat16), 'fsdp', axis=0, tiled=True)  19.3 us
    unnamed x40, local copies, waits for them, and re-layouts  16.2 us
    dot_general x1, matrix products, predict(): jnp.dot(columns, lax.all_gather(conv_master.astype(jnp.bfloat16), 'fsdp',...  10.6 us
  transfers between devices with their start and end apart: 7, of which 4 were waited for; matrix products, arithmetic and copies ran while one was open for 30% of the time, Pallas kernels for 0%

commit v1 on v0

v1 whole, which is shorter than its diff:
```python
import functools
import math

import jax
import jax.numpy as jnp
from jax import lax
from jax.experimental import pallas as pl
from jax.experimental.pallas import tpu as pltpu
from jax.sharding import PartitionSpec as P

GROUPS = 32
SIDE = 16
LANES = 128

bf16 = jnp.bfloat16
f32 = jnp.float32


def tiles_per_step(number):
    return max(size for size in range(1, 6) if number % size == 0)


def norm_kernel(group_width, same_ref, tiles_ref, out_ref):
    same_group = same_ref[...]
    number, channels, pixels = tiles_ref.shape
    scale = 1.0 / (group_width * pixels)
    lane = lax.broadcasted_iota(jnp.int32, (channels, LANES), 1)

    def group_mean(row_sums):
        high = row_sums.astype(bf16).astype(f32)
        middle = (row_sums - high).astype(bf16).astype(f32)
        low = row_sums - high - middle
        terms = jnp.where(
            lane == 0, high, jnp.where(lane == 1, middle, jnp.where(lane == 2, low, 0.0))
        ).astype(bf16)
        summed = jnp.dot(same_group, terms, preferred_element_type=f32)
        return jnp.sum(summed, axis=1, keepdims=True) * scale

    for at in range(number):
        values = tiles_ref[at].astype(f32)
        centred = values - group_mean(jnp.sum(values, axis=1, keepdims=True))
        variance = group_mean(jnp.sum(centred * centred, axis=1, keepdims=True))
        scaled = centred * lax.rsqrt(variance + 1e-05)
        out_ref[at] = (scaled / (1.0 + jnp.exp(-scaled))).astype(bf16)


def group_norm(tiles):
    number, channels, pixels = tiles.shape
    step = tiles_per_step(number)
    group_width = channels // GROUPS
    group = jnp.arange(channels, dtype=jnp.int32) // group_width
    same_group = (group[:, None] == group[None, :]).astype(bf16)
    block = pl.BlockSpec((step, channels, pixels), lambda i: (i, 0, 0))
    return pl.pallas_call(
        functools.partial(norm_kernel, group_width),
        grid=(number // step,),
        in_specs=[pl.BlockSpec((channels, channels), lambda i: (0, 0)), block],
        out_specs=block,
        out_shape=jax.ShapeDtypeStruct(tiles.shape, bf16),
        compiler_params=pltpu.CompilerParams(vmem_limit_bytes=32 * 2**20),
        cost_estimate=pl.CostEstimate(
            flops=20 * tiles.size, bytes_accessed=4 * tiles.size, transcendentals=tiles.size
        ),
        name="group_norm",
    )(same_group, tiles)


def write_columns(values, columns_ref, at):
    channels, pixels = values.shape
    cell = lax.broadcasted_iota(jnp.int32, (channels, pixels), 1)
    column = cell % SIDE
    wide = values.astype(f32)
    for b in range(3):
        if b == 1:
            moved = wide
        else:
            moved = pltpu.roll(wide, (1 - b) % pixels, 1)
            moved = jnp.where(column == (0 if b == 0 else SIDE - 1), 0.0, moved)
        for a in range(3):
            if a == 1:
                shifted = moved
            else:
                shifted = pltpu.roll(moved, ((1 - a) * SIDE) % pixels, 1)
                outside = (cell < SIDE) if a == 0 else (cell >= pixels - SIDE)
                shifted = jnp.where(outside, 0.0, shifted)
            tap = 3 * a + b
            columns_ref[
                tap * channels : (tap + 1) * channels, at * pixels : (at + 1) * pixels
            ] = shifted.astype(values.dtype)


def conv_kernel(
    steps,
    count_ref,
    weight_ref,
    normed_ref,
    tiles_ref,
    target_ref,
    bias_ref,
    predicted_ref,
    sums_ref,
    grad_ref,
    weight,
    columns,
    total,
):
    i = pl.program_id(0)
    shards, outs, rows = weight_ref.shape
    step, channels, pixels = normed_ref.shape
    count = count_ref[0]

    @pl.when(i == 0)
    def _():
        for f in range(shards):
            weight[:, f * rows : (f + 1) * rows] = weight_ref[f]
        total[...] = jnp.zeros_like(total)
        sums_ref[...] = jnp.zeros_like(sums_ref)

    @pl.when(i * step < count)
    def _():
        for t in range(step):
            write_columns(normed_ref[t], columns, t)
        conv = jnp.dot(weight[...], columns[...], preferred_element_type=f32)
        lane = lax.broadcasted_iota(jnp.int32, (outs, LANES), 1)
        errors = []
        sums = sums_ref[...]
        for t in range(step):
            slot = i * step + t
            live = slot < count
            bias = jnp.sum(jnp.where(lane == slot, bias_ref[...], 0.0), axis=1, keepdims=True)
            pred32 = tiles_ref[t].astype(f32) + conv[:, t * pixels : (t + 1) * pixels] + bias
            predicted_ref[t] = jnp.where(live, pred32, 0.0).astype(bf16)
            error = jnp.where(
                live, (pred32 - target_ref[t].astype(f32)) * (1.0 / pixels), 0.0
            ).astype(bf16)
            error_sum = jnp.sum(error.astype(f32), axis=1, keepdims=True)
            sums = jnp.where(lane == slot, error_sum, sums)
            errors.append(error)
        sums_ref[...] = sums
        total[...] += lax.dot_general(
            jnp.concatenate(errors, axis=1),
            columns[...],
            (((1,), (1,)), ((), ())),
            preferred_element_type=f32,
        )

    @pl.when(i * step >= count)
    def _():
        predicted_ref[...] = jnp.zeros_like(predicted_ref)

    @pl.when(i == steps - 1)
    def _():
        for f in range(shards):
            grad_ref[f] = total[:, f * rows : (f + 1) * rows].astype(bf16)


def conv_both(count, weight, normed, tiles, targets, bias):
    number, channels, pixels = normed.shape
    shards, outs, rows = weight.shape
    depth = shards * rows
    step = tiles_per_step(number)
    steps = number // step

    def whole(shape):
        return pl.BlockSpec(shape, lambda i, c: (0,) * len(shape))

    block = pl.BlockSpec((step, channels, pixels), lambda i, c: (i, 0, 0))
    return pl.pallas_call(
        functools.partial(conv_kernel, steps),
        grid_spec=pltpu.PrefetchScalarGridSpec(
            num_scalar_prefetch=1,
            grid=(steps,),
            in_specs=[whole(weight.shape), block, block, block, whole(bias.shape)],
            out_specs=[block, whole((outs, LANES)), whole(weight.shape)],
            scratch_shapes=[
                pltpu.VMEM((outs, depth), bf16),
                pltpu.VMEM((depth, step * pixels), bf16),
                pltpu.VMEM((outs, depth), f32),
            ],
        ),
        out_shape=[
            jax.ShapeDtypeStruct(tiles.shape, bf16),
            jax.ShapeDtypeStruct((outs, LANES), f32),
            jax.ShapeDtypeStruct(weight.shape, bf16),
        ],
        compiler_params=pltpu.CompilerParams(vmem_limit_bytes=56 * 2**20),
        cost_estimate=pl.CostEstimate(
            flops=4 * number * pixels * depth * outs, bytes_accessed=8 * tiles.size, transcendentals=0
        ),
        name="conv_both",
    )(count, weight, normed, tiles, targets, bias)


def swap(values, axis, mask):
    pairs = [(i, i ^ mask) for i in range(lax.axis_size(axis))]
    return lax.ppermute(values, axis, pairs)


def bit_groups(low, high, width=2):
    return [(at, min(width, high - at)) for at in range(low, high, width)]


def block_at(values, index):
    return lax.dynamic_index_in_dim(values, index, 0, keepdims=False)


def scatter_bits(values, axis, low, width):
    mine = (lax.axis_index(axis) >> low) & ((1 << width) - 1)
    got = [
        swap(block_at(values, mine ^ other), axis, other << low) for other in range(1, 1 << width)
    ]
    total = block_at(values, mine).astype(f32)
    for part in got:
        total = total + part.astype(f32)
    return total.astype(values.dtype)


def gather_bits(values, axis, low, width):
    mine = (lax.axis_index(axis) >> low) & ((1 << width) - 1)
    got = [values] + [swap(values, axis, other << low) for other in range(1, 1 << width)]
    if width == 1:
        first = mine == 0
        return jnp.stack([jnp.where(first, got[0], got[1]), jnp.where(first, got[1], got[0])])
    stacked = jnp.stack(got)
    return jnp.stack([block_at(stacked, mine ^ s) for s in range(1 << width)])


def bits_of(axis):
    return (lax.axis_size(axis) - 1).bit_length()


def gather_axis(values, axis):
    shape = values.shape
    values = values[None]
    for low in range(bits_of(axis)):
        values = gather_bits(values, axis, low, 1)
        values = values.reshape((-1,) + shape)
    return values


def time_rows(timesteps, emb, first, rows):
    half_width = emb // 2
    index = first + jnp.arange(rows, dtype=jnp.int32)
    place = (index % half_width).astype(f32)
    frequency = jnp.exp(-math.log(10000.0) * place / half_width)
    angles = timesteps.astype(f32)[:, None] * frequency[None, :]
    waves = jnp.where(index[None, :] < half_width, jnp.cos(angles), jnp.sin(angles))
    return jax.nn.silu(waves).astype(bf16)


def per_device(latents, target_noise, counts, timesteps, conv_master, temb_master):
    tiles = jnp.swapaxes(latents[0], 1, 2)
    targets = jnp.swapaxes(target_noise[0], 1, 2)
    number, channels, pixels = tiles.shape
    shards, peers = lax.axis_size("fsdp"), lax.axis_size("dp")
    shard_bits, peer_bits = bits_of("fsdp"), bits_of("dp")
    my_shard, my_peer = lax.axis_index("fsdp"), lax.axis_index("dp")
    rows, outs = conv_master.shape
    time_depth = temb_master.shape[0]
    emb = time_depth * shards
    count = lax.dynamic_slice(counts[0], (my_peer,), (1,))

    weight = lax.all_gather(conv_master.T.astype(bf16), "fsdp", axis=0, tiled=False)
    normed = group_norm(tiles)

    column_times = gather_axis(timesteps[0], "fsdp")
    column_rows = time_rows(column_times.reshape(-1), emb, my_shard * time_depth, time_depth)
    bias = jnp.dot(column_rows, temb_master.astype(bf16), preferred_element_type=f32)
    bias = bias.reshape((shards, number, outs))
    for low in range(shard_bits):
        bias = bias.reshape((-1, 2, number, outs)).swapaxes(0, 1)
        bias = scatter_bits(bias, "fsdp", low, 1)
    bias = jnp.pad(bias.reshape(number, outs).T, ((0, 0), (0, LANES - number)))

    predicted, error_sums, grad = conv_both(count, weight, normed, tiles, targets, bias)

    all_times = gather_axis(column_times, "dp")
    sums = error_sums[:, :number].T.astype(bf16)
    all_sums = gather_axis(gather_axis(sums, "dp"), "fsdp")
    all_times = all_times.swapaxes(0, 1)
    all_rows = time_rows(all_times.reshape(-1), emb, my_shard * time_depth, time_depth)
    temb_grad = lax.dot_general(
        all_rows,
        all_sums.reshape(-1, outs),
        (((0,), (0,)), ((), ())),
        preferred_element_type=f32,
    )

    grad = scatter_bits(grad.reshape((shards // 2, 2, outs, rows)).swapaxes(0, 1), "fsdp", 0, 1)
    grad = grad.reshape((shards // 2, peers, outs // peers, rows)).swapaxes(0, 1)
    for low, width in bit_groups(0, peer_bits):
        if width < peer_bits:
            grad = grad.reshape((-1, 1 << width) + grad.shape[1:]).swapaxes(0, 1)
        grad = scatter_bits(grad, "dp", low, width)
    grad = grad.reshape((shards // 2, outs // peers, rows))
    for low, width in bit_groups(1, shard_bits):
        grad = grad.reshape((-1, 1 << width, outs // peers, rows)).swapaxes(0, 1)
        grad = scatter_bits(grad, "fsdp", low, width)
    grad = grad.reshape((1, outs // peers, rows))
    for low, width in bit_groups(0, peer_bits):
        grad = gather_bits(grad, "dp", low, width)
        grad = grad.reshape((-1, outs // peers, rows))
    conv_grad = grad.reshape(outs, rows).T.astype(f32)

    return (jnp.swapaxes(predicted, 1, 2)[None], conv_grad, temb_grad)


def solution(mesh):
    placed = (
        P("fsdp", "dp", None, None),
        P("fsdp", "dp", None, None),
        P("fsdp", None),
        P("fsdp", "dp"),
        P("fsdp", None),
        P("fsdp", None),
    )
    return jax.shard_map(
        per_device,
        mesh=mesh,
        in_specs=placed,
        out_specs=(P("fsdp", "dp", None, None), P("fsdp", None), P("fsdp", None)),
        check_vma=False,
    )
```

time: 349 us -> 139 us (0.40)
  waiting for transfers between devices: 124 us -> 43.2 us
  local copies, waits for them, and re-layouts: 88 us -> 7.45 us
  blocking collectives: 54.8 us -> 0 us
  Pallas kernels: 0 us -> 28 us
  starting transfers between devices: 13.8 us -> 35.7 us
  other arithmetic: 27.5 us -> 5.88 us
  matrix products: 23.9 us -> 4.48 us
    unnamed x5 -> x1, waiting for transfers between devices: 50.1 us -> 0.02 us
    ppermute x0 -> x23, waiting for transfers between devices: none -> 43.2 us  [swap(): return lax.ppermute(values, axis, pairs)]
    concatenate x10 -> x0, local copies, waits for them, and re-layouts: 40.8 us -> none  [unfold(): jnp.concatenate(shifted, axis=-1).reshape(number * pixels, 9 * channels)]
    psum x1 -> x0, waiting for transfers between devices: 38.4 us -> none  [per_device(): lax.psum(conv_part, 'dp').astype(jnp.float32)]
    ppermute x0 -> x23, starting transfers between devices: none -> 35.6 us  [swap(): return lax.ppermute(values, axis, pairs)]
    all_to_all x1 -> x0, blocking collectives: 35.5 us -> none  [per_device(): lax.all_to_all(out_targets, 'dp', split_axis=0, concat_axis=0, tiled=True)]
    reduce_scatter x1 -> x0, waiting for transfers between devices: 32.3 us -> none  [per_device(): lax.psum_scatter(temb_term.astype(jnp.bfloat16), 'fsdp', scatter_dimensio...]
    pallas_call x0 -> x2, Pallas kernels: none -> 28 us  [the longest x1 19.4 us: conv_both(): pl.pallas_call(functools.partial(conv_kernel, steps), grid_spec=pltpu.Pre...]
  transfers between devices with their start and end apart: 7 -> 24, of which waited for: 4 -> 13; matrix products, arithmetic and copies ran while one was open for 30% -> 9% of each run, Pallas kernels for 0% -> 6%
where the time goes in v1:
time: 139 us
  waiting for transfers between devices  43.2 us (31%)
  starting transfers between devices  35.7 us (26%)
  Pallas kernels  28 us (20%)
  between operations  14.4 us (10%)
  local copies, waits for them, and re-layouts  7.45 us (5%)
  other arithmetic  5.88 us (4%)
  matrix products  4.48 us (3%)
    ppermute x23, waiting for transfers between devices, swap(): return lax.ppermute(values, axis, pairs)  43.2 us
    ppermute x23, starting transfers between devices, swap(): return lax.ppermute(values, axis, pairs)  35.6 us
    pallas_call x1, Pallas kernels, conv_both(): pl.pallas_call(functools.partial(conv_kernel, steps), grid_spec=pltpu.Pre...  19.4 us
    pallas_call x1, Pallas kernels, group_norm(): pl.pallas_call(functools.partial(norm_kernel, group_width), grid=(number...  8.67 us
    dot_general x1, matrix products, per_device(): lax.dot_general(all_rows, all_sums.reshape(-1, outs), (((0,), (0,)), ((),...  2.79 us
  transfers between devices with their start and end apart: 24, of which 13 were waited for; matrix products, arithmetic and copies ran while one was open for 9% of the time, Pallas kernels for 6%

profile of v1, /device:TPU:0, one launch (start us, length us, event | category | flops | bytes accessed | tf_op | source)
XLA Modules:
  0.0 139.1 jit_solution(2572744443468366393)
XLA Ops:
  7.2 1.9 %convert_bitcast_fusion.1 = bf16[320,360]{1,0:T(8,128)(2,1)} fusion(f32[360,320]{0,1:T(8,128)} %param.10), kind=kLoop, calls=%fused_computation.29 | loop fusion | flops 115200 | bytes 691200 | tf_op jit(solution)/shard_map/convert_element_type | solution.py:263
  9.2 0.5 collective-permute-start
  9.7 0.9 collective-permute-done
  10.6 0.7 fusion.41
  11.3 2.9 %collective-permute-start.1 = (s32[2,15]{1,0:T(2,128)S(1)}, s32[2,15]{1,0:T(2,128)S(1)}, u32[]{:S(2)}, u32[]{:S(2)}) collective-permute-start(s32[2,15]{1,0:T(2,128)S(1)} %bitcast.158), channel_id=1, source_target_pairs={{0,8},{4,12},{8,0},{12,4},{16,24},{20,28},{24,16},{28,20},{1,9},{5... | collective-permute-start | bytes 368 | tf_op jit(solution)/shard_map/ppermute | solution.py:196
  14.2 1.5 %collective-permute-done.1 = s32[2,15]{1,0:T(2,128)S(1)} collective-permute-done((s32[2,15]{1,0:T(2,128)S(1)}, s32[2,15]{1,0:T(2,128)S(1)}, u32[]{:S(2)}, u32[]{:S(2)}) %collective-permute-start.1) | collective-permute-done | bytes 152 | tf_op jit(solution)/shard_map/ppermute | solution.py:196
  15.7 3.1 %collective-permute-start.2 = (s32[4,15]{1,0:T(4,128)S(1)}, s32[4,15]{1,0:T(4,128)S(1)}, u32[]{:S(2)}, u32[]{:S(2)}) collective-permute-start(s32[4,15]{1,0:T(4,128)S(1)} %bitcast.156), channel_id=1, source_target_pairs={{0,16},{4,20},{8,24},{12,28},{16,0},{20,4},{24,8},{28,12},{1,17},{... | collective-permute-start | bytes 728 | tf_op jit(solution)/shard_map/ppermute | solution.py:196
  18.8 1.6 %collective-permute-done.2 = s32[4,15]{1,0:T(4,128)S(1)} collective-permute-done((s32[4,15]{1,0:T(4,128)S(1)}, s32[4,15]{1,0:T(4,128)S(1)}, u32[]{:S(2)}, u32[]{:S(2)}) %collective-permute-start.2) | collective-permute-done | bytes 272 | tf_op jit(solution)/shard_map/ppermute | solution.py:196
  20.5 1.7 %fusion.24 = f32[120,320]{1,0:T(8,128)S(1)} fusion(f32[160,320]{1,0:T(8,128)} %param.11, f32[160]{0:T(256)S(1)} %fusion.39, f32[120]{0:T(128)S(1)} %convert_element_type.118, pred[160]{0:T(512)(128)(4,1)S(1)} %fusion.40), kind=kOutput, calls=%fused_computation.46 | convolution fusion | flops 12473600 | bytes 359680 | tf_op jit(solution)/shard_map/dot_general | solution.py:268
  22.4 1.3 collective-permute-done.3
  23.7 0.2 copy.37
  23.8 1.9 %collective-permute-start.4 = (f32[2,15,320]{1,2,0:T(8,128)S(1)}, f32[2,15,320]{1,2,0:T(8,128)S(1)}, u32[]{:S(2)}, u32[]{:S(2)}) collective-permute-start(f32[2,15,320]{1,2,0:T(8,128)S(1)} %bitcast.145), channel_id=1, source_target_pairs={{0,8},{4,12},{8,0},{12,4},{16,24},{20,28},{24,16},{28,20},{1,9},{5... | collective-permute-start | bytes 115208 | tf_op jit(solution)/shard_map/ppermute | solution.py:196
  25.9 0.7 constant_dynamic-slice_fusion.10
  26.6 8.7 %group_norm.1.normed_ref = bf16[15,320,256]{2,1,0:T(8,128)(2,1)S(1)} custom-call(bf16[320,320]{1,0:T(8,128)(2,1)S(1)} %compare_convert_fusion.same_ref, bf16[15,320,256]{2,1,0:T(8,128)(2,1)S(1)} %bitcast.137), custom_call_target="tpu_custom_call" | custom-call | flops 24576000 | bytes 4915200 | tf_op jit(solution)/shard_map/group_norm/pallas_call | solution.py:54
  35.3 1.4 %copy-done.2 = bf16[15,320,256]{2,1,0:T(8,128)(2,1)} copy-done((bf16[15,320,256]{2,1,0:T(8,128)(2,1)}, bf16[15,320,256]{2,1,0:T(8,128)(2,1)S(1)}, u32[]{:S(2)}) %copy-start.2) | copy-done | bytes 2457624
  36.7 1.5 %collective-permute-start.16 = (s32[1,8,15]{2,1,0:T(8,128)S(1)}, s32[1,8,15]{2,1,0:T(8,128)S(1)}, u32[]{:S(2)}, u32[]{:S(2)}) collective-permute-start(s32[1,8,15]{2,1,0:T(8,128)S(1)} %bitcast.154), channel_id=1, source_target_pairs={{0,1},{1,0},{2,3},{3,2},{4,5},{5,4},{6,7},{7,6},{8,9},{9,8},{10,11... | collective-permute-start | bytes 1448 | tf_op jit(solution)/shard_map/ppermute | solution.py:196
  38.4 7.6 %collective-permute-done.4 = f32[2,15,320]{1,2,0:T(8,128)S(1)} collective-permute-done((f32[2,15,320]{1,2,0:T(8,128)S(1)}, f32[2,15,320]{1,2,0:T(8,128)S(1)}, u32[]{:S(2)}, u32[]{:S(2)}) %collective-permute-start.4) | collective-permute-done | bytes 38432 | tf_op jit(solution)/shard_map/ppermute | solution.py:196
  46.1 0.5 collective-permute-start.5
  46.6 9.8 %collective-permute-done.5 = f32[1,15,320]{1,2,0:T(8,128)S(1)} collective-permute-done((f32[1,15,320]{1,2,0:T(8,128)S(1)}, f32[1,15,320]{1,2,0:T(8,128)S(1)}, u32[]{:S(2)}, u32[]{:S(2)}) %collective-permute-start.5) | collective-permute-done | bytes 19232 | tf_op jit(solution)/shard_map/ppermute | solution.py:196
  56.4 0.7 pad.4.bias_ref
  57.1 19.4 %conv_both.1 = (bf16[15,320,256]{2,1,0:T(8,128)(2,1)}, f32[320,128]{1,0:T(8,128)}, bf16[8,320,360]{2,1,0:T(8,128)(2,1)}) custom-call(s32[1]{0:T(128)} %bitcast.count_ref, bf16[8,320,360]{2,1,0:T(8,128)(2,1)} %bitcast.161, bf16[15,320,256]{2,1,0:T(8,128)(2,1)} %copy-done.2, bf16[15,320,256]{2,1,0:T(8,128)(2,1)} %bitcast.136, bf16[15,320,256]{2,1,0:T(8,128)(2,1)} %bitcast.160, ...), custom_call_target="tpu_custom_call" | custom-call | flops 14155776000 | bytes 9830400 | tf_op jit(solution)/shard_map/conv_both/pallas_call | solution.py:168
  76.5 0.9 fusion.26
  77.5 7.9 %collective-permute-start.17 = (s32[2,8,15]{2,1,0:T(8,128)S(1)}, s32[2,8,15]{2,1,0:T(8,128)S(1)}, u32[]{:S(2)}, u32[]{:S(2)}) collective-permute-start(s32[2,8,15]{2,1,0:T(8,128)S(1)} %add_bitcast_fusion.1), channel_id=1, source_target_pairs={{0,2},{1,3},{2,0},{3,1},{4,6},{5,7},{6,4},{7,5},{8,10},{9,11},{10,... | collective-permute-start | bytes 2888 | tf_op jit(solution)/shard_map/ppermute | solution.py:196
  85.4 0.9 select_bitcast_fusion.5
  86.7 4.4 %collective-permute-start.19 = (bf16[2,15,320]{2,0,1:T(2,128)(2,1)S(1)}, bf16[2,15,320]{2,0,1:T(2,128)(2,1)S(1)}, u32[]{:S(2)}, u32[]{:S(2)}) collective-permute-start(bf16[2,15,320]{2,0,1:T(2,128)(2,1)S(1)} %maximum_bitcast_fusion.1), channel_id=1, source_target_pairs={{0,2},{1,3},{2,0},{3,1},{4,6},{5,7},{6,4},{7,5},{8,10},{9,11},{10,... | collective-permute-start | bytes 57608 | tf_op jit(solution)/shard_map/ppermute | solution.py:196
  91.1 2.4 %dynamic-slice_bitcast_fusion = bf16[4,320,360]{2,1,0:T(8,128)(2,1)} fusion(bf16[4,2,320,360]{3,2,1,0:T(8,128)(2,1)} %bitcast.140, s32[]{:T(128)S(6)} %select_n.225), kind=kLoop, calls=%fused_computation.2 | loop fusion | bytes 1843204 | tf_op jit(solution)/shard_map/jit(dynamic_index_in_dim)/squeeze | solution.py:204
  93.7 0.6 collective-permute-start.20
  94.3 1.9 %collective-permute-done.20 = bf16[1,4,15,320]{3,2,1,0:T(8,128)(2,1)S(1)} collective-permute-done((bf16[1,4,15,320]{3,2,1,0:T(8,128)(2,1)S(1)}, bf16[1,4,15,320]{3,2,1,0:T(8,128)(2,1)S(1)}, u32[]{:S(2)}, u32[]{:S(2)}) %collective-permute-start.20) | collective-permute-done | bytes 38432 | tf_op jit(solution)/shard_map/ppermute | solution.py:196
  96.5 4.6 %collective-permute-done.21 = bf16[2,4,15,320]{3,1,2,0:T(4,128)(2,1)S(1)} collective-permute-done((bf16[2,4,15,320]{3,1,2,0:T(4,128)(2,1)S(1)}, bf16[2,4,15,320]{3,1,2,0:T(4,128)(2,1)S(1)}, u32[]{:S(2)}, u32[]{:S(2)}) %collective-permute-start.21) | collective-permute-done | bytes 76832 | tf_op jit(solution)/shard_map/ppermute | solution.py:196
  101.4 0.5 collective-permute-start.22
  101.9 0.3 fusion
  102.3 1.5 %collective-permute-start.7 = (bf16[4,80,360]{2,1,0:T(8,128)(2,1)S(1)}, bf16[4,80,360]{2,1,0:T(8,128)(2,1)S(1)}, u32[]{:S(2)}, u32[]{:S(2)}) collective-permute-start(bf16[4,80,360]{2,1,0:T(8,128)(2,1)S(1)} %get-tuple-element.9), channel_id=1, source_target_pairs={{0,1},{1,0},{2,3},{3,2},{4,5},{5,4},{6,7},{7,6},{8,9},{9,8},{10,11... | collective-permute-start | bytes 691208 | tf_op jit(solution)/shard_map/ppermute | solution.py:196
  103.8 0.3 collective-permute-start.8
  104.1 1.8 %collective-permute-start.9 = (bf16[4,80,360]{2,1,0:T(8,128)(2,1)S(1)}, bf16[4,80,360]{2,1,0:T(8,128)(2,1)S(1)}, u32[]{:S(2)}, u32[]{:S(2)}) collective-permute-start(bf16[4,80,360]{2,1,0:T(8,128)(2,1)S(1)} %get-tuple-element.10), channel_id=1, source_target_pairs={{0,3},{1,2},{2,1},{3,0},{4,7},{5,6},{6,5},{7,4},{8,11},{9,10},{10,... | collective-permute-start | bytes 691208 | tf_op jit(solution)/shard_map/ppermute | solution.py:196
  105.8 6.8 %collective-permute-done.22 = bf16[4,4,15,320]{3,2,1,0:T(8,128)(2,1)S(1)} collective-permute-done((bf16[4,4,15,320]{3,2,1,0:T(8,128)(2,1)S(1)}, bf16[4,4,15,320]{3,2,1,0:T(8,128)(2,1)S(1)}, u32[]{:S(2)}, u32[]{:S(2)}) %collective-permute-start.22) | collective-permute-done | bytes 153632 | tf_op jit(solution)/shard_map/ppermute | solution.py:196
  112.8 3.2 %collective-permute-done.8 = bf16[4,80,360]{2,1,0:T(8,128)(2,1)S(1)} collective-permute-done((bf16[4,80,360]{2,1,0:T(8,128)(2,1)S(1)}, bf16[4,80,360]{2,1,0:T(8,128)(2,1)S(1)}, u32[]{:S(2)}, u32[]{:S(2)}) %collective-permute-start.8) | collective-permute-done | bytes 230432 | tf_op jit(solution)/shard_map/ppermute | solution.py:196
  116.2 1.5 %collective-permute-start.10 = (bf16[1,80,360]{2,1,0:T(8,128)(2,1)S(1)}, bf16[1,80,360]{2,1,0:T(8,128)(2,1)S(1)}, u32[]{:S(2)}, u32[]{:S(2)}) collective-permute-start(bf16[1,80,360]{2,1,0:T(8,128)(2,1)S(1)} %get-tuple-element.18), channel_id=1, source_target_pairs={{0,8},{4,12},{8,0},{12,4},{16,24},{20,28},{24,16},{28,20},{1,9},{5... | collective-permute-start | bytes 172808 | tf_op jit(solution)/shard_map/ppermute | solution.py:196
  117.7 0.3 collective-permute-start.11
  118.0 2.7 %collective-permute-start.12 = (bf16[1,80,360]{2,1,0:T(8,128)(2,1)S(1)}, bf16[1,80,360]{2,1,0:T(8,128)(2,1)S(1)}, u32[]{:S(2)}, u32[]{:S(2)}) collective-permute-start(bf16[1,80,360]{2,1,0:T(8,128)(2,1)S(1)} %get-tuple-element.19), channel_id=1, source_target_pairs={{0,24},{4,28},{8,16},{12,20},{16,8},{20,12},{24,0},{28,4},{1,25},{... | collective-permute-start | bytes 172808 | tf_op jit(solution)/shard_map/ppermute | solution.py:196
  120.7 0.2 reshape_reshape.9
  120.9 0.2 collective-permute-done.10
  121.1 3.0 %collective-permute-done.11 = bf16[1,80,360]{2,1,0:T(8,128)(2,1)S(1)} collective-permute-done((bf16[1,80,360]{2,1,0:T(8,128)(2,1)S(1)}, bf16[1,80,360]{2,1,0:T(8,128)(2,1)S(1)}, u32[]{:S(2)}, u32[]{:S(2)}) %collective-permute-start.11) | collective-permute-done | bytes 57632 | tf_op jit(solution)/shard_map/ppermute | solution.py:196
  124.2 1.6 %collective-permute-start.13 = (bf16[1,80,360]{2,1,0:T(8,128)(2,1)S(1)}, bf16[1,80,360]{2,1,0:T(8,128)(2,1)S(1)}, u32[]{:S(2)}, u32[]{:S(2)}) collective-permute-start(bf16[1,80,360]{2,1,0:T(8,128)(2,1)S(1)} %add_convert_fusion), channel_id=1, source_target_pairs={{0,1},{1,0},{2,3},{3,2},{4,5},{5,4},{6,7},{7,6},{8,9},{9,8},{10,11... | collective-permute-start | bytes 172808 | tf_op jit(solution)/shard_map/ppermute | solution.py:196
  125.7 0.4 collective-permute-start.14
  126.1 1.6 %collective-permute-start.15 = (bf16[1,80,360]{2,1,0:T(8,128)(2,1)S(1)}, bf16[1,80,360]{2,1,0:T(8,128)(2,1)S(1)}, u32[]{:S(2)}, u32[]{:S(2)}) collective-permute-start(bf16[1,80,360]{2,1,0:T(8,128)(2,1)S(1)} %add_convert_fusion), channel_id=1, source_target_pairs={{0,3},{1,2},{2,1},{3,0},{4,7},{5,6},{6,5},{7,4},{8,11},{9,10},{10,... | collective-permute-start | bytes 172808 | tf_op jit(solution)/shard_map/ppermute | solution.py:196
  127.7 2.8 %fusion.11 = f32[160,320]{1,0:T(8,128)} fusion(bf16[480,320]{1,0:T(8,128)(2,1)S(1)} %reshape_reshape.9, f32[160]{0:T(256)S(1)} %fusion.39, f32[480]{0:T(512)S(1)} %convert_element_type.143, pred[160]{0:T(512)(128)(4,1)S(1)} %fusion.40), kind=kOutput, calls=%fused_computation.20 | convolution fusion | flops 49689600 | bytes 514720 | tf_op jit(solution)/shard_map/dot_general | solution.py:282
  130.5 0.7 collective-permute-done.15
  131.4 0.8 convert_bitcast_fusion
  (70 shorter events, 2.6 us)
Async XLA Ops:
  7.2 18.8 %copy-start = (s32[1,4]{1,0:T(1,128)S(1)}, s32[1,4]{1,0:T(1,128)}, u32[]{:S(2)}) copy-start(s32[1,4]{1,0:T(1,128)} %param.8) | copy-start | bytes 52
  7.2 19.4 %copy-start.1 = (bf16[1,15,256,320]{2,3,1,0:T(8,128)(2,1)S(1)}, bf16[1,15,256,320]{2,3,1,0:T(8,128)(2,1)}, u32[]{:S(2)}) copy-start(bf16[1,15,256,320]{2,3,1,0:T(8,128)(2,1)} %param.6) | copy-start | bytes 7372804
  7.2 49.9 %all-gather.3.cloned.1.call-start = ((), (), s32[]{:S(2)}) async-start(), calls=%async_computation | async-start | bytes 2211840 | tf_op jit(solution)/shard_map/all_gather | solution.py:263
  9.2 1.5 %collective-permute-start = (s32[1,15]{1,0:T(1,128)}, s32[1,15]{1,0:T(1,128)S(1)}, u32[]{:S(2)}, u32[]{:S(2)}) collective-permute-start(s32[1,15]{1,0:T(1,128)} %param.9), channel_id=1, source_target_pairs={{0,4},{4,0},{8,12},{12,8},{16,20},{20,16},{24,28},{28,24},{1,5},{5... | collective-permute-start | bytes 188 | tf_op jit(solution)/shard_map/ppermute | solution.py:196
  11.3 4.4 %collective-permute-start.1 = (s32[2,15]{1,0:T(2,128)S(1)}, s32[2,15]{1,0:T(2,128)S(1)}, u32[]{:S(2)}, u32[]{:S(2)}) collective-permute-start(s32[2,15]{1,0:T(2,128)S(1)} %bitcast.158), channel_id=1, source_target_pairs={{0,8},{4,12},{8,0},{12,4},{16,24},{20,28},{24,16},{28,20},{1,9},{5... | collective-permute-start | bytes 368 | tf_op jit(solution)/shard_map/ppermute | solution.py:196
  15.7 4.7 %collective-permute-start.2 = (s32[4,15]{1,0:T(4,128)S(1)}, s32[4,15]{1,0:T(4,128)S(1)}, u32[]{:S(2)}, u32[]{:S(2)}) collective-permute-start(s32[4,15]{1,0:T(4,128)S(1)} %bitcast.156), channel_id=1, source_target_pairs={{0,16},{4,20},{8,24},{12,28},{16,0},{20,4},{24,8},{28,12},{1,17},{... | collective-permute-start | bytes 728 | tf_op jit(solution)/shard_map/ppermute | solution.py:196
  22.3 1.4 collective-permute-start.3
  23.8 22.2 %collective-permute-start.4 = (f32[2,15,320]{1,2,0:T(8,128)S(1)}, f32[2,15,320]{1,2,0:T(8,128)S(1)}, u32[]{:S(2)}, u32[]{:S(2)}) collective-permute-start(f32[2,15,320]{1,2,0:T(8,128)S(1)} %bitcast.145), channel_id=1, source_target_pairs={{0,8},{4,12},{8,0},{12,4},{16,24},{20,28},{24,16},{28,20},{1,9},{5... | collective-permute-start | bytes 115208 | tf_op jit(solution)/shard_map/ppermute | solution.py:196
  35.3 1.4 %copy-start.2 = (bf16[15,320,256]{2,1,0:T(8,128)(2,1)}, bf16[15,320,256]{2,1,0:T(8,128)(2,1)S(1)}, u32[]{:S(2)}) copy-start(bf16[15,320,256]{2,1,0:T(8,128)(2,1)S(1)} %group_norm.1.normed_ref) | copy-start | bytes 7372804
  36.7 9.9 %collective-permute-start.16 = (s32[1,8,15]{2,1,0:T(8,128)S(1)}, s32[1,8,15]{2,1,0:T(8,128)S(1)}, u32[]{:S(2)}, u32[]{:S(2)}) collective-permute-start(s32[1,8,15]{2,1,0:T(8,128)S(1)} %bitcast.154), channel_id=1, source_target_pairs={{0,1},{1,0},{2,3},{3,2},{4,5},{5,4},{6,7},{7,6},{8,9},{9,8},{10,11... | collective-permute-start | bytes 1448 | tf_op jit(solution)/shard_map/ppermute | solution.py:196
  46.1 10.3 %collective-permute-start.5 = (f32[1,15,320]{1,2,0:T(8,128)S(1)}, f32[1,15,320]{1,2,0:T(8,128)S(1)}, u32[]{:S(2)}, u32[]{:S(2)}) collective-permute-start(f32[1,15,320]{1,2,0:T(8,128)S(1)} %constant_dynamic-slice_fusion.7), channel_id=1, source_target_pairs={{0,16},{4,20},{8,24},{12,28},{16,0},{20,4},{24,8},{28,12},{1,17},{... | collective-permute-start | bytes 57608 | tf_op jit(solution)/shard_map/ppermute | solution.py:196
  77.4 8.0 %collective-permute-start.18 = (bf16[1,15,320]{1,2,0:T(8,128)(2,1)S(1)}, bf16[1,15,320]{1,2,0:T(8,128)(2,1)S(1)}, u32[]{:S(2)}, u32[]{:S(2)}) collective-permute-start(bf16[1,15,320]{1,2,0:T(8,128)(2,1)S(1)} %fusion.26), channel_id=1, source_target_pairs={{0,1},{1,0},{2,3},{3,2},{4,5},{5,4},{6,7},{7,6},{8,9},{9,8},{10,11... | collective-permute-start | bytes 28808 | tf_op jit(solution)/shard_map/ppermute | solution.py:196
  77.5 16.8 %collective-permute-start.17 = (s32[2,8,15]{2,1,0:T(8,128)S(1)}, s32[2,8,15]{2,1,0:T(8,128)S(1)}, u32[]{:S(2)}, u32[]{:S(2)}) collective-permute-start(s32[2,8,15]{2,1,0:T(8,128)S(1)} %add_bitcast_fusion.1), channel_id=1, source_target_pairs={{0,2},{1,3},{2,0},{3,1},{4,6},{5,7},{6,4},{7,5},{8,10},{9,11},{10,... | collective-permute-start | bytes 2888 | tf_op jit(solution)/shard_map/ppermute | solution.py:196
  86.7 6.8 %collective-permute-start.19 = (bf16[2,15,320]{2,0,1:T(2,128)(2,1)S(1)}, bf16[2,15,320]{2,0,1:T(2,128)(2,1)S(1)}, u32[]{:S(2)}, u32[]{:S(2)}) collective-permute-start(bf16[2,15,320]{2,0,1:T(2,128)(2,1)S(1)} %maximum_bitcast_fusion.1), channel_id=1, source_target_pairs={{0,2},{1,3},{2,0},{3,1},{4,6},{5,7},{6,4},{7,5},{8,10},{9,11},{10,... | collective-permute-start | bytes 57608 | tf_op jit(solution)/shard_map/ppermute | solution.py:196
  91.1 10.8 %copy-start.3 = (bf16[8,320,360]{2,1,0:T(8,128)(2,1)S(1)}, bf16[8,320,360]{2,1,0:T(8,128)(2,1)}, u32[]{:S(2)}) copy-start(bf16[8,320,360]{2,1,0:T(8,128)(2,1)} %get-tuple-element.7) | copy-start | bytes 5529604
  93.5 8.4 %collective-permute-start.6 = (bf16[4,320,360]{2,1,0:T(8,128)(2,1)}, bf16[4,320,360]{2,1,0:T(8,128)(2,1)S(1)}, u32[]{:S(2)}, u32[]{:S(2)}) collective-permute-start(bf16[4,320,360]{2,1,0:T(8,128)(2,1)} %dynamic-slice_bitcast_fusion), channel_id=1, source_target_pairs={{0,4},{4,0},{8,12},{12,8},{16,20},{20,16},{24,28},{28,24},{1,5},{5... | collective-permute-start | bytes 2764808 | tf_op jit(solution)/shard_map/ppermute | solution.py:196
  93.7 2.4 %collective-permute-start.20 = (bf16[1,4,15,320]{3,2,1,0:T(8,128)(2,1)S(1)}, bf16[1,4,15,320]{3,2,1,0:T(8,128)(2,1)S(1)}, u32[]{:S(2)}, u32[]{:S(2)}) collective-permute-start(bf16[1,4,15,320]{3,2,1,0:T(8,128)(2,1)S(1)} %bitcast.147), channel_id=1, source_target_pairs={{0,4},{4,0},{8,12},{12,8},{16,20},{20,16},{24,28},{28,24},{1,5},{5... | collective-permute-start | bytes 115208 | tf_op jit(solution)/shard_map/ppermute | solution.py:196
  96.3 4.8 %collective-permute-start.21 = (bf16[2,4,15,320]{3,1,2,0:T(4,128)(2,1)S(1)}, bf16[2,4,15,320]{3,1,2,0:T(4,128)(2,1)S(1)}, u32[]{:S(2)}, u32[]{:S(2)}) collective-permute-start(bf16[2,4,15,320]{3,1,2,0:T(4,128)(2,1)S(1)} %maximum_bitcast_fusion), channel_id=1, source_target_pairs={{0,8},{4,12},{8,0},{12,4},{16,24},{20,28},{24,16},{28,20},{1,9},{5... | collective-permute-start | bytes 230408 | tf_op jit(solution)/shard_map/ppermute | solution.py:196
  101.4 11.3 %collective-permute-start.22 = (bf16[4,4,15,320]{3,2,1,0:T(8,128)(2,1)S(1)}, bf16[4,4,15,320]{3,2,1,0:T(8,128)(2,1)S(1)}, u32[]{:S(2)}, u32[]{:S(2)}) collective-permute-start(bf16[4,4,15,320]{3,2,1,0:T(8,128)(2,1)S(1)} %copy.49), channel_id=1, source_target_pairs={{0,16},{4,20},{8,24},{12,28},{16,0},{20,4},{24,8},{28,12},{1,17},{... | collective-permute-start | bytes 460808 | tf_op jit(solution)/shard_map/ppermute | solution.py:196
  102.3 10.5 %collective-permute-start.7 = (bf16[4,80,360]{2,1,0:T(8,128)(2,1)S(1)}, bf16[4,80,360]{2,1,0:T(8,128)(2,1)S(1)}, u32[]{:S(2)}, u32[]{:S(2)}) collective-permute-start(bf16[4,80,360]{2,1,0:T(8,128)(2,1)S(1)} %get-tuple-element.9), channel_id=1, source_target_pairs={{0,1},{1,0},{2,3},{3,2},{4,5},{5,4},{6,7},{7,6},{8,9},{9,8},{10,11... | collective-permute-start | bytes 691208 | tf_op jit(solution)/shard_map/ppermute | solution.py:196
  103.8 12.2 %collective-permute-start.8 = (bf16[4,80,360]{2,1,0:T(8,128)(2,1)S(1)}, bf16[4,80,360]{2,1,0:T(8,128)(2,1)S(1)}, u32[]{:S(2)}, u32[]{:S(2)}) collective-permute-start(bf16[4,80,360]{2,1,0:T(8,128)(2,1)S(1)} %get-tuple-element.11), channel_id=1, source_target_pairs={{0,2},{1,3},{2,0},{3,1},{4,6},{5,7},{6,4},{7,5},{8,10},{9,11},{10,... | collective-permute-start | bytes 691208 | tf_op jit(solution)/shard_map/ppermute | solution.py:196
  104.1 11.9 %collective-permute-start.9 = (bf16[4,80,360]{2,1,0:T(8,128)(2,1)S(1)}, bf16[4,80,360]{2,1,0:T(8,128)(2,1)S(1)}, u32[]{:S(2)}, u32[]{:S(2)}) collective-permute-start(bf16[4,80,360]{2,1,0:T(8,128)(2,1)S(1)} %get-tuple-element.10), channel_id=1, source_target_pairs={{0,3},{1,2},{2,1},{3,0},{4,7},{5,6},{6,5},{7,4},{8,11},{9,10},{10,... | collective-permute-start | bytes 691208 | tf_op jit(solution)/shard_map/ppermute | solution.py:196
  116.2 4.9 %collective-permute-start.10 = (bf16[1,80,360]{2,1,0:T(8,128)(2,1)S(1)}, bf16[1,80,360]{2,1,0:T(8,128)(2,1)S(1)}, u32[]{:S(2)}, u32[]{:S(2)}) collective-permute-start(bf16[1,80,360]{2,1,0:T(8,128)(2,1)S(1)} %get-tuple-element.18), channel_id=1, source_target_pairs={{0,8},{4,12},{8,0},{12,4},{16,24},{20,28},{24,16},{28,20},{1,9},{5... | collective-permute-start | bytes 172808 | tf_op jit(solution)/shard_map/ppermute | solution.py:196
  117.7 6.4 %collective-permute-start.11 = (bf16[1,80,360]{2,1,0:T(8,128)(2,1)S(1)}, bf16[1,80,360]{2,1,0:T(8,128)(2,1)S(1)}, u32[]{:S(2)}, u32[]{:S(2)}) collective-permute-start(bf16[1,80,360]{2,1,0:T(8,128)(2,1)S(1)} %get-tuple-element.20), channel_id=1, source_target_pairs={{0,16},{4,20},{8,24},{12,28},{16,0},{20,4},{24,8},{28,12},{1,17},{... | collective-permute-start | bytes 172808 | tf_op jit(solution)/shard_map/ppermute | solution.py:196
  118.0 6.1 %collective-permute-start.12 = (bf16[1,80,360]{2,1,0:T(8,128)(2,1)S(1)}, bf16[1,80,360]{2,1,0:T(8,128)(2,1)S(1)}, u32[]{:S(2)}, u32[]{:S(2)}) collective-permute-start(bf16[1,80,360]{2,1,0:T(8,128)(2,1)S(1)} %get-tuple-element.19), channel_id=1, source_target_pairs={{0,24},{4,28},{8,16},{12,20},{16,8},{20,12},{24,0},{28,4},{1,25},{... | collective-permute-start | bytes 172808 | tf_op jit(solution)/shard_map/ppermute | solution.py:196
  124.2 6.3 %collective-permute-start.13 = (bf16[1,80,360]{2,1,0:T(8,128)(2,1)S(1)}, bf16[1,80,360]{2,1,0:T(8,128)(2,1)S(1)}, u32[]{:S(2)}, u32[]{:S(2)}) collective-permute-start(bf16[1,80,360]{2,1,0:T(8,128)(2,1)S(1)} %add_convert_fusion), channel_id=1, source_target_pairs={{0,1},{1,0},{2,3},{3,2},{4,5},{5,4},{6,7},{7,6},{8,9},{9,8},{10,11... | collective-permute-start | bytes 172808 | tf_op jit(solution)/shard_map/ppermute | solution.py:196
  125.7 4.8 %collective-permute-start.14 = (bf16[1,80,360]{2,1,0:T(8,128)(2,1)S(1)}, bf16[1,80,360]{2,1,0:T(8,128)(2,1)S(1)}, u32[]{:S(2)}, u32[]{:S(2)}) collective-permute-start(bf16[1,80,360]{2,1,0:T(8,128)(2,1)S(1)} %add_convert_fusion), channel_id=1, source_target_pairs={{0,2},{1,3},{2,0},{3,1},{4,6},{5,7},{6,4},{7,5},{8,10},{9,11},{10,... | collective-permute-start | bytes 172808 | tf_op jit(solution)/shard_map/ppermute | solution.py:196
  126.1 5.1 %collective-permute-start.15 = (bf16[1,80,360]{2,1,0:T(8,128)(2,1)S(1)}, bf16[1,80,360]{2,1,0:T(8,128)(2,1)S(1)}, u32[]{:S(2)}, u32[]{:S(2)}) collective-permute-start(bf16[1,80,360]{2,1,0:T(8,128)(2,1)S(1)} %add_convert_fusion), channel_id=1, source_target_pairs={{0,3},{1,2},{2,1},{3,0},{4,7},{5,6},{6,5},{7,4},{8,11},{9,10},{10,... | collective-permute-start | bytes 172808 | tf_op jit(solution)/shard_map/ppermute | solution.py:196
Sparse Core Ops, SparseCore 0:
  10.2 36.4 all-gather.2

commit v2 on v1

v2 whole, which is shorter than its diff:
```python
import functools
import math

import jax
import jax.numpy as jnp
from jax import lax
from jax.experimental import pallas as pl
from jax.experimental.pallas import tpu as pltpu
from jax.sharding import PartitionSpec as P

GROUPS = 32
SIDE = 16
LANES = 128

bf16 = jnp.bfloat16
f32 = jnp.float32


def tiles_per_step(number):
    return max(size for size in range(1, 6) if number % size == 0)


def norm_kernel(group_width, same_ref, tiles_ref, out_ref):
    same_group = same_ref[...]
    number, channels, pixels = tiles_ref.shape
    scale = 1.0 / (group_width * pixels)
    lane = lax.broadcasted_iota(jnp.int32, (channels, LANES), 1)

    def group_mean(row_sums):
        high = row_sums.astype(bf16).astype(f32)
        middle = (row_sums - high).astype(bf16).astype(f32)
        low = row_sums - high - middle
        terms = jnp.where(
            lane == 0, high, jnp.where(lane == 1, middle, jnp.where(lane == 2, low, 0.0))
        ).astype(bf16)
        summed = jnp.dot(same_group, terms, preferred_element_type=f32)
        return jnp.sum(summed, axis=1, keepdims=True) * scale

    for at in range(number):
        values = tiles_ref[at].astype(f32)
        centred = values - group_mean(jnp.sum(values, axis=1, keepdims=True))
        variance = group_mean(jnp.sum(centred * centred, axis=1, keepdims=True))
        scaled = centred * lax.rsqrt(variance + 1e-05)
        out_ref[at] = (scaled / (1.0 + jnp.exp(-scaled))).astype(bf16)


def group_norm(tiles):
    number, channels, pixels = tiles.shape
    step = tiles_per_step(number)
    group_width = channels // GROUPS
    group = jnp.arange(channels, dtype=jnp.int32) // group_width
    same_group = (group[:, None] == group[None, :]).astype(bf16)
    block = pl.BlockSpec((step, channels, pixels), lambda i: (i, 0, 0))
    return pl.pallas_call(
        functools.partial(norm_kernel, group_width),
        grid=(number // step,),
        in_specs=[pl.BlockSpec((channels, channels), lambda i: (0, 0)), block],
        out_specs=block,
        out_shape=jax.ShapeDtypeStruct(tiles.shape, bf16),
        compiler_params=pltpu.CompilerParams(vmem_limit_bytes=32 * 2**20),
        cost_estimate=pl.CostEstimate(
            flops=20 * tiles.size, bytes_accessed=4 * tiles.size, transcendentals=tiles.size
        ),
        name="group_norm",
    )(same_group, tiles)


def write_columns(values, columns_ref, at):
    channels, pixels = values.shape
    cell = lax.broadcasted_iota(jnp.int32, (channels, pixels), 1)
    column = cell % SIDE
    wide = values.astype(f32)
    for b in range(3):
        if b == 1:
            moved = wide
        else:
            moved = pltpu.roll(wide, (1 - b) % pixels, 1)
            moved = jnp.where(column == (0 if b == 0 else SIDE - 1), 0.0, moved)
        for a in range(3):
            if a == 1:
                shifted = moved
            else:
                shifted = pltpu.roll(moved, ((1 - a) * SIDE) % pixels, 1)
                outside = (cell < SIDE) if a == 0 else (cell >= pixels - SIDE)
                shifted = jnp.where(outside, 0.0, shifted)
            tap = 3 * a + b
            columns_ref[
                tap * channels : (tap + 1) * channels, at * pixels : (at + 1) * pixels
            ] = shifted.astype(values.dtype)


def conv_kernel(
    steps,
    where_ref,
    own_ref,
    other_ref,
    features_ref,
    normed_ref,
    tiles_ref,
    target_ref,
    predicted_ref,
    keep_ref,
    send_ref,
    weight,
    time_weight,
    bias,
    sums,
    columns,
    total,
):
    i = pl.program_id(0)
    parts, planes, part_rows, width = own_ref.shape
    step, channels, pixels = normed_ref.shape
    shards = 2 * planes
    rows = weight.shape[1] // shards
    time_rows = width - rows
    count, core, plane, part = (where_ref[n] for n in range(4))
    outs = parts * part_rows
    lane = lax.broadcasted_iota(jnp.int32, (outs, LANES), 1)

    @pl.when(i == 0)
    def _():
        for f in range(shards):
            for q in range(parts):
                at = (q ^ part, (f // 2) ^ plane)
                block = jnp.where(core == f % 2, own_ref[at], other_ref[at])
                into = slice(q * part_rows, (q + 1) * part_rows)
                weight[into, f * rows : (f + 1) * rows] = block[:, :rows]
                time_weight[into, f * time_rows : (f + 1) * time_rows] = block[:, rows:]
        bias[...] = jnp.dot(time_weight[...], features_ref[...], preferred_element_type=f32)
        total[...] = jnp.zeros_like(total)
        sums[...] = jnp.zeros_like(sums)

    @pl.when(i * step < count)
    def _():
        for t in range(step):
            write_columns(normed_ref[t], columns, t)
        conv = jnp.dot(weight[...], columns[...], preferred_element_type=f32)
        errors = []
        error_sums = sums[...]
        for t in range(step):
            slot = i * step + t
            live = slot < count
            tile_bias = jnp.sum(jnp.where(lane == slot, bias[...], 0.0), axis=1, keepdims=True)
            pred32 = tiles_ref[t].astype(f32) + conv[:, t * pixels : (t + 1) * pixels] + tile_bias
            predicted_ref[t] = jnp.where(live, pred32, 0.0).astype(bf16)
            error = jnp.where(
                live, (pred32 - target_ref[t].astype(f32)) * (1.0 / pixels), 0.0
            ).astype(bf16)
            error_sum = jnp.sum(error.astype(f32), axis=1, keepdims=True)
            error_sums = jnp.where(lane == slot, error_sum, error_sums)
            errors.append(error)
        sums[...] = error_sums
        total[...] += lax.dot_general(
            jnp.concatenate(errors, axis=1),
            columns[...],
            (((1,), (1,)), ((), ())),
            preferred_element_type=f32,
        )

    @pl.when(i * step >= count)
    def _():
        predicted_ref[...] = jnp.zeros_like(predicted_ref)

    @pl.when(i == steps - 1)
    def _():
        high = sums[...].astype(bf16)
        low = (sums[...] - high.astype(f32)).astype(bf16)
        time_total = sum(
            lax.dot_general(
                term, features_ref[...], (((1,), (1,)), ((), ())), preferred_element_type=f32
            )
            for term in (high, low)
        )
        for c in range(2):
            for f in range(shards):
                into = keep_ref if f % 2 == c else send_ref

                @pl.when(core == c)
                def _():
                    for q in range(parts):
                        at = (q ^ part, (f // 2) ^ plane)
                        here = slice(q * part_rows, (q + 1) * part_rows)
                        into[at] = jnp.concatenate(
                            [
                                total[here, f * rows : (f + 1) * rows],
                                time_total[here, f * time_rows : (f + 1) * time_rows],
                            ],
                            axis=1,
                        ).astype(bf16)


def conv_both(where, own, other, features, normed, tiles, targets, rows):
    number, channels, pixels = normed.shape
    parts, planes, part_rows, width = own.shape
    shards, outs = 2 * planes, parts * part_rows
    depth, emb = shards * rows, shards * (width - rows)
    step = tiles_per_step(number)
    steps = number // step

    def whole(shape):
        return pl.BlockSpec(shape, lambda i, c: (0,) * len(shape))

    block = pl.BlockSpec((step, channels, pixels), lambda i, c: (i, 0, 0))
    return pl.pallas_call(
        functools.partial(conv_kernel, steps),
        grid_spec=pltpu.PrefetchScalarGridSpec(
            num_scalar_prefetch=1,
            grid=(steps,),
            in_specs=[whole(own.shape), whole(own.shape), whole(features.shape)] + [block] * 3,
            out_specs=[block, whole(own.shape), whole(own.shape)],
            scratch_shapes=[
                pltpu.VMEM((outs, depth), bf16),
                pltpu.VMEM((outs, emb), bf16),
                pltpu.VMEM((outs, LANES), f32),
                pltpu.VMEM((outs, LANES), f32),
                pltpu.VMEM((depth, step * pixels), bf16),
                pltpu.VMEM((outs, depth), f32),
            ],
        ),
        out_shape=[
            jax.ShapeDtypeStruct(tiles.shape, bf16),
            jax.ShapeDtypeStruct(own.shape, bf16),
            jax.ShapeDtypeStruct(own.shape, bf16),
        ],
        compiler_params=pltpu.CompilerParams(vmem_limit_bytes=56 * 2**20),
        cost_estimate=pl.CostEstimate(
            flops=4 * number * pixels * depth * outs, bytes_accessed=8 * tiles.size, transcendentals=0
        ),
        name="conv_both",
    )(where, own, other, features, normed, tiles, targets)


def swap(values, axis, mask):
    pairs = [(i, i ^ mask) for i in range(lax.axis_size(axis))]
    return lax.ppermute(values, axis, pairs)


def bits_of(axis):
    return (lax.axis_size(axis) - 1).bit_length()


def bit_groups(bits):
    return [(at, min(2, bits - at)) for at in range(0, bits, 2)]


def gather_partners(values, axis, low, bits):
    shape = values.shape
    values = values[None]
    for at, width in bit_groups(bits):
        parts = [values] + [swap(values, axis, m << (low + at)) for m in range(1, 1 << width)]
        values = jnp.concatenate(parts)
    return values.reshape((1 << bits,) + shape)


def add_up(parts):
    total = parts[0].astype(f32)
    for part in parts[1:]:
        total = total + part.astype(f32)
    return total.astype(parts[0].dtype)


def scatter_partners(values, axis, low, bits):
    shape = values.shape[1:]
    for at, width in bit_groups(bits):
        values = values.reshape((-1, 1 << width) + shape)
        parts = [values[:, 0]]
        parts += [swap(values[:, m], axis, m << (low + at)) for m in range(1, 1 << width)]
        values = add_up(parts)
    return values.reshape(shape)


def time_features(timesteps, emb):
    half_width = emb // 2
    frequency = jnp.exp(-math.log(10000.0) * jnp.arange(half_width, dtype=f32) / half_width)
    angles = frequency[:, None] * timesteps.astype(f32)[None, :]
    return jax.nn.silu(jnp.concatenate([jnp.cos(angles), jnp.sin(angles)])).astype(bf16)


def per_device(latents, target_noise, counts, timesteps, conv_master, temb_master):
    tiles = jnp.swapaxes(latents[0], 1, 2)
    targets = jnp.swapaxes(target_noise[0], 1, 2)
    number = tiles.shape[0]
    shards = lax.axis_size("fsdp")
    shard_bits, peer_bits = bits_of("fsdp"), bits_of("dp")
    my_shard, my_peer = lax.axis_index("fsdp"), lax.axis_index("dp")
    rows, outs = conv_master.shape
    time_rows = temb_master.shape[0]
    part_bits = max(n for n in range(peer_bits + 1) if outs % (16 << n) == 0)
    parts = 1 << part_bits
    part = my_peer & (parts - 1)
    plane_bits = shard_bits - 1
    core, plane = my_shard & 1, my_shard >> 1
    where = jnp.stack([counts[0][my_peer], core, plane, part]).astype(jnp.int32)

    master = jnp.concatenate([conv_master.T, temb_master.T], axis=1).astype(bf16)
    master = master.reshape(parts, outs // parts, rows + time_rows)
    mine = [lax.dynamic_index_in_dim(master, part ^ m, 0, keepdims=False) for m in range(parts)]
    over_planes = gather_partners(mine[0], "fsdp", 1, plane_bits)
    tiles_then, over_planes = lax.optimization_barrier((tiles, over_planes))
    normed = group_norm(tiles_then)
    features = time_features(jnp.pad(timesteps[0], (0, LANES - number)), time_rows * shards)
    far = gather_partners(over_planes[1:], "dp", 0, part_bits)
    own = jnp.concatenate([jnp.stack(mine)[:, None], far], axis=1)
    other = swap(own, "fsdp", 1)

    predicted, keep, send = conv_both(where, own, other, features, normed, tiles, targets, rows)

    grad = add_up([keep, swap(send, "fsdp", 1)])
    grad = scatter_partners(grad, "dp", 0, part_bits)
    for bit in range(part_bits, peer_bits):
        grad = add_up([grad, swap(grad, "dp", 1 << bit)])
    grad = scatter_partners(grad, "fsdp", 1, plane_bits)
    grad = gather_partners(grad, "dp", 0, part_bits)
    grad = jnp.concatenate(
        [lax.dynamic_index_in_dim(grad, part ^ q, 0, keepdims=False) for q in range(parts)]
    ).astype(f32)
    return (jnp.swapaxes(predicted, 1, 2)[None], grad[:, :rows].T, grad[:, rows:].T)


def solution(mesh):
    placed = (
        P("fsdp", "dp", None, None),
        P("fsdp", "dp", None, None),
        P("fsdp", None),
        P("fsdp", "dp"),
        P("fsdp", None),
        P("fsdp", None),
    )
    return jax.shard_map(
        per_device,
        mesh=mesh,
        in_specs=placed,
        out_specs=(P("fsdp", "dp", None, None), P("fsdp", None), P("fsdp", None)),
        check_vma=False,
    )
```

time: 139 us -> 127 us (0.914)
  between operations: 14.4 us -> 0.81 us
  waiting for transfers between devices: 43.2 us -> 55.5 us
  starting transfers between devices: 35.7 us -> 25.8 us
  matrix products: 4.48 us -> 0 us
  other arithmetic: 5.88 us -> 9.82 us
  local copies, waits for them, and re-layouts: 7.45 us -> 4.11 us
  Pallas kernels: 28 us -> 30.7 us
    ppermute x23 -> x17, waiting for transfers between devices: 43.2 us -> 55.5 us  [swap(): return lax.ppermute(values, axis, pairs)]
    ppermute x23 -> x17, starting transfers between devices: 35.6 us -> 25.8 us  [swap(): return lax.ppermute(values, axis, pairs)]
    dot_general x2 -> x0, matrix products: 4.48 us -> none  [the longest x1 2.79 us: per_device(): lax.dot_general(all_rows, all_sums.reshape(-1, outs), (((0,), (0,)), ((),...]
    pallas_call x1, Pallas kernels: 19.4 us -> 22.1 us  [conv_both(): pl.pallas_call(functools.partial(conv_kernel, steps), grid_spec=pltpu.Pre...]
    squeeze x5 -> x3, local copies, waits for them, and re-layouts: 2.59 us -> 0.2 us  [the longest x2 0.14 us: scatter_partners(): values[:, m]]
    convert_element_type x6 -> x5, other arithmetic: 3.19 us -> 1.25 us  [the longest x1 0.91 us: time_features(): jax.nn.silu(jnp.concatenate([jnp.cos(angles), jnp.sin(angles)]))]
    concatenate x0 -> x3, other arithmetic: none -> 1.76 us  [the longest x1 1.52 us: per_device(): own = jnp.concatenate([jnp.stack(mine)[:, None], far], axis=1)]
    reshape x3 -> x1, other arithmetic: 0.14 us -> 1.86 us  [scatter_partners(): values = values.reshape((-1, 1 << width) + shape)]
  transfers between devices with their start and end apart: 24 -> 17, of which waited for: 13 -> 15; matrix products, arithmetic and copies ran while one was open for 9% -> 3% of each run, Pallas kernels for 6% -> 7%
where the time goes in v2:
time: 127 us
  waiting for transfers between devices  55.5 us (44%)
  Pallas kernels  30.7 us (24%)
  starting transfers between devices  25.8 us (20%)
  other arithmetic  9.82 us (8%)
  local copies, waits for them, and re-layouts  4.11 us (3%)
    ppermute x17, waiting for transfers between devices, swap(): return lax.ppermute(values, axis, pairs)  55.5 us
    ppermute x17, starting transfers between devices, swap(): return lax.ppermute(values, axis, pairs)  25.8 us
    pallas_call x1, Pallas kernels, conv_both(): pl.pallas_call(functools.partial(conv_kernel, steps), grid_spec=pltpu.Pre...  22.1 us
    pallas_call x1, Pallas kernels, group_norm(): pl.pallas_call(functools.partial(norm_kernel, group_width), grid=(number...  8.65 us
  transfers between devices with their start and end apart: 17, of which 15 were waited for; matrix products, arithmetic and copies ran while one was open for 3% of the time, Pallas kernels for 7%

profile of v2, /device:TPU:0, one launch (start us, length us, event | category | flops | bytes accessed | tf_op | source)
XLA Modules:
  0.0 126.7 jit_solution(8728409296057165247)
XLA Ops:
  0.7 1.0 convert_bitcast_fusion.1
  1.6 0.1 copy.12
  1.8 1.1 convert.12
  2.8 0.2 fusion.14
  3.0 5.1 %collective-permute-start.2 = (bf16[1,80,520]{2,1,0:T(8,128)(2,1)S(1)}, bf16[1,80,520]{2,1,0:T(8,128)(2,1)S(1)}, u32[]{:S(2)}, u32[]{:S(2)}) collective-permute-start(bf16[1,80,520]{2,1,0:T(8,128)(2,1)S(1)} %get-tuple-element.30), channel_id=1, source_target_pairs={{0,24},{4,28},{8,16},{12,20},{16,8},{20,12},{24,0},{28,4},{1,25},{... | collective-permute-start | bytes 249608 | tf_op jit(solution)/shard_map/ppermute | solution.py:236
  8.1 0.6 collective-permute-start
  8.8 3.2 %collective-permute-done.2 = bf16[1,80,520]{2,1,0:T(8,128)(2,1)S(1)} collective-permute-done((bf16[1,80,520]{2,1,0:T(8,128)(2,1)S(1)}, bf16[1,80,520]{2,1,0:T(8,128)(2,1)S(1)}, u32[]{:S(2)}, u32[]{:S(2)}) %collective-permute-start.2) | collective-permute-done | bytes 83232 | tf_op jit(solution)/shard_map/ppermute | solution.py:236
  11.9 4.8 %collective-permute-done.1 = bf16[1,80,520]{2,1,0:T(8,128)(2,1)S(1)} collective-permute-done((bf16[1,80,520]{2,1,0:T(8,128)(2,1)S(1)}, bf16[1,80,520]{2,1,0:T(8,128)(2,1)S(1)}, u32[]{:S(2)}, u32[]{:S(2)}) %collective-permute-start.1) | collective-permute-done | bytes 83232 | tf_op jit(solution)/shard_map/ppermute | solution.py:236
  16.7 0.1 fusion.6
  16.9 2.5 %collective-permute-start.5 = (bf16[1,3,80,520]{3,2,1,0:T(8,128)(2,1)S(1)}, bf16[1,3,80,520]{3,2,1,0:T(8,128)(2,1)S(1)}, u32[]{:S(2)}, u32[]{:S(2)}) collective-permute-start(bf16[1,3,80,520]{3,2,1,0:T(8,128)(2,1)S(1)} %slice_bitcast_fusion.5), channel_id=1, source_target_pairs={{0,3},{1,2},{2,1},{3,0},{4,7},{5,6},{6,5},{7,4},{8,11},{9,10},{10,... | collective-permute-start | bytes 748808 | tf_op jit(solution)/shard_map/ppermute | solution.py:236
  19.4 0.5 collective-permute-start.4
  20.0 0.5 collective-permute-start.3
  20.5 7.7 %collective-permute-done.5 = bf16[1,3,80,520]{3,2,1,0:T(8,128)(2,1)S(1)} collective-permute-done((bf16[1,3,80,520]{3,2,1,0:T(8,128)(2,1)S(1)}, bf16[1,3,80,520]{3,2,1,0:T(8,128)(2,1)S(1)}, u32[]{:S(2)}, u32[]{:S(2)}) %collective-permute-start.5) | collective-permute-done | bytes 249632 | tf_op jit(solution)/shard_map/ppermute | solution.py:236
  28.1 4.7 %collective-permute-done.4 = bf16[1,3,80,520]{3,2,1,0:T(8,128)(2,1)S(1)} collective-permute-done((bf16[1,3,80,520]{3,2,1,0:T(8,128)(2,1)S(1)}, bf16[1,3,80,520]{3,2,1,0:T(8,128)(2,1)S(1)}, u32[]{:S(2)}, u32[]{:S(2)}) %collective-permute-start.4) | collective-permute-done | bytes 249632 | tf_op jit(solution)/shard_map/ppermute | solution.py:236
  32.8 0.1 collective-permute-done.3
  32.9 1.5 %maximum_maximum_fusion.own_ref = bf16[4,4,80,520]{3,2,1,0:T(8,128)(2,1)} fusion(bf16[1,3,80,520]{3,2,1,0:T(8,128)(2,1)S(1)} %collective-permute-done.5, bf16[1,3,80,520]{3,2,1,0:T(8,128)(2,1)S(1)} %collective-permute-done.4, bf16[1,3,80,520]{3,2,1,0:T(8,128)(2,1)S(1)} %collective-permute-done.3, bf16[1,3,80,520]{3,2,1,0:T(8,128)(2,1)S(1)} %slice_bitcast_fusion.5, ...), kind=kLoop, calls=%fused_computation.2 | loop fusion | flops 2662400 | bytes 2662400 | tf_op jit(solution)/shard_map/concatenate | solution.py:304
  34.4 0.6 constant_dynamic-slice_fusion
  35.1 1.3 %pad_add_fusion.where_ref = s32[4]{0:T(128)} fusion(s32[1]{0:T(128)} %bitcast.3, s32[1]{0:T(128)} %bitcast.2, s32[1]{0:T(128)} %bitcast.1, s32[1]{0:T(128)} %bitcast), kind=kLoop, calls=%fused_computation.62 | loop fusion | flops 12 | bytes 32 | tf_op jit(solution)/shard_map/stack | solution.py:294
  36.4 0.1 compare_convert_fusion.same_ref
  36.6 1.2 multiply_cosine_fusion
  37.8 0.9 multiply_convert_fusion.features_ref
  38.7 8.7 %group_norm.1.normed_ref = bf16[15,320,256]{2,1,0:T(8,128)(2,1)S(1)} custom-call(bf16[320,320]{1,0:T(8,128)(2,1)S(1)} %compare_convert_fusion.same_ref, bf16[15,320,256]{2,1,0:T(8,128)(2,1)S(1)} %bitcast.63), custom_call_target="tpu_custom_call" | custom-call | flops 24576000 | bytes 4915200 | tf_op jit(solution)/shard_map/group_norm/pallas_call | solution.py:54
  47.3 1.4 %copy-done.2 = bf16[15,320,256]{2,1,0:T(8,128)(2,1)} copy-done((bf16[15,320,256]{2,1,0:T(8,128)(2,1)}, bf16[15,320,256]{2,1,0:T(8,128)(2,1)S(1)}, u32[]{:S(2)}) %copy-start.2) | copy-done | bytes 2457624
  48.8 22.1 %conv_both.1 = (bf16[15,320,256]{2,1,0:T(8,128)(2,1)}, bf16[4,4,80,520]{3,2,1,0:T(8,128)(2,1)}, bf16[4,4,80,520]{3,2,1,0:T(8,128)(2,1)}) custom-call(s32[4]{0:T(128)} %pad_add_fusion.where_ref, bf16[4,4,80,520]{3,2,1,0:T(8,128)(2,1)} %maximum_maximum_fusion.own_ref, bf16[4,4,80,520]{3,2,1,0:T(8,128)(2,1)} %collective-permute-done.6.other_ref, ...), custom_call_target="tpu_custom_call" | custom-call | flops 14155776000 | bytes 9830400 | tf_op jit(solution)/shard_map/conv_both/pallas_call | solution.py:205
  70.9 3.7 %collective-permute-done.7 = bf16[4,4,80,520]{3,2,1,0:T(8,128)(2,1)S(1)} collective-permute-done((bf16[4,4,80,520]{3,2,1,0:T(8,128)(2,1)}, bf16[4,4,80,520]{3,2,1,0:T(8,128)(2,1)S(1)}, u32[]{:S(2)}, u32[]{:S(2)}) %collective-permute-start.7) | collective-permute-done | bytes 1331232 | tf_op jit(solution)/shard_map/ppermute | solution.py:236
  74.6 1.9 %fusion = bf16[1,4,4,80,520]{4,3,2,1,0:T(8,128)(2,1)S(1)} fusion(bf16[4,4,80,520]{3,2,1,0:T(8,128)(2,1)S(1)} %collective-permute-done.7, bf16[4,4,80,520]{3,2,1,0:T(8,128)(2,1)} %get-tuple-element.11), kind=kLoop, calls=%fused_computation.1 | loop fusion | flops 2662400 | bytes 3993600 | tf_op jit(solution)/shard_map/reshape | solution.py:266
  76.4 0.1 slice_bitcast_fusion.3
  76.5 1.7 %collective-permute-start.8 = (bf16[1,4,80,520]{3,2,1,0:T(8,128)(2,1)S(1)}, bf16[1,4,80,520]{3,2,1,0:T(8,128)(2,1)S(1)}, u32[]{:S(2)}, u32[]{:S(2)}) collective-permute-start(bf16[1,4,80,520]{3,2,1,0:T(8,128)(2,1)S(1)} %get-tuple-element.19), channel_id=1, source_target_pairs={{0,1},{1,0},{2,3},{3,2},{4,5},{5,4},{6,7},{7,6},{8,9},{9,8},{10,11... | collective-permute-start | bytes 998408 | tf_op jit(solution)/shard_map/ppermute | solution.py:236
  78.2 7.5 %collective-permute-start.10 = (bf16[1,4,80,520]{3,2,1,0:T(8,128)(2,1)S(1)}, bf16[1,4,80,520]{3,2,1,0:T(8,128)(2,1)S(1)}, u32[]{:S(2)}, u32[]{:S(2)}) collective-permute-start(bf16[1,4,80,520]{3,2,1,0:T(8,128)(2,1)S(1)} %get-tuple-element.20), channel_id=1, source_target_pairs={{0,3},{1,2},{2,1},{3,0},{4,7},{5,6},{6,5},{7,4},{8,11},{9,10},{10,... | collective-permute-start | bytes 998408 | tf_op jit(solution)/shard_map/ppermute | solution.py:236
  85.8 3.1 %collective-permute-done.8 = bf16[1,4,80,520]{3,2,1,0:T(8,128)(2,1)S(1)} collective-permute-done((bf16[1,4,80,520]{3,2,1,0:T(8,128)(2,1)S(1)}, bf16[1,4,80,520]{3,2,1,0:T(8,128)(2,1)S(1)}, u32[]{:S(2)}, u32[]{:S(2)}) %collective-permute-start.8) | collective-permute-done | bytes 332832 | tf_op jit(solution)/shard_map/ppermute | solution.py:236
  88.9 15.3 %collective-permute-done.10 = bf16[1,4,80,520]{3,2,1,0:T(8,128)(2,1)S(1)} collective-permute-done((bf16[1,4,80,520]{3,2,1,0:T(8,128)(2,1)S(1)}, bf16[1,4,80,520]{3,2,1,0:T(8,128)(2,1)S(1)}, u32[]{:S(2)}, u32[]{:S(2)}) %collective-permute-start.10) | collective-permute-done | bytes 332832 | tf_op jit(solution)/shard_map/ppermute | solution.py:236
  104.2 1.4 %collective-permute-done.9 = bf16[1,4,80,520]{3,2,1,0:T(8,128)(2,1)S(1)} collective-permute-done((bf16[1,4,80,520]{3,2,1,0:T(8,128)(2,1)S(1)}, bf16[1,4,80,520]{3,2,1,0:T(8,128)(2,1)S(1)}, u32[]{:S(2)}, u32[]{:S(2)}) %collective-permute-start.9) | collective-permute-done | bytes 332832 | tf_op jit(solution)/shard_map/ppermute | solution.py:236
  105.5 0.2 fusion.3
  105.8 0.1 collective-permute-start.11
  105.8 2.1 %collective-permute-start.13 = (bf16[1,80,520]{2,1,0:T(8,128)(2,1)S(1)}, bf16[1,80,520]{2,1,0:T(8,128)(2,1)S(1)}, u32[]{:S(2)}, u32[]{:S(2)}) collective-permute-start(bf16[1,80,520]{2,1,0:T(8,128)(2,1)S(1)} %get-tuple-element.27), channel_id=1, source_target_pairs={{0,24},{4,28},{8,16},{12,20},{16,8},{20,12},{24,0},{28,4},{1,25},{... | collective-permute-start | bytes 249608 | tf_op jit(solution)/shard_map/ppermute | solution.py:236
  107.9 1.4 %collective-permute-start.12 = (bf16[1,80,520]{2,1,0:T(8,128)(2,1)S(1)}, bf16[1,80,520]{2,1,0:T(8,128)(2,1)S(1)}, u32[]{:S(2)}, u32[]{:S(2)}) collective-permute-start(bf16[1,80,520]{2,1,0:T(8,128)(2,1)S(1)} %get-tuple-element.28), channel_id=1, source_target_pairs={{0,16},{4,20},{8,24},{12,28},{16,0},{20,4},{24,8},{28,12},{1,17},{... | collective-permute-start | bytes 249608 | tf_op jit(solution)/shard_map/ppermute | solution.py:236
  109.3 2.7 %collective-permute-done.11 = bf16[1,80,520]{2,1,0:T(8,128)(2,1)S(1)} collective-permute-done((bf16[1,80,520]{2,1,0:T(8,128)(2,1)S(1)}, bf16[1,80,520]{2,1,0:T(8,128)(2,1)S(1)}, u32[]{:S(2)}, u32[]{:S(2)}) %collective-permute-start.11) | collective-permute-done | bytes 83232 | tf_op jit(solution)/shard_map/ppermute | solution.py:236
  112.0 1.0 collective-permute-done.13
  113.0 3.3 %collective-permute-done.12 = bf16[1,80,520]{2,1,0:T(8,128)(2,1)S(1)} collective-permute-done((bf16[1,80,520]{2,1,0:T(8,128)(2,1)S(1)}, bf16[1,80,520]{2,1,0:T(8,128)(2,1)S(1)}, u32[]{:S(2)}, u32[]{:S(2)}) %collective-permute-start.12) | collective-permute-done | bytes 83232 | tf_op jit(solution)/shard_map/ppermute | solution.py:236
  116.4 2.8 %collective-permute-start.16 = (bf16[1,80,520]{2,1,0:T(8,128)(2,1)S(1)}, bf16[1,80,520]{2,1,0:T(8,128)(2,1)S(1)}, u32[]{:S(2)}, u32[]{:S(2)}) collective-permute-start(bf16[1,80,520]{2,1,0:T(8,128)(2,1)S(1)} %fusion.11), channel_id=1, source_target_pairs={{0,3},{1,2},{2,1},{3,0},{4,7},{5,6},{6,5},{7,4},{8,11},{9,10},{10,... | collective-permute-start | bytes 249608 | tf_op jit(solution)/shard_map/ppermute | solution.py:236
  119.1 0.9 collective-permute-start.15
  120.0 2.3 %collective-permute-done.16 = bf16[1,80,520]{2,1,0:T(8,128)(2,1)S(1)} collective-permute-done((bf16[1,80,520]{2,1,0:T(8,128)(2,1)S(1)}, bf16[1,80,520]{2,1,0:T(8,128)(2,1)S(1)}, u32[]{:S(2)}, u32[]{:S(2)}) %collective-permute-start.16) | collective-permute-done | bytes 83232 | tf_op jit(solution)/shard_map/ppermute | solution.py:236
  122.3 1.5 %collective-permute-done.15 = bf16[1,80,520]{2,1,0:T(8,128)(2,1)S(1)} collective-permute-done((bf16[1,80,520]{2,1,0:T(8,128)(2,1)S(1)}, bf16[1,80,520]{2,1,0:T(8,128)(2,1)S(1)}, u32[]{:S(2)}, u32[]{:S(2)}) %collective-permute-start.15) | collective-permute-done | bytes 83232 | tf_op jit(solution)/shard_map/ppermute | solution.py:236
  123.8 0.9 collective-permute-done.14
  124.7 0.1 pad_maximum_fusion.3
  124.9 0.1 convert_bitcast_fusion
  125.0 0.8 copy.14
  125.9 0.8 slice_bitcast_fusion
  (22 shorter events, 0.3 us)
Async XLA Ops:
  0.6 33.8 %copy-start = (s32[1,4]{1,0:T(1,128)S(1)}, s32[1,4]{1,0:T(1,128)}, u32[]{:S(2)}) copy-start(s32[1,4]{1,0:T(1,128)} %param.8) | copy-start | bytes 52
  3.0 8.9 %collective-permute-start.2 = (bf16[1,80,520]{2,1,0:T(8,128)(2,1)S(1)}, bf16[1,80,520]{2,1,0:T(8,128)(2,1)S(1)}, u32[]{:S(2)}, u32[]{:S(2)}) collective-permute-start(bf16[1,80,520]{2,1,0:T(8,128)(2,1)S(1)} %get-tuple-element.30), channel_id=1, source_target_pairs={{0,24},{4,28},{8,16},{12,20},{16,8},{20,12},{24,0},{28,4},{1,25},{... | collective-permute-start | bytes 249608 | tf_op jit(solution)/shard_map/ppermute | solution.py:236
  8.1 8.6 %collective-permute-start.1 = (bf16[1,80,520]{2,1,0:T(8,128)(2,1)S(1)}, bf16[1,80,520]{2,1,0:T(8,128)(2,1)S(1)}, u32[]{:S(2)}, u32[]{:S(2)}) collective-permute-start(bf16[1,80,520]{2,1,0:T(8,128)(2,1)S(1)} %get-tuple-element.30), channel_id=1, source_target_pairs={{0,16},{4,20},{8,24},{12,28},{16,0},{20,4},{24,8},{28,12},{1,17},{... | collective-permute-start | bytes 249608 | tf_op jit(solution)/shard_map/ppermute | solution.py:236
  8.1 8.6 %collective-permute-start = (bf16[1,80,520]{2,1,0:T(8,128)(2,1)S(1)}, bf16[1,80,520]{2,1,0:T(8,128)(2,1)S(1)}, u32[]{:S(2)}, u32[]{:S(2)}) collective-permute-start(bf16[1,80,520]{2,1,0:T(8,128)(2,1)S(1)} %get-tuple-element.30), channel_id=1, source_target_pairs={{0,8},{4,12},{8,0},{12,4},{16,24},{20,28},{24,16},{28,20},{1,9},{5... | collective-permute-start | bytes 249608 | tf_op jit(solution)/shard_map/ppermute | solution.py:236
  16.9 11.2 %collective-permute-start.5 = (bf16[1,3,80,520]{3,2,1,0:T(8,128)(2,1)S(1)}, bf16[1,3,80,520]{3,2,1,0:T(8,128)(2,1)S(1)}, u32[]{:S(2)}, u32[]{:S(2)}) collective-permute-start(bf16[1,3,80,520]{3,2,1,0:T(8,128)(2,1)S(1)} %slice_bitcast_fusion.5), channel_id=1, source_target_pairs={{0,3},{1,2},{2,1},{3,0},{4,7},{5,6},{6,5},{7,4},{8,11},{9,10},{10,... | collective-permute-start | bytes 748808 | tf_op jit(solution)/shard_map/ppermute | solution.py:236
  19.4 13.4 %collective-permute-start.4 = (bf16[1,3,80,520]{3,2,1,0:T(8,128)(2,1)S(1)}, bf16[1,3,80,520]{3,2,1,0:T(8,128)(2,1)S(1)}, u32[]{:S(2)}, u32[]{:S(2)}) collective-permute-start(bf16[1,3,80,520]{3,2,1,0:T(8,128)(2,1)S(1)} %slice_bitcast_fusion.5), channel_id=1, source_target_pairs={{0,2},{1,3},{2,0},{3,1},{4,6},{5,7},{6,4},{7,5},{8,10},{9,11},{10,... | collective-permute-start | bytes 748808 | tf_op jit(solution)/shard_map/ppermute | solution.py:236
  20.0 13.0 %collective-permute-start.3 = (bf16[1,3,80,520]{3,2,1,0:T(8,128)(2,1)S(1)}, bf16[1,3,80,520]{3,2,1,0:T(8,128)(2,1)S(1)}, u32[]{:S(2)}, u32[]{:S(2)}) collective-permute-start(bf16[1,3,80,520]{3,2,1,0:T(8,128)(2,1)S(1)} %slice_bitcast_fusion.5), channel_id=1, source_target_pairs={{0,1},{1,0},{2,3},{3,2},{4,5},{5,4},{6,7},{7,6},{8,9},{9,8},{10,11... | collective-permute-start | bytes 748808 | tf_op jit(solution)/shard_map/ppermute | solution.py:236
  32.9 2.2 %copy-start.3 = (s32[1,15]{1,0:T(1,128)S(1)}, s32[1,15]{1,0:T(1,128)}, u32[]{:S(2)}) copy-start(s32[1,15]{1,0:T(1,128)} %param.9) | copy-start | bytes 184
  32.9 5.8 %copy-start.1 = (bf16[1,15,256,320]{2,3,1,0:T(8,128)(2,1)S(1)}, bf16[1,15,256,320]{2,3,1,0:T(8,128)(2,1)}, u32[]{:S(2)}) copy-start(bf16[1,15,256,320]{2,3,1,0:T(8,128)(2,1)} %param.6) | copy-start | bytes 7372804
  34.4 14.4 %collective-permute-start.6 = (bf16[4,4,80,520]{3,2,1,0:T(8,128)(2,1)}, bf16[4,4,80,520]{3,2,1,0:T(8,128)(2,1)}, u32[]{:S(2)}, u32[]{:S(2)}) collective-permute-start(bf16[4,4,80,520]{3,2,1,0:T(8,128)(2,1)} %maximum_maximum_fusion.own_ref), channel_id=1, source_target_pairs={{0,4},{4,0},{8,12},{12,8},{16,20},{20,16},{24,28},{28,24},{1,5},{5... | collective-permute-start | bytes 3993608 | tf_op jit(solution)/shard_map/ppermute | solution.py:236
  47.3 1.4 %copy-start.2 = (bf16[15,320,256]{2,1,0:T(8,128)(2,1)}, bf16[15,320,256]{2,1,0:T(8,128)(2,1)S(1)}, u32[]{:S(2)}) copy-start(bf16[15,320,256]{2,1,0:T(8,128)(2,1)S(1)} %group_norm.1.normed_ref) | copy-start | bytes 7372804
  70.9 3.7 %collective-permute-start.7 = (bf16[4,4,80,520]{3,2,1,0:T(8,128)(2,1)}, bf16[4,4,80,520]{3,2,1,0:T(8,128)(2,1)S(1)}, u32[]{:S(2)}, u32[]{:S(2)}) collective-permute-start(bf16[4,4,80,520]{3,2,1,0:T(8,128)(2,1)} %get-tuple-element.12), channel_id=1, source_target_pairs={{0,4},{4,0},{8,12},{12,8},{16,20},{20,16},{24,28},{28,24},{1,5},{5... | collective-permute-start | bytes 3993608 | tf_op jit(solution)/shard_map/ppermute | solution.py:236
  76.5 12.4 %collective-permute-start.8 = (bf16[1,4,80,520]{3,2,1,0:T(8,128)(2,1)S(1)}, bf16[1,4,80,520]{3,2,1,0:T(8,128)(2,1)S(1)}, u32[]{:S(2)}, u32[]{:S(2)}) collective-permute-start(bf16[1,4,80,520]{3,2,1,0:T(8,128)(2,1)S(1)} %get-tuple-element.19), channel_id=1, source_target_pairs={{0,1},{1,0},{2,3},{3,2},{4,5},{5,4},{6,7},{7,6},{8,9},{9,8},{10,11... | collective-permute-start | bytes 998408 | tf_op jit(solution)/shard_map/ppermute | solution.py:236
  78.2 25.9 %collective-permute-start.10 = (bf16[1,4,80,520]{3,2,1,0:T(8,128)(2,1)S(1)}, bf16[1,4,80,520]{3,2,1,0:T(8,128)(2,1)S(1)}, u32[]{:S(2)}, u32[]{:S(2)}) collective-permute-start(bf16[1,4,80,520]{3,2,1,0:T(8,128)(2,1)S(1)} %get-tuple-element.20), channel_id=1, source_target_pairs={{0,3},{1,2},{2,1},{3,0},{4,7},{5,6},{6,5},{7,4},{8,11},{9,10},{10,... | collective-permute-start | bytes 998408 | tf_op jit(solution)/shard_map/ppermute | solution.py:236
  85.8 19.7 %collective-permute-start.9 = (bf16[1,4,80,520]{3,2,1,0:T(8,128)(2,1)S(1)}, bf16[1,4,80,520]{3,2,1,0:T(8,128)(2,1)S(1)}, u32[]{:S(2)}, u32[]{:S(2)}) collective-permute-start(bf16[1,4,80,520]{3,2,1,0:T(8,128)(2,1)S(1)} %get-tuple-element.21), channel_id=1, source_target_pairs={{0,2},{1,3},{2,0},{3,1},{4,6},{5,7},{6,4},{7,5},{8,10},{9,11},{10,... | collective-permute-start | bytes 998408 | tf_op jit(solution)/shard_map/ppermute | solution.py:236
  105.8 6.2 %collective-permute-start.11 = (bf16[1,80,520]{2,1,0:T(8,128)(2,1)S(1)}, bf16[1,80,520]{2,1,0:T(8,128)(2,1)S(1)}, u32[]{:S(2)}, u32[]{:S(2)}) collective-permute-start(bf16[1,80,520]{2,1,0:T(8,128)(2,1)S(1)} %get-tuple-element.26), channel_id=1, source_target_pairs={{0,8},{4,12},{8,0},{12,4},{16,24},{20,28},{24,16},{28,20},{1,9},{5... | collective-permute-start | bytes 249608 | tf_op jit(solution)/shard_map/ppermute | solution.py:236
  105.8 7.2 %collective-permute-start.13 = (bf16[1,80,520]{2,1,0:T(8,128)(2,1)S(1)}, bf16[1,80,520]{2,1,0:T(8,128)(2,1)S(1)}, u32[]{:S(2)}, u32[]{:S(2)}) collective-permute-start(bf16[1,80,520]{2,1,0:T(8,128)(2,1)S(1)} %get-tuple-element.27), channel_id=1, source_target_pairs={{0,24},{4,28},{8,16},{12,20},{16,8},{20,12},{24,0},{28,4},{1,25},{... | collective-permute-start | bytes 249608 | tf_op jit(solution)/shard_map/ppermute | solution.py:236
  107.9 8.4 %collective-permute-start.12 = (bf16[1,80,520]{2,1,0:T(8,128)(2,1)S(1)}, bf16[1,80,520]{2,1,0:T(8,128)(2,1)S(1)}, u32[]{:S(2)}, u32[]{:S(2)}) collective-permute-start(bf16[1,80,520]{2,1,0:T(8,128)(2,1)S(1)} %get-tuple-element.28), channel_id=1, source_target_pairs={{0,16},{4,20},{8,24},{12,28},{16,0},{20,4},{24,8},{28,12},{1,17},{... | collective-permute-start | bytes 249608 | tf_op jit(solution)/shard_map/ppermute | solution.py:236
  116.4 5.9 %collective-permute-start.16 = (bf16[1,80,520]{2,1,0:T(8,128)(2,1)S(1)}, bf16[1,80,520]{2,1,0:T(8,128)(2,1)S(1)}, u32[]{:S(2)}, u32[]{:S(2)}) collective-permute-start(bf16[1,80,520]{2,1,0:T(8,128)(2,1)S(1)} %fusion.11), channel_id=1, source_target_pairs={{0,3},{1,2},{2,1},{3,0},{4,7},{5,6},{6,5},{7,4},{8,11},{9,10},{10,... | collective-permute-start | bytes 249608 | tf_op jit(solution)/shard_map/ppermute | solution.py:236
  119.1 4.7 %collective-permute-start.15 = (bf16[1,80,520]{2,1,0:T(8,128)(2,1)S(1)}, bf16[1,80,520]{2,1,0:T(8,128)(2,1)S(1)}, u32[]{:S(2)}, u32[]{:S(2)}) collective-permute-start(bf16[1,80,520]{2,1,0:T(8,128)(2,1)S(1)} %fusion.11), channel_id=1, source_target_pairs={{0,2},{1,3},{2,0},{3,1},{4,6},{5,7},{6,4},{7,5},{8,10},{9,11},{10,... | collective-permute-start | bytes 249608 | tf_op jit(solution)/shard_map/ppermute | solution.py:236
  120.0 4.7 %collective-permute-start.14 = (bf16[1,80,520]{2,1,0:T(8,128)(2,1)S(1)}, bf16[1,80,520]{2,1,0:T(8,128)(2,1)S(1)}, u32[]{:S(2)}, u32[]{:S(2)}) collective-permute-start(bf16[1,80,520]{2,1,0:T(8,128)(2,1)S(1)} %fusion.11), channel_id=1, source_target_pairs={{0,1},{1,0},{2,3},{3,2},{4,5},{5,4},{6,7},{7,6},{8,9},{9,8},{10,11... | collective-permute-start | bytes 249608 | tf_op jit(solution)/shard_map/ppermute | solution.py:236

commit v3 on v2

--- a/solution.py
+++ b/solution.py
@@ -94,6 +94,8 @@
     where_ref,
     own_ref,
     other_ref,
+    own_time_ref,
+    other_time_ref,
     features_ref,
     normed_ref,
     tiles_ref,
@@ -101,6 +103,8 @@
     predicted_ref,
     keep_ref,
     send_ref,
+    keep_time_ref,
+    send_time_ref,
     weight,
     time_weight,
     bias,
@@ -109,11 +113,10 @@
     total,
 ):
     i = pl.program_id(0)
-    parts, planes, part_rows, width = own_ref.shape
+    parts, planes, part_rows, rows = own_ref.shape
     step, channels, pixels = normed_ref.shape
     shards = 2 * planes
-    rows = weight.shape[1] // shards
-    time_rows = width - rows
+    time_rows = own_time_ref.shape[1]
     count, core, plane, part = (where_ref[n] for n in range(4))
     outs = parts * part_rows
     lane = lax.broadcasted_iota(jnp.int32, (outs, LANES), 1)
@@ -125,9 +128,17 @@
                 at = (q ^ part, (f // 2) ^ plane)
                 block = jnp.where(core == f % 2, own_ref[at], other_ref[at])
                 into = slice(q * part_rows, (q + 1) * part_rows)
-                weight[into, f * rows : (f + 1) * rows] = block[:, :rows]
-                time_weight[into, f * time_rows : (f + 1) * time_rows] = block[:, rows:]
-        bias[...] = jnp.dot(time_weight[...], features_ref[...], preferred_element_type=f32)
+                weight[into, f * rows : (f + 1) * rows] = block
+            block = jnp.where(
+                core == f % 2, own_time_ref[(f // 2) ^ plane], other_time_ref[(f // 2) ^ plane]
+            )
+            time_weight[f * time_rows : (f + 1) * time_rows, :] = block.astype(f32)
+        bias[...] = lax.dot_general(
+            time_weight[...].astype(bf16),
+            features_ref[...],
+            (((0,), (0,)), ((), ())),
+            preferred_element_type=f32,
+        )
         total[...] = jnp.zeros_like(total)
         sums[...] = jnp.zeros_like(sums)
 
@@ -168,33 +179,29 @@
         low = (sums[...] - high.astype(f32)).astype(bf16)
         time_total = sum(
             lax.dot_general(
-                term, features_ref[...], (((1,), (1,)), ((), ())), preferred_element_type=f32
+                features_ref[...], term, (((1,), (1,)), ((), ())), preferred_element_type=f32
             )
             for term in (high, low)
         )
         for c in range(2):
             for f in range(shards):
                 into = keep_ref if f % 2 == c else send_ref
+                time_into = keep_time_ref if f % 2 == c else send_time_ref
 
                 @pl.when(core == c)
                 def _():
+                    at = (f // 2) ^ plane
                     for q in range(parts):
-                        at = (q ^ part, (f // 2) ^ plane)
                         here = slice(q * part_rows, (q + 1) * part_rows)
-                        into[at] = jnp.concatenate(
-                            [
-                                total[here, f * rows : (f + 1) * rows],
-                                time_total[here, f * time_rows : (f + 1) * time_rows],
-                            ],
-                            axis=1,
-                        ).astype(bf16)
-
-
-def conv_both(where, own, other, features, normed, tiles, targets, rows):
+                        into[q ^ part, at] = total[here, f * rows : (f + 1) * rows].astype(bf16)
+                    time_into[at] = time_total[f * time_rows : (f + 1) * time_rows].astype(bf16)
+
+
+def conv_both(where, own, other, own_time, other_time, features, normed, tiles, targets):
     number, channels, pixels = normed.shape
-    parts, planes, part_rows, width = own.shape
+    parts, planes, part_rows, rows = own.shape
     shards, outs = 2 * planes, parts * part_rows
-    depth, emb = shards * rows, shards * (width - rows)
+    depth, emb = shards * rows, features.shape[0]
     step = tiles_per_step(number)
     steps = number // step
 
@@ -207,11 +214,14 @@
         grid_spec=pltpu.PrefetchScalarGridSpec(
             num_scalar_prefetch=1,
             grid=(steps,),
-            in_specs=[whole(own.shape), whole(own.shape), whole(features.shape)] + [block] * 3,
-            out_specs=[block, whole(own.shape), whole(own.shape)],
+            in_specs=[whole(own.shape)] * 2
+            + [whole(own_time.shape)] * 2
+            + [whole(features.shape)]
+            + [block] * 3,
+            out_specs=[block] + [whole(own.shape)] * 2 + [whole(own_time.shape)] * 2,
             scratch_shapes=[
                 pltpu.VMEM((outs, depth), bf16),
-                pltpu.VMEM((outs, emb), bf16),
+                pltpu.VMEM((emb, outs), f32),
                 pltpu.VMEM((outs, LANES), f32),
                 pltpu.VMEM((outs, LANES), f32),
                 pltpu.VMEM((depth, step * pixels), bf16),
@@ -222,13 +232,15 @@
             jax.ShapeDtypeStruct(tiles.shape, bf16),
             jax.ShapeDtypeStruct(own.shape, bf16),
             jax.ShapeDtypeStruct(own.shape, bf16),
+            jax.ShapeDtypeStruct(own_time.shape, bf16),
+            jax.ShapeDtypeStruct(own_time.shape, bf16),
         ],
         compiler_params=pltpu.CompilerParams(vmem_limit_bytes=56 * 2**20),
         cost_estimate=pl.CostEstimate(
             flops=4 * number * pixels * depth * outs, bytes_accessed=8 * tiles.size, transcendentals=0
         ),
         name="conv_both",
-    )(where, own, other, features, normed, tiles, targets)
+    )(where, own, other, own_time, other_time, features, normed, tiles, targets)
 
 
 def swap(values, axis, mask):
@@ -254,10 +266,18 @@
 
 
 def add_up(parts):
-    total = parts[0].astype(f32)
-    for part in parts[1:]:
-        total = total + part.astype(f32)
-    return total.astype(parts[0].dtype)
+    kept_as = parts[0].dtype
+    parts = [part.astype(f32) for part in parts]
+    while len(parts) > 1:
+        parts = [sum(parts[n : n + 2]) for n in range(0, len(parts), 2)]
+    return parts[0].astype(kept_as)
+
+
+def sum_partners(values, axis, low, bits):
+    for at, width in bit_groups(bits):
+        parts = [values] + [swap(values, axis, m << (low + at)) for m in range(1, 1 << width)]
+        values = add_up(parts)
+    return values
 
 
 def scatter_partners(values, axis, low, bits):
@@ -293,29 +313,43 @@
     core, plane = my_shard & 1, my_shard >> 1
     where = jnp.stack([counts[0][my_peer], core, plane, part]).astype(jnp.int32)
 
-    master = jnp.concatenate([conv_master.T, temb_master.T], axis=1).astype(bf16)
-    master = master.reshape(parts, outs // parts, rows + time_rows)
+    master = conv_master.T.astype(bf16).reshape(parts, outs // parts, rows)
+    time_master = temb_master.astype(bf16)
     mine = [lax.dynamic_index_in_dim(master, part ^ m, 0, keepdims=False) for m in range(parts)]
     over_planes = gather_partners(mine[0], "fsdp", 1, plane_bits)
-    tiles_then, over_planes = lax.optimization_barrier((tiles, over_planes))
+    features = time_features(jnp.pad(timesteps[0], (0, LANES - number)), time_rows * shards)
+    over_planes, features, tiles_then, time_master, where = lax.optimization_barrier(
+        (over_planes, features, tiles, time_master, where)
+    )
+    far = gather_partners(over_planes[1:], "dp", 0, part_bits)
+    own_time = gather_partners(time_master, "fsdp", 1, plane_bits)
     normed = group_norm(tiles_then)
-    features = time_features(jnp.pad(timesteps[0], (0, LANES - number)), time_rows * shards)
-    far = gather_partners(over_planes[1:], "dp", 0, part_bits)
     own = jnp.concatenate([jnp.stack(mine)[:, None], far], axis=1)
-    other = swap(own, "fsdp", 1)
-
-    predicted, keep, send = conv_both(where, own, other, features, normed, tiles, targets, rows)
+    own, own_time, normed = lax.optimization_barrier((own, own_time, normed))
+    other, other_time = swap(own, "fsdp", 1), swap(own_time, "fsdp", 1)
+
+    predicted, keep, send, keep_time, send_time = conv_both(
+        where, own, other, own_time, other_time, features, normed, tiles, targets
+    )
 
     grad = add_up([keep, swap(send, "fsdp", 1)])
+    time_grad = add_up([keep_time, swap(send_time, "fsdp", 1)])
+    grad, time_grad = lax.optimization_barrier((grad, time_grad))
     grad = scatter_partners(grad, "dp", 0, part_bits)
     for bit in range(part_bits, peer_bits):
-        grad = add_up([grad, swap(grad, "dp", 1 << bit)])
+        grad = sum_partners(grad, "dp", bit, 1)
+    time_grad = scatter_partners(time_grad, "fsdp", 1, plane_bits)
     grad = scatter_partners(grad, "fsdp", 1, plane_bits)
+    time_grad = sum_partners(time_grad, "dp", 0, peer_bits)
     grad = gather_partners(grad, "dp", 0, part_bits)
     grad = jnp.concatenate(
         [lax.dynamic_index_in_dim(grad, part ^ q, 0, keepdims=False) for q in range(parts)]
-    ).astype(f32)
-    return (jnp.swapaxes(predicted, 1, 2)[None], grad[:, :rows].T, grad[:, rows:].T)
+    )
+    return (
+        jnp.swapaxes(predicted, 1, 2)[None],
+        grad.T.astype(f32),
+        time_grad.astype(f32),
+    )
 
 
 def solution(mesh):

time: 127 us -> 107 us (0.84)
  waiting for transfers between devices: 55.5 us -> 12.7 us
  starting transfers between devices: 25.8 us -> 53 us
  Pallas kernels: 30.7 us -> 25.6 us
  other arithmetic: 9.82 us -> 11.2 us
    ppermute x17 -> x28, waiting for transfers between devices: 55.5 us -> 12.7 us  [swap(): return lax.ppermute(values, axis, pairs)]
    ppermute x17 -> x28, starting transfers between devices: 25.8 us -> 53 us  [swap(): return lax.ppermute(values, axis, pairs)]
    convert_element_type x3 -> x8, other arithmetic: 0.34 us -> 6.52 us  [the longest x4 2.77 us: add_up(): return parts[0].astype(kept_as)]
    pallas_call x1, Pallas kernels: 22.1 us -> 16.7 us  [conv_both(): pl.pallas_call(functools.partial(conv_kernel, steps), grid_spec=pltpu.Pre...]
    reshape x1, other arithmetic: 1.86 us -> 0.07 us  [scatter_partners(): return values.reshape(shape)]
    unnamed x9 -> x14, local copies, waits for them, and re-layouts: 2.3 us -> 2.56 us
  transfers between devices with their start and end apart: 17 -> 28, of which waited for: 15 -> 9; matrix products, arithmetic and copies ran while one was open for 3% -> 7% of each run, Pallas kernels for 7% -> 8%
where the time goes in v3:
time: 107 us
  starting transfers between devices  53 us (50%)
  Pallas kernels  25.6 us (24%)
  waiting for transfers between devices  12.7 us (12%)
  other arithmetic  11.2 us (10%)
  local copies, waits for them, and re-layouts  3.39 us (3%)
    ppermute x28, starting transfers between devices, swap(): return lax.ppermute(values, axis, pairs)  53 us
    pallas_call x1, Pallas kernels, conv_both(): pl.pallas_call(functools.partial(conv_kernel, steps), grid_spec=pltpu.Pre...  16.7 us
    ppermute x28, waiting for transfers between devices, swap(): return lax.ppermute(values, axis, pairs)  12.7 us
    pallas_call x1, Pallas kernels, group_norm(): pl.pallas_call(functools.partial(norm_kernel, group_width), grid=(number...  8.84 us
    convert_element_type x4, other arithmetic, add_up(): return parts[0].astype(kept_as)  2.77 us
    unnamed x14, local copies, waits for them, and re-layouts  2.56 us
  transfers between devices with their start and end apart: 28, of which 9 were waited for; matrix products, arithmetic and copies ran while one was open for 7% of the time, Pallas kernels for 8%

profile of v3, /device:TPU:0, one launch (start us, length us, event | category | flops | bytes accessed | tf_op | source)
XLA Modules:
  0.0 106.8 jit_solution(3034532454785842290)
XLA Ops:
  0.7 1.2 %convert_element_type.138 = bf16[360,320]{0,1:T(8,128)(2,1)S(1)} convert(f32[360,320]{0,1:T(8,128)} %param.10) | non-fusion elementwise | flops 115200 | bytes 691200 | tf_op jit(solution)/shard_map/convert_element_type | solution.py:316
  1.9 5.1 %collective-permute-start.2 = (bf16[1,80,360]{2,1,0:T(8,128)(2,1)S(1)}, bf16[1,80,360]{2,1,0:T(8,128)(2,1)S(1)}, u32[]{:S(2)}, u32[]{:S(2)}) collective-permute-start(bf16[1,80,360]{2,1,0:T(8,128)(2,1)S(1)} %get-tuple-element.49), channel_id=1, source_target_pairs={{0,24},{4,28},{8,16},{12,20},{16,8},{20,12},{24,0},{28,4},{1,25},{... | collective-permute-start | bytes 172808 | tf_op jit(solution)/shard_map/ppermute | solution.py:248
  7.1 0.6 collective-permute-start
  7.7 0.7 pad_convert_fusion
  8.4 1.0 convert_element_type.142
  9.4 0.6 constant_dynamic-slice_fusion.3
  10.0 1.2 %multiply_cosine_fusion = (f32[640,128]{1,0:T(8,128)S(1)}, f32[640,128]{1,0:T(8,128)S(1)}) fusion(f32[128]{0:T(128)S(1)} %pad_convert_fusion, f32[640]{0:T(1024)S(1)} %multiply_exponential_fusion), kind=kLoop, calls=%fused_computation.12 | loop fusion | flops 81920 | bytes 658432 | tf_op jit(solution)/shard_map/cos | solution.py:297
  11.2 1.0 multiply_convert_fusion.features_ref
  12.1 1.1 %pad_add_fusion.where_ref = s32[4]{0:T(128)} fusion(s32[1]{0:T(128)} %bitcast.8, s32[1]{0:T(128)} %bitcast.7, s32[1]{0:T(128)} %bitcast.6, s32[1]{0:T(128)} %bitcast.5), kind=kLoop, calls=%fused_computation.60 | loop fusion | flops 12 | bytes 32 | tf_op jit(solution)/shard_map/stack | solution.py:314
  13.4 3.8 %collective-permute-start.8 = (bf16[1,160,320]{2,1,0:T(8,128)(2,1)S(1)}, bf16[1,160,320]{2,1,0:T(8,128)(2,1)S(1)}, u32[]{:S(2)}, u32[]{:S(2)}) collective-permute-start(bf16[1,160,320]{2,1,0:T(8,128)(2,1)S(1)} %bitcast.78), channel_id=1, source_target_pairs={{0,24},{4,28},{8,16},{12,20},{16,8},{20,12},{24,0},{28,4},{1,25},{... | collective-permute-start | bytes 307208 | tf_op jit(solution)/shard_map/ppermute | solution.py:248
  17.2 0.6 collective-permute-start.6
  17.9 2.7 %collective-permute-start.5 = (bf16[1,3,80,360]{3,2,1,0:T(8,128)(2,1)S(1)}, bf16[1,3,80,360]{3,2,1,0:T(8,128)(2,1)S(1)}, u32[]{:S(2)}, u32[]{:S(2)}) collective-permute-start(bf16[1,3,80,360]{3,2,1,0:T(8,128)(2,1)S(1)} %slice_bitcast_fusion.4), channel_id=1, source_target_pairs={{0,3},{1,2},{2,1},{3,0},{4,7},{5,6},{6,5},{7,4},{8,11},{9,10},{10,... | collective-permute-start | bytes 518408 | tf_op jit(solution)/shard_map/ppermute | solution.py:248
  20.5 0.5 collective-permute-start.4
  21.0 0.5 collective-permute-done.8
  21.5 1.6 %collective-permute-start.3 = (bf16[1,3,80,360]{3,2,1,0:T(8,128)(2,1)S(1)}, bf16[1,3,80,360]{3,2,1,0:T(8,128)(2,1)S(1)}, u32[]{:S(2)}, u32[]{:S(2)}) collective-permute-start(bf16[1,3,80,360]{3,2,1,0:T(8,128)(2,1)S(1)} %slice_bitcast_fusion.4), channel_id=1, source_target_pairs={{0,1},{1,0},{2,3},{3,2},{4,5},{5,4},{6,7},{7,6},{8,9},{9,8},{10,11... | collective-permute-start | bytes 518408 | tf_op jit(solution)/shard_map/ppermute | solution.py:248
  23.2 8.8 %group_norm.1.normed_ref = bf16[15,320,256]{2,1,0:T(8,128)(2,1)S(1)} custom-call(bf16[320,320]{1,0:T(8,128)(2,1)S(1)} %compare_convert_fusion.same_ref, bf16[15,320,256]{2,1,0:T(8,128)(2,1)S(1)} %bitcast.72), custom_call_target="tpu_custom_call" | custom-call | flops 24576000 | bytes 4915200 | tf_op jit(solution)/shard_map/group_norm/pallas_call | solution.py:54
  32.0 1.4 %copy-done.2 = bf16[15,320,256]{2,1,0:T(8,128)(2,1)} copy-done((bf16[15,320,256]{2,1,0:T(8,128)(2,1)}, bf16[15,320,256]{2,1,0:T(8,128)(2,1)S(1)}, u32[]{:S(2)}) %copy-start.2) | copy-done | bytes 2457624
  33.7 0.3 maximum_maximum_fusion.own_ref
  34.0 0.5 collective-permute-start.10
  34.5 2.8 %collective-permute-done.10.other_time_ref = bf16[4,160,320]{2,1,0:T(8,128)(2,1)S(1)} collective-permute-done((bf16[4,160,320]{2,1,0:T(8,128)(2,1)S(1)}, bf16[4,160,320]{2,1,0:T(8,128)(2,1)S(1)}, u32[]{:S(2)}, u32[]{:S(2)}) %collective-permute-start.10) | collective-permute-done | bytes 409632 | tf_op jit(solution)/shard_map/ppermute | solution.py:248
  37.3 0.8 copy-done.6
  38.1 0.3 copy-done.5
  38.4 16.7 %conv_both.1 = (bf16[15,320,256]{2,1,0:T(8,128)(2,1)}, bf16[4,4,80,360]{3,2,1,0:T(8,128)(2,1)}, bf16[4,4,80,360]{3,2,1,0:T(8,128)(2,1)}, bf16[4,160,320]{2,1,0:T(8,128)(2,1)}, bf16[4,160,320]{2,1,0:T(8,128)(2,1)}) custom-call(s32[4]{0:T(128)} %pad_add_fusion.where_ref, bf16[4,4,80,360]{3,2,1,0:T(8,128)(2,1)} %copy-done.3, bf16[4,4,80,360]{3,2,1,0:T(8,128)(2,1)} %copy-done.5, ...), custom_call_target="tpu_custom_call" | custom-call | flops 14155776000 | bytes 9830400 | tf_op jit(solution)/shard_map/conv_both/pallas_call | solution.py:212
  55.1 4.4 %collective-permute-start.11 = (bf16[4,4,80,360]{3,2,1,0:T(8,128)(2,1)}, bf16[4,4,80,360]{3,2,1,0:T(8,128)(2,1)S(1)}, u32[]{:S(2)}, u32[]{:S(2)}) collective-permute-start(bf16[4,4,80,360]{3,2,1,0:T(8,128)(2,1)} %get-tuple-element.28), channel_id=1, source_target_pairs={{0,4},{4,0},{8,12},{12,8},{16,20},{20,16},{24,28},{28,24},{1,5},{5... | collective-permute-start | bytes 2764808 | tf_op jit(solution)/shard_map/ppermute | solution.py:248
  59.6 3.0 %collective-permute-done.12 = bf16[4,160,320]{2,1,0:T(8,128)(2,1)S(1)} collective-permute-done((bf16[4,160,320]{2,1,0:T(8,128)(2,1)}, bf16[4,160,320]{2,1,0:T(8,128)(2,1)S(1)}, u32[]{:S(2)}, u32[]{:S(2)}) %collective-permute-start.12) | collective-permute-done | bytes 409632 | tf_op jit(solution)/shard_map/ppermute | solution.py:248
  62.7 1.2 %add_convert_fusion.1 = bf16[4,160,320]{2,1,0:T(8,128)(2,1)S(1)} fusion(bf16[4,160,320]{2,1,0:T(8,128)(2,1)S(1)} %collective-permute-done.12, bf16[4,160,320]{2,1,0:T(8,128)(2,1)} %get-tuple-element.29), kind=kLoop, calls=%fused_computation.2 | loop fusion | flops 819200 | bytes 1228800 | tf_op jit(solution)/shard_map/convert_element_type | solution.py:273
  63.8 1.5 %add_convert_fusion = bf16[4,4,80,360]{3,2,1,0:T(8,128)(2,1)S(1)} fusion(bf16[4,4,80,360]{3,2,1,0:T(8,128)(2,1)S(1)} %collective-permute-done.11, bf16[4,4,80,360]{3,2,1,0:T(8,128)(2,1)} %get-tuple-element.27), kind=kLoop, calls=%fused_computation | loop fusion | flops 1843200 | bytes 2764800 | tf_op jit(solution)/shard_map/convert_element_type | solution.py:273
  65.4 7.1 %collective-permute-start.13 = (bf16[1,4,80,360]{3,2,1,0:T(8,128)(2,1)S(1)}, bf16[1,4,80,360]{3,2,1,0:T(8,128)(2,1)S(1)}, u32[]{:S(2)}, u32[]{:S(2)}) collective-permute-start(bf16[1,4,80,360]{3,2,1,0:T(8,128)(2,1)S(1)} %get-tuple-element.33), channel_id=1, source_target_pairs={{0,1},{1,0},{2,3},{3,2},{4,5},{5,4},{6,7},{7,6},{8,9},{9,8},{10,11... | collective-permute-start | bytes 691208 | tf_op jit(solution)/shard_map/ppermute | solution.py:248
  72.4 2.3 %collective-permute-start.15 = (bf16[1,4,80,360]{3,2,1,0:T(8,128)(2,1)S(1)}, bf16[1,4,80,360]{3,2,1,0:T(8,128)(2,1)S(1)}, u32[]{:S(2)}, u32[]{:S(2)}) collective-permute-start(bf16[1,4,80,360]{3,2,1,0:T(8,128)(2,1)S(1)} %get-tuple-element.34), channel_id=1, source_target_pairs={{0,3},{1,2},{2,1},{3,0},{4,7},{5,6},{6,5},{7,4},{8,11},{9,10},{10,... | collective-permute-start | bytes 691208 | tf_op jit(solution)/shard_map/ppermute | solution.py:248
  74.8 4.7 %collective-permute-start.22 = (bf16[1,160,320]{2,1,0:T(8,128)(2,1)S(1)}, bf16[1,160,320]{2,1,0:T(8,128)(2,1)S(1)}, u32[]{:S(2)}, u32[]{:S(2)}) collective-permute-start(bf16[1,160,320]{2,1,0:T(8,128)(2,1)S(1)} %get-tuple-element.36), channel_id=1, source_target_pairs={{0,8},{4,12},{8,0},{12,4},{16,24},{20,28},{24,16},{28,20},{1,9},{5... | collective-permute-start | bytes 307208 | tf_op jit(solution)/shard_map/ppermute | solution.py:248
  79.5 2.0 %collective-permute-start.24 = (bf16[1,160,320]{2,1,0:T(8,128)(2,1)S(1)}, bf16[1,160,320]{2,1,0:T(8,128)(2,1)S(1)}, u32[]{:S(2)}, u32[]{:S(2)}) collective-permute-start(bf16[1,160,320]{2,1,0:T(8,128)(2,1)S(1)} %get-tuple-element.37), channel_id=1, source_target_pairs={{0,24},{4,28},{8,16},{12,20},{16,8},{20,12},{24,0},{28,4},{1,25},{... | collective-permute-start | bytes 307208 | tf_op jit(solution)/shard_map/ppermute | solution.py:248
  81.6 2.9 %collective-permute-start.23 = (bf16[1,160,320]{2,1,0:T(8,128)(2,1)S(1)}, bf16[1,160,320]{2,1,0:T(8,128)(2,1)S(1)}, u32[]{:S(2)}, u32[]{:S(2)}) collective-permute-start(bf16[1,160,320]{2,1,0:T(8,128)(2,1)S(1)} %get-tuple-element.38), channel_id=1, source_target_pairs={{0,16},{4,20},{8,24},{12,28},{16,0},{20,4},{24,8},{28,12},{1,17},{... | collective-permute-start | bytes 307208 | tf_op jit(solution)/shard_map/ppermute | solution.py:248
  84.5 1.8 %collective-permute-done.15 = bf16[1,4,80,360]{3,2,1,0:T(8,128)(2,1)S(1)} collective-permute-done((bf16[1,4,80,360]{3,2,1,0:T(8,128)(2,1)S(1)}, bf16[1,4,80,360]{3,2,1,0:T(8,128)(2,1)S(1)}, u32[]{:S(2)}, u32[]{:S(2)}) %collective-permute-start.15) | collective-permute-done | bytes 230432 | tf_op jit(solution)/shard_map/ppermute | solution.py:248
  86.3 1.4 %collective-permute-done.14 = bf16[1,4,80,360]{3,2,1,0:T(8,128)(2,1)S(1)} collective-permute-done((bf16[1,4,80,360]{3,2,1,0:T(8,128)(2,1)S(1)}, bf16[1,4,80,360]{3,2,1,0:T(8,128)(2,1)S(1)}, u32[]{:S(2)}, u32[]{:S(2)}) %collective-permute-start.14) | collective-permute-done | bytes 230432 | tf_op jit(solution)/shard_map/ppermute | solution.py:248
  87.7 0.1 fusion.1
  87.8 3.1 %collective-permute-start.16 = (bf16[1,80,360]{2,1,0:T(8,128)(2,1)S(1)}, bf16[1,80,360]{2,1,0:T(8,128)(2,1)S(1)}, u32[]{:S(2)}, u32[]{:S(2)}) collective-permute-start(bf16[1,80,360]{2,1,0:T(8,128)(2,1)S(1)} %get-tuple-element.43), channel_id=1, source_target_pairs={{0,8},{4,12},{8,0},{12,4},{16,24},{20,28},{24,16},{28,20},{1,9},{5... | collective-permute-start | bytes 172808 | tf_op jit(solution)/shard_map/ppermute | solution.py:248
  90.9 3.7 %collective-permute-start.18 = (bf16[1,80,360]{2,1,0:T(8,128)(2,1)S(1)}, bf16[1,80,360]{2,1,0:T(8,128)(2,1)S(1)}, u32[]{:S(2)}, u32[]{:S(2)}) collective-permute-start(bf16[1,80,360]{2,1,0:T(8,128)(2,1)S(1)} %get-tuple-element.44), channel_id=1, source_target_pairs={{0,24},{4,28},{8,16},{12,20},{16,8},{20,12},{24,0},{28,4},{1,25},{... | collective-permute-start | bytes 172808 | tf_op jit(solution)/shard_map/ppermute | solution.py:248
  94.7 0.5 collective-permute-start.27
  95.2 1.4 %collective-permute-start.26 = (bf16[160,320]{1,0:T(8,128)(2,1)S(1)}, bf16[160,320]{1,0:T(8,128)(2,1)S(1)}, u32[]{:S(2)}, u32[]{:S(2)}) collective-permute-start(bf16[160,320]{1,0:T(8,128)(2,1)S(1)} %fusion.10), channel_id=1, source_target_pairs={{0,2},{1,3},{2,0},{3,1},{4,6},{5,7},{6,4},{7,5},{8,10},{9,11},{10,... | collective-permute-start | bytes 307208 | tf_op jit(solution)/shard_map/ppermute | solution.py:248
  96.6 1.7 %collective-permute-start.25 = (bf16[160,320]{1,0:T(8,128)(2,1)S(1)}, bf16[160,320]{1,0:T(8,128)(2,1)S(1)}, u32[]{:S(2)}, u32[]{:S(2)}) collective-permute-start(bf16[160,320]{1,0:T(8,128)(2,1)S(1)} %fusion.10), channel_id=1, source_target_pairs={{0,1},{1,0},{2,3},{3,2},{4,5},{5,4},{6,7},{7,6},{8,9},{9,8},{10,11... | collective-permute-start | bytes 307208 | tf_op jit(solution)/shard_map/ppermute | solution.py:248
  98.3 1.5 %collective-permute-done.17 = bf16[1,80,360]{2,1,0:T(8,128)(2,1)S(1)} collective-permute-done((bf16[1,80,360]{2,1,0:T(8,128)(2,1)S(1)}, bf16[1,80,360]{2,1,0:T(8,128)(2,1)S(1)}, u32[]{:S(2)}, u32[]{:S(2)}) %collective-permute-start.17) | collective-permute-done | bytes 57632 | tf_op jit(solution)/shard_map/ppermute | solution.py:248
  99.8 0.5 collective-permute-start.21
  100.3 1.4 %collective-permute-start.20 = (bf16[1,80,360]{2,1,0:T(8,128)(2,1)S(1)}, bf16[1,80,360]{2,1,0:T(8,128)(2,1)S(1)}, u32[]{:S(2)}, u32[]{:S(2)}) collective-permute-start(bf16[1,80,360]{2,1,0:T(8,128)(2,1)S(1)} %fusion.12), channel_id=1, source_target_pairs={{0,2},{1,3},{2,0},{3,1},{4,6},{5,7},{6,4},{7,5},{8,10},{9,11},{10,... | collective-permute-start | bytes 172808 | tf_op jit(solution)/shard_map/ppermute | solution.py:248
  101.7 1.7 %collective-permute-start.19 = (bf16[1,80,360]{2,1,0:T(8,128)(2,1)S(1)}, bf16[1,80,360]{2,1,0:T(8,128)(2,1)S(1)}, u32[]{:S(2)}, u32[]{:S(2)}) collective-permute-start(bf16[1,80,360]{2,1,0:T(8,128)(2,1)S(1)} %fusion.12), channel_id=1, source_target_pairs={{0,1},{1,0},{2,3},{3,2},{4,5},{5,4},{6,7},{7,6},{8,9},{9,8},{10,11... | collective-permute-start | bytes 172808 | tf_op jit(solution)/shard_map/ppermute | solution.py:248
  103.3 0.8 fusion.9
  104.1 1.0 collective-permute-done.21
  105.2 0.7 collective-permute-done.19
  106.0 0.8 convert_bitcast_fusion
  (51 shorter events, 1.1 us)
Async XLA Ops:
  0.6 8.7 %copy-start = (s32[1,4]{1,0:T(1,128)S(1)}, s32[1,4]{1,0:T(1,128)}, u32[]{:S(2)}) copy-start(s32[1,4]{1,0:T(1,128)} %param.8) | copy-start | bytes 52
  0.6 22.5 %copy-start.1 = (bf16[1,15,256,320]{2,3,1,0:T(8,128)(2,1)S(1)}, bf16[1,15,256,320]{2,3,1,0:T(8,128)(2,1)}, u32[]{:S(2)}) copy-start(bf16[1,15,256,320]{2,3,1,0:T(8,128)(2,1)} %param.6) | copy-start | bytes 7372804
  1.9 11.3 %collective-permute-start.2 = (bf16[1,80,360]{2,1,0:T(8,128)(2,1)S(1)}, bf16[1,80,360]{2,1,0:T(8,128)(2,1)S(1)}, u32[]{:S(2)}, u32[]{:S(2)}) collective-permute-start(bf16[1,80,360]{2,1,0:T(8,128)(2,1)S(1)} %get-tuple-element.49), channel_id=1, source_target_pairs={{0,24},{4,28},{8,16},{12,20},{16,8},{20,12},{24,0},{28,4},{1,25},{... | collective-permute-start | bytes 172808 | tf_op jit(solution)/shard_map/ppermute | solution.py:248
  7.1 6.2 %collective-permute-start.1 = (bf16[1,80,360]{2,1,0:T(8,128)(2,1)S(1)}, bf16[1,80,360]{2,1,0:T(8,128)(2,1)S(1)}, u32[]{:S(2)}, u32[]{:S(2)}) collective-permute-start(bf16[1,80,360]{2,1,0:T(8,128)(2,1)S(1)} %get-tuple-element.49), channel_id=1, source_target_pairs={{0,16},{4,20},{8,24},{12,28},{16,0},{20,4},{24,8},{28,12},{1,17},{... | collective-permute-start | bytes 172808 | tf_op jit(solution)/shard_map/ppermute | solution.py:248
  7.1 6.2 %collective-permute-start = (bf16[1,80,360]{2,1,0:T(8,128)(2,1)S(1)}, bf16[1,80,360]{2,1,0:T(8,128)(2,1)S(1)}, u32[]{:S(2)}, u32[]{:S(2)}) collective-permute-start(bf16[1,80,360]{2,1,0:T(8,128)(2,1)S(1)} %get-tuple-element.49), channel_id=1, source_target_pairs={{0,8},{4,12},{8,0},{12,4},{16,24},{20,28},{24,16},{28,20},{1,9},{5... | collective-permute-start | bytes 172808 | tf_op jit(solution)/shard_map/ppermute | solution.py:248
  13.4 8.1 %collective-permute-start.8 = (bf16[1,160,320]{2,1,0:T(8,128)(2,1)S(1)}, bf16[1,160,320]{2,1,0:T(8,128)(2,1)S(1)}, u32[]{:S(2)}, u32[]{:S(2)}) collective-permute-start(bf16[1,160,320]{2,1,0:T(8,128)(2,1)S(1)} %bitcast.78), channel_id=1, source_target_pairs={{0,24},{4,28},{8,16},{12,20},{16,8},{20,12},{24,0},{28,4},{1,25},{... | collective-permute-start | bytes 307208 | tf_op jit(solution)/shard_map/ppermute | solution.py:248
  17.2 16.3 %collective-permute-start.7 = (bf16[1,160,320]{2,1,0:T(8,128)(2,1)S(1)}, bf16[1,160,320]{2,1,0:T(8,128)(2,1)S(1)}, u32[]{:S(2)}, u32[]{:S(2)}) collective-permute-start(bf16[1,160,320]{2,1,0:T(8,128)(2,1)S(1)} %bitcast.79), channel_id=1, source_target_pairs={{0,16},{4,20},{8,24},{12,28},{16,0},{20,4},{24,8},{28,12},{1,17},{... | collective-permute-start | bytes 307208 | tf_op jit(solution)/shard_map/ppermute | solution.py:248
  17.2 16.3 %collective-permute-start.6 = (bf16[1,160,320]{2,1,0:T(8,128)(2,1)S(1)}, bf16[1,160,320]{2,1,0:T(8,128)(2,1)S(1)}, u32[]{:S(2)}, u32[]{:S(2)}) collective-permute-start(bf16[1,160,320]{2,1,0:T(8,128)(2,1)S(1)} %bitcast.80), channel_id=1, source_target_pairs={{0,8},{4,12},{8,0},{12,4},{16,24},{20,28},{24,16},{28,20},{1,9},{5... | collective-permute-start | bytes 307208 | tf_op jit(solution)/shard_map/ppermute | solution.py:248
  17.9 15.8 %collective-permute-start.5 = (bf16[1,3,80,360]{3,2,1,0:T(8,128)(2,1)S(1)}, bf16[1,3,80,360]{3,2,1,0:T(8,128)(2,1)S(1)}, u32[]{:S(2)}, u32[]{:S(2)}) collective-permute-start(bf16[1,3,80,360]{3,2,1,0:T(8,128)(2,1)S(1)} %slice_bitcast_fusion.4), channel_id=1, source_target_pairs={{0,3},{1,2},{2,1},{3,0},{4,7},{5,6},{6,5},{7,4},{8,11},{9,10},{10,... | collective-permute-start | bytes 518408 | tf_op jit(solution)/shard_map/ppermute | solution.py:248
  20.5 13.1 %collective-permute-start.4 = (bf16[1,3,80,360]{3,2,1,0:T(8,128)(2,1)S(1)}, bf16[1,3,80,360]{3,2,1,0:T(8,128)(2,1)S(1)}, u32[]{:S(2)}, u32[]{:S(2)}) collective-permute-start(bf16[1,3,80,360]{3,2,1,0:T(8,128)(2,1)S(1)} %slice_bitcast_fusion.4), channel_id=1, source_target_pairs={{0,2},{1,3},{2,0},{3,1},{4,6},{5,7},{6,4},{7,5},{8,10},{9,11},{10,... | collective-permute-start | bytes 518408 | tf_op jit(solution)/shard_map/ppermute | solution.py:248
  21.5 12.2 %collective-permute-start.3 = (bf16[1,3,80,360]{3,2,1,0:T(8,128)(2,1)S(1)}, bf16[1,3,80,360]{3,2,1,0:T(8,128)(2,1)S(1)}, u32[]{:S(2)}, u32[]{:S(2)}) collective-permute-start(bf16[1,3,80,360]{3,2,1,0:T(8,128)(2,1)S(1)} %slice_bitcast_fusion.4), channel_id=1, source_target_pairs={{0,1},{1,0},{2,3},{3,2},{4,5},{5,4},{6,7},{7,6},{8,9},{9,8},{10,11... | collective-permute-start | bytes 518408 | tf_op jit(solution)/shard_map/ppermute | solution.py:248
  32.0 1.5 %copy-start.2 = (bf16[15,320,256]{2,1,0:T(8,128)(2,1)}, bf16[15,320,256]{2,1,0:T(8,128)(2,1)S(1)}, u32[]{:S(2)}) copy-start(bf16[15,320,256]{2,1,0:T(8,128)(2,1)S(1)} %group_norm.1.normed_ref) | copy-start | bytes 7372804
  33.6 3.7 %copy-start.4 = (bf16[4,160,320]{2,1,0:T(8,128)(2,1)}, bf16[4,160,320]{2,1,0:T(8,128)(2,1)S(1)}, u32[]{:S(2)}) copy-start(bf16[4,160,320]{2,1,0:T(8,128)(2,1)S(1)} %pad_maximum_fusion.1.own_time_ref) | copy-start | bytes 1228804
  33.9 3.4 %copy-start.3 = (bf16[4,4,80,360]{3,2,1,0:T(8,128)(2,1)}, bf16[4,4,80,360]{3,2,1,0:T(8,128)(2,1)S(1)}, u32[]{:S(2)}) copy-start(bf16[4,4,80,360]{3,2,1,0:T(8,128)(2,1)S(1)} %maximum_maximum_fusion.own_ref) | copy-start | bytes 2764804
  33.9 3.3 %collective-permute-start.9 = (bf16[4,4,80,360]{3,2,1,0:T(8,128)(2,1)S(1)}, bf16[4,4,80,360]{3,2,1,0:T(8,128)(2,1)S(1)}, u32[]{:S(2)}, u32[]{:S(2)}) collective-permute-start(bf16[4,4,80,360]{3,2,1,0:T(8,128)(2,1)S(1)} %maximum_maximum_fusion.own_ref), channel_id=1, source_target_pairs={{0,4},{4,0},{8,12},{12,8},{16,20},{20,16},{24,28},{28,24},{1,5},{5... | collective-permute-start | bytes 2764808 | tf_op jit(solution)/shard_map/ppermute | solution.py:248
  34.0 3.3 %collective-permute-start.10 = (bf16[4,160,320]{2,1,0:T(8,128)(2,1)S(1)}, bf16[4,160,320]{2,1,0:T(8,128)(2,1)S(1)}, u32[]{:S(2)}, u32[]{:S(2)}) collective-permute-start(bf16[4,160,320]{2,1,0:T(8,128)(2,1)S(1)} %pad_maximum_fusion.1.own_time_ref), channel_id=1, source_target_pairs={{0,4},{4,0},{8,12},{12,8},{16,20},{20,16},{24,28},{28,24},{1,5},{5... | collective-permute-start | bytes 1228808 | tf_op jit(solution)/shard_map/ppermute | solution.py:248
  37.3 0.8 copy-start.6
  37.3 1.1 %copy-start.5 = (bf16[4,4,80,360]{3,2,1,0:T(8,128)(2,1)}, bf16[4,4,80,360]{3,2,1,0:T(8,128)(2,1)S(1)}, u32[]{:S(2)}) copy-start(bf16[4,4,80,360]{3,2,1,0:T(8,128)(2,1)S(1)} %collective-permute-done.9.other_ref) | copy-start | bytes 2764804
  55.1 8.7 %collective-permute-start.11 = (bf16[4,4,80,360]{3,2,1,0:T(8,128)(2,1)}, bf16[4,4,80,360]{3,2,1,0:T(8,128)(2,1)S(1)}, u32[]{:S(2)}, u32[]{:S(2)}) collective-permute-start(bf16[4,4,80,360]{3,2,1,0:T(8,128)(2,1)} %get-tuple-element.28), channel_id=1, source_target_pairs={{0,4},{4,0},{8,12},{12,8},{16,20},{20,16},{24,28},{28,24},{1,5},{5... | collective-permute-start | bytes 2764808 | tf_op jit(solution)/shard_map/ppermute | solution.py:248
  59.6 3.1 %collective-permute-start.12 = (bf16[4,160,320]{2,1,0:T(8,128)(2,1)}, bf16[4,160,320]{2,1,0:T(8,128)(2,1)S(1)}, u32[]{:S(2)}, u32[]{:S(2)}) collective-permute-start(bf16[4,160,320]{2,1,0:T(8,128)(2,1)} %get-tuple-element.30), channel_id=1, source_target_pairs={{0,4},{4,0},{8,12},{12,8},{16,20},{20,16},{24,28},{28,24},{1,5},{5... | collective-permute-start | bytes 1228808 | tf_op jit(solution)/shard_map/ppermute | solution.py:248
  65.4 16.2 %collective-permute-start.13 = (bf16[1,4,80,360]{3,2,1,0:T(8,128)(2,1)S(1)}, bf16[1,4,80,360]{3,2,1,0:T(8,128)(2,1)S(1)}, u32[]{:S(2)}, u32[]{:S(2)}) collective-permute-start(bf16[1,4,80,360]{3,2,1,0:T(8,128)(2,1)S(1)} %get-tuple-element.33), channel_id=1, source_target_pairs={{0,1},{1,0},{2,3},{3,2},{4,5},{5,4},{6,7},{7,6},{8,9},{9,8},{10,11... | collective-permute-start | bytes 691208 | tf_op jit(solution)/shard_map/ppermute | solution.py:248
  72.4 13.9 %collective-permute-start.15 = (bf16[1,4,80,360]{3,2,1,0:T(8,128)(2,1)S(1)}, bf16[1,4,80,360]{3,2,1,0:T(8,128)(2,1)S(1)}, u32[]{:S(2)}, u32[]{:S(2)}) collective-permute-start(bf16[1,4,80,360]{3,2,1,0:T(8,128)(2,1)S(1)} %get-tuple-element.34), channel_id=1, source_target_pairs={{0,3},{1,2},{2,1},{3,0},{4,7},{5,6},{6,5},{7,4},{8,11},{9,10},{10,... | collective-permute-start | bytes 691208 | tf_op jit(solution)/shard_map/ppermute | solution.py:248
  74.7 12.9 %collective-permute-start.14 = (bf16[1,4,80,360]{3,2,1,0:T(8,128)(2,1)S(1)}, bf16[1,4,80,360]{3,2,1,0:T(8,128)(2,1)S(1)}, u32[]{:S(2)}, u32[]{:S(2)}) collective-permute-start(bf16[1,4,80,360]{3,2,1,0:T(8,128)(2,1)S(1)} %get-tuple-element.35), channel_id=1, source_target_pairs={{0,2},{1,3},{2,0},{3,1},{4,6},{5,7},{6,4},{7,5},{8,10},{9,11},{10,... | collective-permute-start | bytes 691208 | tf_op jit(solution)/shard_map/ppermute | solution.py:248
  74.8 19.8 %collective-permute-start.22 = (bf16[1,160,320]{2,1,0:T(8,128)(2,1)S(1)}, bf16[1,160,320]{2,1,0:T(8,128)(2,1)S(1)}, u32[]{:S(2)}, u32[]{:S(2)}) collective-permute-start(bf16[1,160,320]{2,1,0:T(8,128)(2,1)S(1)} %get-tuple-element.36), channel_id=1, source_target_pairs={{0,8},{4,12},{8,0},{12,4},{16,24},{20,28},{24,16},{28,20},{1,9},{5... | collective-permute-start | bytes 307208 | tf_op jit(solution)/shard_map/ppermute | solution.py:248
  79.5 15.1 %collective-permute-start.24 = (bf16[1,160,320]{2,1,0:T(8,128)(2,1)S(1)}, bf16[1,160,320]{2,1,0:T(8,128)(2,1)S(1)}, u32[]{:S(2)}, u32[]{:S(2)}) collective-permute-start(bf16[1,160,320]{2,1,0:T(8,128)(2,1)S(1)} %get-tuple-element.37), channel_id=1, source_target_pairs={{0,24},{4,28},{8,16},{12,20},{16,8},{20,12},{24,0},{28,4},{1,25},{... | collective-permute-start | bytes 307208 | tf_op jit(solution)/shard_map/ppermute | solution.py:248
  81.6 13.1 %collective-permute-start.23 = (bf16[1,160,320]{2,1,0:T(8,128)(2,1)S(1)}, bf16[1,160,320]{2,1,0:T(8,128)(2,1)S(1)}, u32[]{:S(2)}, u32[]{:S(2)}) collective-permute-start(bf16[1,160,320]{2,1,0:T(8,128)(2,1)S(1)} %get-tuple-element.38), channel_id=1, source_target_pairs={{0,16},{4,20},{8,24},{12,28},{16,0},{20,4},{24,8},{28,12},{1,17},{... | collective-permute-start | bytes 307208 | tf_op jit(solution)/shard_map/ppermute | solution.py:248
  87.8 8.8 %collective-permute-start.16 = (bf16[1,80,360]{2,1,0:T(8,128)(2,1)S(1)}, bf16[1,80,360]{2,1,0:T(8,128)(2,1)S(1)}, u32[]{:S(2)}, u32[]{:S(2)}) collective-permute-start(bf16[1,80,360]{2,1,0:T(8,128)(2,1)S(1)} %get-tuple-element.43), channel_id=1, source_target_pairs={{0,8},{4,12},{8,0},{12,4},{16,24},{20,28},{24,16},{28,20},{1,9},{5... | collective-permute-start | bytes 172808 | tf_op jit(solution)/shard_map/ppermute | solution.py:248
  90.9 7.3 %collective-permute-start.18 = (bf16[1,80,360]{2,1,0:T(8,128)(2,1)S(1)}, bf16[1,80,360]{2,1,0:T(8,128)(2,1)S(1)}, u32[]{:S(2)}, u32[]{:S(2)}) collective-permute-start(bf16[1,80,360]{2,1,0:T(8,128)(2,1)S(1)} %get-tuple-element.44), channel_id=1, source_target_pairs={{0,24},{4,28},{8,16},{12,20},{16,8},{20,12},{24,0},{28,4},{1,25},{... | collective-permute-start | bytes 172808 | tf_op jit(solution)/shard_map/ppermute | solution.py:248
  94.6 5.1 %collective-permute-start.17 = (bf16[1,80,360]{2,1,0:T(8,128)(2,1)S(1)}, bf16[1,80,360]{2,1,0:T(8,128)(2,1)S(1)}, u32[]{:S(2)}, u32[]{:S(2)}) collective-permute-start(bf16[1,80,360]{2,1,0:T(8,128)(2,1)S(1)} %get-tuple-element.45), channel_id=1, source_target_pairs={{0,16},{4,20},{8,24},{12,28},{16,0},{20,4},{24,8},{28,12},{1,17},{... | collective-permute-start | bytes 172808 | tf_op jit(solution)/shard_map/ppermute | solution.py:248
  94.7 7.0 %collective-permute-start.27 = (bf16[160,320]{1,0:T(8,128)(2,1)S(1)}, bf16[160,320]{1,0:T(8,128)(2,1)S(1)}, u32[]{:S(2)}, u32[]{:S(2)}) collective-permute-start(bf16[160,320]{1,0:T(8,128)(2,1)S(1)} %fusion.10), channel_id=1, source_target_pairs={{0,3},{1,2},{2,1},{3,0},{4,7},{5,6},{6,5},{7,4},{8,11},{9,10},{10,... | collective-permute-start | bytes 307208 | tf_op jit(solution)/shard_map/ppermute | solution.py:248
  95.2 8.1 %collective-permute-start.26 = (bf16[160,320]{1,0:T(8,128)(2,1)S(1)}, bf16[160,320]{1,0:T(8,128)(2,1)S(1)}, u32[]{:S(2)}, u32[]{:S(2)}) collective-permute-start(bf16[160,320]{1,0:T(8,128)(2,1)S(1)} %fusion.10), channel_id=1, source_target_pairs={{0,2},{1,3},{2,0},{3,1},{4,6},{5,7},{6,4},{7,5},{8,10},{9,11},{10,... | collective-permute-start | bytes 307208 | tf_op jit(solution)/shard_map/ppermute | solution.py:248
  96.6 6.7 %collective-permute-start.25 = (bf16[160,320]{1,0:T(8,128)(2,1)S(1)}, bf16[160,320]{1,0:T(8,128)(2,1)S(1)}, u32[]{:S(2)}, u32[]{:S(2)}) collective-permute-start(bf16[160,320]{1,0:T(8,128)(2,1)S(1)} %fusion.10), channel_id=1, source_target_pairs={{0,1},{1,0},{2,3},{3,2},{4,5},{5,4},{6,7},{7,6},{8,9},{9,8},{10,11... | collective-permute-start | bytes 307208 | tf_op jit(solution)/shard_map/ppermute | solution.py:248
  99.8 5.3 %collective-permute-start.21 = (bf16[1,80,360]{2,1,0:T(8,128)(2,1)S(1)}, bf16[1,80,360]{2,1,0:T(8,128)(2,1)S(1)}, u32[]{:S(2)}, u32[]{:S(2)}) collective-permute-start(bf16[1,80,360]{2,1,0:T(8,128)(2,1)S(1)} %fusion.12), channel_id=1, source_target_pairs={{0,3},{1,2},{2,1},{3,0},{4,7},{5,6},{6,5},{7,4},{8,11},{9,10},{10,... | collective-permute-start | bytes 172808 | tf_op jit(solution)/shard_map/ppermute | solution.py:248
  100.3 4.9 %collective-permute-start.20 = (bf16[1,80,360]{2,1,0:T(8,128)(2,1)S(1)}, bf16[1,80,360]{2,1,0:T(8,128)(2,1)S(1)}, u32[]{:S(2)}, u32[]{:S(2)}) collective-permute-start(bf16[1,80,360]{2,1,0:T(8,128)(2,1)S(1)} %fusion.12), channel_id=1, source_target_pairs={{0,2},{1,3},{2,0},{3,1},{4,6},{5,7},{6,4},{7,5},{8,10},{9,11},{10,... | collective-permute-start | bytes 172808 | tf_op jit(solution)/shard_map/ppermute | solution.py:248
  101.7 4.2 %collective-permute-start.19 = (bf16[1,80,360]{2,1,0:T(8,128)(2,1)S(1)}, bf16[1,80,360]{2,1,0:T(8,128)(2,1)S(1)}, u32[]{:S(2)}, u32[]{:S(2)}) collective-permute-start(bf16[1,80,360]{2,1,0:T(8,128)(2,1)S(1)} %fusion.12), channel_id=1, source_target_pairs={{0,1},{1,0},{2,3},{3,2},{4,5},{5,4},{6,7},{7,6},{8,9},{9,8},{10,11... | collective-permute-start | bytes 172808 | tf_op jit(solution)/shard_map/ppermute | solution.py:248

commit v4 on v3

--- a/solution.py
+++ b/solution.py
@@ -41,7 +41,8 @@
         centred = values - group_mean(jnp.sum(values, axis=1, keepdims=True))
         variance = group_mean(jnp.sum(centred * centred, axis=1, keepdims=True))
         scaled = centred * lax.rsqrt(variance + 1e-05)
-        out_ref[at] = (scaled / (1.0 + jnp.exp(-scaled))).astype(bf16)
+        half = 0.5 * scaled
+        out_ref[at] = (half + half * jnp.tanh(half)).astype(bf16)
 
 
 def group_norm(tiles):
@@ -57,7 +58,7 @@
         in_specs=[pl.BlockSpec((channels, channels), lambda i: (0, 0)), block],
         out_specs=block,
         out_shape=jax.ShapeDtypeStruct(tiles.shape, bf16),
-        compiler_params=pltpu.CompilerParams(vmem_limit_bytes=32 * 2**20),
+        compiler_params=pltpu.CompilerParams(vmem_limit_bytes=60 * 2**20),
         cost_estimate=pl.CostEstimate(
             flops=20 * tiles.size, bytes_accessed=4 * tiles.size, transcendentals=tiles.size
         ),
@@ -91,7 +92,7 @@
 
 def conv_kernel(
     steps,
-    where_ref,
+    counts_ref,
     own_ref,
     other_ref,
     own_time_ref,
@@ -117,7 +118,9 @@
     step, channels, pixels = normed_ref.shape
     shards = 2 * planes
     time_rows = own_time_ref.shape[1]
-    count, core, plane, part = (where_ref[n] for n in range(4))
+    my_shard, my_peer = lax.axis_index("fsdp"), lax.axis_index("dp")
+    count = counts_ref[0, my_peer]
+    core, plane, part = my_shard & 1, my_shard >> 1, my_peer & (parts - 1)
     outs = parts * part_rows
     lane = lax.broadcasted_iota(jnp.int32, (outs, LANES), 1)
 
@@ -197,7 +200,7 @@
                     time_into[at] = time_total[f * time_rows : (f + 1) * time_rows].astype(bf16)
 
 
-def conv_both(where, own, other, own_time, other_time, features, normed, tiles, targets):
+def conv_both(counts, own, other, own_time, other_time, features, normed, tiles, targets):
     number, channels, pixels = normed.shape
     parts, planes, part_rows, rows = own.shape
     shards, outs = 2 * planes, parts * part_rows
@@ -235,12 +238,12 @@
             jax.ShapeDtypeStruct(own_time.shape, bf16),
             jax.ShapeDtypeStruct(own_time.shape, bf16),
         ],
-        compiler_params=pltpu.CompilerParams(vmem_limit_bytes=56 * 2**20),
+        compiler_params=pltpu.CompilerParams(vmem_limit_bytes=44 * 2**20),
         cost_estimate=pl.CostEstimate(
             flops=4 * number * pixels * depth * outs, bytes_accessed=8 * tiles.size, transcendentals=0
         ),
         name="conv_both",
-    )(where, own, other, own_time, other_time, features, normed, tiles, targets)
+    )(counts, own, other, own_time, other_time, features, normed, tiles, targets)
 
 
 def swap(values, axis, mask):
@@ -303,33 +306,29 @@
     number = tiles.shape[0]
     shards = lax.axis_size("fsdp")
     shard_bits, peer_bits = bits_of("fsdp"), bits_of("dp")
-    my_shard, my_peer = lax.axis_index("fsdp"), lax.axis_index("dp")
     rows, outs = conv_master.shape
     time_rows = temb_master.shape[0]
     part_bits = max(n for n in range(peer_bits + 1) if outs % (16 << n) == 0)
     parts = 1 << part_bits
-    part = my_peer & (parts - 1)
+    part = lax.axis_index("dp") & (parts - 1)
     plane_bits = shard_bits - 1
-    core, plane = my_shard & 1, my_shard >> 1
-    where = jnp.stack([counts[0][my_peer], core, plane, part]).astype(jnp.int32)
 
     master = conv_master.T.astype(bf16).reshape(parts, outs // parts, rows)
     time_master = temb_master.astype(bf16)
     mine = [lax.dynamic_index_in_dim(master, part ^ m, 0, keepdims=False) for m in range(parts)]
     over_planes = gather_partners(mine[0], "fsdp", 1, plane_bits)
     features = time_features(jnp.pad(timesteps[0], (0, LANES - number)), time_rows * shards)
-    over_planes, features, tiles_then, time_master, where = lax.optimization_barrier(
-        (over_planes, features, tiles, time_master, where)
-    )
+    time_master, features = lax.optimization_barrier((time_master, features))
+    own_time = gather_partners(time_master, "fsdp", 1, plane_bits)
+    over_planes, tiles_then = lax.optimization_barrier((over_planes, tiles))
     far = gather_partners(over_planes[1:], "dp", 0, part_bits)
-    own_time = gather_partners(time_master, "fsdp", 1, plane_bits)
     normed = group_norm(tiles_then)
     own = jnp.concatenate([jnp.stack(mine)[:, None], far], axis=1)
     own, own_time, normed = lax.optimization_barrier((own, own_time, normed))
     other, other_time = swap(own, "fsdp", 1), swap(own_time, "fsdp", 1)
 
     predicted, keep, send, keep_time, send_time = conv_both(
-        where, own, other, own_time, other_time, features, normed, tiles, targets
+        counts, own, other, own_time, other_time, features, normed, tiles, targets
     )
 
     grad = add_up([keep, swap(send, "fsdp", 1)])

time: 107 us -> 98.5 us (0.921)
  other arithmetic: 11.2 us -> 7.64 us
  local copies, waits for them, and re-layouts: 3.39 us -> 0.25 us
  waiting for transfers between devices: 12.7 us -> 10.5 us
  starting transfers between devices: 53 us -> 54.4 us
  Pallas kernels: 25.6 us -> 24.3 us
    pallas_call x1, Pallas kernels: 16.7 us -> 13.9 us  [conv_both(): pl.pallas_call(functools.partial(conv_kernel, steps), grid_spec=pltpu.Pre...]
    unnamed x14 -> x4, local copies, waits for them, and re-layouts: 2.56 us -> 0.01 us
    ppermute x28, waiting for transfers between devices: 12.7 us -> 10.5 us  [swap(): return lax.ppermute(values, axis, pairs)]
    convert_element_type x4, other arithmetic: 2.77 us -> 0.55 us  [add_up(): return parts[0].astype(kept_as)]
    pallas_call x1, Pallas kernels: 8.84 us -> 10.3 us  [group_norm(): pl.pallas_call(functools.partial(norm_kernel, group_width), grid=(number...]
    ppermute x28, starting transfers between devices: 53 us -> 54.4 us  [swap(): return lax.ppermute(values, axis, pairs)]
    another operation x1 -> x0, other arithmetic: 1.13 us -> none  [per_device(): where = jnp.stack([counts[0][my_peer], core, plane, part]).astype(jnp.int32)]
  transfers between devices with their start and end apart: 28 -> 28, of which waited for: 9 -> 9; matrix products, arithmetic and copies ran while one was open for 7% -> 5% of each run, Pallas kernels for 8% -> 11%
where the time goes in v4:
time: 98.5 us; the launch traced here: 97.9 us
  starting transfers between devices  54.4 us (55%)
  Pallas kernels  24.3 us (25%)
  waiting for transfers between devices  10.5 us (11%)
  other arithmetic  7.64 us (8%)
    ppermute x28, starting transfers between devices, swap(): return lax.ppermute(values, axis, pairs)  54.4 us
    pallas_call x1, Pallas kernels, conv_both(): pl.pallas_call(functools.partial(conv_kernel, steps), grid_spec=pltpu.Pre...  13.9 us
    ppermute x28, waiting for transfers between devices, swap(): return lax.ppermute(values, axis, pairs)  10.5 us
    pallas_call x1, Pallas kernels, group_norm(): pl.pallas_call(functools.partial(norm_kernel, group_width), grid=(number...  10.3 us
  transfers between devices with their start and end apart: 28, of which 9 were waited for; matrix products, arithmetic and copies ran while one was open for 5% of the time, Pallas kernels for 11%

profile of v4, /device:TPU:0, one launch (start us, length us, event | category | flops | bytes accessed | tf_op | source)
XLA Modules:
  0.0 97.9 jit_solution(18384323683517721102)
XLA Ops:
  0.6 1.1 %convert_element_type.138 = bf16[360,320]{0,1:T(8,128)(2,1)S(1)} convert(f32[360,320]{0,1:T(8,128)} %param.10) | non-fusion elementwise | flops 115200 | bytes 691200 | tf_op jit(solution)/shard_map/convert_element_type | solution.py:316
  1.8 5.1 %collective-permute-start.2 = (bf16[1,80,360]{2,1,0:T(8,128)(2,1)S(1)}, bf16[1,80,360]{2,1,0:T(8,128)(2,1)S(1)}, u32[]{:S(2)}, u32[]{:S(2)}) collective-permute-start(bf16[1,80,360]{2,1,0:T(8,128)(2,1)S(1)} %get-tuple-element.47), channel_id=1, source_target_pairs={{0,24},{4,28},{8,16},{12,20},{16,8},{20,12},{24,0},{28,4},{1,25},{... | collective-permute-start | bytes 172808 | tf_op jit(solution)/shard_map/ppermute | solution.py:251
  6.9 0.6 collective-permute-start
  7.5 0.7 pad_convert_fusion
  8.2 1.0 convert_element_type.140
  9.2 1.2 %multiply_cosine_fusion = (f32[640,128]{1,0:T(8,128)S(1)}, f32[640,128]{1,0:T(8,128)S(1)}) fusion(f32[128]{0:T(128)S(1)} %pad_convert_fusion, f32[640]{0:T(1024)S(1)} %multiply_exponential_fusion), kind=kLoop, calls=%fused_computation.12 | loop fusion | flops 81920 | bytes 658432 | tf_op jit(solution)/shard_map/cos | solution.py:300
  10.4 0.2 multiply_convert_fusion.features_ref
  10.6 3.8 %collective-permute-start.8 = (bf16[1,160,320]{2,1,0:T(8,128)(2,1)S(1)}, bf16[1,160,320]{2,1,0:T(8,128)(2,1)S(1)}, u32[]{:S(2)}, u32[]{:S(2)}) collective-permute-start(bf16[1,160,320]{2,1,0:T(8,128)(2,1)S(1)} %bitcast.74), channel_id=1, source_target_pairs={{0,24},{4,28},{8,16},{12,20},{16,8},{20,12},{24,0},{28,4},{1,25},{... | collective-permute-start | bytes 307208 | tf_op jit(solution)/shard_map/ppermute | solution.py:251
  14.4 0.7 collective-permute-start.6
  15.1 0.1 fusion.4
  15.2 2.7 %collective-permute-start.5 = (bf16[1,3,80,360]{3,2,1,0:T(8,128)(2,1)S(1)}, bf16[1,3,80,360]{3,2,1,0:T(8,128)(2,1)S(1)}, u32[]{:S(2)}, u32[]{:S(2)}) collective-permute-start(bf16[1,3,80,360]{3,2,1,0:T(8,128)(2,1)S(1)} %slice_bitcast_fusion.4), channel_id=1, source_target_pairs={{0,3},{1,2},{2,1},{3,0},{4,7},{5,6},{6,5},{7,4},{8,11},{9,10},{10,... | collective-permute-start | bytes 518408 | tf_op jit(solution)/shard_map/ppermute | solution.py:251
  17.9 0.5 collective-permute-start.4
  18.4 0.3 collective-permute-done.8
  18.7 1.5 %collective-permute-start.3 = (bf16[1,3,80,360]{3,2,1,0:T(8,128)(2,1)S(1)}, bf16[1,3,80,360]{3,2,1,0:T(8,128)(2,1)S(1)}, u32[]{:S(2)}, u32[]{:S(2)}) collective-permute-start(bf16[1,3,80,360]{3,2,1,0:T(8,128)(2,1)S(1)} %slice_bitcast_fusion.4), channel_id=1, source_target_pairs={{0,1},{1,0},{2,3},{3,2},{4,5},{5,4},{6,7},{7,6},{8,9},{9,8},{10,11... | collective-permute-start | bytes 518408 | tf_op jit(solution)/shard_map/ppermute | solution.py:251
  20.2 0.8 compare_convert_fusion.same_ref
  21.0 10.3 %group_norm.1.normed_ref = bf16[15,320,256]{2,1,0:T(8,128)(2,1)} custom-call(bf16[320,320]{1,0:T(8,128)(2,1)} %compare_convert_fusion.same_ref, bf16[15,320,256]{2,1,0:T(8,128)(2,1)} %bitcast.69), custom_call_target="tpu_custom_call" | custom-call | flops 24576000 | bytes 4915200 | tf_op jit(solution)/shard_map/group_norm/pallas_call | solution.py:55
  31.3 0.1 pad_maximum_fusion.1.own_time_ref
  31.5 0.3 maximum_maximum_fusion.own_ref
  31.8 0.5 collective-permute-start.10
  32.3 2.8 %collective-permute-done.10.other_time_ref = bf16[4,160,320]{2,1,0:T(8,128)(2,1)S(1)} collective-permute-done((bf16[4,160,320]{2,1,0:T(8,128)(2,1)S(1)}, bf16[4,160,320]{2,1,0:T(8,128)(2,1)S(1)}, u32[]{:S(2)}, u32[]{:S(2)}) %collective-permute-start.10) | collective-permute-done | bytes 409632 | tf_op jit(solution)/shard_map/ppermute | solution.py:251
  35.1 13.9 %conv_both.1 = (bf16[15,320,256]{2,1,0:T(8,128)(2,1)}, bf16[4,4,80,360]{3,2,1,0:T(8,128)(2,1)S(1)}, bf16[4,4,80,360]{3,2,1,0:T(8,128)(2,1)S(1)}, bf16[4,160,320]...) custom-call(s32[1,4]{1,0:T(1,128)S(1)} %copy-done.1, bf16[4,4,80,360]{3,2,1,0:T(8,128)(2,1)S(1)} %maximum_maximum_fusion.own_ref, ...), custom_call_target="tpu_custom_call" | custom-call | flops 14155776000 | bytes 9830400 | tf_op jit(solution)/shard_map/conv_both/pallas_call | solution.py:215
  49.0 0.1 collective-permute-start.11
  49.2 0.4 collective-permute-start.12
  49.5 2.8 %collective-permute-done.12 = bf16[4,160,320]{2,1,0:T(8,128)(2,1)S(1)} collective-permute-done((bf16[4,160,320]{2,1,0:T(8,128)(2,1)S(1)}, bf16[4,160,320]{2,1,0:T(8,128)(2,1)S(1)}, u32[]{:S(2)}, u32[]{:S(2)}) %collective-permute-start.12) | collective-permute-done | bytes 409632 | tf_op jit(solution)/shard_map/ppermute | solution.py:251
  52.3 0.1 add_convert_fusion.1
  52.4 0.3 add_convert_fusion
  52.8 11.3 %collective-permute-start.13 = (bf16[1,4,80,360]{3,2,1,0:T(8,128)(2,1)S(1)}, bf16[1,4,80,360]{3,2,1,0:T(8,128)(2,1)S(1)}, u32[]{:S(2)}, u32[]{:S(2)}) collective-permute-start(bf16[1,4,80,360]{3,2,1,0:T(8,128)(2,1)S(1)} %get-tuple-element.31), channel_id=1, source_target_pairs={{0,1},{1,0},{2,3},{3,2},{4,5},{5,4},{6,7},{7,6},{8,9},{9,8},{10,11... | collective-permute-start | bytes 691208 | tf_op jit(solution)/shard_map/ppermute | solution.py:251
  64.1 1.0 %collective-permute-start.15 = (bf16[1,4,80,360]{3,2,1,0:T(8,128)(2,1)S(1)}, bf16[1,4,80,360]{3,2,1,0:T(8,128)(2,1)S(1)}, u32[]{:S(2)}, u32[]{:S(2)}) collective-permute-start(bf16[1,4,80,360]{3,2,1,0:T(8,128)(2,1)S(1)} %get-tuple-element.32), channel_id=1, source_target_pairs={{0,3},{1,2},{2,1},{3,0},{4,7},{5,6},{6,5},{7,4},{8,11},{9,10},{10,... | collective-permute-start | bytes 691208 | tf_op jit(solution)/shard_map/ppermute | solution.py:251
  65.1 0.5 collective-permute-start.14
  65.7 5.5 %collective-permute-start.22 = (bf16[1,160,320]{2,1,0:T(8,128)(2,1)S(1)}, bf16[1,160,320]{2,1,0:T(8,128)(2,1)S(1)}, u32[]{:S(2)}, u32[]{:S(2)}) collective-permute-start(bf16[1,160,320]{2,1,0:T(8,128)(2,1)S(1)} %get-tuple-element.34), channel_id=1, source_target_pairs={{0,8},{4,12},{8,0},{12,4},{16,24},{20,28},{24,16},{28,20},{1,9},{5... | collective-permute-start | bytes 307208 | tf_op jit(solution)/shard_map/ppermute | solution.py:251
  71.2 2.5 %collective-permute-start.24 = (bf16[1,160,320]{2,1,0:T(8,128)(2,1)S(1)}, bf16[1,160,320]{2,1,0:T(8,128)(2,1)S(1)}, u32[]{:S(2)}, u32[]{:S(2)}) collective-permute-start(bf16[1,160,320]{2,1,0:T(8,128)(2,1)S(1)} %get-tuple-element.35), channel_id=1, source_target_pairs={{0,24},{4,28},{8,16},{12,20},{16,8},{20,12},{24,0},{28,4},{1,25},{... | collective-permute-start | bytes 307208 | tf_op jit(solution)/shard_map/ppermute | solution.py:251
  73.7 3.7 %collective-permute-start.23 = (bf16[1,160,320]{2,1,0:T(8,128)(2,1)S(1)}, bf16[1,160,320]{2,1,0:T(8,128)(2,1)S(1)}, u32[]{:S(2)}, u32[]{:S(2)}) collective-permute-start(bf16[1,160,320]{2,1,0:T(8,128)(2,1)S(1)} %get-tuple-element.36), channel_id=1, source_target_pairs={{0,16},{4,20},{8,24},{12,28},{16,0},{20,4},{24,8},{28,12},{1,17},{... | collective-permute-start | bytes 307208 | tf_op jit(solution)/shard_map/ppermute | solution.py:251
  77.4 0.7 collective-permute-done.14
  78.1 0.1 fusion.1
  78.3 4.2 %collective-permute-start.16 = (bf16[1,80,360]{2,1,0:T(8,128)(2,1)S(1)}, bf16[1,80,360]{2,1,0:T(8,128)(2,1)S(1)}, u32[]{:S(2)}, u32[]{:S(2)}) collective-permute-start(bf16[1,80,360]{2,1,0:T(8,128)(2,1)S(1)} %get-tuple-element.41), channel_id=1, source_target_pairs={{0,8},{4,12},{8,0},{12,4},{16,24},{20,28},{24,16},{28,20},{1,9},{5... | collective-permute-start | bytes 172808 | tf_op jit(solution)/shard_map/ppermute | solution.py:251
  82.4 2.6 %collective-permute-start.18 = (bf16[1,80,360]{2,1,0:T(8,128)(2,1)S(1)}, bf16[1,80,360]{2,1,0:T(8,128)(2,1)S(1)}, u32[]{:S(2)}, u32[]{:S(2)}) collective-permute-start(bf16[1,80,360]{2,1,0:T(8,128)(2,1)S(1)} %get-tuple-element.42), channel_id=1, source_target_pairs={{0,24},{4,28},{8,16},{12,20},{16,8},{20,12},{24,0},{28,4},{1,25},{... | collective-permute-start | bytes 172808 | tf_op jit(solution)/shard_map/ppermute | solution.py:251
  85.1 1.8 %collective-permute-start.27 = (bf16[160,320]{1,0:T(8,128)(2,1)S(1)}, bf16[160,320]{1,0:T(8,128)(2,1)S(1)}, u32[]{:S(2)}, u32[]{:S(2)}) collective-permute-start(bf16[160,320]{1,0:T(8,128)(2,1)S(1)} %fusion.10), channel_id=1, source_target_pairs={{0,3},{1,2},{2,1},{3,0},{4,7},{5,6},{6,5},{7,4},{8,11},{9,10},{10,... | collective-permute-start | bytes 307208 | tf_op jit(solution)/shard_map/ppermute | solution.py:251
  86.9 0.3 collective-permute-start.26
  87.2 1.4 %collective-permute-start.25 = (bf16[160,320]{1,0:T(8,128)(2,1)S(1)}, bf16[160,320]{1,0:T(8,128)(2,1)S(1)}, u32[]{:S(2)}, u32[]{:S(2)}) collective-permute-start(bf16[160,320]{1,0:T(8,128)(2,1)S(1)} %fusion.10), channel_id=1, source_target_pairs={{0,1},{1,0},{2,3},{3,2},{4,5},{5,4},{6,7},{7,6},{8,9},{9,8},{10,11... | collective-permute-start | bytes 307208 | tf_op jit(solution)/shard_map/ppermute | solution.py:251
  88.7 0.6 collective-permute-done.18
  89.2 1.9 %collective-permute-done.17 = bf16[1,80,360]{2,1,0:T(8,128)(2,1)S(1)} collective-permute-done((bf16[1,80,360]{2,1,0:T(8,128)(2,1)S(1)}, bf16[1,80,360]{2,1,0:T(8,128)(2,1)S(1)}, u32[]{:S(2)}, u32[]{:S(2)}) %collective-permute-start.17) | collective-permute-done | bytes 57632 | tf_op jit(solution)/shard_map/ppermute | solution.py:251
  91.2 0.8 collective-permute-start.21
  92.0 0.3 collective-permute-start.20
  92.3 2.4 %collective-permute-start.19 = (bf16[1,80,360]{2,1,0:T(8,128)(2,1)S(1)}, bf16[1,80,360]{2,1,0:T(8,128)(2,1)S(1)}, u32[]{:S(2)}, u32[]{:S(2)}) collective-permute-start(bf16[1,80,360]{2,1,0:T(8,128)(2,1)S(1)} %fusion.12), channel_id=1, source_target_pairs={{0,1},{1,0},{2,3},{3,2},{4,5},{5,4},{6,7},{7,6},{8,9},{9,8},{10,11... | collective-permute-start | bytes 172808 | tf_op jit(solution)/shard_map/ppermute | solution.py:251
  94.7 0.8 fusion.9
  95.5 1.3 %collective-permute-done.21 = bf16[1,80,360]{2,1,0:T(8,128)(2,1)S(1)} collective-permute-done((bf16[1,80,360]{2,1,0:T(8,128)(2,1)S(1)}, bf16[1,80,360]{2,1,0:T(8,128)(2,1)S(1)}, u32[]{:S(2)}, u32[]{:S(2)}) %collective-permute-start.21) | collective-permute-done | bytes 57632 | tf_op jit(solution)/shard_map/ppermute | solution.py:251
  96.9 0.1 collective-permute-done.19
  97.1 0.8 convert_bitcast_fusion
  (39 shorter events, 0.7 us)
Async XLA Ops:
  1.8 12.6 %collective-permute-start.2 = (bf16[1,80,360]{2,1,0:T(8,128)(2,1)S(1)}, bf16[1,80,360]{2,1,0:T(8,128)(2,1)S(1)}, u32[]{:S(2)}, u32[]{:S(2)}) collective-permute-start(bf16[1,80,360]{2,1,0:T(8,128)(2,1)S(1)} %get-tuple-element.47), channel_id=1, source_target_pairs={{0,24},{4,28},{8,16},{12,20},{16,8},{20,12},{24,0},{28,4},{1,25},{... | collective-permute-start | bytes 172808 | tf_op jit(solution)/shard_map/ppermute | solution.py:251
  6.9 8.2 %collective-permute-start.1 = (bf16[1,80,360]{2,1,0:T(8,128)(2,1)S(1)}, bf16[1,80,360]{2,1,0:T(8,128)(2,1)S(1)}, u32[]{:S(2)}, u32[]{:S(2)}) collective-permute-start(bf16[1,80,360]{2,1,0:T(8,128)(2,1)S(1)} %get-tuple-element.47), channel_id=1, source_target_pairs={{0,16},{4,20},{8,24},{12,28},{16,0},{20,4},{24,8},{28,12},{1,17},{... | collective-permute-start | bytes 172808 | tf_op jit(solution)/shard_map/ppermute | solution.py:251
  6.9 8.2 %collective-permute-start = (bf16[1,80,360]{2,1,0:T(8,128)(2,1)S(1)}, bf16[1,80,360]{2,1,0:T(8,128)(2,1)S(1)}, u32[]{:S(2)}, u32[]{:S(2)}) collective-permute-start(bf16[1,80,360]{2,1,0:T(8,128)(2,1)S(1)} %get-tuple-element.47), channel_id=1, source_target_pairs={{0,8},{4,12},{8,0},{12,4},{16,24},{20,28},{24,16},{28,20},{1,9},{5... | collective-permute-start | bytes 172808 | tf_op jit(solution)/shard_map/ppermute | solution.py:251
  10.6 8.1 %collective-permute-start.8 = (bf16[1,160,320]{2,1,0:T(8,128)(2,1)S(1)}, bf16[1,160,320]{2,1,0:T(8,128)(2,1)S(1)}, u32[]{:S(2)}, u32[]{:S(2)}) collective-permute-start(bf16[1,160,320]{2,1,0:T(8,128)(2,1)S(1)} %bitcast.74), channel_id=1, source_target_pairs={{0,24},{4,28},{8,16},{12,20},{16,8},{20,12},{24,0},{28,4},{1,25},{... | collective-permute-start | bytes 307208 | tf_op jit(solution)/shard_map/ppermute | solution.py:251
  14.4 16.9 %collective-permute-start.7 = (bf16[1,160,320]{2,1,0:T(8,128)(2,1)S(1)}, bf16[1,160,320]{2,1,0:T(8,128)(2,1)S(1)}, u32[]{:S(2)}, u32[]{:S(2)}) collective-permute-start(bf16[1,160,320]{2,1,0:T(8,128)(2,1)S(1)} %bitcast.75), channel_id=1, source_target_pairs={{0,16},{4,20},{8,24},{12,28},{16,0},{20,4},{24,8},{28,12},{1,17},{... | collective-permute-start | bytes 307208 | tf_op jit(solution)/shard_map/ppermute | solution.py:251
  14.4 16.9 %collective-permute-start.6 = (bf16[1,160,320]{2,1,0:T(8,128)(2,1)S(1)}, bf16[1,160,320]{2,1,0:T(8,128)(2,1)S(1)}, u32[]{:S(2)}, u32[]{:S(2)}) collective-permute-start(bf16[1,160,320]{2,1,0:T(8,128)(2,1)S(1)} %bitcast.76), channel_id=1, source_target_pairs={{0,8},{4,12},{8,0},{12,4},{16,24},{20,28},{24,16},{28,20},{1,9},{5... | collective-permute-start | bytes 307208 | tf_op jit(solution)/shard_map/ppermute | solution.py:251
  15.2 16.2 %collective-permute-start.5 = (bf16[1,3,80,360]{3,2,1,0:T(8,128)(2,1)S(1)}, bf16[1,3,80,360]{3,2,1,0:T(8,128)(2,1)S(1)}, u32[]{:S(2)}, u32[]{:S(2)}) collective-permute-start(bf16[1,3,80,360]{3,2,1,0:T(8,128)(2,1)S(1)} %slice_bitcast_fusion.4), channel_id=1, source_target_pairs={{0,3},{1,2},{2,1},{3,0},{4,7},{5,6},{6,5},{7,4},{8,11},{9,10},{10,... | collective-permute-start | bytes 518408 | tf_op jit(solution)/shard_map/ppermute | solution.py:251
  17.9 13.6 %collective-permute-start.4 = (bf16[1,3,80,360]{3,2,1,0:T(8,128)(2,1)S(1)}, bf16[1,3,80,360]{3,2,1,0:T(8,128)(2,1)S(1)}, u32[]{:S(2)}, u32[]{:S(2)}) collective-permute-start(bf16[1,3,80,360]{3,2,1,0:T(8,128)(2,1)S(1)} %slice_bitcast_fusion.4), channel_id=1, source_target_pairs={{0,2},{1,3},{2,0},{3,1},{4,6},{5,7},{6,4},{7,5},{8,10},{9,11},{10,... | collective-permute-start | bytes 518408 | tf_op jit(solution)/shard_map/ppermute | solution.py:251
  18.7 12.8 %collective-permute-start.3 = (bf16[1,3,80,360]{3,2,1,0:T(8,128)(2,1)S(1)}, bf16[1,3,80,360]{3,2,1,0:T(8,128)(2,1)S(1)}, u32[]{:S(2)}, u32[]{:S(2)}) collective-permute-start(bf16[1,3,80,360]{3,2,1,0:T(8,128)(2,1)S(1)} %slice_bitcast_fusion.4), channel_id=1, source_target_pairs={{0,1},{1,0},{2,3},{3,2},{4,5},{5,4},{6,7},{7,6},{8,9},{9,8},{10,11... | collective-permute-start | bytes 518408 | tf_op jit(solution)/shard_map/ppermute | solution.py:251
  31.3 3.8 %copy-start = (bf16[15,320,256]{2,1,0:T(8,128)(2,1)S(1)}, bf16[15,320,256]{2,1,0:T(8,128)(2,1)}, u32[]{:S(2)}) copy-start(bf16[15,320,256]{2,1,0:T(8,128)(2,1)} %group_norm.1.normed_ref) | copy-start | bytes 7372804
  31.3 3.8 %copy-start.1 = (s32[1,4]{1,0:T(1,128)S(1)}, s32[1,4]{1,0:T(1,128)}, u32[]{:S(2)}) copy-start(s32[1,4]{1,0:T(1,128)} %counts_ref.1) | copy-start | bytes 52
  31.7 3.3 %collective-permute-start.9 = (bf16[4,4,80,360]{3,2,1,0:T(8,128)(2,1)S(1)}, bf16[4,4,80,360]{3,2,1,0:T(8,128)(2,1)S(1)}, u32[]{:S(2)}, u32[]{:S(2)}) collective-permute-start(bf16[4,4,80,360]{3,2,1,0:T(8,128)(2,1)S(1)} %maximum_maximum_fusion.own_ref), channel_id=1, source_target_pairs={{0,4},{4,0},{8,12},{12,8},{16,20},{20,16},{24,28},{28,24},{1,5},{5... | collective-permute-start | bytes 2764808 | tf_op jit(solution)/shard_map/ppermute | solution.py:251
  31.8 3.3 %collective-permute-start.10 = (bf16[4,160,320]{2,1,0:T(8,128)(2,1)S(1)}, bf16[4,160,320]{2,1,0:T(8,128)(2,1)S(1)}, u32[]{:S(2)}, u32[]{:S(2)}) collective-permute-start(bf16[4,160,320]{2,1,0:T(8,128)(2,1)S(1)} %pad_maximum_fusion.1.own_time_ref), channel_id=1, source_target_pairs={{0,4},{4,0},{8,12},{12,8},{16,20},{20,16},{24,28},{28,24},{1,5},{5... | collective-permute-start | bytes 1228808 | tf_op jit(solution)/shard_map/ppermute | solution.py:251
  49.0 3.4 %collective-permute-start.11 = (bf16[4,4,80,360]{3,2,1,0:T(8,128)(2,1)S(1)}, bf16[4,4,80,360]{3,2,1,0:T(8,128)(2,1)S(1)}, u32[]{:S(2)}, u32[]{:S(2)}) collective-permute-start(bf16[4,4,80,360]{3,2,1,0:T(8,128)(2,1)S(1)} %get-tuple-element.26), channel_id=1, source_target_pairs={{0,4},{4,0},{8,12},{12,8},{16,20},{20,16},{24,28},{28,24},{1,5},{5... | collective-permute-start | bytes 2764808 | tf_op jit(solution)/shard_map/ppermute | solution.py:251
  49.2 3.1 %collective-permute-start.12 = (bf16[4,160,320]{2,1,0:T(8,128)(2,1)S(1)}, bf16[4,160,320]{2,1,0:T(8,128)(2,1)S(1)}, u32[]{:S(2)}, u32[]{:S(2)}) collective-permute-start(bf16[4,160,320]{2,1,0:T(8,128)(2,1)S(1)} %get-tuple-element.28), channel_id=1, source_target_pairs={{0,4},{4,0},{8,12},{12,8},{16,20},{20,16},{24,28},{28,24},{1,5},{5... | collective-permute-start | bytes 1228808 | tf_op jit(solution)/shard_map/ppermute | solution.py:251
  52.8 20.9 %collective-permute-start.13 = (bf16[1,4,80,360]{3,2,1,0:T(8,128)(2,1)S(1)}, bf16[1,4,80,360]{3,2,1,0:T(8,128)(2,1)S(1)}, u32[]{:S(2)}, u32[]{:S(2)}) collective-permute-start(bf16[1,4,80,360]{3,2,1,0:T(8,128)(2,1)S(1)} %get-tuple-element.31), channel_id=1, source_target_pairs={{0,1},{1,0},{2,3},{3,2},{4,5},{5,4},{6,7},{7,6},{8,9},{9,8},{10,11... | collective-permute-start | bytes 691208 | tf_op jit(solution)/shard_map/ppermute | solution.py:251
  64.1 13.3 %collective-permute-start.15 = (bf16[1,4,80,360]{3,2,1,0:T(8,128)(2,1)S(1)}, bf16[1,4,80,360]{3,2,1,0:T(8,128)(2,1)S(1)}, u32[]{:S(2)}, u32[]{:S(2)}) collective-permute-start(bf16[1,4,80,360]{3,2,1,0:T(8,128)(2,1)S(1)} %get-tuple-element.32), channel_id=1, source_target_pairs={{0,3},{1,2},{2,1},{3,0},{4,7},{5,6},{6,5},{7,4},{8,11},{9,10},{10,... | collective-permute-start | bytes 691208 | tf_op jit(solution)/shard_map/ppermute | solution.py:251
  65.1 13.0 %collective-permute-start.14 = (bf16[1,4,80,360]{3,2,1,0:T(8,128)(2,1)S(1)}, bf16[1,4,80,360]{3,2,1,0:T(8,128)(2,1)S(1)}, u32[]{:S(2)}, u32[]{:S(2)}) collective-permute-start(bf16[1,4,80,360]{3,2,1,0:T(8,128)(2,1)S(1)} %get-tuple-element.33), channel_id=1, source_target_pairs={{0,2},{1,3},{2,0},{3,1},{4,6},{5,7},{6,4},{7,5},{8,10},{9,11},{10,... | collective-permute-start | bytes 691208 | tf_op jit(solution)/shard_map/ppermute | solution.py:251
  65.7 19.3 %collective-permute-start.22 = (bf16[1,160,320]{2,1,0:T(8,128)(2,1)S(1)}, bf16[1,160,320]{2,1,0:T(8,128)(2,1)S(1)}, u32[]{:S(2)}, u32[]{:S(2)}) collective-permute-start(bf16[1,160,320]{2,1,0:T(8,128)(2,1)S(1)} %get-tuple-element.34), channel_id=1, source_target_pairs={{0,8},{4,12},{8,0},{12,4},{16,24},{20,28},{24,16},{28,20},{1,9},{5... | collective-permute-start | bytes 307208 | tf_op jit(solution)/shard_map/ppermute | solution.py:251
  71.2 13.8 %collective-permute-start.24 = (bf16[1,160,320]{2,1,0:T(8,128)(2,1)S(1)}, bf16[1,160,320]{2,1,0:T(8,128)(2,1)S(1)}, u32[]{:S(2)}, u32[]{:S(2)}) collective-permute-start(bf16[1,160,320]{2,1,0:T(8,128)(2,1)S(1)} %get-tuple-element.35), channel_id=1, source_target_pairs={{0,24},{4,28},{8,16},{12,20},{16,8},{20,12},{24,0},{28,4},{1,25},{... | collective-permute-start | bytes 307208 | tf_op jit(solution)/shard_map/ppermute | solution.py:251
  73.7 11.3 %collective-permute-start.23 = (bf16[1,160,320]{2,1,0:T(8,128)(2,1)S(1)}, bf16[1,160,320]{2,1,0:T(8,128)(2,1)S(1)}, u32[]{:S(2)}, u32[]{:S(2)}) collective-permute-start(bf16[1,160,320]{2,1,0:T(8,128)(2,1)S(1)} %get-tuple-element.36), channel_id=1, source_target_pairs={{0,16},{4,20},{8,24},{12,28},{16,0},{20,4},{24,8},{28,12},{1,17},{... | collective-permute-start | bytes 307208 | tf_op jit(solution)/shard_map/ppermute | solution.py:251
  78.3 8.9 %collective-permute-start.16 = (bf16[1,80,360]{2,1,0:T(8,128)(2,1)S(1)}, bf16[1,80,360]{2,1,0:T(8,128)(2,1)S(1)}, u32[]{:S(2)}, u32[]{:S(2)}) collective-permute-start(bf16[1,80,360]{2,1,0:T(8,128)(2,1)S(1)} %get-tuple-element.41), channel_id=1, source_target_pairs={{0,8},{4,12},{8,0},{12,4},{16,24},{20,28},{24,16},{28,20},{1,9},{5... | collective-permute-start | bytes 172808 | tf_op jit(solution)/shard_map/ppermute | solution.py:251
  82.4 6.8 %collective-permute-start.18 = (bf16[1,80,360]{2,1,0:T(8,128)(2,1)S(1)}, bf16[1,80,360]{2,1,0:T(8,128)(2,1)S(1)}, u32[]{:S(2)}, u32[]{:S(2)}) collective-permute-start(bf16[1,80,360]{2,1,0:T(8,128)(2,1)S(1)} %get-tuple-element.42), channel_id=1, source_target_pairs={{0,24},{4,28},{8,16},{12,20},{16,8},{20,12},{24,0},{28,4},{1,25},{... | collective-permute-start | bytes 172808 | tf_op jit(solution)/shard_map/ppermute | solution.py:251
  85.0 6.1 %collective-permute-start.17 = (bf16[1,80,360]{2,1,0:T(8,128)(2,1)S(1)}, bf16[1,80,360]{2,1,0:T(8,128)(2,1)S(1)}, u32[]{:S(2)}, u32[]{:S(2)}) collective-permute-start(bf16[1,80,360]{2,1,0:T(8,128)(2,1)S(1)} %get-tuple-element.43), channel_id=1, source_target_pairs={{0,16},{4,20},{8,24},{12,28},{16,0},{20,4},{24,8},{28,12},{1,17},{... | collective-permute-start | bytes 172808 | tf_op jit(solution)/shard_map/ppermute | solution.py:251
  85.1 7.2 %collective-permute-start.27 = (bf16[160,320]{1,0:T(8,128)(2,1)S(1)}, bf16[160,320]{1,0:T(8,128)(2,1)S(1)}, u32[]{:S(2)}, u32[]{:S(2)}) collective-permute-start(bf16[160,320]{1,0:T(8,128)(2,1)S(1)} %fusion.10), channel_id=1, source_target_pairs={{0,3},{1,2},{2,1},{3,0},{4,7},{5,6},{6,5},{7,4},{8,11},{9,10},{10,... | collective-permute-start | bytes 307208 | tf_op jit(solution)/shard_map/ppermute | solution.py:251
  86.9 7.8 %collective-permute-start.26 = (bf16[160,320]{1,0:T(8,128)(2,1)S(1)}, bf16[160,320]{1,0:T(8,128)(2,1)S(1)}, u32[]{:S(2)}, u32[]{:S(2)}) collective-permute-start(bf16[160,320]{1,0:T(8,128)(2,1)S(1)} %fusion.10), channel_id=1, source_target_pairs={{0,2},{1,3},{2,0},{3,1},{4,6},{5,7},{6,4},{7,5},{8,10},{9,11},{10,... | collective-permute-start | bytes 307208 | tf_op jit(solution)/shard_map/ppermute | solution.py:251
  87.2 7.5 %collective-permute-start.25 = (bf16[160,320]{1,0:T(8,128)(2,1)S(1)}, bf16[160,320]{1,0:T(8,128)(2,1)S(1)}, u32[]{:S(2)}, u32[]{:S(2)}) collective-permute-start(bf16[160,320]{1,0:T(8,128)(2,1)S(1)} %fusion.10), channel_id=1, source_target_pairs={{0,1},{1,0},{2,3},{3,2},{4,5},{5,4},{6,7},{7,6},{8,9},{9,8},{10,11... | collective-permute-start | bytes 307208 | tf_op jit(solution)/shard_map/ppermute | solution.py:251
  91.2 5.6 %collective-permute-start.21 = (bf16[1,80,360]{2,1,0:T(8,128)(2,1)S(1)}, bf16[1,80,360]{2,1,0:T(8,128)(2,1)S(1)}, u32[]{:S(2)}, u32[]{:S(2)}) collective-permute-start(bf16[1,80,360]{2,1,0:T(8,128)(2,1)S(1)} %fusion.12), channel_id=1, source_target_pairs={{0,3},{1,2},{2,1},{3,0},{4,7},{5,6},{6,5},{7,4},{8,11},{9,10},{10,... | collective-permute-start | bytes 172808 | tf_op jit(solution)/shard_map/ppermute | solution.py:251
  92.0 4.9 %collective-permute-start.20 = (bf16[1,80,360]{2,1,0:T(8,128)(2,1)S(1)}, bf16[1,80,360]{2,1,0:T(8,128)(2,1)S(1)}, u32[]{:S(2)}, u32[]{:S(2)}) collective-permute-start(bf16[1,80,360]{2,1,0:T(8,128)(2,1)S(1)} %fusion.12), channel_id=1, source_target_pairs={{0,2},{1,3},{2,0},{3,1},{4,6},{5,7},{6,4},{7,5},{8,10},{9,11},{10,... | collective-permute-start | bytes 172808 | tf_op jit(solution)/shard_map/ppermute | solution.py:251
  92.3 4.7 %collective-permute-start.19 = (bf16[1,80,360]{2,1,0:T(8,128)(2,1)S(1)}, bf16[1,80,360]{2,1,0:T(8,128)(2,1)S(1)}, u32[]{:S(2)}, u32[]{:S(2)}) collective-permute-start(bf16[1,80,360]{2,1,0:T(8,128)(2,1)S(1)} %fusion.12), channel_id=1, source_target_pairs={{0,1},{1,0},{2,3},{3,2},{4,5},{5,4},{6,7},{7,6},{8,9},{9,8},{10,11... | collective-permute-start | bytes 172808 | tf_op jit(solution)/shard_map/ppermute | solution.py:251

commit v5 on v4

--- a/solution.py
+++ b/solution.py
@@ -3,6 +3,7 @@
 
 import jax
 import jax.numpy as jnp
+import numpy as np
 from jax import lax
 from jax.experimental import pallas as pl
 from jax.experimental.pallas import tpu as pltpu
@@ -26,31 +27,32 @@
     scale = 1.0 / (group_width * pixels)
     lane = lax.broadcasted_iota(jnp.int32, (channels, LANES), 1)
 
-    def group_mean(row_sums):
-        high = row_sums.astype(bf16).astype(f32)
-        middle = (row_sums - high).astype(bf16).astype(f32)
-        low = row_sums - high - middle
-        terms = jnp.where(
-            lane == 0, high, jnp.where(lane == 1, middle, jnp.where(lane == 2, low, 0.0))
-        ).astype(bf16)
-        summed = jnp.dot(same_group, terms, preferred_element_type=f32)
-        return jnp.sum(summed, axis=1, keepdims=True) * scale
-
-    for at in range(number):
-        values = tiles_ref[at].astype(f32)
-        centred = values - group_mean(jnp.sum(values, axis=1, keepdims=True))
-        variance = group_mean(jnp.sum(centred * centred, axis=1, keepdims=True))
-        scaled = centred * lax.rsqrt(variance + 1e-05)
-        half = 0.5 * scaled
-        out_ref[at] = (half + half * jnp.tanh(half)).astype(bf16)
+    def group_means(values):
+        row_sums = jnp.zeros((channels, LANES), f32)
+        for t, value in enumerate(values):
+            row_sums = jnp.where(lane == t, jnp.sum(value, axis=1, keepdims=True), row_sums)
+        high = row_sums.astype(bf16)
+        rest = row_sums - high.astype(f32)
+        middle = rest.astype(bf16)
+        low = (rest - middle.astype(f32)).astype(bf16)
+        return scale * sum(
+            jnp.dot(same_group, term, preferred_element_type=f32) for term in (high, middle, low)
+        )
+
+    mean = group_means([tiles_ref[t].astype(f32) for t in range(number)])
+    centred = [tiles_ref[t].astype(f32) - mean[:, t : t + 1] for t in range(number)]
+    spread = lax.rsqrt(group_means([value * value for value in centred]) + 1e-05)
+    for t in range(number):
+        half = (tiles_ref[t].astype(f32) - mean[:, t : t + 1]) * (0.5 * spread[:, t : t + 1])
+        out_ref[t] = (half + half * jnp.tanh(half)).astype(bf16)
 
 
 def group_norm(tiles):
     number, channels, pixels = tiles.shape
     step = tiles_per_step(number)
     group_width = channels // GROUPS
-    group = jnp.arange(channels, dtype=jnp.int32) // group_width
-    same_group = (group[:, None] == group[None, :]).astype(bf16)
+    group = np.arange(channels) // group_width
+    same_group = jnp.asarray(group[:, None] == group[None, :], bf16)
     block = pl.BlockSpec((step, channels, pixels), lambda i: (i, 0, 0))
     return pl.pallas_call(
         functools.partial(norm_kernel, group_width),
@@ -314,17 +316,17 @@
     plane_bits = shard_bits - 1
 
     master = conv_master.T.astype(bf16).reshape(parts, outs // parts, rows)
-    time_master = temb_master.astype(bf16)
     mine = [lax.dynamic_index_in_dim(master, part ^ m, 0, keepdims=False) for m in range(parts)]
-    over_planes = gather_partners(mine[0], "fsdp", 1, plane_bits)
-    features = time_features(jnp.pad(timesteps[0], (0, LANES - number)), time_rows * shards)
-    time_master, features = lax.optimization_barrier((time_master, features))
+    time_master, first = lax.optimization_barrier((temb_master, mine[0]))
+    time_master = time_master.astype(bf16)
+    over_planes = gather_partners(first, "fsdp", 1, plane_bits)
     own_time = gather_partners(time_master, "fsdp", 1, plane_bits)
     over_planes, tiles_then = lax.optimization_barrier((over_planes, tiles))
     far = gather_partners(over_planes[1:], "dp", 0, part_bits)
     normed = group_norm(tiles_then)
     own = jnp.concatenate([jnp.stack(mine)[:, None], far], axis=1)
-    own, own_time, normed = lax.optimization_barrier((own, own_time, normed))
+    own, own_time, normed, times = lax.optimization_barrier((own, own_time, normed, timesteps[0]))
+    features = time_features(jnp.pad(times, (0, LANES - number)), time_rows * shards)
     other, other_time = swap(own, "fsdp", 1), swap(own_time, "fsdp", 1)
 
     predicted, keep, send, keep_time, send_time = conv_both(

time: 98.5 us -> 94.2 us (0.956)
  starting transfers between devices: 54.4 us -> 41.9 us
  Pallas kernels: 24.3 us -> 32.6 us
  waiting for transfers between devices: 10.5 us -> 12.2 us
  other arithmetic: 7.64 us -> 6.2 us
    ppermute x28, starting transfers between devices: 54.4 us -> 41.9 us  [swap(): return lax.ppermute(values, axis, pairs)]
    pallas_call x1, Pallas kernels: 13.9 us -> 24.8 us  [conv_both(): pl.pallas_call(functools.partial(conv_kernel, steps), grid_spec=pltpu.Pre...]
    pallas_call x1, Pallas kernels: 10.3 us -> 7.73 us  [group_norm(): pl.pallas_call(functools.partial(norm_kernel, group_width), grid=(number...]
    convert_element_type x2 -> x0, other arithmetic: 1.76 us -> none  [the longest x1 0.96 us: per_device(): time_master = temb_master.astype(bf16)]
    ppermute x28, waiting for transfers between devices: 10.5 us -> 12.2 us  [swap(): return lax.ppermute(values, axis, pairs)]
  transfers between devices with their start and end apart: 28 -> 28, of which waited for: 9 -> 9; matrix products, arithmetic and copies ran while one was open for 5% -> 4% of each run, Pallas kernels for 11% -> 8%
where the time goes in v5:
time: 94.2 us; the launch traced here: 94 us
  starting transfers between devices  41.9 us (44%)
  Pallas kernels  32.6 us (35%)
  waiting for transfers between devices  12.2 us (13%)
  other arithmetic  6.2 us (7%)
    ppermute x28, starting transfers between devices, swap(): return lax.ppermute(values, axis, pairs)  41.9 us
    pallas_call x1, Pallas kernels, conv_both(): pl.pallas_call(functools.partial(conv_kernel, steps), grid_spec=pltpu.Pre...  24.8 us
    ppermute x28, waiting for transfers between devices, swap(): return lax.ppermute(values, axis, pairs)  12.2 us
    pallas_call x1, Pallas kernels, group_norm(): pl.pallas_call(functools.partial(norm_kernel, group_width), grid=(number...  7.73 us
  transfers between devices with their start and end apart: 28, of which 9 were waited for; matrix products, arithmetic and copies ran while one was open for 4% of the time, Pallas kernels for 8%

profile of v5, /device:TPU:0, one launch (start us, length us, event | category | flops | bytes accessed | tf_op | source)
XLA Modules:
  0.0 94.0 jit_solution(4236941982815607316)
XLA Ops:
  0.6 1.1 %convert_element_type.135 = bf16[360,320]{0,1:T(8,128)(2,1)S(1)} convert(f32[360,320]{0,1:T(8,128)} %param.11) | non-fusion elementwise | flops 115200 | bytes 691200 | tf_op jit(solution)/shard_map/convert_element_type | solution.py:318
  1.8 5.1 %collective-permute-start.2 = (bf16[1,80,360]{2,1,0:T(8,128)(2,1)S(1)}, bf16[1,80,360]{2,1,0:T(8,128)(2,1)S(1)}, u32[]{:S(2)}, u32[]{:S(2)}) collective-permute-start(bf16[1,80,360]{2,1,0:T(8,128)(2,1)S(1)} %get-tuple-element.49), channel_id=1, source_target_pairs={{0,24},{4,28},{8,16},{12,20},{16,8},{20,12},{24,0},{28,4},{1,25},{... | collective-permute-start | bytes 172808 | tf_op jit(solution)/shard_map/ppermute | solution.py:253
  6.9 0.6 collective-permute-start
  7.5 1.0 %convert_bitcast_fusion.1 = bf16[1,160,320]{2,1,0:T(8,128)(2,1)S(1)} fusion(f32[160,320]{1,0:T(8,128)} %param.12), kind=kLoop, calls=%fused_computation.33 | loop fusion | flops 51200 | bytes 307200 | tf_op jit(solution)/shard_map/broadcast_in_dim | solution.py:266
  8.5 3.8 %collective-permute-start.8 = (bf16[1,160,320]{2,1,0:T(8,128)(2,1)S(1)}, bf16[1,160,320]{2,1,0:T(8,128)(2,1)S(1)}, u32[]{:S(2)}, u32[]{:S(2)}) collective-permute-start(bf16[1,160,320]{2,1,0:T(8,128)(2,1)S(1)} %convert_bitcast_fusion.1), channel_id=1, source_target_pairs={{0,24},{4,28},{8,16},{12,20},{16,8},{20,12},{24,0},{28,4},{1,25},{... | collective-permute-start | bytes 307208 | tf_op jit(solution)/shard_map/ppermute | solution.py:253
  12.3 0.6 collective-permute-start.6
  12.9 0.8 collective-permute-done.1
  13.8 2.5 %collective-permute-start.5 = (bf16[1,3,80,360]{3,2,1,0:T(8,128)(2,1)S(1)}, bf16[1,3,80,360]{3,2,1,0:T(8,128)(2,1)S(1)}, u32[]{:S(2)}, u32[]{:S(2)}) collective-permute-start(bf16[1,3,80,360]{3,2,1,0:T(8,128)(2,1)S(1)} %slice_bitcast_fusion.4), channel_id=1, source_target_pairs={{0,3},{1,2},{2,1},{3,0},{4,7},{5,6},{6,5},{7,4},{8,11},{9,10},{10,... | collective-permute-start | bytes 518408 | tf_op jit(solution)/shard_map/ppermute | solution.py:253
  16.4 0.5 collective-permute-start.4
  16.9 1.4 %collective-permute-start.3 = (bf16[1,3,80,360]{3,2,1,0:T(8,128)(2,1)S(1)}, bf16[1,3,80,360]{3,2,1,0:T(8,128)(2,1)S(1)}, u32[]{:S(2)}, u32[]{:S(2)}) collective-permute-start(bf16[1,3,80,360]{3,2,1,0:T(8,128)(2,1)S(1)} %slice_bitcast_fusion.4), channel_id=1, source_target_pairs={{0,1},{1,0},{2,3},{3,2},{4,5},{5,4},{6,7},{7,6},{8,9},{9,8},{10,11... | collective-permute-start | bytes 518408 | tf_op jit(solution)/shard_map/ppermute | solution.py:253
  18.3 7.7 %group_norm.1.normed_ref = bf16[15,320,256]{2,1,0:T(8,128)(2,1)} custom-call(bf16[320,320]{1,0:T(8,128)(2,1)} %constant.41.clone.same_ref, bf16[15,320,256]{2,1,0:T(8,128)(2,1)} %bitcast.70), custom_call_target="tpu_custom_call" | custom-call | flops 24576000 | bytes 4915200 | tf_op jit(solution)/shard_map/group_norm/pallas_call | solution.py:57
  26.1 0.1 pad_maximum_fusion.1.own_time_ref
  26.2 0.3 maximum_maximum_fusion.own_ref
  26.5 0.1 collective-permute-start.9
  26.6 0.5 collective-permute-start.10
  27.1 1.2 %multiply_cosine_fusion = (f32[640,128]{1,0:T(8,128)S(1)}, f32[640,128]{1,0:T(8,128)S(1)}) fusion(f32[128]{0:T(128)S(1)} %pad_convert_fusion, f32[640]{0:T(1024)S(1)} %multiply_exponential_fusion), kind=kLoop, calls=%fused_computation.11 | loop fusion | flops 81920 | bytes 658432 | tf_op jit(solution)/shard_map/cos | solution.py:302
  28.3 0.2 multiply_convert_fusion.features_ref
  28.5 1.3 %collective-permute-done.10.other_time_ref = bf16[4,160,320]{2,1,0:T(8,128)(2,1)S(1)} collective-permute-done((bf16[4,160,320]{2,1,0:T(8,128)(2,1)S(1)}, bf16[4,160,320]{2,1,0:T(8,128)(2,1)S(1)}, u32[]{:S(2)}, u32[]{:S(2)}) %collective-permute-start.10) | collective-permute-done | bytes 409632 | tf_op jit(solution)/shard_map/ppermute | solution.py:253
  29.8 24.8 %conv_both.1 = (bf16[15,320,256]{2,1,0:T(8,128)(2,1)}, bf16[4,4,80,360]{3,2,1,0:T(8,128)(2,1)S(1)}, bf16[4,4,80,360]{3,2,1,0:T(8,128)(2,1)S(1)}, bf16[4,160,320]...) custom-call(s32[1,4]{1,0:T(1,128)S(1)} %copy-done.1, bf16[4,4,80,360]{3,2,1,0:T(8,128)(2,1)S(1)} %maximum_maximum_fusion.own_ref, ...), custom_call_target="tpu_custom_call" | custom-call | flops 14155776000 | bytes 9830400 | tf_op jit(solution)/shard_map/conv_both/pallas_call | solution.py:217
  54.7 0.5 collective-permute-start.12
  55.2 2.8 %collective-permute-done.12 = bf16[4,160,320]{2,1,0:T(8,128)(2,1)S(1)} collective-permute-done((bf16[4,160,320]{2,1,0:T(8,128)(2,1)S(1)}, bf16[4,160,320]{2,1,0:T(8,128)(2,1)S(1)}, u32[]{:S(2)}, u32[]{:S(2)}) %collective-permute-start.12) | collective-permute-done | bytes 409632 | tf_op jit(solution)/shard_map/ppermute | solution.py:253
  57.9 0.1 add_convert_fusion.1
  58.1 0.3 add_convert_fusion
  58.3 0.1 slice_bitcast_fusion.2
  58.4 0.7 collective-permute-start.13
  59.1 2.1 %collective-permute-start.15 = (bf16[1,4,80,360]{3,2,1,0:T(8,128)(2,1)S(1)}, bf16[1,4,80,360]{3,2,1,0:T(8,128)(2,1)S(1)}, u32[]{:S(2)}, u32[]{:S(2)}) collective-permute-start(bf16[1,4,80,360]{3,2,1,0:T(8,128)(2,1)S(1)} %get-tuple-element.34), channel_id=1, source_target_pairs={{0,3},{1,2},{2,1},{3,0},{4,7},{5,6},{6,5},{7,4},{8,11},{9,10},{10,... | collective-permute-start | bytes 691208 | tf_op jit(solution)/shard_map/ppermute | solution.py:253
  61.3 0.7 collective-permute-start.14
  62.0 3.0 %collective-permute-start.22 = (bf16[1,160,320]{2,1,0:T(8,128)(2,1)S(1)}, bf16[1,160,320]{2,1,0:T(8,128)(2,1)S(1)}, u32[]{:S(2)}, u32[]{:S(2)}) collective-permute-start(bf16[1,160,320]{2,1,0:T(8,128)(2,1)S(1)} %get-tuple-element.36), channel_id=1, source_target_pairs={{0,8},{4,12},{8,0},{12,4},{16,24},{20,28},{24,16},{28,20},{1,9},{5... | collective-permute-start | bytes 307208 | tf_op jit(solution)/shard_map/ppermute | solution.py:253
  65.1 2.8 %collective-permute-start.24 = (bf16[1,160,320]{2,1,0:T(8,128)(2,1)S(1)}, bf16[1,160,320]{2,1,0:T(8,128)(2,1)S(1)}, u32[]{:S(2)}, u32[]{:S(2)}) collective-permute-start(bf16[1,160,320]{2,1,0:T(8,128)(2,1)S(1)} %get-tuple-element.37), channel_id=1, source_target_pairs={{0,24},{4,28},{8,16},{12,20},{16,8},{20,12},{24,0},{28,4},{1,25},{... | collective-permute-start | bytes 307208 | tf_op jit(solution)/shard_map/ppermute | solution.py:253
  67.9 3.6 %collective-permute-start.23 = (bf16[1,160,320]{2,1,0:T(8,128)(2,1)S(1)}, bf16[1,160,320]{2,1,0:T(8,128)(2,1)S(1)}, u32[]{:S(2)}, u32[]{:S(2)}) collective-permute-start(bf16[1,160,320]{2,1,0:T(8,128)(2,1)S(1)} %get-tuple-element.38), channel_id=1, source_target_pairs={{0,16},{4,20},{8,24},{12,28},{16,0},{20,4},{24,8},{28,12},{1,17},{... | collective-permute-start | bytes 307208 | tf_op jit(solution)/shard_map/ppermute | solution.py:253
  71.5 1.3 %collective-permute-done.15 = bf16[1,4,80,360]{3,2,1,0:T(8,128)(2,1)S(1)} collective-permute-done((bf16[1,4,80,360]{3,2,1,0:T(8,128)(2,1)S(1)}, bf16[1,4,80,360]{3,2,1,0:T(8,128)(2,1)S(1)}, u32[]{:S(2)}, u32[]{:S(2)}) %collective-permute-start.15) | collective-permute-done | bytes 230432 | tf_op jit(solution)/shard_map/ppermute | solution.py:253
  72.8 1.4 %collective-permute-done.14 = bf16[1,4,80,360]{3,2,1,0:T(8,128)(2,1)S(1)} collective-permute-done((bf16[1,4,80,360]{3,2,1,0:T(8,128)(2,1)S(1)}, bf16[1,4,80,360]{3,2,1,0:T(8,128)(2,1)S(1)}, u32[]{:S(2)}, u32[]{:S(2)}) %collective-permute-start.14) | collective-permute-done | bytes 230432 | tf_op jit(solution)/shard_map/ppermute | solution.py:253
  74.2 0.1 fusion.1
  74.3 3.3 %collective-permute-start.16 = (bf16[1,80,360]{2,1,0:T(8,128)(2,1)S(1)}, bf16[1,80,360]{2,1,0:T(8,128)(2,1)S(1)}, u32[]{:S(2)}, u32[]{:S(2)}) collective-permute-start(bf16[1,80,360]{2,1,0:T(8,128)(2,1)S(1)} %get-tuple-element.43), channel_id=1, source_target_pairs={{0,8},{4,12},{8,0},{12,4},{16,24},{20,28},{24,16},{28,20},{1,9},{5... | collective-permute-start | bytes 172808 | tf_op jit(solution)/shard_map/ppermute | solution.py:253
  77.7 2.8 %collective-permute-start.18 = (bf16[1,80,360]{2,1,0:T(8,128)(2,1)S(1)}, bf16[1,80,360]{2,1,0:T(8,128)(2,1)S(1)}, u32[]{:S(2)}, u32[]{:S(2)}) collective-permute-start(bf16[1,80,360]{2,1,0:T(8,128)(2,1)S(1)} %get-tuple-element.44), channel_id=1, source_target_pairs={{0,24},{4,28},{8,16},{12,20},{16,8},{20,12},{24,0},{28,4},{1,25},{... | collective-permute-start | bytes 172808 | tf_op jit(solution)/shard_map/ppermute | solution.py:253
  80.5 0.1 fusion.5
  80.6 1.7 %collective-permute-start.27 = (bf16[160,320]{1,0:T(8,128)(2,1)S(1)}, bf16[160,320]{1,0:T(8,128)(2,1)S(1)}, u32[]{:S(2)}, u32[]{:S(2)}) collective-permute-start(bf16[160,320]{1,0:T(8,128)(2,1)S(1)} %fusion.5), channel_id=1, source_target_pairs={{0,3},{1,2},{2,1},{3,0},{4,7},{5,6},{6,5},{7,4},{8,11},{9,10},{10,... | collective-permute-start | bytes 307208 | tf_op jit(solution)/shard_map/ppermute | solution.py:253
  82.2 1.5 %collective-permute-start.26 = (bf16[160,320]{1,0:T(8,128)(2,1)S(1)}, bf16[160,320]{1,0:T(8,128)(2,1)S(1)}, u32[]{:S(2)}, u32[]{:S(2)}) collective-permute-start(bf16[160,320]{1,0:T(8,128)(2,1)S(1)} %fusion.5), channel_id=1, source_target_pairs={{0,2},{1,3},{2,0},{3,1},{4,6},{5,7},{6,4},{7,5},{8,10},{9,11},{10,... | collective-permute-start | bytes 307208 | tf_op jit(solution)/shard_map/ppermute | solution.py:253
  83.8 0.4 collective-permute-start.25
  84.1 1.5 %collective-permute-done.17 = bf16[1,80,360]{2,1,0:T(8,128)(2,1)S(1)} collective-permute-done((bf16[1,80,360]{2,1,0:T(8,128)(2,1)S(1)}, bf16[1,80,360]{2,1,0:T(8,128)(2,1)S(1)}, u32[]{:S(2)}, u32[]{:S(2)}) %collective-permute-start.17) | collective-permute-done | bytes 57632 | tf_op jit(solution)/shard_map/ppermute | solution.py:253
  85.6 1.7 %collective-permute-start.21 = (bf16[1,80,360]{2,1,0:T(8,128)(2,1)S(1)}, bf16[1,80,360]{2,1,0:T(8,128)(2,1)S(1)}, u32[]{:S(2)}, u32[]{:S(2)}) collective-permute-start(bf16[1,80,360]{2,1,0:T(8,128)(2,1)S(1)} %fusion.7), channel_id=1, source_target_pairs={{0,3},{1,2},{2,1},{3,0},{4,7},{5,6},{6,5},{7,4},{8,11},{9,10},{10,... | collective-permute-start | bytes 172808 | tf_op jit(solution)/shard_map/ppermute | solution.py:253
  87.3 1.5 %collective-permute-start.20 = (bf16[1,80,360]{2,1,0:T(8,128)(2,1)S(1)}, bf16[1,80,360]{2,1,0:T(8,128)(2,1)S(1)}, u32[]{:S(2)}, u32[]{:S(2)}) collective-permute-start(bf16[1,80,360]{2,1,0:T(8,128)(2,1)S(1)} %fusion.7), channel_id=1, source_target_pairs={{0,2},{1,3},{2,0},{3,1},{4,6},{5,7},{6,4},{7,5},{8,10},{9,11},{10,... | collective-permute-start | bytes 172808 | tf_op jit(solution)/shard_map/ppermute | solution.py:253
  88.8 0.4 collective-permute-start.19
  89.2 0.8 fusion.4
  89.9 0.9 collective-permute-done.21
  90.8 0.7 collective-permute-done.20
  91.5 1.5 %collective-permute-done.19 = bf16[1,80,360]{2,1,0:T(8,128)(2,1)S(1)} collective-permute-done((bf16[1,80,360]{2,1,0:T(8,128)(2,1)S(1)}, bf16[1,80,360]{2,1,0:T(8,128)(2,1)S(1)}, u32[]{:S(2)}, u32[]{:S(2)}) %collective-permute-start.19) | collective-permute-done | bytes 57632 | tf_op jit(solution)/shard_map/ppermute | solution.py:253
  93.2 0.8 convert_bitcast_fusion
  (40 shorter events, 0.5 us)
Async XLA Ops:
  1.8 10.5 %collective-permute-start.2 = (bf16[1,80,360]{2,1,0:T(8,128)(2,1)S(1)}, bf16[1,80,360]{2,1,0:T(8,128)(2,1)S(1)}, u32[]{:S(2)}, u32[]{:S(2)}) collective-permute-start(bf16[1,80,360]{2,1,0:T(8,128)(2,1)S(1)} %get-tuple-element.49), channel_id=1, source_target_pairs={{0,24},{4,28},{8,16},{12,20},{16,8},{20,12},{24,0},{28,4},{1,25},{... | collective-permute-start | bytes 172808 | tf_op jit(solution)/shard_map/ppermute | solution.py:253
  6.9 6.9 %collective-permute-start.1 = (bf16[1,80,360]{2,1,0:T(8,128)(2,1)S(1)}, bf16[1,80,360]{2,1,0:T(8,128)(2,1)S(1)}, u32[]{:S(2)}, u32[]{:S(2)}) collective-permute-start(bf16[1,80,360]{2,1,0:T(8,128)(2,1)S(1)} %get-tuple-element.49), channel_id=1, source_target_pairs={{0,16},{4,20},{8,24},{12,28},{16,0},{20,4},{24,8},{28,12},{1,17},{... | collective-permute-start | bytes 172808 | tf_op jit(solution)/shard_map/ppermute | solution.py:253
  6.9 6.9 %collective-permute-start = (bf16[1,80,360]{2,1,0:T(8,128)(2,1)S(1)}, bf16[1,80,360]{2,1,0:T(8,128)(2,1)S(1)}, u32[]{:S(2)}, u32[]{:S(2)}) collective-permute-start(bf16[1,80,360]{2,1,0:T(8,128)(2,1)S(1)} %get-tuple-element.49), channel_id=1, source_target_pairs={{0,8},{4,12},{8,0},{12,4},{16,24},{20,28},{24,16},{28,20},{1,9},{5... | collective-permute-start | bytes 172808 | tf_op jit(solution)/shard_map/ppermute | solution.py:253
  8.5 8.4 %collective-permute-start.8 = (bf16[1,160,320]{2,1,0:T(8,128)(2,1)S(1)}, bf16[1,160,320]{2,1,0:T(8,128)(2,1)S(1)}, u32[]{:S(2)}, u32[]{:S(2)}) collective-permute-start(bf16[1,160,320]{2,1,0:T(8,128)(2,1)S(1)} %convert_bitcast_fusion.1), channel_id=1, source_target_pairs={{0,24},{4,28},{8,16},{12,20},{16,8},{20,12},{24,0},{28,4},{1,25},{... | collective-permute-start | bytes 307208 | tf_op jit(solution)/shard_map/ppermute | solution.py:253
  12.3 13.8 %collective-permute-start.7 = (bf16[1,160,320]{2,1,0:T(8,128)(2,1)S(1)}, bf16[1,160,320]{2,1,0:T(8,128)(2,1)S(1)}, u32[]{:S(2)}, u32[]{:S(2)}) collective-permute-start(bf16[1,160,320]{2,1,0:T(8,128)(2,1)S(1)} %convert_bitcast_fusion.1), channel_id=1, source_target_pairs={{0,16},{4,20},{8,24},{12,28},{16,0},{20,4},{24,8},{28,12},{1,17},{... | collective-permute-start | bytes 307208 | tf_op jit(solution)/shard_map/ppermute | solution.py:253
  12.3 13.8 %collective-permute-start.6 = (bf16[1,160,320]{2,1,0:T(8,128)(2,1)S(1)}, bf16[1,160,320]{2,1,0:T(8,128)(2,1)S(1)}, u32[]{:S(2)}, u32[]{:S(2)}) collective-permute-start(bf16[1,160,320]{2,1,0:T(8,128)(2,1)S(1)} %convert_bitcast_fusion.1), channel_id=1, source_target_pairs={{0,8},{4,12},{8,0},{12,4},{16,24},{20,28},{24,16},{28,20},{1,9},{5... | collective-permute-start | bytes 307208 | tf_op jit(solution)/shard_map/ppermute | solution.py:253
  13.8 12.4 %collective-permute-start.5 = (bf16[1,3,80,360]{3,2,1,0:T(8,128)(2,1)S(1)}, bf16[1,3,80,360]{3,2,1,0:T(8,128)(2,1)S(1)}, u32[]{:S(2)}, u32[]{:S(2)}) collective-permute-start(bf16[1,3,80,360]{3,2,1,0:T(8,128)(2,1)S(1)} %slice_bitcast_fusion.4), channel_id=1, source_target_pairs={{0,3},{1,2},{2,1},{3,0},{4,7},{5,6},{6,5},{7,4},{8,11},{9,10},{10,... | collective-permute-start | bytes 518408 | tf_op jit(solution)/shard_map/ppermute | solution.py:253
  16.4 9.9 %collective-permute-start.4 = (bf16[1,3,80,360]{3,2,1,0:T(8,128)(2,1)S(1)}, bf16[1,3,80,360]{3,2,1,0:T(8,128)(2,1)S(1)}, u32[]{:S(2)}, u32[]{:S(2)}) collective-permute-start(bf16[1,3,80,360]{3,2,1,0:T(8,128)(2,1)S(1)} %slice_bitcast_fusion.4), channel_id=1, source_target_pairs={{0,2},{1,3},{2,0},{3,1},{4,6},{5,7},{6,4},{7,5},{8,10},{9,11},{10,... | collective-permute-start | bytes 518408 | tf_op jit(solution)/shard_map/ppermute | solution.py:253
  16.9 9.4 %collective-permute-start.3 = (bf16[1,3,80,360]{3,2,1,0:T(8,128)(2,1)S(1)}, bf16[1,3,80,360]{3,2,1,0:T(8,128)(2,1)S(1)}, u32[]{:S(2)}, u32[]{:S(2)}) collective-permute-start(bf16[1,3,80,360]{3,2,1,0:T(8,128)(2,1)S(1)} %slice_bitcast_fusion.4), channel_id=1, source_target_pairs={{0,1},{1,0},{2,3},{3,2},{4,5},{5,4},{6,7},{7,6},{8,9},{9,8},{10,11... | collective-permute-start | bytes 518408 | tf_op jit(solution)/shard_map/ppermute | solution.py:253
  26.0 1.0 %copy-start.2 = (s32[1,15]{1,0:T(1,128)S(1)}, s32[1,15]{1,0:T(1,128)}, u32[]{:S(2)}) copy-start(s32[1,15]{1,0:T(1,128)} %param.10) | copy-start | bytes 184
  26.0 3.8 %copy-start = (bf16[15,320,256]{2,1,0:T(8,128)(2,1)S(1)}, bf16[15,320,256]{2,1,0:T(8,128)(2,1)}, u32[]{:S(2)}) copy-start(bf16[15,320,256]{2,1,0:T(8,128)(2,1)} %group_norm.1.normed_ref) | copy-start | bytes 7372804
  26.0 3.8 %copy-start.1 = (s32[1,4]{1,0:T(1,128)S(1)}, s32[1,4]{1,0:T(1,128)}, u32[]{:S(2)}) copy-start(s32[1,4]{1,0:T(1,128)} %counts_ref.1) | copy-start | bytes 52
  26.5 3.3 %collective-permute-start.9 = (bf16[4,4,80,360]{3,2,1,0:T(8,128)(2,1)S(1)}, bf16[4,4,80,360]{3,2,1,0:T(8,128)(2,1)S(1)}, u32[]{:S(2)}, u32[]{:S(2)}) collective-permute-start(bf16[4,4,80,360]{3,2,1,0:T(8,128)(2,1)S(1)} %maximum_maximum_fusion.own_ref), channel_id=1, source_target_pairs={{0,4},{4,0},{8,12},{12,8},{16,20},{20,16},{24,28},{28,24},{1,5},{5... | collective-permute-start | bytes 2764808 | tf_op jit(solution)/shard_map/ppermute | solution.py:253
  26.6 3.2 %collective-permute-start.10 = (bf16[4,160,320]{2,1,0:T(8,128)(2,1)S(1)}, bf16[4,160,320]{2,1,0:T(8,128)(2,1)S(1)}, u32[]{:S(2)}, u32[]{:S(2)}) collective-permute-start(bf16[4,160,320]{2,1,0:T(8,128)(2,1)S(1)} %pad_maximum_fusion.1.own_time_ref), channel_id=1, source_target_pairs={{0,4},{4,0},{8,12},{12,8},{16,20},{20,16},{24,28},{28,24},{1,5},{5... | collective-permute-start | bytes 1228808 | tf_op jit(solution)/shard_map/ppermute | solution.py:253
  54.7 3.4 %collective-permute-start.11 = (bf16[4,4,80,360]{3,2,1,0:T(8,128)(2,1)S(1)}, bf16[4,4,80,360]{3,2,1,0:T(8,128)(2,1)S(1)}, u32[]{:S(2)}, u32[]{:S(2)}) collective-permute-start(bf16[4,4,80,360]{3,2,1,0:T(8,128)(2,1)S(1)} %get-tuple-element.28), channel_id=1, source_target_pairs={{0,4},{4,0},{8,12},{12,8},{16,20},{20,16},{24,28},{28,24},{1,5},{5... | collective-permute-start | bytes 2764808 | tf_op jit(solution)/shard_map/ppermute | solution.py:253
  54.7 3.3 %collective-permute-start.12 = (bf16[4,160,320]{2,1,0:T(8,128)(2,1)S(1)}, bf16[4,160,320]{2,1,0:T(8,128)(2,1)S(1)}, u32[]{:S(2)}, u32[]{:S(2)}) collective-permute-start(bf16[4,160,320]{2,1,0:T(8,128)(2,1)S(1)} %get-tuple-element.30), channel_id=1, source_target_pairs={{0,4},{4,0},{8,12},{12,8},{16,20},{20,16},{24,28},{28,24},{1,5},{5... | collective-permute-start | bytes 1228808 | tf_op jit(solution)/shard_map/ppermute | solution.py:253
  58.4 9.4 %collective-permute-start.13 = (bf16[1,4,80,360]{3,2,1,0:T(8,128)(2,1)S(1)}, bf16[1,4,80,360]{3,2,1,0:T(8,128)(2,1)S(1)}, u32[]{:S(2)}, u32[]{:S(2)}) collective-permute-start(bf16[1,4,80,360]{3,2,1,0:T(8,128)(2,1)S(1)} %get-tuple-element.33), channel_id=1, source_target_pairs={{0,1},{1,0},{2,3},{3,2},{4,5},{5,4},{6,7},{7,6},{8,9},{9,8},{10,11... | collective-permute-start | bytes 691208 | tf_op jit(solution)/shard_map/ppermute | solution.py:253
  59.1 13.7 %collective-permute-start.15 = (bf16[1,4,80,360]{3,2,1,0:T(8,128)(2,1)S(1)}, bf16[1,4,80,360]{3,2,1,0:T(8,128)(2,1)S(1)}, u32[]{:S(2)}, u32[]{:S(2)}) collective-permute-start(bf16[1,4,80,360]{3,2,1,0:T(8,128)(2,1)S(1)} %get-tuple-element.34), channel_id=1, source_target_pairs={{0,3},{1,2},{2,1},{3,0},{4,7},{5,6},{6,5},{7,4},{8,11},{9,10},{10,... | collective-permute-start | bytes 691208 | tf_op jit(solution)/shard_map/ppermute | solution.py:253
  61.3 12.9 %collective-permute-start.14 = (bf16[1,4,80,360]{3,2,1,0:T(8,128)(2,1)S(1)}, bf16[1,4,80,360]{3,2,1,0:T(8,128)(2,1)S(1)}, u32[]{:S(2)}, u32[]{:S(2)}) collective-permute-start(bf16[1,4,80,360]{3,2,1,0:T(8,128)(2,1)S(1)} %get-tuple-element.35), channel_id=1, source_target_pairs={{0,2},{1,3},{2,0},{3,1},{4,6},{5,7},{6,4},{7,5},{8,10},{9,11},{10,... | collective-permute-start | bytes 691208 | tf_op jit(solution)/shard_map/ppermute | solution.py:253
  62.0 18.4 %collective-permute-start.22 = (bf16[1,160,320]{2,1,0:T(8,128)(2,1)S(1)}, bf16[1,160,320]{2,1,0:T(8,128)(2,1)S(1)}, u32[]{:S(2)}, u32[]{:S(2)}) collective-permute-start(bf16[1,160,320]{2,1,0:T(8,128)(2,1)S(1)} %get-tuple-element.36), channel_id=1, source_target_pairs={{0,8},{4,12},{8,0},{12,4},{16,24},{20,28},{24,16},{28,20},{1,9},{5... | collective-permute-start | bytes 307208 | tf_op jit(solution)/shard_map/ppermute | solution.py:253
  65.1 15.4 %collective-permute-start.24 = (bf16[1,160,320]{2,1,0:T(8,128)(2,1)S(1)}, bf16[1,160,320]{2,1,0:T(8,128)(2,1)S(1)}, u32[]{:S(2)}, u32[]{:S(2)}) collective-permute-start(bf16[1,160,320]{2,1,0:T(8,128)(2,1)S(1)} %get-tuple-element.37), channel_id=1, source_target_pairs={{0,24},{4,28},{8,16},{12,20},{16,8},{20,12},{24,0},{28,4},{1,25},{... | collective-permute-start | bytes 307208 | tf_op jit(solution)/shard_map/ppermute | solution.py:253
  67.9 12.6 %collective-permute-start.23 = (bf16[1,160,320]{2,1,0:T(8,128)(2,1)S(1)}, bf16[1,160,320]{2,1,0:T(8,128)(2,1)S(1)}, u32[]{:S(2)}, u32[]{:S(2)}) collective-permute-start(bf16[1,160,320]{2,1,0:T(8,128)(2,1)S(1)} %get-tuple-element.38), channel_id=1, source_target_pairs={{0,16},{4,20},{8,24},{12,28},{16,0},{20,4},{24,8},{28,12},{1,17},{... | collective-permute-start | bytes 307208 | tf_op jit(solution)/shard_map/ppermute | solution.py:253
  74.3 9.4 %collective-permute-start.16 = (bf16[1,80,360]{2,1,0:T(8,128)(2,1)S(1)}, bf16[1,80,360]{2,1,0:T(8,128)(2,1)S(1)}, u32[]{:S(2)}, u32[]{:S(2)}) collective-permute-start(bf16[1,80,360]{2,1,0:T(8,128)(2,1)S(1)} %get-tuple-element.43), channel_id=1, source_target_pairs={{0,8},{4,12},{8,0},{12,4},{16,24},{20,28},{24,16},{28,20},{1,9},{5... | collective-permute-start | bytes 172808 | tf_op jit(solution)/shard_map/ppermute | solution.py:253
  77.7 6.4 %collective-permute-start.18 = (bf16[1,80,360]{2,1,0:T(8,128)(2,1)S(1)}, bf16[1,80,360]{2,1,0:T(8,128)(2,1)S(1)}, u32[]{:S(2)}, u32[]{:S(2)}) collective-permute-start(bf16[1,80,360]{2,1,0:T(8,128)(2,1)S(1)} %get-tuple-element.44), channel_id=1, source_target_pairs={{0,24},{4,28},{8,16},{12,20},{16,8},{20,12},{24,0},{28,4},{1,25},{... | collective-permute-start | bytes 172808 | tf_op jit(solution)/shard_map/ppermute | solution.py:253
  80.5 5.1 %collective-permute-start.17 = (bf16[1,80,360]{2,1,0:T(8,128)(2,1)S(1)}, bf16[1,80,360]{2,1,0:T(8,128)(2,1)S(1)}, u32[]{:S(2)}, u32[]{:S(2)}) collective-permute-start(bf16[1,80,360]{2,1,0:T(8,128)(2,1)S(1)} %get-tuple-element.45), channel_id=1, source_target_pairs={{0,16},{4,20},{8,24},{12,28},{16,0},{20,4},{24,8},{28,12},{1,17},{... | collective-permute-start | bytes 172808 | tf_op jit(solution)/shard_map/ppermute | solution.py:253
  80.6 8.3 %collective-permute-start.27 = (bf16[160,320]{1,0:T(8,128)(2,1)S(1)}, bf16[160,320]{1,0:T(8,128)(2,1)S(1)}, u32[]{:S(2)}, u32[]{:S(2)}) collective-permute-start(bf16[160,320]{1,0:T(8,128)(2,1)S(1)} %fusion.5), channel_id=1, source_target_pairs={{0,3},{1,2},{2,1},{3,0},{4,7},{5,6},{6,5},{7,4},{8,11},{9,10},{10,... | collective-permute-start | bytes 307208 | tf_op jit(solution)/shard_map/ppermute | solution.py:253
  82.2 6.9 %collective-permute-start.26 = (bf16[160,320]{1,0:T(8,128)(2,1)S(1)}, bf16[160,320]{1,0:T(8,128)(2,1)S(1)}, u32[]{:S(2)}, u32[]{:S(2)}) collective-permute-start(bf16[160,320]{1,0:T(8,128)(2,1)S(1)} %fusion.5), channel_id=1, source_target_pairs={{0,2},{1,3},{2,0},{3,1},{4,6},{5,7},{6,4},{7,5},{8,10},{9,11},{10,... | collective-permute-start | bytes 307208 | tf_op jit(solution)/shard_map/ppermute | solution.py:253
  83.8 5.4 %collective-permute-start.25 = (bf16[160,320]{1,0:T(8,128)(2,1)S(1)}, bf16[160,320]{1,0:T(8,128)(2,1)S(1)}, u32[]{:S(2)}, u32[]{:S(2)}) collective-permute-start(bf16[160,320]{1,0:T(8,128)(2,1)S(1)} %fusion.5), channel_id=1, source_target_pairs={{0,1},{1,0},{2,3},{3,2},{4,5},{5,4},{6,7},{7,6},{8,9},{9,8},{10,11... | collective-permute-start | bytes 307208 | tf_op jit(solution)/shard_map/ppermute | solution.py:253
  85.6 5.2 %collective-permute-start.21 = (bf16[1,80,360]{2,1,0:T(8,128)(2,1)S(1)}, bf16[1,80,360]{2,1,0:T(8,128)(2,1)S(1)}, u32[]{:S(2)}, u32[]{:S(2)}) collective-permute-start(bf16[1,80,360]{2,1,0:T(8,128)(2,1)S(1)} %fusion.7), channel_id=1, source_target_pairs={{0,3},{1,2},{2,1},{3,0},{4,7},{5,6},{6,5},{7,4},{8,11},{9,10},{10,... | collective-permute-start | bytes 172808 | tf_op jit(solution)/shard_map/ppermute | solution.py:253
  87.3 4.2 %collective-permute-start.20 = (bf16[1,80,360]{2,1,0:T(8,128)(2,1)S(1)}, bf16[1,80,360]{2,1,0:T(8,128)(2,1)S(1)}, u32[]{:S(2)}, u32[]{:S(2)}) collective-permute-start(bf16[1,80,360]{2,1,0:T(8,128)(2,1)S(1)} %fusion.7), channel_id=1, source_target_pairs={{0,2},{1,3},{2,0},{3,1},{4,6},{5,7},{6,4},{7,5},{8,10},{9,11},{10,... | collective-permute-start | bytes 172808 | tf_op jit(solution)/shard_map/ppermute | solution.py:253
  88.8 4.2 %collective-permute-start.19 = (bf16[1,80,360]{2,1,0:T(8,128)(2,1)S(1)}, bf16[1,80,360]{2,1,0:T(8,128)(2,1)S(1)}, u32[]{:S(2)}, u32[]{:S(2)}) collective-permute-start(bf16[1,80,360]{2,1,0:T(8,128)(2,1)S(1)} %fusion.7), channel_id=1, source_target_pairs={{0,1},{1,0},{2,3},{3,2},{4,5},{5,4},{6,7},{7,6},{8,9},{9,8},{10,11... | collective-permute-start | bytes 172808 | tf_op jit(solution)/shard_map/ppermute | solution.py:253

commit v6 on v5

--- a/solution.py
+++ b/solution.py
@@ -257,14 +257,14 @@
     return (lax.axis_size(axis) - 1).bit_length()
 
 
-def bit_groups(bits):
-    return [(at, min(2, bits - at)) for at in range(0, bits, 2)]
-
-
-def gather_partners(values, axis, low, bits):
+def bit_groups(bits, most):
+    return [(at, min(most, bits - at)) for at in range(0, bits, most)]
+
+
+def gather_partners(values, axis, low, bits, most=2):
     shape = values.shape
     values = values[None]
-    for at, width in bit_groups(bits):
+    for at, width in bit_groups(bits, most):
         parts = [values] + [swap(values, axis, m << (low + at)) for m in range(1, 1 << width)]
         values = jnp.concatenate(parts)
     return values.reshape((1 << bits,) + shape)
@@ -278,16 +278,16 @@
     return parts[0].astype(kept_as)
 
 
-def sum_partners(values, axis, low, bits):
-    for at, width in bit_groups(bits):
+def sum_partners(values, axis, low, bits, most=2):
+    for at, width in bit_groups(bits, most):
         parts = [values] + [swap(values, axis, m << (low + at)) for m in range(1, 1 << width)]
         values = add_up(parts)
     return values
 
 
-def scatter_partners(values, axis, low, bits):
+def scatter_partners(values, axis, low, bits, most=2):
     shape = values.shape[1:]
-    for at, width in bit_groups(bits):
+    for at, width in bit_groups(bits, most):
         values = values.reshape((-1, 1 << width) + shape)
         parts = [values[:, 0]]
         parts += [swap(values[:, m], axis, m << (low + at)) for m in range(1, 1 << width)]
@@ -320,7 +320,7 @@
     time_master, first = lax.optimization_barrier((temb_master, mine[0]))
     time_master = time_master.astype(bf16)
     over_planes = gather_partners(first, "fsdp", 1, plane_bits)
-    own_time = gather_partners(time_master, "fsdp", 1, plane_bits)
+    own_time = gather_partners(time_master, "fsdp", 1, plane_bits, most=1)
     over_planes, tiles_then = lax.optimization_barrier((over_planes, tiles))
     far = gather_partners(over_planes[1:], "dp", 0, part_bits)
     normed = group_norm(tiles_then)
@@ -334,15 +334,18 @@
     )
 
     grad = add_up([keep, swap(send, "fsdp", 1)])
+    grad, send_time = lax.optimization_barrier((grad, send_time))
     time_grad = add_up([keep_time, swap(send_time, "fsdp", 1)])
-    grad, time_grad = lax.optimization_barrier((grad, time_grad))
     grad = scatter_partners(grad, "dp", 0, part_bits)
     for bit in range(part_bits, peer_bits):
         grad = sum_partners(grad, "dp", bit, 1)
     time_grad = scatter_partners(time_grad, "fsdp", 1, plane_bits)
+    grad, time_grad = lax.optimization_barrier((grad, time_grad))
     grad = scatter_partners(grad, "fsdp", 1, plane_bits)
-    time_grad = sum_partners(time_grad, "dp", 0, peer_bits)
+    time_grad = sum_partners(time_grad, "dp", 0, peer_bits // 2, most=1)
+    grad, time_grad = lax.optimization_barrier((grad, time_grad))
     grad = gather_partners(grad, "dp", 0, part_bits)
+    time_grad = sum_partners(time_grad, "dp", peer_bits // 2, peer_bits - peer_bits // 2, most=1)
     grad = jnp.concatenate(
         [lax.dynamic_index_in_dim(grad, part ^ q, 0, keepdims=False) for q in range(parts)]
     )

time: 94.2 us -> 95.8 us (1.017)
  waiting for transfers between devices: 12.2 us -> 27.1 us
  starting transfers between devices: 41.9 us -> 34.8 us
  Pallas kernels: 32.6 us -> 26.3 us
    ppermute x28 -> x26, waiting for transfers between devices: 12.2 us -> 27.1 us  [swap(): return lax.ppermute(values, axis, pairs)]
    ppermute x28 -> x26, starting transfers between devices: 41.9 us -> 34.8 us  [swap(): return lax.ppermute(values, axis, pairs)]
    pallas_call x1, Pallas kernels: 24.8 us -> 18.5 us  [conv_both(): pl.pallas_call(functools.partial(conv_kernel, steps), grid_spec=pltpu.Pre...]
  transfers between devices with their start and end apart: 28 -> 26, of which waited for: 9 -> 15; matrix products, arithmetic and copies ran while one was open for 4% -> 4% of each run, Pallas kernels for 8% -> 8%
where the time goes in v6:
time: 95.8 us; the launch traced here: 95.5 us
  starting transfers between devices  34.8 us (36%)
  waiting for transfers between devices  27.1 us (28%)
  Pallas kernels  26.3 us (27%)
  other arithmetic  6.2 us (6%)
    ppermute x26, starting transfers between devices, swap(): return lax.ppermute(values, axis, pairs)  34.8 us
    ppermute x26, waiting for transfers between devices, swap(): return lax.ppermute(values, axis, pairs)  27.1 us
    pallas_call x1, Pallas kernels, conv_both(): pl.pallas_call(functools.partial(conv_kernel, steps), grid_spec=pltpu.Pre...  18.5 us
    pallas_call x1, Pallas kernels, group_norm(): pl.pallas_call(functools.partial(norm_kernel, group_width), grid=(number...  7.73 us
  transfers between devices with their start and end apart: 26, of which 15 were waited for; matrix products, arithmetic and copies ran while one was open for 4% of the time, Pallas kernels for 8%

profile of v6, /device:TPU:0, one launch (start us, length us, event | category | flops | bytes accessed | tf_op | source)
XLA Modules:
  0.0 95.5 jit_solution(11788041563768856124)
XLA Ops:
  0.6 1.1 %convert_element_type.138 = bf16[360,320]{0,1:T(8,128)(2,1)S(1)} convert(f32[360,320]{0,1:T(8,128)} %param.11) | non-fusion elementwise | flops 115200 | bytes 691200 | tf_op jit(solution)/shard_map/convert_element_type | solution.py:318
  1.8 5.1 %collective-permute-start.2 = (bf16[1,80,360]{2,1,0:T(8,128)(2,1)S(1)}, bf16[1,80,360]{2,1,0:T(8,128)(2,1)S(1)}, u32[]{:S(2)}, u32[]{:S(2)}) collective-permute-start(bf16[1,80,360]{2,1,0:T(8,128)(2,1)S(1)} %get-tuple-element.57), channel_id=1, source_target_pairs={{0,24},{4,28},{8,16},{12,20},{16,8},{20,12},{24,0},{28,4},{1,25},{... | collective-permute-start | bytes 172808 | tf_op jit(solution)/shard_map/ppermute | solution.py:253
  6.9 0.6 collective-permute-start
  7.5 1.0 %convert_bitcast_fusion.1 = bf16[1,160,320]{2,1,0:T(8,128)(2,1)S(1)} fusion(f32[160,320]{1,0:T(8,128)} %param.12), kind=kLoop, calls=%fused_computation.37 | loop fusion | flops 51200 | bytes 307200 | tf_op jit(solution)/shard_map/broadcast_in_dim | solution.py:266
  8.5 1.5 %collective-permute-start.6 = (bf16[1,160,320]{2,1,0:T(8,128)(2,1)S(1)}, bf16[1,160,320]{2,1,0:T(8,128)(2,1)S(1)}, u32[]{:S(2)}, u32[]{:S(2)}) collective-permute-start(bf16[1,160,320]{2,1,0:T(8,128)(2,1)S(1)} %convert_bitcast_fusion.1), channel_id=1, source_target_pairs={{0,8},{4,12},{8,0},{12,4},{16,24},{20,28},{24,16},{28,20},{1,9},{5... | collective-permute-start | bytes 307208 | tf_op jit(solution)/shard_map/ppermute | solution.py:253
  9.9 2.3 %collective-permute-done.1 = bf16[1,80,360]{2,1,0:T(8,128)(2,1)S(1)} collective-permute-done((bf16[1,80,360]{2,1,0:T(8,128)(2,1)S(1)}, bf16[1,80,360]{2,1,0:T(8,128)(2,1)S(1)}, u32[]{:S(2)}, u32[]{:S(2)}) %collective-permute-start.1) | collective-permute-done | bytes 57632 | tf_op jit(solution)/shard_map/ppermute | solution.py:253
  12.3 0.6 collective-permute-done
  12.9 2.6 %collective-permute-start.5 = (bf16[1,3,80,360]{3,2,1,0:T(8,128)(2,1)S(1)}, bf16[1,3,80,360]{3,2,1,0:T(8,128)(2,1)S(1)}, u32[]{:S(2)}, u32[]{:S(2)}) collective-permute-start(bf16[1,3,80,360]{3,2,1,0:T(8,128)(2,1)S(1)} %slice_bitcast_fusion.4), channel_id=1, source_target_pairs={{0,3},{1,2},{2,1},{3,0},{4,7},{5,6},{6,5},{7,4},{8,11},{9,10},{10,... | collective-permute-start | bytes 518408 | tf_op jit(solution)/shard_map/ppermute | solution.py:253
  15.6 0.5 collective-permute-start.4
  16.1 0.4 collective-permute-start.3
  16.6 1.9 %collective-permute-start.7 = (bf16[2,160,320]{2,1,0:T(8,128)(2,1)S(1)}, bf16[2,160,320]{2,1,0:T(8,128)(2,1)S(1)}, u32[]{:S(2)}, u32[]{:S(2)}) collective-permute-start(bf16[2,160,320]{2,1,0:T(8,128)(2,1)S(1)} %pad_maximum_fusion.3), channel_id=1, source_target_pairs={{0,16},{4,20},{8,24},{12,28},{16,0},{20,4},{24,8},{28,12},{1,17},{... | collective-permute-start | bytes 614408 | tf_op jit(solution)/shard_map/ppermute | solution.py:253
  18.5 7.7 %group_norm.1.normed_ref = bf16[15,320,256]{2,1,0:T(8,128)(2,1)} custom-call(bf16[320,320]{1,0:T(8,128)(2,1)} %constant.41.clone.same_ref, bf16[15,320,256]{2,1,0:T(8,128)(2,1)} %bitcast.77), custom_call_target="tpu_custom_call" | custom-call | flops 24576000 | bytes 4915200 | tf_op jit(solution)/shard_map/group_norm/pallas_call | solution.py:57
  26.2 0.3 maximum_maximum_fusion.own_ref
  26.5 2.0 %collective-permute-done.7 = bf16[2,160,320]{2,1,0:T(8,128)(2,1)S(1)} collective-permute-done((bf16[2,160,320]{2,1,0:T(8,128)(2,1)S(1)}, bf16[2,160,320]{2,1,0:T(8,128)(2,1)S(1)}, u32[]{:S(2)}, u32[]{:S(2)}) %collective-permute-start.7) | collective-permute-done | bytes 204832 | tf_op jit(solution)/shard_map/ppermute | solution.py:253
  28.5 0.1 pad_maximum_fusion.1.own_time_ref
  28.7 0.5 collective-permute-start.9
  29.2 1.2 %multiply_cosine_fusion = (f32[640,128]{1,0:T(8,128)S(1)}, f32[640,128]{1,0:T(8,128)S(1)}) fusion(f32[128]{0:T(128)S(1)} %pad_convert_fusion, f32[640]{0:T(1024)S(1)} %multiply_exponential_fusion), kind=kLoop, calls=%fused_computation.12 | loop fusion | flops 81920 | bytes 658432 | tf_op jit(solution)/shard_map/cos | solution.py:302
  30.4 0.2 multiply_convert_fusion.features_ref
  30.6 1.3 %collective-permute-done.9.other_time_ref = bf16[4,160,320]{2,1,0:T(8,128)(2,1)S(1)} collective-permute-done((bf16[4,160,320]{2,1,0:T(8,128)(2,1)S(1)}, bf16[4,160,320]{2,1,0:T(8,128)(2,1)S(1)}, u32[]{:S(2)}, u32[]{:S(2)}) %collective-permute-start.9) | collective-permute-done | bytes 409632 | tf_op jit(solution)/shard_map/ppermute | solution.py:253
  32.0 18.5 %conv_both.1 = (bf16[15,320,256]{2,1,0:T(8,128)(2,1)}, bf16[4,4,80,360]{3,2,1,0:T(8,128)(2,1)S(1)}, bf16[4,4,80,360]{3,2,1,0:T(8,128)(2,1)S(1)}, bf16[4,160,320]...) custom-call(s32[1,4]{1,0:T(1,128)S(1)} %copy-done.1, bf16[4,4,80,360]{3,2,1,0:T(8,128)(2,1)S(1)} %maximum_maximum_fusion.own_ref, ...), custom_call_target="tpu_custom_call" | custom-call | flops 14155776000 | bytes 9830400 | tf_op jit(solution)/shard_map/conv_both/pallas_call | solution.py:217
  50.5 2.6 %collective-permute-done.10 = bf16[4,4,80,360]{3,2,1,0:T(8,128)(2,1)S(1)} collective-permute-done((bf16[4,4,80,360]{3,2,1,0:T(8,128)(2,1)S(1)}, bf16[4,4,80,360]{3,2,1,0:T(8,128)(2,1)S(1)}, u32[]{:S(2)}, u32[]{:S(2)}) %collective-permute-start.10) | collective-permute-done | bytes 921632 | tf_op jit(solution)/shard_map/ppermute | solution.py:253
  53.1 0.3 add_convert_fusion
  53.4 0.2 collective-permute-start.14
  53.6 7.9 %collective-permute-start.11 = (bf16[1,4,80,360]{3,2,1,0:T(8,128)(2,1)S(1)}, bf16[1,4,80,360]{3,2,1,0:T(8,128)(2,1)S(1)}, u32[]{:S(2)}, u32[]{:S(2)}) collective-permute-start(bf16[1,4,80,360]{3,2,1,0:T(8,128)(2,1)S(1)} %get-tuple-element.41), channel_id=1, source_target_pairs={{0,1},{1,0},{2,3},{3,2},{4,5},{5,4},{6,7},{7,6},{8,9},{9,8},{10,11... | collective-permute-start | bytes 691208 | tf_op jit(solution)/shard_map/ppermute | solution.py:253
  61.5 1.0 %collective-permute-start.13 = (bf16[1,4,80,360]{3,2,1,0:T(8,128)(2,1)S(1)}, bf16[1,4,80,360]{3,2,1,0:T(8,128)(2,1)S(1)}, u32[]{:S(2)}, u32[]{:S(2)}) collective-permute-start(bf16[1,4,80,360]{3,2,1,0:T(8,128)(2,1)S(1)} %get-tuple-element.42), channel_id=1, source_target_pairs={{0,3},{1,2},{2,1},{3,0},{4,7},{5,6},{6,5},{7,4},{8,11},{9,10},{10,... | collective-permute-start | bytes 691208 | tf_op jit(solution)/shard_map/ppermute | solution.py:253
  62.5 0.5 collective-permute-start.12
  63.0 0.1 fusion
  63.3 2.3 %collective-permute-start.17 = (bf16[1,160,320]{2,1,0:T(8,128)(2,1)S(1)}, bf16[1,160,320]{2,1,0:T(8,128)(2,1)S(1)}, u32[]{:S(2)}, u32[]{:S(2)}) collective-permute-start(bf16[1,160,320]{2,1,0:T(8,128)(2,1)S(1)} %get-tuple-element.45), channel_id=1, source_target_pairs={{0,24},{4,28},{8,16},{12,20},{16,8},{20,12},{24,0},{28,4},{1,25},{... | collective-permute-start | bytes 307208 | tf_op jit(solution)/shard_map/ppermute | solution.py:253
  65.6 2.7 %collective-permute-done.11 = bf16[1,4,80,360]{3,2,1,0:T(8,128)(2,1)S(1)} collective-permute-done((bf16[1,4,80,360]{3,2,1,0:T(8,128)(2,1)S(1)}, bf16[1,4,80,360]{3,2,1,0:T(8,128)(2,1)S(1)}, u32[]{:S(2)}, u32[]{:S(2)}) %collective-permute-start.11) | collective-permute-done | bytes 230432 | tf_op jit(solution)/shard_map/ppermute | solution.py:253
  68.3 5.7 %collective-permute-done.13 = bf16[1,4,80,360]{3,2,1,0:T(8,128)(2,1)S(1)} collective-permute-done((bf16[1,4,80,360]{3,2,1,0:T(8,128)(2,1)S(1)}, bf16[1,4,80,360]{3,2,1,0:T(8,128)(2,1)S(1)}, u32[]{:S(2)}, u32[]{:S(2)}) %collective-permute-start.13) | collective-permute-done | bytes 230432 | tf_op jit(solution)/shard_map/ppermute | solution.py:253
  74.1 1.4 %collective-permute-done.12 = bf16[1,4,80,360]{3,2,1,0:T(8,128)(2,1)S(1)} collective-permute-done((bf16[1,4,80,360]{3,2,1,0:T(8,128)(2,1)S(1)}, bf16[1,4,80,360]{3,2,1,0:T(8,128)(2,1)S(1)}, u32[]{:S(2)}, u32[]{:S(2)}) %collective-permute-start.12) | collective-permute-done | bytes 230432 | tf_op jit(solution)/shard_map/ppermute | solution.py:253
  75.5 0.1 fusion.3
  75.6 1.7 %collective-permute-done.16 = bf16[1,160,320]{2,1,0:T(8,128)(2,1)S(1)} collective-permute-done((bf16[1,160,320]{2,1,0:T(8,128)(2,1)S(1)}, bf16[1,160,320]{2,1,0:T(8,128)(2,1)S(1)}, u32[]{:S(2)}, u32[]{:S(2)}) %collective-permute-start.16) | collective-permute-done | bytes 102432 | tf_op jit(solution)/shard_map/ppermute | solution.py:253
  77.6 2.0 %collective-permute-start.20 = (bf16[1,80,360]{2,1,0:T(8,128)(2,1)S(1)}, bf16[1,80,360]{2,1,0:T(8,128)(2,1)S(1)}, u32[]{:S(2)}, u32[]{:S(2)}) collective-permute-start(bf16[1,80,360]{2,1,0:T(8,128)(2,1)S(1)} %get-tuple-element.52), channel_id=1, source_target_pairs={{0,24},{4,28},{8,16},{12,20},{16,8},{20,12},{24,0},{28,4},{1,25},{... | collective-permute-start | bytes 172808 | tf_op jit(solution)/shard_map/ppermute | solution.py:253
  79.6 1.5 %collective-permute-start.19 = (bf16[1,80,360]{2,1,0:T(8,128)(2,1)S(1)}, bf16[1,80,360]{2,1,0:T(8,128)(2,1)S(1)}, u32[]{:S(2)}, u32[]{:S(2)}) collective-permute-start(bf16[1,80,360]{2,1,0:T(8,128)(2,1)S(1)} %get-tuple-element.53), channel_id=1, source_target_pairs={{0,16},{4,20},{8,24},{12,28},{16,0},{20,4},{24,8},{28,12},{1,17},{... | collective-permute-start | bytes 172808 | tf_op jit(solution)/shard_map/ppermute | solution.py:253
  81.0 1.7 %collective-permute-start.21 = (bf16[160,320]{1,0:T(8,128)(2,1)S(1)}, bf16[160,320]{1,0:T(8,128)(2,1)S(1)}, u32[]{:S(2)}, u32[]{:S(2)}) collective-permute-start(bf16[160,320]{1,0:T(8,128)(2,1)S(1)} %fusion.7), channel_id=1, source_target_pairs={{0,1},{1,0},{2,3},{3,2},{4,5},{5,4},{6,7},{7,6},{8,9},{9,8},{10,11... | collective-permute-start | bytes 307208 | tf_op jit(solution)/shard_map/ppermute | solution.py:253
  82.7 1.1 %collective-permute-done.20 = bf16[1,80,360]{2,1,0:T(8,128)(2,1)S(1)} collective-permute-done((bf16[1,80,360]{2,1,0:T(8,128)(2,1)S(1)}, bf16[1,80,360]{2,1,0:T(8,128)(2,1)S(1)}, u32[]{:S(2)}, u32[]{:S(2)}) %collective-permute-start.20) | collective-permute-done | bytes 57632 | tf_op jit(solution)/shard_map/ppermute | solution.py:253
  83.8 2.5 %collective-permute-done.19 = bf16[1,80,360]{2,1,0:T(8,128)(2,1)S(1)} collective-permute-done((bf16[1,80,360]{2,1,0:T(8,128)(2,1)S(1)}, bf16[1,80,360]{2,1,0:T(8,128)(2,1)S(1)}, u32[]{:S(2)}, u32[]{:S(2)}) %collective-permute-start.19) | collective-permute-done | bytes 57632 | tf_op jit(solution)/shard_map/ppermute | solution.py:253
  86.3 2.1 %collective-permute-start.24 = (bf16[1,80,360]{2,1,0:T(8,128)(2,1)S(1)}, bf16[1,80,360]{2,1,0:T(8,128)(2,1)S(1)}, u32[]{:S(2)}, u32[]{:S(2)}) collective-permute-start(bf16[1,80,360]{2,1,0:T(8,128)(2,1)S(1)} %bitcast.82), channel_id=1, source_target_pairs={{0,3},{1,2},{2,1},{3,0},{4,7},{5,6},{6,5},{7,4},{8,11},{9,10},{10,... | collective-permute-start | bytes 172808 | tf_op jit(solution)/shard_map/ppermute | solution.py:253
  88.4 0.8 collective-permute-start.23
  89.3 0.6 collective-permute-start.22
  89.9 0.9 collective-permute-start.25
  90.8 1.5 %collective-permute-done.24 = bf16[1,80,360]{2,1,0:T(8,128)(2,1)S(1)} collective-permute-done((bf16[1,80,360]{2,1,0:T(8,128)(2,1)S(1)}, bf16[1,80,360]{2,1,0:T(8,128)(2,1)S(1)}, u32[]{:S(2)}, u32[]{:S(2)}) %collective-permute-start.24) | collective-permute-done | bytes 57632 | tf_op jit(solution)/shard_map/ppermute | solution.py:253
  92.3 1.0 %collective-permute-done.23 = bf16[1,80,360]{2,1,0:T(8,128)(2,1)S(1)} collective-permute-done((bf16[1,80,360]{2,1,0:T(8,128)(2,1)S(1)}, bf16[1,80,360]{2,1,0:T(8,128)(2,1)S(1)}, u32[]{:S(2)}, u32[]{:S(2)}) %collective-permute-start.23) | collective-permute-done | bytes 57632 | tf_op jit(solution)/shard_map/ppermute | solution.py:253
  93.3 0.2 collective-permute-done.22
  93.6 0.8 convert_bitcast_fusion
  94.4 0.4 collective-permute-done.25
  94.8 0.7 fusion.6
  (38 shorter events, 0.9 us)
Async XLA Ops:
  1.8 8.2 %collective-permute-start.2 = (bf16[1,80,360]{2,1,0:T(8,128)(2,1)S(1)}, bf16[1,80,360]{2,1,0:T(8,128)(2,1)S(1)}, u32[]{:S(2)}, u32[]{:S(2)}) collective-permute-start(bf16[1,80,360]{2,1,0:T(8,128)(2,1)S(1)} %get-tuple-element.57), channel_id=1, source_target_pairs={{0,24},{4,28},{8,16},{12,20},{16,8},{20,12},{24,0},{28,4},{1,25},{... | collective-permute-start | bytes 172808 | tf_op jit(solution)/shard_map/ppermute | solution.py:253
  6.9 5.4 %collective-permute-start.1 = (bf16[1,80,360]{2,1,0:T(8,128)(2,1)S(1)}, bf16[1,80,360]{2,1,0:T(8,128)(2,1)S(1)}, u32[]{:S(2)}, u32[]{:S(2)}) collective-permute-start(bf16[1,80,360]{2,1,0:T(8,128)(2,1)S(1)} %get-tuple-element.57), channel_id=1, source_target_pairs={{0,16},{4,20},{8,24},{12,28},{16,0},{20,4},{24,8},{28,12},{1,17},{... | collective-permute-start | bytes 172808 | tf_op jit(solution)/shard_map/ppermute | solution.py:253
  6.9 6.0 %collective-permute-start = (bf16[1,80,360]{2,1,0:T(8,128)(2,1)S(1)}, bf16[1,80,360]{2,1,0:T(8,128)(2,1)S(1)}, u32[]{:S(2)}, u32[]{:S(2)}) collective-permute-start(bf16[1,80,360]{2,1,0:T(8,128)(2,1)S(1)} %get-tuple-element.57), channel_id=1, source_target_pairs={{0,8},{4,12},{8,0},{12,4},{16,24},{20,28},{24,16},{28,20},{1,9},{5... | collective-permute-start | bytes 172808 | tf_op jit(solution)/shard_map/ppermute | solution.py:253
  8.5 8.0 %collective-permute-start.6 = (bf16[1,160,320]{2,1,0:T(8,128)(2,1)S(1)}, bf16[1,160,320]{2,1,0:T(8,128)(2,1)S(1)}, u32[]{:S(2)}, u32[]{:S(2)}) collective-permute-start(bf16[1,160,320]{2,1,0:T(8,128)(2,1)S(1)} %convert_bitcast_fusion.1), channel_id=1, source_target_pairs={{0,8},{4,12},{8,0},{12,4},{16,24},{20,28},{24,16},{28,20},{1,9},{5... | collective-permute-start | bytes 307208 | tf_op jit(solution)/shard_map/ppermute | solution.py:253
  12.9 13.3 %collective-permute-start.5 = (bf16[1,3,80,360]{3,2,1,0:T(8,128)(2,1)S(1)}, bf16[1,3,80,360]{3,2,1,0:T(8,128)(2,1)S(1)}, u32[]{:S(2)}, u32[]{:S(2)}) collective-permute-start(bf16[1,3,80,360]{3,2,1,0:T(8,128)(2,1)S(1)} %slice_bitcast_fusion.4), channel_id=1, source_target_pairs={{0,3},{1,2},{2,1},{3,0},{4,7},{5,6},{6,5},{7,4},{8,11},{9,10},{10,... | collective-permute-start | bytes 518408 | tf_op jit(solution)/shard_map/ppermute | solution.py:253
  15.6 10.7 %collective-permute-start.4 = (bf16[1,3,80,360]{3,2,1,0:T(8,128)(2,1)S(1)}, bf16[1,3,80,360]{3,2,1,0:T(8,128)(2,1)S(1)}, u32[]{:S(2)}, u32[]{:S(2)}) collective-permute-start(bf16[1,3,80,360]{3,2,1,0:T(8,128)(2,1)S(1)} %slice_bitcast_fusion.4), channel_id=1, source_target_pairs={{0,2},{1,3},{2,0},{3,1},{4,6},{5,7},{6,4},{7,5},{8,10},{9,11},{10,... | collective-permute-start | bytes 518408 | tf_op jit(solution)/shard_map/ppermute | solution.py:253
  16.1 10.2 %collective-permute-start.3 = (bf16[1,3,80,360]{3,2,1,0:T(8,128)(2,1)S(1)}, bf16[1,3,80,360]{3,2,1,0:T(8,128)(2,1)S(1)}, u32[]{:S(2)}, u32[]{:S(2)}) collective-permute-start(bf16[1,3,80,360]{3,2,1,0:T(8,128)(2,1)S(1)} %slice_bitcast_fusion.4), channel_id=1, source_target_pairs={{0,1},{1,0},{2,3},{3,2},{4,5},{5,4},{6,7},{7,6},{8,9},{9,8},{10,11... | collective-permute-start | bytes 518408 | tf_op jit(solution)/shard_map/ppermute | solution.py:253
  16.6 12.0 %collective-permute-start.7 = (bf16[2,160,320]{2,1,0:T(8,128)(2,1)S(1)}, bf16[2,160,320]{2,1,0:T(8,128)(2,1)S(1)}, u32[]{:S(2)}, u32[]{:S(2)}) collective-permute-start(bf16[2,160,320]{2,1,0:T(8,128)(2,1)S(1)} %pad_maximum_fusion.3), channel_id=1, source_target_pairs={{0,16},{4,20},{8,24},{12,28},{16,0},{20,4},{24,8},{28,12},{1,17},{... | collective-permute-start | bytes 614408 | tf_op jit(solution)/shard_map/ppermute | solution.py:253
  26.2 3.0 %copy-start.2 = (s32[1,15]{1,0:T(1,128)S(1)}, s32[1,15]{1,0:T(1,128)}, u32[]{:S(2)}) copy-start(s32[1,15]{1,0:T(1,128)} %param.10) | copy-start | bytes 184
  26.2 5.8 %copy-start = (bf16[15,320,256]{2,1,0:T(8,128)(2,1)S(1)}, bf16[15,320,256]{2,1,0:T(8,128)(2,1)}, u32[]{:S(2)}) copy-start(bf16[15,320,256]{2,1,0:T(8,128)(2,1)} %group_norm.1.normed_ref) | copy-start | bytes 7372804
  26.2 5.8 %copy-start.1 = (s32[1,4]{1,0:T(1,128)S(1)}, s32[1,4]{1,0:T(1,128)}, u32[]{:S(2)}) copy-start(s32[1,4]{1,0:T(1,128)} %counts_ref.1) | copy-start | bytes 52
  28.6 3.3 %collective-permute-start.8 = (bf16[4,4,80,360]{3,2,1,0:T(8,128)(2,1)S(1)}, bf16[4,4,80,360]{3,2,1,0:T(8,128)(2,1)S(1)}, u32[]{:S(2)}, u32[]{:S(2)}) collective-permute-start(bf16[4,4,80,360]{3,2,1,0:T(8,128)(2,1)S(1)} %maximum_maximum_fusion.own_ref), channel_id=1, source_target_pairs={{0,4},{4,0},{8,12},{12,8},{16,20},{20,16},{24,28},{28,24},{1,5},{5... | collective-permute-start | bytes 2764808 | tf_op jit(solution)/shard_map/ppermute | solution.py:253
  28.7 3.2 %collective-permute-start.9 = (bf16[4,160,320]{2,1,0:T(8,128)(2,1)S(1)}, bf16[4,160,320]{2,1,0:T(8,128)(2,1)S(1)}, u32[]{:S(2)}, u32[]{:S(2)}) collective-permute-start(bf16[4,160,320]{2,1,0:T(8,128)(2,1)S(1)} %pad_maximum_fusion.1.own_time_ref), channel_id=1, source_target_pairs={{0,4},{4,0},{8,12},{12,8},{16,20},{20,16},{24,28},{28,24},{1,5},{5... | collective-permute-start | bytes 1228808 | tf_op jit(solution)/shard_map/ppermute | solution.py:253
  50.5 2.6 %collective-permute-start.10 = (bf16[4,4,80,360]{3,2,1,0:T(8,128)(2,1)S(1)}, bf16[4,4,80,360]{3,2,1,0:T(8,128)(2,1)S(1)}, u32[]{:S(2)}, u32[]{:S(2)}) collective-permute-start(bf16[4,4,80,360]{3,2,1,0:T(8,128)(2,1)S(1)} %get-tuple-element.32), channel_id=1, source_target_pairs={{0,4},{4,0},{8,12},{12,8},{16,20},{20,16},{24,28},{28,24},{1,5},{5... | collective-permute-start | bytes 2764808 | tf_op jit(solution)/shard_map/ppermute | solution.py:253
  53.4 9.7 %collective-permute-start.14 = (bf16[4,160,320]{2,1,0:T(8,128)(2,1)S(1)}, bf16[4,160,320]{2,1,0:T(8,128)(2,1)S(1)}, u32[]{:S(2)}, u32[]{:S(2)}) collective-permute-start(bf16[4,160,320]{2,1,0:T(8,128)(2,1)S(1)} %get-tuple-element.36), channel_id=1, source_target_pairs={{0,4},{4,0},{8,12},{12,8},{16,20},{20,16},{24,28},{28,24},{1,5},{5... | collective-permute-start | bytes 1228808 | tf_op jit(solution)/shard_map/ppermute | solution.py:253
  53.6 14.7 %collective-permute-start.11 = (bf16[1,4,80,360]{3,2,1,0:T(8,128)(2,1)S(1)}, bf16[1,4,80,360]{3,2,1,0:T(8,128)(2,1)S(1)}, u32[]{:S(2)}, u32[]{:S(2)}) collective-permute-start(bf16[1,4,80,360]{3,2,1,0:T(8,128)(2,1)S(1)} %get-tuple-element.41), channel_id=1, source_target_pairs={{0,1},{1,0},{2,3},{3,2},{4,5},{5,4},{6,7},{7,6},{8,9},{9,8},{10,11... | collective-permute-start | bytes 691208 | tf_op jit(solution)/shard_map/ppermute | solution.py:253
  61.5 12.6 %collective-permute-start.13 = (bf16[1,4,80,360]{3,2,1,0:T(8,128)(2,1)S(1)}, bf16[1,4,80,360]{3,2,1,0:T(8,128)(2,1)S(1)}, u32[]{:S(2)}, u32[]{:S(2)}) collective-permute-start(bf16[1,4,80,360]{3,2,1,0:T(8,128)(2,1)S(1)} %get-tuple-element.42), channel_id=1, source_target_pairs={{0,3},{1,2},{2,1},{3,0},{4,7},{5,6},{6,5},{7,4},{8,11},{9,10},{10,... | collective-permute-start | bytes 691208 | tf_op jit(solution)/shard_map/ppermute | solution.py:253
  62.5 13.0 %collective-permute-start.12 = (bf16[1,4,80,360]{3,2,1,0:T(8,128)(2,1)S(1)}, bf16[1,4,80,360]{3,2,1,0:T(8,128)(2,1)S(1)}, u32[]{:S(2)}, u32[]{:S(2)}) collective-permute-start(bf16[1,4,80,360]{3,2,1,0:T(8,128)(2,1)S(1)} %get-tuple-element.43), channel_id=1, source_target_pairs={{0,2},{1,3},{2,0},{3,1},{4,6},{5,7},{6,4},{7,5},{8,10},{9,11},{10,... | collective-permute-start | bytes 691208 | tf_op jit(solution)/shard_map/ppermute | solution.py:253
  63.2 12.4 %collective-permute-start.15 = (bf16[1,160,320]{2,1,0:T(8,128)(2,1)S(1)}, bf16[1,160,320]{2,1,0:T(8,128)(2,1)S(1)}, u32[]{:S(2)}, u32[]{:S(2)}) collective-permute-start(bf16[1,160,320]{2,1,0:T(8,128)(2,1)S(1)} %get-tuple-element.44), channel_id=1, source_target_pairs={{0,8},{4,12},{8,0},{12,4},{16,24},{20,28},{24,16},{28,20},{1,9},{5... | collective-permute-start | bytes 307208 | tf_op jit(solution)/shard_map/ppermute | solution.py:253
  63.3 12.3 %collective-permute-start.17 = (bf16[1,160,320]{2,1,0:T(8,128)(2,1)S(1)}, bf16[1,160,320]{2,1,0:T(8,128)(2,1)S(1)}, u32[]{:S(2)}, u32[]{:S(2)}) collective-permute-start(bf16[1,160,320]{2,1,0:T(8,128)(2,1)S(1)} %get-tuple-element.45), channel_id=1, source_target_pairs={{0,24},{4,28},{8,16},{12,20},{16,8},{20,12},{24,0},{28,4},{1,25},{... | collective-permute-start | bytes 307208 | tf_op jit(solution)/shard_map/ppermute | solution.py:253
  68.3 9.1 %collective-permute-start.16 = (bf16[1,160,320]{2,1,0:T(8,128)(2,1)S(1)}, bf16[1,160,320]{2,1,0:T(8,128)(2,1)S(1)}, u32[]{:S(2)}, u32[]{:S(2)}) collective-permute-start(bf16[1,160,320]{2,1,0:T(8,128)(2,1)S(1)} %get-tuple-element.46), channel_id=1, source_target_pairs={{0,16},{4,20},{8,24},{12,28},{16,0},{20,4},{24,8},{28,12},{1,17},{... | collective-permute-start | bytes 307208 | tf_op jit(solution)/shard_map/ppermute | solution.py:253
  77.5 5.2 %collective-permute-start.18 = (bf16[1,80,360]{2,1,0:T(8,128)(2,1)S(1)}, bf16[1,80,360]{2,1,0:T(8,128)(2,1)S(1)}, u32[]{:S(2)}, u32[]{:S(2)}) collective-permute-start(bf16[1,80,360]{2,1,0:T(8,128)(2,1)S(1)} %get-tuple-element.51), channel_id=1, source_target_pairs={{0,8},{4,12},{8,0},{12,4},{16,24},{20,28},{24,16},{28,20},{1,9},{5... | collective-permute-start | bytes 172808 | tf_op jit(solution)/shard_map/ppermute | solution.py:253
  77.6 6.2 %collective-permute-start.20 = (bf16[1,80,360]{2,1,0:T(8,128)(2,1)S(1)}, bf16[1,80,360]{2,1,0:T(8,128)(2,1)S(1)}, u32[]{:S(2)}, u32[]{:S(2)}) collective-permute-start(bf16[1,80,360]{2,1,0:T(8,128)(2,1)S(1)} %get-tuple-element.52), channel_id=1, source_target_pairs={{0,24},{4,28},{8,16},{12,20},{16,8},{20,12},{24,0},{28,4},{1,25},{... | collective-permute-start | bytes 172808 | tf_op jit(solution)/shard_map/ppermute | solution.py:253
  79.6 6.7 %collective-permute-start.19 = (bf16[1,80,360]{2,1,0:T(8,128)(2,1)S(1)}, bf16[1,80,360]{2,1,0:T(8,128)(2,1)S(1)}, u32[]{:S(2)}, u32[]{:S(2)}) collective-permute-start(bf16[1,80,360]{2,1,0:T(8,128)(2,1)S(1)} %get-tuple-element.53), channel_id=1, source_target_pairs={{0,16},{4,20},{8,24},{12,28},{16,0},{20,4},{24,8},{28,12},{1,17},{... | collective-permute-start | bytes 172808 | tf_op jit(solution)/shard_map/ppermute | solution.py:253
  81.0 5.3 %collective-permute-start.21 = (bf16[160,320]{1,0:T(8,128)(2,1)S(1)}, bf16[160,320]{1,0:T(8,128)(2,1)S(1)}, u32[]{:S(2)}, u32[]{:S(2)}) collective-permute-start(bf16[160,320]{1,0:T(8,128)(2,1)S(1)} %fusion.7), channel_id=1, source_target_pairs={{0,1},{1,0},{2,3},{3,2},{4,5},{5,4},{6,7},{7,6},{8,9},{9,8},{10,11... | collective-permute-start | bytes 307208 | tf_op jit(solution)/shard_map/ppermute | solution.py:253
  86.3 5.9 %collective-permute-start.24 = (bf16[1,80,360]{2,1,0:T(8,128)(2,1)S(1)}, bf16[1,80,360]{2,1,0:T(8,128)(2,1)S(1)}, u32[]{:S(2)}, u32[]{:S(2)}) collective-permute-start(bf16[1,80,360]{2,1,0:T(8,128)(2,1)S(1)} %bitcast.82), channel_id=1, source_target_pairs={{0,3},{1,2},{2,1},{3,0},{4,7},{5,6},{6,5},{7,4},{8,11},{9,10},{10,... | collective-permute-start | bytes 172808 | tf_op jit(solution)/shard_map/ppermute | solution.py:253
  88.4 4.9 %collective-permute-start.23 = (bf16[1,80,360]{2,1,0:T(8,128)(2,1)S(1)}, bf16[1,80,360]{2,1,0:T(8,128)(2,1)S(1)}, u32[]{:S(2)}, u32[]{:S(2)}) collective-permute-start(bf16[1,80,360]{2,1,0:T(8,128)(2,1)S(1)} %bitcast.83), channel_id=1, source_target_pairs={{0,2},{1,3},{2,0},{3,1},{4,6},{5,7},{6,4},{7,5},{8,10},{9,11},{10,... | collective-permute-start | bytes 172808 | tf_op jit(solution)/shard_map/ppermute | solution.py:253
  89.3 4.2 %collective-permute-start.22 = (bf16[1,80,360]{2,1,0:T(8,128)(2,1)S(1)}, bf16[1,80,360]{2,1,0:T(8,128)(2,1)S(1)}, u32[]{:S(2)}, u32[]{:S(2)}) collective-permute-start(bf16[1,80,360]{2,1,0:T(8,128)(2,1)S(1)} %bitcast.84), channel_id=1, source_target_pairs={{0,1},{1,0},{2,3},{3,2},{4,5},{5,4},{6,7},{7,6},{8,9},{9,8},{10,11... | collective-permute-start | bytes 172808 | tf_op jit(solution)/shard_map/ppermute | solution.py:253
  89.9 4.9 %collective-permute-start.25 = (bf16[160,320]{1,0:T(8,128)(2,1)S(1)}, bf16[160,320]{1,0:T(8,128)(2,1)S(1)}, u32[]{:S(2)}, u32[]{:S(2)}) collective-permute-start(bf16[160,320]{1,0:T(8,128)(2,1)S(1)} %add_convert_fusion.3), channel_id=1, source_target_pairs={{0,2},{1,3},{2,0},{3,1},{4,6},{5,7},{6,4},{7,5},{8,10},{9,11},{10,... | collective-permute-start | bytes 307208 | tf_op jit(solution)/shard_map/ppermute | solution.py:253

commit v7 on v6

--- a/solution.py
+++ b/solution.py
@@ -264,10 +264,10 @@
 def gather_partners(values, axis, low, bits, most=2):
     shape = values.shape
     values = values[None]
-    for at, width in bit_groups(bits, most):
+    for at, width in reversed(bit_groups(bits, most)):
         parts = [values] + [swap(values, axis, m << (low + at)) for m in range(1, 1 << width)]
-        values = jnp.concatenate(parts)
-    return values.reshape((1 << bits,) + shape)
+        values = jnp.stack(parts, axis=1).reshape((-1,) + shape)
+    return values
 
 
 def add_up(parts):
@@ -320,9 +320,12 @@
     time_master, first = lax.optimization_barrier((temb_master, mine[0]))
     time_master = time_master.astype(bf16)
     over_planes = gather_partners(first, "fsdp", 1, plane_bits)
-    own_time = gather_partners(time_master, "fsdp", 1, plane_bits, most=1)
-    over_planes, tiles_then = lax.optimization_barrier((over_planes, tiles))
+    near_bits = plane_bits // 2
+    far_time = gather_partners(time_master, "fsdp", 1 + near_bits, plane_bits - near_bits, most=1)
+    over_planes, far_time, tiles_then = lax.optimization_barrier((over_planes, far_time, tiles))
     far = gather_partners(over_planes[1:], "dp", 0, part_bits)
+    own_time = gather_partners(far_time, "fsdp", 1, near_bits, most=1)
+    own_time = own_time.swapaxes(0, 1).reshape((-1,) + time_master.shape)
     normed = group_norm(tiles_then)
     own = jnp.concatenate([jnp.stack(mine)[:, None], far], axis=1)
     own, own_time, normed, times = lax.optimization_barrier((own, own_time, normed, timesteps[0]))
@@ -334,18 +337,15 @@
     )
 
     grad = add_up([keep, swap(send, "fsdp", 1)])
-    grad, send_time = lax.optimization_barrier((grad, send_time))
     time_grad = add_up([keep_time, swap(send_time, "fsdp", 1)])
+    grad, time_grad = lax.optimization_barrier((grad, time_grad))
     grad = scatter_partners(grad, "dp", 0, part_bits)
     for bit in range(part_bits, peer_bits):
         grad = sum_partners(grad, "dp", bit, 1)
     time_grad = scatter_partners(time_grad, "fsdp", 1, plane_bits)
-    grad, time_grad = lax.optimization_barrier((grad, time_grad))
     grad = scatter_partners(grad, "fsdp", 1, plane_bits)
-    time_grad = sum_partners(time_grad, "dp", 0, peer_bits // 2, most=1)
-    grad, time_grad = lax.optimization_barrier((grad, time_grad))
+    time_grad = sum_partners(time_grad, "dp", 0, peer_bits)
     grad = gather_partners(grad, "dp", 0, part_bits)
-    time_grad = sum_partners(time_grad, "dp", peer_bits // 2, peer_bits - peer_bits // 2, most=1)
     grad = jnp.concatenate(
         [lax.dynamic_index_in_dim(grad, part ^ q, 0, keepdims=False) for q in range(parts)]
     )

time: 95.8 us -> 95.7 us (level)
  waiting for transfers between devices: 27.1 us -> 19.2 us
  starting transfers between devices: 34.8 us -> 42.4 us
    ppermute x26 -> x27, waiting for transfers between devices: 27.1 us -> 19.2 us  [swap(): return lax.ppermute(values, axis, pairs)]
    ppermute x26 -> x27, starting transfers between devices: 34.8 us -> 42.4 us  [swap(): return lax.ppermute(values, axis, pairs)]
    another operation x0 -> x2, other arithmetic: none -> 1.03 us  [gather_partners(): values = jnp.stack(parts, axis=1).reshape((-1,) + shape)]
    broadcast_in_dim x1 -> x0, other arithmetic: 0.96 us -> none  [gather_partners(): values = values[None]]
  transfers between devices with their start and end apart: 26 -> 27, of which waited for: 15 -> 11; matrix products, arithmetic and copies ran while one was open for 4% -> 4% of each run, Pallas kernels for 8% -> 8%
where the time goes in v7:
time: 95.7 us; the launch traced here: 95.4 us
  starting transfers between devices  42.4 us (44%)
  Pallas kernels  26.3 us (27%)
  waiting for transfers between devices  19.2 us (20%)
  other arithmetic  6.34 us (7%)
    ppermute x27, starting transfers between devices, swap(): return lax.ppermute(values, axis, pairs)  42.4 us
    ppermute x27, waiting for transfers between devices, swap(): return lax.ppermute(values, axis, pairs)  19.2 us
    pallas_call x1, Pallas kernels, conv_both(): pl.pallas_call(functools.partial(conv_kernel, steps), grid_spec=pltpu.Pre...  18.5 us
    pallas_call x1, Pallas kernels, group_norm(): pl.pallas_call(functools.partial(norm_kernel, group_width), grid=(number...  7.73 us
  transfers between devices with their start and end apart: 27, of which 11 were waited for; matrix products, arithmetic and copies ran while one was open for 4% of the time, Pallas kernels for 8%

profile of v7, /device:TPU:0, one launch (start us, length us, event | category | flops | bytes accessed | tf_op | source)
XLA Modules:
  0.0 95.4 jit_solution(4085317268344601571)
XLA Ops:
  0.6 1.1 %convert_element_type.135 = bf16[360,320]{0,1:T(8,128)(2,1)S(1)} convert(f32[360,320]{0,1:T(8,128)} %param.11) | non-fusion elementwise | flops 115200 | bytes 691200 | tf_op jit(solution)/shard_map/convert_element_type | solution.py:318
  1.8 5.1 %collective-permute-start.2 = (bf16[1,80,360]{2,1,0:T(8,128)(2,1)S(1)}, bf16[1,80,360]{2,1,0:T(8,128)(2,1)S(1)}, u32[]{:S(2)}, u32[]{:S(2)}) collective-permute-start(bf16[1,80,360]{2,1,0:T(8,128)(2,1)S(1)} %get-tuple-element.51), channel_id=1, source_target_pairs={{0,24},{4,28},{8,16},{12,20},{16,8},{20,12},{24,0},{28,4},{1,25},{... | collective-permute-start | bytes 172808 | tf_op jit(solution)/shard_map/ppermute | solution.py:253
  6.9 0.6 collective-permute-start
  7.5 1.0 %convert_bitcast_fusion.2 = (bf16[1,1,160,320]{3,2,1,0:T(8,128)(2,1)S(1)}, bf16[1,160,320]{2,1,0:T(8,128)(2,1)S(1)}) fusion(f32[160,320]{1,0:T(8,128)} %param.12), kind=kLoop, calls=%fused_computation.45 | loop fusion | flops 51200 | bytes 409600 | tf_op jit(solution)/shard_map/stack;broadcast_in_dim | solution.py:269
  8.5 2.4 %collective-permute-start.3 = (bf16[1,160,320]{2,1,0:T(8,128)(2,1)S(1)}, bf16[1,160,320]{2,1,0:T(8,128)(2,1)S(1)}, u32[]{:S(2)}, u32[]{:S(2)}) collective-permute-start(bf16[1,160,320]{2,1,0:T(8,128)(2,1)S(1)} %get-tuple-element.55), channel_id=1, source_target_pairs={{0,16},{4,20},{8,24},{12,28},{16,0},{20,4},{24,8},{28,12},{1,17},{... | collective-permute-start | bytes 307208 | tf_op jit(solution)/shard_map/ppermute | solution.py:253
  10.9 3.0 %collective-permute-done.1 = bf16[1,80,360]{2,1,0:T(8,128)(2,1)S(1)} collective-permute-done((bf16[1,80,360]{2,1,0:T(8,128)(2,1)S(1)}, bf16[1,80,360]{2,1,0:T(8,128)(2,1)S(1)}, u32[]{:S(2)}, u32[]{:S(2)}) %collective-permute-start.1) | collective-permute-done | bytes 57632 | tf_op jit(solution)/shard_map/ppermute | solution.py:253
  13.9 3.5 %collective-permute-done.3 = bf16[1,160,320]{2,1,0:T(8,128)(2,1)S(1)} collective-permute-done((bf16[1,160,320]{2,1,0:T(8,128)(2,1)S(1)}, bf16[1,160,320]{2,1,0:T(8,128)(2,1)S(1)}, u32[]{:S(2)}, u32[]{:S(2)}) %collective-permute-start.3) | collective-permute-done | bytes 102432 | tf_op jit(solution)/shard_map/ppermute | solution.py:253
  17.5 2.6 %collective-permute-start.6 = (bf16[1,3,80,360]{3,2,1,0:T(8,128)(2,1)S(1)}, bf16[1,3,80,360]{3,2,1,0:T(8,128)(2,1)S(1)}, u32[]{:S(2)}, u32[]{:S(2)}) collective-permute-start(bf16[1,3,80,360]{3,2,1,0:T(8,128)(2,1)S(1)} %get-tuple-element.53), channel_id=1, source_target_pairs={{0,3},{1,2},{2,1},{3,0},{4,7},{5,6},{6,5},{7,4},{8,11},{9,10},{10,... | collective-permute-start | bytes 518408 | tf_op jit(solution)/shard_map/ppermute | solution.py:253
  20.1 0.5 collective-permute-start.5
  20.6 0.5 collective-permute-start.4
  21.2 7.7 %group_norm.1.normed_ref = bf16[15,320,256]{2,1,0:T(8,128)(2,1)} custom-call(bf16[320,320]{1,0:T(8,128)(2,1)} %constant.45.clone.same_ref, bf16[15,320,256]{2,1,0:T(8,128)(2,1)} %bitcast.102), custom_call_target="tpu_custom_call" | custom-call | flops 24576000 | bytes 4915200 | tf_op jit(solution)/shard_map/group_norm/pallas_call | solution.py:57
  29.0 0.2 maximum_bitcast_fusion
  29.2 0.2 pad_maximum_fusion.own_ref
  29.4 0.1 maximum_bitcast_fusion.1
  29.7 0.5 collective-permute-start.9
  30.2 1.2 %multiply_cosine_fusion = (f32[640,128]{1,0:T(8,128)S(1)}, f32[640,128]{1,0:T(8,128)S(1)}) fusion(f32[128]{0:T(128)S(1)} %pad_convert_fusion, f32[640]{0:T(1024)S(1)} %multiply_exponential_fusion), kind=kLoop, calls=%fused_computation.12 | loop fusion | flops 81920 | bytes 658432 | tf_op jit(solution)/shard_map/cos | solution.py:302
  31.4 0.2 multiply_convert_fusion.features_ref
  31.6 1.3 %collective-permute-done.9.other_time_ref = bf16[4,160,320]{2,1,0:T(8,128)(2,1)S(1)} collective-permute-done((bf16[4,160,320]{2,1,0:T(8,128)(2,1)S(1)}, bf16[4,160,320]{2,1,0:T(8,128)(2,1)S(1)}, u32[]{:S(2)}, u32[]{:S(2)}) %collective-permute-start.9) | collective-permute-done | bytes 409632 | tf_op jit(solution)/shard_map/ppermute | solution.py:253
  32.9 18.5 %conv_both.1 = (bf16[15,320,256]{2,1,0:T(8,128)(2,1)}, bf16[4,4,80,360]{3,2,1,0:T(8,128)(2,1)S(1)}, bf16[4,4,80,360]{3,2,1,0:T(8,128)(2,1)S(1)}, bf16[4,160,320]...) custom-call(s32[1,4]{1,0:T(1,128)S(1)} %copy-done.1, bf16[4,4,80,360]{3,2,1,0:T(8,128)(2,1)S(1)} %pad_maximum_fusion.own_ref, ...), custom_call_target="tpu_custom_call" | custom-call | flops 14155776000 | bytes 9830400 | tf_op jit(solution)/shard_map/conv_both/pallas_call | solution.py:217
  51.5 0.1 collective-permute-start.10
  51.6 0.4 collective-permute-start.11
  52.0 2.8 %collective-permute-done.11 = bf16[4,160,320]{2,1,0:T(8,128)(2,1)S(1)} collective-permute-done((bf16[4,160,320]{2,1,0:T(8,128)(2,1)S(1)}, bf16[4,160,320]{2,1,0:T(8,128)(2,1)S(1)}, u32[]{:S(2)}, u32[]{:S(2)}) %collective-permute-start.11) | collective-permute-done | bytes 409632 | tf_op jit(solution)/shard_map/ppermute | solution.py:253
  54.7 0.1 add_convert_fusion.1
  54.9 0.3 add_convert_fusion
  55.2 7.7 %collective-permute-start.12 = (bf16[1,4,80,360]{3,2,1,0:T(8,128)(2,1)S(1)}, bf16[1,4,80,360]{3,2,1,0:T(8,128)(2,1)S(1)}, u32[]{:S(2)}, u32[]{:S(2)}) collective-permute-start(bf16[1,4,80,360]{3,2,1,0:T(8,128)(2,1)S(1)} %get-tuple-element.35), channel_id=1, source_target_pairs={{0,1},{1,0},{2,3},{3,2},{4,5},{5,4},{6,7},{7,6},{8,9},{9,8},{10,11... | collective-permute-start | bytes 691208 | tf_op jit(solution)/shard_map/ppermute | solution.py:253
  62.9 1.3 %collective-permute-start.14 = (bf16[1,4,80,360]{3,2,1,0:T(8,128)(2,1)S(1)}, bf16[1,4,80,360]{3,2,1,0:T(8,128)(2,1)S(1)}, u32[]{:S(2)}, u32[]{:S(2)}) collective-permute-start(bf16[1,4,80,360]{3,2,1,0:T(8,128)(2,1)S(1)} %get-tuple-element.36), channel_id=1, source_target_pairs={{0,3},{1,2},{2,1},{3,0},{4,7},{5,6},{6,5},{7,4},{8,11},{9,10},{10,... | collective-permute-start | bytes 691208 | tf_op jit(solution)/shard_map/ppermute | solution.py:253
  64.2 0.5 collective-permute-start.13
  64.7 2.1 %collective-permute-start.21 = (bf16[1,160,320]{2,1,0:T(8,128)(2,1)S(1)}, bf16[1,160,320]{2,1,0:T(8,128)(2,1)S(1)}, u32[]{:S(2)}, u32[]{:S(2)}) collective-permute-start(bf16[1,160,320]{2,1,0:T(8,128)(2,1)S(1)} %get-tuple-element.38), channel_id=1, source_target_pairs={{0,8},{4,12},{8,0},{12,4},{16,24},{20,28},{24,16},{28,20},{1,9},{5... | collective-permute-start | bytes 307208 | tf_op jit(solution)/shard_map/ppermute | solution.py:253
  66.7 2.7 %collective-permute-start.23 = (bf16[1,160,320]{2,1,0:T(8,128)(2,1)S(1)}, bf16[1,160,320]{2,1,0:T(8,128)(2,1)S(1)}, u32[]{:S(2)}, u32[]{:S(2)}) collective-permute-start(bf16[1,160,320]{2,1,0:T(8,128)(2,1)S(1)} %get-tuple-element.39), channel_id=1, source_target_pairs={{0,24},{4,28},{8,16},{12,20},{16,8},{20,12},{24,0},{28,4},{1,25},{... | collective-permute-start | bytes 307208 | tf_op jit(solution)/shard_map/ppermute | solution.py:253
  69.4 0.3 collective-permute-done.12
  69.7 3.4 %collective-permute-start.22 = (bf16[1,160,320]{2,1,0:T(8,128)(2,1)S(1)}, bf16[1,160,320]{2,1,0:T(8,128)(2,1)S(1)}, u32[]{:S(2)}, u32[]{:S(2)}) collective-permute-start(bf16[1,160,320]{2,1,0:T(8,128)(2,1)S(1)} %get-tuple-element.40), channel_id=1, source_target_pairs={{0,16},{4,20},{8,24},{12,28},{16,0},{20,4},{24,8},{28,12},{1,17},{... | collective-permute-start | bytes 307208 | tf_op jit(solution)/shard_map/ppermute | solution.py:253
  73.1 2.6 %collective-permute-done.14 = bf16[1,4,80,360]{3,2,1,0:T(8,128)(2,1)S(1)} collective-permute-done((bf16[1,4,80,360]{3,2,1,0:T(8,128)(2,1)S(1)}, bf16[1,4,80,360]{3,2,1,0:T(8,128)(2,1)S(1)}, u32[]{:S(2)}, u32[]{:S(2)}) %collective-permute-start.14) | collective-permute-done | bytes 230432 | tf_op jit(solution)/shard_map/ppermute | solution.py:253
  75.7 1.4 %collective-permute-done.13 = bf16[1,4,80,360]{3,2,1,0:T(8,128)(2,1)S(1)} collective-permute-done((bf16[1,4,80,360]{3,2,1,0:T(8,128)(2,1)S(1)}, bf16[1,4,80,360]{3,2,1,0:T(8,128)(2,1)S(1)}, u32[]{:S(2)}, u32[]{:S(2)}) %collective-permute-start.13) | collective-permute-done | bytes 230432 | tf_op jit(solution)/shard_map/ppermute | solution.py:253
  77.1 0.1 fusion.1
  77.3 2.0 %collective-permute-start.15 = (bf16[1,80,360]{2,1,0:T(8,128)(2,1)S(1)}, bf16[1,80,360]{2,1,0:T(8,128)(2,1)S(1)}, u32[]{:S(2)}, u32[]{:S(2)}) collective-permute-start(bf16[1,80,360]{2,1,0:T(8,128)(2,1)S(1)} %get-tuple-element.45), channel_id=1, source_target_pairs={{0,8},{4,12},{8,0},{12,4},{16,24},{20,28},{24,16},{28,20},{1,9},{5... | collective-permute-start | bytes 172808 | tf_op jit(solution)/shard_map/ppermute | solution.py:253
  79.3 2.9 %collective-permute-start.17 = (bf16[1,80,360]{2,1,0:T(8,128)(2,1)S(1)}, bf16[1,80,360]{2,1,0:T(8,128)(2,1)S(1)}, u32[]{:S(2)}, u32[]{:S(2)}) collective-permute-start(bf16[1,80,360]{2,1,0:T(8,128)(2,1)S(1)} %get-tuple-element.46), channel_id=1, source_target_pairs={{0,24},{4,28},{8,16},{12,20},{16,8},{20,12},{24,0},{28,4},{1,25},{... | collective-permute-start | bytes 172808 | tf_op jit(solution)/shard_map/ppermute | solution.py:253
  82.3 1.5 %collective-permute-start.26 = (bf16[160,320]{1,0:T(8,128)(2,1)S(1)}, bf16[160,320]{1,0:T(8,128)(2,1)S(1)}, u32[]{:S(2)}, u32[]{:S(2)}) collective-permute-start(bf16[160,320]{1,0:T(8,128)(2,1)S(1)} %fusion.5), channel_id=1, source_target_pairs={{0,3},{1,2},{2,1},{3,0},{4,7},{5,6},{6,5},{7,4},{8,11},{9,10},{10,... | collective-permute-start | bytes 307208 | tf_op jit(solution)/shard_map/ppermute | solution.py:253
  83.8 0.4 collective-permute-start.25
  84.2 1.7 %collective-permute-start.24 = (bf16[160,320]{1,0:T(8,128)(2,1)S(1)}, bf16[160,320]{1,0:T(8,128)(2,1)S(1)}, u32[]{:S(2)}, u32[]{:S(2)}) collective-permute-start(bf16[160,320]{1,0:T(8,128)(2,1)S(1)} %fusion.5), channel_id=1, source_target_pairs={{0,1},{1,0},{2,3},{3,2},{4,5},{5,4},{6,7},{7,6},{8,9},{9,8},{10,11... | collective-permute-start | bytes 307208 | tf_op jit(solution)/shard_map/ppermute | solution.py:253
  85.9 1.5 %collective-permute-done.16 = bf16[1,80,360]{2,1,0:T(8,128)(2,1)S(1)} collective-permute-done((bf16[1,80,360]{2,1,0:T(8,128)(2,1)S(1)}, bf16[1,80,360]{2,1,0:T(8,128)(2,1)S(1)}, u32[]{:S(2)}, u32[]{:S(2)}) %collective-permute-start.16) | collective-permute-done | bytes 57632 | tf_op jit(solution)/shard_map/ppermute | solution.py:253
  87.4 1.5 %collective-permute-start.20 = (bf16[1,80,360]{2,1,0:T(8,128)(2,1)S(1)}, bf16[1,80,360]{2,1,0:T(8,128)(2,1)S(1)}, u32[]{:S(2)}, u32[]{:S(2)}) collective-permute-start(bf16[1,80,360]{2,1,0:T(8,128)(2,1)S(1)} %fusion.7), channel_id=1, source_target_pairs={{0,3},{1,2},{2,1},{3,0},{4,7},{5,6},{6,5},{7,4},{8,11},{9,10},{10,... | collective-permute-start | bytes 172808 | tf_op jit(solution)/shard_map/ppermute | solution.py:253
  88.9 1.4 %collective-permute-start.19 = (bf16[1,80,360]{2,1,0:T(8,128)(2,1)S(1)}, bf16[1,80,360]{2,1,0:T(8,128)(2,1)S(1)}, u32[]{:S(2)}, u32[]{:S(2)}) collective-permute-start(bf16[1,80,360]{2,1,0:T(8,128)(2,1)S(1)} %fusion.7), channel_id=1, source_target_pairs={{0,2},{1,3},{2,0},{3,1},{4,6},{5,7},{6,4},{7,5},{8,10},{9,11},{10,... | collective-permute-start | bytes 172808 | tf_op jit(solution)/shard_map/ppermute | solution.py:253
  90.2 0.7 collective-permute-start.18
  90.9 0.8 fusion.4
  91.7 1.3 %collective-permute-done.20 = bf16[1,80,360]{2,1,0:T(8,128)(2,1)S(1)} collective-permute-done((bf16[1,80,360]{2,1,0:T(8,128)(2,1)S(1)}, bf16[1,80,360]{2,1,0:T(8,128)(2,1)S(1)}, u32[]{:S(2)}, u32[]{:S(2)}) %collective-permute-start.20) | collective-permute-done | bytes 57632 | tf_op jit(solution)/shard_map/ppermute | solution.py:253
  93.0 0.4 collective-permute-done.19
  93.5 1.0 %collective-permute-done.18 = bf16[1,80,360]{2,1,0:T(8,128)(2,1)S(1)} collective-permute-done((bf16[1,80,360]{2,1,0:T(8,128)(2,1)S(1)}, bf16[1,80,360]{2,1,0:T(8,128)(2,1)S(1)}, u32[]{:S(2)}, u32[]{:S(2)}) %collective-permute-start.18) | collective-permute-done | bytes 57632 | tf_op jit(solution)/shard_map/ppermute | solution.py:253
  94.6 0.8 convert_bitcast_fusion
  (41 shorter events, 0.9 us)
Async XLA Ops:
  1.8 9.1 %collective-permute-start.2 = (bf16[1,80,360]{2,1,0:T(8,128)(2,1)S(1)}, bf16[1,80,360]{2,1,0:T(8,128)(2,1)S(1)}, u32[]{:S(2)}, u32[]{:S(2)}) collective-permute-start(bf16[1,80,360]{2,1,0:T(8,128)(2,1)S(1)} %get-tuple-element.51), channel_id=1, source_target_pairs={{0,24},{4,28},{8,16},{12,20},{16,8},{20,12},{24,0},{28,4},{1,25},{... | collective-permute-start | bytes 172808 | tf_op jit(solution)/shard_map/ppermute | solution.py:253
  6.9 7.0 %collective-permute-start.1 = (bf16[1,80,360]{2,1,0:T(8,128)(2,1)S(1)}, bf16[1,80,360]{2,1,0:T(8,128)(2,1)S(1)}, u32[]{:S(2)}, u32[]{:S(2)}) collective-permute-start(bf16[1,80,360]{2,1,0:T(8,128)(2,1)S(1)} %get-tuple-element.51), channel_id=1, source_target_pairs={{0,16},{4,20},{8,24},{12,28},{16,0},{20,4},{24,8},{28,12},{1,17},{... | collective-permute-start | bytes 172808 | tf_op jit(solution)/shard_map/ppermute | solution.py:253
  6.9 7.0 %collective-permute-start = (bf16[1,80,360]{2,1,0:T(8,128)(2,1)S(1)}, bf16[1,80,360]{2,1,0:T(8,128)(2,1)S(1)}, u32[]{:S(2)}, u32[]{:S(2)}) collective-permute-start(bf16[1,80,360]{2,1,0:T(8,128)(2,1)S(1)} %get-tuple-element.51), channel_id=1, source_target_pairs={{0,8},{4,12},{8,0},{12,4},{16,24},{20,28},{24,16},{28,20},{1,9},{5... | collective-permute-start | bytes 172808 | tf_op jit(solution)/shard_map/ppermute | solution.py:253
  8.5 8.9 %collective-permute-start.3 = (bf16[1,160,320]{2,1,0:T(8,128)(2,1)S(1)}, bf16[1,160,320]{2,1,0:T(8,128)(2,1)S(1)}, u32[]{:S(2)}, u32[]{:S(2)}) collective-permute-start(bf16[1,160,320]{2,1,0:T(8,128)(2,1)S(1)} %get-tuple-element.55), channel_id=1, source_target_pairs={{0,16},{4,20},{8,24},{12,28},{16,0},{20,4},{24,8},{28,12},{1,17},{... | collective-permute-start | bytes 307208 | tf_op jit(solution)/shard_map/ppermute | solution.py:253
  17.5 11.4 %collective-permute-start.6 = (bf16[1,3,80,360]{3,2,1,0:T(8,128)(2,1)S(1)}, bf16[1,3,80,360]{3,2,1,0:T(8,128)(2,1)S(1)}, u32[]{:S(2)}, u32[]{:S(2)}) collective-permute-start(bf16[1,3,80,360]{3,2,1,0:T(8,128)(2,1)S(1)} %get-tuple-element.53), channel_id=1, source_target_pairs={{0,3},{1,2},{2,1},{3,0},{4,7},{5,6},{6,5},{7,4},{8,11},{9,10},{10,... | collective-permute-start | bytes 518408 | tf_op jit(solution)/shard_map/ppermute | solution.py:253
  20.1 8.9 %collective-permute-start.5 = (bf16[1,3,80,360]{3,2,1,0:T(8,128)(2,1)S(1)}, bf16[1,3,80,360]{3,2,1,0:T(8,128)(2,1)S(1)}, u32[]{:S(2)}, u32[]{:S(2)}) collective-permute-start(bf16[1,3,80,360]{3,2,1,0:T(8,128)(2,1)S(1)} %get-tuple-element.53), channel_id=1, source_target_pairs={{0,2},{1,3},{2,0},{3,1},{4,6},{5,7},{6,4},{7,5},{8,10},{9,11},{10,... | collective-permute-start | bytes 518408 | tf_op jit(solution)/shard_map/ppermute | solution.py:253
  20.6 8.4 %collective-permute-start.4 = (bf16[1,3,80,360]{3,2,1,0:T(8,128)(2,1)S(1)}, bf16[1,3,80,360]{3,2,1,0:T(8,128)(2,1)S(1)}, u32[]{:S(2)}, u32[]{:S(2)}) collective-permute-start(bf16[1,3,80,360]{3,2,1,0:T(8,128)(2,1)S(1)} %get-tuple-element.53), channel_id=1, source_target_pairs={{0,1},{1,0},{2,3},{3,2},{4,5},{5,4},{6,7},{7,6},{8,9},{9,8},{10,11... | collective-permute-start | bytes 518408 | tf_op jit(solution)/shard_map/ppermute | solution.py:253
  21.2 8.2 %collective-permute-start.7 = (bf16[1,2,160,320]{3,2,1,0:T(8,128)(2,1)S(1)}, bf16[1,2,160,320]{3,2,1,0:T(8,128)(2,1)S(1)}, u32[]{:S(2)}, u32[]{:S(2)}) collective-permute-start(bf16[1,2,160,320]{3,2,1,0:T(8,128)(2,1)S(1)} %bitcast.107), channel_id=1, source_target_pairs={{0,8},{4,12},{8,0},{12,4},{16,24},{20,28},{24,16},{28,20},{1,9},{5... | collective-permute-start | bytes 614408 | tf_op jit(solution)/shard_map/ppermute | solution.py:253
  29.0 1.2 %copy-start.2 = (s32[1,15]{1,0:T(1,128)S(1)}, s32[1,15]{1,0:T(1,128)}, u32[]{:S(2)}) copy-start(s32[1,15]{1,0:T(1,128)} %param.10) | copy-start | bytes 184
  29.2 3.7 %copy-start = (bf16[15,320,256]{2,1,0:T(8,128)(2,1)S(1)}, bf16[15,320,256]{2,1,0:T(8,128)(2,1)}, u32[]{:S(2)}) copy-start(bf16[15,320,256]{2,1,0:T(8,128)(2,1)} %group_norm.1.normed_ref) | copy-start | bytes 7372804
  29.2 3.7 %copy-start.1 = (s32[1,4]{1,0:T(1,128)S(1)}, s32[1,4]{1,0:T(1,128)}, u32[]{:S(2)}) copy-start(s32[1,4]{1,0:T(1,128)} %counts_ref.1) | copy-start | bytes 52
  29.6 3.3 %collective-permute-start.8 = (bf16[4,4,80,360]{3,2,1,0:T(8,128)(2,1)S(1)}, bf16[4,4,80,360]{3,2,1,0:T(8,128)(2,1)S(1)}, u32[]{:S(2)}, u32[]{:S(2)}) collective-permute-start(bf16[4,4,80,360]{3,2,1,0:T(8,128)(2,1)S(1)} %pad_maximum_fusion.own_ref), channel_id=1, source_target_pairs={{0,4},{4,0},{8,12},{12,8},{16,20},{20,16},{24,28},{28,24},{1,5},{5... | collective-permute-start | bytes 2764808 | tf_op jit(solution)/shard_map/ppermute | solution.py:253
  29.7 3.2 %collective-permute-start.9 = (bf16[4,160,320]{2,1,0:T(8,128)(2,1)S(1)}, bf16[4,160,320]{2,1,0:T(8,128)(2,1)S(1)}, u32[]{:S(2)}, u32[]{:S(2)}) collective-permute-start(bf16[4,160,320]{2,1,0:T(8,128)(2,1)S(1)} %bitcast.98), channel_id=1, source_target_pairs={{0,4},{4,0},{8,12},{12,8},{16,20},{20,16},{24,28},{28,24},{1,5},{5... | collective-permute-start | bytes 1228808 | tf_op jit(solution)/shard_map/ppermute | solution.py:253
  51.5 3.4 %collective-permute-start.10 = (bf16[4,4,80,360]{3,2,1,0:T(8,128)(2,1)S(1)}, bf16[4,4,80,360]{3,2,1,0:T(8,128)(2,1)S(1)}, u32[]{:S(2)}, u32[]{:S(2)}) collective-permute-start(bf16[4,4,80,360]{3,2,1,0:T(8,128)(2,1)S(1)} %get-tuple-element.30), channel_id=1, source_target_pairs={{0,4},{4,0},{8,12},{12,8},{16,20},{20,16},{24,28},{28,24},{1,5},{5... | collective-permute-start | bytes 2764808 | tf_op jit(solution)/shard_map/ppermute | solution.py:253
  51.6 3.1 %collective-permute-start.11 = (bf16[4,160,320]{2,1,0:T(8,128)(2,1)S(1)}, bf16[4,160,320]{2,1,0:T(8,128)(2,1)S(1)}, u32[]{:S(2)}, u32[]{:S(2)}) collective-permute-start(bf16[4,160,320]{2,1,0:T(8,128)(2,1)S(1)} %get-tuple-element.32), channel_id=1, source_target_pairs={{0,4},{4,0},{8,12},{12,8},{16,20},{20,16},{24,28},{28,24},{1,5},{5... | collective-permute-start | bytes 1228808 | tf_op jit(solution)/shard_map/ppermute | solution.py:253
  55.2 14.5 %collective-permute-start.12 = (bf16[1,4,80,360]{3,2,1,0:T(8,128)(2,1)S(1)}, bf16[1,4,80,360]{3,2,1,0:T(8,128)(2,1)S(1)}, u32[]{:S(2)}, u32[]{:S(2)}) collective-permute-start(bf16[1,4,80,360]{3,2,1,0:T(8,128)(2,1)S(1)} %get-tuple-element.35), channel_id=1, source_target_pairs={{0,1},{1,0},{2,3},{3,2},{4,5},{5,4},{6,7},{7,6},{8,9},{9,8},{10,11... | collective-permute-start | bytes 691208 | tf_op jit(solution)/shard_map/ppermute | solution.py:253
  62.9 12.8 %collective-permute-start.14 = (bf16[1,4,80,360]{3,2,1,0:T(8,128)(2,1)S(1)}, bf16[1,4,80,360]{3,2,1,0:T(8,128)(2,1)S(1)}, u32[]{:S(2)}, u32[]{:S(2)}) collective-permute-start(bf16[1,4,80,360]{3,2,1,0:T(8,128)(2,1)S(1)} %get-tuple-element.36), channel_id=1, source_target_pairs={{0,3},{1,2},{2,1},{3,0},{4,7},{5,6},{6,5},{7,4},{8,11},{9,10},{10,... | collective-permute-start | bytes 691208 | tf_op jit(solution)/shard_map/ppermute | solution.py:253
  64.2 13.0 %collective-permute-start.13 = (bf16[1,4,80,360]{3,2,1,0:T(8,128)(2,1)S(1)}, bf16[1,4,80,360]{3,2,1,0:T(8,128)(2,1)S(1)}, u32[]{:S(2)}, u32[]{:S(2)}) collective-permute-start(bf16[1,4,80,360]{3,2,1,0:T(8,128)(2,1)S(1)} %get-tuple-element.37), channel_id=1, source_target_pairs={{0,2},{1,3},{2,0},{3,1},{4,6},{5,7},{6,4},{7,5},{8,10},{9,11},{10,... | collective-permute-start | bytes 691208 | tf_op jit(solution)/shard_map/ppermute | solution.py:253
  64.7 17.5 %collective-permute-start.21 = (bf16[1,160,320]{2,1,0:T(8,128)(2,1)S(1)}, bf16[1,160,320]{2,1,0:T(8,128)(2,1)S(1)}, u32[]{:S(2)}, u32[]{:S(2)}) collective-permute-start(bf16[1,160,320]{2,1,0:T(8,128)(2,1)S(1)} %get-tuple-element.38), channel_id=1, source_target_pairs={{0,8},{4,12},{8,0},{12,4},{16,24},{20,28},{24,16},{28,20},{1,9},{5... | collective-permute-start | bytes 307208 | tf_op jit(solution)/shard_map/ppermute | solution.py:253
  66.7 15.5 %collective-permute-start.23 = (bf16[1,160,320]{2,1,0:T(8,128)(2,1)S(1)}, bf16[1,160,320]{2,1,0:T(8,128)(2,1)S(1)}, u32[]{:S(2)}, u32[]{:S(2)}) collective-permute-start(bf16[1,160,320]{2,1,0:T(8,128)(2,1)S(1)} %get-tuple-element.39), channel_id=1, source_target_pairs={{0,24},{4,28},{8,16},{12,20},{16,8},{20,12},{24,0},{28,4},{1,25},{... | collective-permute-start | bytes 307208 | tf_op jit(solution)/shard_map/ppermute | solution.py:253
  69.7 12.5 %collective-permute-start.22 = (bf16[1,160,320]{2,1,0:T(8,128)(2,1)S(1)}, bf16[1,160,320]{2,1,0:T(8,128)(2,1)S(1)}, u32[]{:S(2)}, u32[]{:S(2)}) collective-permute-start(bf16[1,160,320]{2,1,0:T(8,128)(2,1)S(1)} %get-tuple-element.40), channel_id=1, source_target_pairs={{0,16},{4,20},{8,24},{12,28},{16,0},{20,4},{24,8},{28,12},{1,17},{... | collective-permute-start | bytes 307208 | tf_op jit(solution)/shard_map/ppermute | solution.py:253
  77.3 6.9 %collective-permute-start.15 = (bf16[1,80,360]{2,1,0:T(8,128)(2,1)S(1)}, bf16[1,80,360]{2,1,0:T(8,128)(2,1)S(1)}, u32[]{:S(2)}, u32[]{:S(2)}) collective-permute-start(bf16[1,80,360]{2,1,0:T(8,128)(2,1)S(1)} %get-tuple-element.45), channel_id=1, source_target_pairs={{0,8},{4,12},{8,0},{12,4},{16,24},{20,28},{24,16},{28,20},{1,9},{5... | collective-permute-start | bytes 172808 | tf_op jit(solution)/shard_map/ppermute | solution.py:253
  79.3 6.5 %collective-permute-start.17 = (bf16[1,80,360]{2,1,0:T(8,128)(2,1)S(1)}, bf16[1,80,360]{2,1,0:T(8,128)(2,1)S(1)}, u32[]{:S(2)}, u32[]{:S(2)}) collective-permute-start(bf16[1,80,360]{2,1,0:T(8,128)(2,1)S(1)} %get-tuple-element.46), channel_id=1, source_target_pairs={{0,24},{4,28},{8,16},{12,20},{16,8},{20,12},{24,0},{28,4},{1,25},{... | collective-permute-start | bytes 172808 | tf_op jit(solution)/shard_map/ppermute | solution.py:253
  82.2 5.1 %collective-permute-start.16 = (bf16[1,80,360]{2,1,0:T(8,128)(2,1)S(1)}, bf16[1,80,360]{2,1,0:T(8,128)(2,1)S(1)}, u32[]{:S(2)}, u32[]{:S(2)}) collective-permute-start(bf16[1,80,360]{2,1,0:T(8,128)(2,1)S(1)} %get-tuple-element.47), channel_id=1, source_target_pairs={{0,16},{4,20},{8,24},{12,28},{16,0},{20,4},{24,8},{28,12},{1,17},{... | collective-permute-start | bytes 172808 | tf_op jit(solution)/shard_map/ppermute | solution.py:253
  82.3 7.9 %collective-permute-start.26 = (bf16[160,320]{1,0:T(8,128)(2,1)S(1)}, bf16[160,320]{1,0:T(8,128)(2,1)S(1)}, u32[]{:S(2)}, u32[]{:S(2)}) collective-permute-start(bf16[160,320]{1,0:T(8,128)(2,1)S(1)} %fusion.5), channel_id=1, source_target_pairs={{0,3},{1,2},{2,1},{3,0},{4,7},{5,6},{6,5},{7,4},{8,11},{9,10},{10,... | collective-permute-start | bytes 307208 | tf_op jit(solution)/shard_map/ppermute | solution.py:253
  83.8 7.1 %collective-permute-start.25 = (bf16[160,320]{1,0:T(8,128)(2,1)S(1)}, bf16[160,320]{1,0:T(8,128)(2,1)S(1)}, u32[]{:S(2)}, u32[]{:S(2)}) collective-permute-start(bf16[160,320]{1,0:T(8,128)(2,1)S(1)} %fusion.5), channel_id=1, source_target_pairs={{0,2},{1,3},{2,0},{3,1},{4,6},{5,7},{6,4},{7,5},{8,10},{9,11},{10,... | collective-permute-start | bytes 307208 | tf_op jit(solution)/shard_map/ppermute | solution.py:253
  84.2 6.7 %collective-permute-start.24 = (bf16[160,320]{1,0:T(8,128)(2,1)S(1)}, bf16[160,320]{1,0:T(8,128)(2,1)S(1)}, u32[]{:S(2)}, u32[]{:S(2)}) collective-permute-start(bf16[160,320]{1,0:T(8,128)(2,1)S(1)} %fusion.5), channel_id=1, source_target_pairs={{0,1},{1,0},{2,3},{3,2},{4,5},{5,4},{6,7},{7,6},{8,9},{9,8},{10,11... | collective-permute-start | bytes 307208 | tf_op jit(solution)/shard_map/ppermute | solution.py:253
  87.4 5.7 %collective-permute-start.20 = (bf16[1,80,360]{2,1,0:T(8,128)(2,1)S(1)}, bf16[1,80,360]{2,1,0:T(8,128)(2,1)S(1)}, u32[]{:S(2)}, u32[]{:S(2)}) collective-permute-start(bf16[1,80,360]{2,1,0:T(8,128)(2,1)S(1)} %fusion.7), channel_id=1, source_target_pairs={{0,3},{1,2},{2,1},{3,0},{4,7},{5,6},{6,5},{7,4},{8,11},{9,10},{10,... | collective-permute-start | bytes 172808 | tf_op jit(solution)/shard_map/ppermute | solution.py:253
  88.9 4.6 %collective-permute-start.19 = (bf16[1,80,360]{2,1,0:T(8,128)(2,1)S(1)}, bf16[1,80,360]{2,1,0:T(8,128)(2,1)S(1)}, u32[]{:S(2)}, u32[]{:S(2)}) collective-permute-start(bf16[1,80,360]{2,1,0:T(8,128)(2,1)S(1)} %fusion.7), channel_id=1, source_target_pairs={{0,2},{1,3},{2,0},{3,1},{4,6},{5,7},{6,4},{7,5},{8,10},{9,11},{10,... | collective-permute-start | bytes 172808 | tf_op jit(solution)/shard_map/ppermute | solution.py:253
  90.2 4.2 %collective-permute-start.18 = (bf16[1,80,360]{2,1,0:T(8,128)(2,1)S(1)}, bf16[1,80,360]{2,1,0:T(8,128)(2,1)S(1)}, u32[]{:S(2)}, u32[]{:S(2)}) collective-permute-start(bf16[1,80,360]{2,1,0:T(8,128)(2,1)S(1)} %fusion.7), channel_id=1, source_target_pairs={{0,1},{1,0},{2,3},{3,2},{4,5},{5,4},{6,7},{7,6},{8,9},{9,8},{10,11... | collective-permute-start | bytes 172808 | tf_op jit(solution)/shard_map/ppermute | solution.py:253

commit v8 on v7

--- a/solution.py
+++ b/solution.py
@@ -21,7 +21,8 @@
     return max(size for size in range(1, 6) if number % size == 0)
 
 
-def norm_kernel(group_width, same_ref, tiles_ref, out_ref):
+def norm_kernel(group_width, same_ref, tiles_ref, *refs):
+    out_ref = refs[-1]
     same_group = same_ref[...]
     number, channels, pixels = tiles_ref.shape
     scale = 1.0 / (group_width * pixels)
@@ -47,25 +48,30 @@
         out_ref[t] = (half + half * jnp.tanh(half)).astype(bf16)
 
 
-def group_norm(tiles):
+def group_norm(tiles, first, last, into=None):
     number, channels, pixels = tiles.shape
     step = tiles_per_step(number)
     group_width = channels // GROUPS
     group = np.arange(channels) // group_width
     same_group = jnp.asarray(group[:, None] == group[None, :], bf16)
-    block = pl.BlockSpec((step, channels, pixels), lambda i: (i, 0, 0))
+    block = pl.BlockSpec((step, channels, pixels), lambda i: (i + first, 0, 0))
+    size = (last - first) * step * channels * pixels
+    operands, specs = [same_group, tiles], [pl.BlockSpec((channels, channels), lambda i: (0, 0)), block]
+    if into is not None:
+        operands, specs = operands + [into], specs + [pl.BlockSpec(memory_space=pl.ANY)]
     return pl.pallas_call(
         functools.partial(norm_kernel, group_width),
-        grid=(number // step,),
-        in_specs=[pl.BlockSpec((channels, channels), lambda i: (0, 0)), block],
+        grid=(last - first,),
+        in_specs=specs,
         out_specs=block,
         out_shape=jax.ShapeDtypeStruct(tiles.shape, bf16),
+        input_output_aliases={} if into is None else {2: 0},
         compiler_params=pltpu.CompilerParams(vmem_limit_bytes=60 * 2**20),
         cost_estimate=pl.CostEstimate(
-            flops=20 * tiles.size, bytes_accessed=4 * tiles.size, transcendentals=tiles.size
+            flops=20 * size, bytes_accessed=4 * size, transcendentals=size
         ),
         name="group_norm",
-    )(same_group, tiles)
+    )(*operands)
 
 
 def write_columns(values, columns_ref, at):
@@ -322,11 +328,16 @@
     over_planes = gather_partners(first, "fsdp", 1, plane_bits)
     near_bits = plane_bits // 2
     far_time = gather_partners(time_master, "fsdp", 1 + near_bits, plane_bits - near_bits, most=1)
-    over_planes, far_time, tiles_then = lax.optimization_barrier((over_planes, far_time, tiles))
+    steps = number // tiles_per_step(number)
+    head = steps // 3
+    tiles_then, first = lax.optimization_barrier((tiles, first))
+    normed = group_norm(tiles_then, 0, head) if head else None
+    over_planes, normed, tiles_then = lax.optimization_barrier((over_planes, normed, tiles))
+    far_time, tiles_then = lax.optimization_barrier((far_time, tiles_then))
     far = gather_partners(over_planes[1:], "dp", 0, part_bits)
     own_time = gather_partners(far_time, "fsdp", 1, near_bits, most=1)
     own_time = own_time.swapaxes(0, 1).reshape((-1,) + time_master.shape)
-    normed = group_norm(tiles_then)
+    normed = group_norm(tiles_then, head, steps, normed)
     own = jnp.concatenate([jnp.stack(mine)[:, None], far], axis=1)
     own, own_time, normed, times = lax.optimization_barrier((own, own_time, normed, timesteps[0]))
     features = time_features(jnp.pad(times, (0, LANES - number)), time_rows * shards)

time: 95.7 us -> 91.3 us (0.954)
  starting transfers between devices: 42.4 us -> 37.6 us
  Pallas kernels: 26.3 us -> 28.4 us
  waiting for transfers between devices: 19.2 us -> 17.5 us
    ppermute x27, starting transfers between devices: 42.4 us -> 37.6 us  [swap(): return lax.ppermute(values, axis, pairs)]
    pallas_call x1 -> x2, Pallas kernels: 7.73 us -> 9.87 us  [group_norm(): pl.pallas_call(functools.partial(norm_kernel, group_width), grid=(last -...]
    ppermute x27, waiting for transfers between devices: 19.2 us -> 17.5 us  [swap(): return lax.ppermute(values, axis, pairs)]
  transfers between devices with their start and end apart: 27 -> 27, of which waited for: 11 -> 9; matrix products, arithmetic and copies ran while one was open for 4% -> 5% of each run, Pallas kernels for 8% -> 11%
where the time goes in v8:
time: 91.3 us; the launch traced here: 91 us
  starting transfers between devices  37.6 us (41%)
  Pallas kernels  28.4 us (31%)
  waiting for transfers between devices  17.5 us (19%)
  other arithmetic  6.34 us (7%)
    ppermute x27, starting transfers between devices, swap(): return lax.ppermute(values, axis, pairs)  37.6 us
    pallas_call x1, Pallas kernels, conv_both(): pl.pallas_call(functools.partial(conv_kernel, steps), grid_spec=pltpu.Pre...  18.5 us
    ppermute x27, waiting for transfers between devices, swap(): return lax.ppermute(values, axis, pairs)  17.5 us
    pallas_call x2, Pallas kernels, group_norm(): pl.pallas_call(functools.partial(norm_kernel, group_width), grid=(last -...  9.87 us
  transfers between devices with their start and end apart: 27, of which 9 were waited for; matrix products, arithmetic and copies ran while one was open for 5% of the time, Pallas kernels for 11%

profile of v8, /device:TPU:0, one launch (start us, length us, event | category | flops | bytes accessed | tf_op | source)
XLA Modules:
  0.0 91.0 jit_solution(1727855233528616476)
XLA Ops:
  0.6 1.1 %convert_element_type.135 = bf16[360,320]{0,1:T(8,128)(2,1)S(1)} convert(f32[360,320]{0,1:T(8,128)} %param.12) | non-fusion elementwise | flops 115200 | bytes 691200 | tf_op jit(solution)/shard_map/convert_element_type | solution.py:324
  1.8 5.1 %collective-permute-start.2 = (bf16[1,80,360]{2,1,0:T(8,128)(2,1)S(1)}, bf16[1,80,360]{2,1,0:T(8,128)(2,1)S(1)}, u32[]{:S(2)}, u32[]{:S(2)}) collective-permute-start(bf16[1,80,360]{2,1,0:T(8,128)(2,1)S(1)} %get-tuple-element.59), channel_id=1, source_target_pairs={{0,24},{4,28},{8,16},{12,20},{16,8},{20,12},{24,0},{28,4},{1,25},{... | collective-permute-start | bytes 172808 | tf_op jit(solution)/shard_map/ppermute | solution.py:259
  6.9 0.6 collective-permute-start
  7.5 1.0 %convert_bitcast_fusion.2 = (bf16[1,1,160,320]{3,2,1,0:T(8,128)(2,1)S(1)}, bf16[1,160,320]{2,1,0:T(8,128)(2,1)S(1)}) fusion(f32[160,320]{1,0:T(8,128)} %param.13), kind=kLoop, calls=%fused_computation.45 | loop fusion | flops 51200 | bytes 409600 | tf_op jit(solution)/shard_map/stack;broadcast_in_dim | solution.py:275
  8.5 2.4 %collective-permute-start.6 = (bf16[1,160,320]{2,1,0:T(8,128)(2,1)S(1)}, bf16[1,160,320]{2,1,0:T(8,128)(2,1)S(1)}, u32[]{:S(2)}, u32[]{:S(2)}) collective-permute-start(bf16[1,160,320]{2,1,0:T(8,128)(2,1)S(1)} %get-tuple-element.55), channel_id=1, source_target_pairs={{0,16},{4,20},{8,24},{12,28},{16,0},{20,4},{24,8},{28,12},{1,17},{... | collective-permute-start | bytes 307208 | tf_op jit(solution)/shard_map/ppermute | solution.py:259
  10.9 4.0 %group_norm.2.refs_0_ = bf16[15,320,256]{2,1,0:T(8,128)(2,1)} custom-call(bf16[320,320]{1,0:T(8,128)(2,1)} %constant.45.clone.same_ref, bf16[15,320,256]{2,1,0:T(8,128)(2,1)} %bitcast.100), custom_call_target="tpu_custom_call" | custom-call | flops 8192000 | bytes 1638400 | tf_op jit(solution)/shard_map/group_norm/pallas_call | solution.py:62
  15.0 2.5 %collective-permute-start.5 = (bf16[1,3,80,360]{3,2,1,0:T(8,128)(2,1)S(1)}, bf16[1,3,80,360]{3,2,1,0:T(8,128)(2,1)S(1)}, u32[]{:S(2)}, u32[]{:S(2)}) collective-permute-start(bf16[1,3,80,360]{3,2,1,0:T(8,128)(2,1)S(1)} %get-tuple-element.61), channel_id=1, source_target_pairs={{0,3},{1,2},{2,1},{3,0},{4,7},{5,6},{6,5},{7,4},{8,11},{9,10},{10,... | collective-permute-start | bytes 518408 | tf_op jit(solution)/shard_map/ppermute | solution.py:259
  17.5 0.5 collective-permute-start.4
  18.0 0.5 collective-permute-start.3
  18.7 2.1 %collective-permute-start.7 = (bf16[1,2,160,320]{3,2,1,0:T(8,128)(2,1)S(1)}, bf16[1,2,160,320]{3,2,1,0:T(8,128)(2,1)S(1)}, u32[]{:S(2)}, u32[]{:S(2)}) collective-permute-start(bf16[1,2,160,320]{3,2,1,0:T(8,128)(2,1)S(1)} %bitcast.108), channel_id=1, source_target_pairs={{0,8},{4,12},{8,0},{12,4},{16,24},{20,28},{24,16},{28,20},{1,9},{5... | collective-permute-start | bytes 614408 | tf_op jit(solution)/shard_map/ppermute | solution.py:259
  20.8 5.8 %group_norm.3.normed_ref = bf16[15,320,256]{2,1,0:T(8,128)(2,1)} custom-call(bf16[320,320]{1,0:T(8,128)(2,1)} %constant.45.clone.same_ref, bf16[15,320,256]{2,1,0:T(8,128)(2,1)} %bitcast.101, bf16[15,320,256]{2,1,0:T(8,128)(2,1)} %group_norm.2.refs_0_), custom_call_target="tpu_custom_call", output_to_operand_aliasing={{}: (2, {})} | custom-call | flops 16384000 | bytes 3276800 | tf_op jit(solution)/shard_map/group_norm/pallas_call | solution.py:62
  26.6 0.2 maximum_bitcast_fusion
  26.9 0.2 pad_maximum_fusion.own_ref
  27.1 0.1 maximum_bitcast_fusion.1
  27.3 0.5 collective-permute-start.9
  27.8 1.2 %multiply_cosine_fusion = (f32[640,128]{1,0:T(8,128)S(1)}, f32[640,128]{1,0:T(8,128)S(1)}) fusion(f32[128]{0:T(128)S(1)} %pad_convert_fusion, f32[640]{0:T(1024)S(1)} %multiply_exponential_fusion), kind=kLoop, calls=%fused_computation.12 | loop fusion | flops 81920 | bytes 658432 | tf_op jit(solution)/shard_map/cos | solution.py:308
  29.0 0.2 multiply_convert_fusion.features_ref
  29.2 1.3 %collective-permute-done.9.other_time_ref = bf16[4,160,320]{2,1,0:T(8,128)(2,1)S(1)} collective-permute-done((bf16[4,160,320]{2,1,0:T(8,128)(2,1)S(1)}, bf16[4,160,320]{2,1,0:T(8,128)(2,1)S(1)}, u32[]{:S(2)}, u32[]{:S(2)}) %collective-permute-start.9) | collective-permute-done | bytes 409632 | tf_op jit(solution)/shard_map/ppermute | solution.py:259
  30.6 18.5 %conv_both.1 = (bf16[15,320,256]{2,1,0:T(8,128)(2,1)}, bf16[4,4,80,360]{3,2,1,0:T(8,128)(2,1)S(1)}, bf16[4,4,80,360]{3,2,1,0:T(8,128)(2,1)S(1)}, bf16[4,160,320]...) custom-call(s32[1,4]{1,0:T(1,128)S(1)} %copy-done.1, bf16[4,4,80,360]{3,2,1,0:T(8,128)(2,1)S(1)} %pad_maximum_fusion.own_ref, ...), custom_call_target="tpu_custom_call" | custom-call | flops 14155776000 | bytes 9830400 | tf_op jit(solution)/shard_map/conv_both/pallas_call | solution.py:223
  49.1 0.1 collective-permute-start.10
  49.2 0.4 collective-permute-start.11
  49.6 2.8 %collective-permute-done.11 = bf16[4,160,320]{2,1,0:T(8,128)(2,1)S(1)} collective-permute-done((bf16[4,160,320]{2,1,0:T(8,128)(2,1)S(1)}, bf16[4,160,320]{2,1,0:T(8,128)(2,1)S(1)}, u32[]{:S(2)}, u32[]{:S(2)}) %collective-permute-start.11) | collective-permute-done | bytes 409632 | tf_op jit(solution)/shard_map/ppermute | solution.py:259
  52.4 0.1 add_convert_fusion.1
  52.5 0.3 add_convert_fusion
  52.8 0.1 slice_bitcast_fusion.2
  52.9 7.8 %collective-permute-start.12 = (bf16[1,4,80,360]{3,2,1,0:T(8,128)(2,1)S(1)}, bf16[1,4,80,360]{3,2,1,0:T(8,128)(2,1)S(1)}, u32[]{:S(2)}, u32[]{:S(2)}) collective-permute-start(bf16[1,4,80,360]{3,2,1,0:T(8,128)(2,1)S(1)} %get-tuple-element.41), channel_id=1, source_target_pairs={{0,1},{1,0},{2,3},{3,2},{4,5},{5,4},{6,7},{7,6},{8,9},{9,8},{10,11... | collective-permute-start | bytes 691208 | tf_op jit(solution)/shard_map/ppermute | solution.py:259
  60.7 1.5 %collective-permute-start.13 = (bf16[1,4,80,360]{3,2,1,0:T(8,128)(2,1)S(1)}, bf16[1,4,80,360]{3,2,1,0:T(8,128)(2,1)S(1)}, u32[]{:S(2)}, u32[]{:S(2)}) collective-permute-start(bf16[1,4,80,360]{3,2,1,0:T(8,128)(2,1)S(1)} %get-tuple-element.43), channel_id=1, source_target_pairs={{0,2},{1,3},{2,0},{3,1},{4,6},{5,7},{6,4},{7,5},{8,10},{9,11},{10,... | collective-permute-start | bytes 691208 | tf_op jit(solution)/shard_map/ppermute | solution.py:259
  62.3 1.1 %collective-permute-start.21 = (bf16[1,160,320]{2,1,0:T(8,128)(2,1)S(1)}, bf16[1,160,320]{2,1,0:T(8,128)(2,1)S(1)}, u32[]{:S(2)}, u32[]{:S(2)}) collective-permute-start(bf16[1,160,320]{2,1,0:T(8,128)(2,1)S(1)} %get-tuple-element.44), channel_id=1, source_target_pairs={{0,8},{4,12},{8,0},{12,4},{16,24},{20,28},{24,16},{28,20},{1,9},{5... | collective-permute-start | bytes 307208 | tf_op jit(solution)/shard_map/ppermute | solution.py:259
  63.4 0.9 collective-permute-start.23
  64.3 3.1 %collective-permute-done.12 = bf16[1,4,80,360]{3,2,1,0:T(8,128)(2,1)S(1)} collective-permute-done((bf16[1,4,80,360]{3,2,1,0:T(8,128)(2,1)S(1)}, bf16[1,4,80,360]{3,2,1,0:T(8,128)(2,1)S(1)}, u32[]{:S(2)}, u32[]{:S(2)}) %collective-permute-start.12) | collective-permute-done | bytes 230432 | tf_op jit(solution)/shard_map/ppermute | solution.py:259
  67.4 0.6 collective-permute-start.22
  68.1 3.5 %collective-permute-done.14 = bf16[1,4,80,360]{3,2,1,0:T(8,128)(2,1)S(1)} collective-permute-done((bf16[1,4,80,360]{3,2,1,0:T(8,128)(2,1)S(1)}, bf16[1,4,80,360]{3,2,1,0:T(8,128)(2,1)S(1)}, u32[]{:S(2)}, u32[]{:S(2)}) %collective-permute-start.14) | collective-permute-done | bytes 230432 | tf_op jit(solution)/shard_map/ppermute | solution.py:259
  71.5 2.2 %collective-permute-done.13 = bf16[1,4,80,360]{3,2,1,0:T(8,128)(2,1)S(1)} collective-permute-done((bf16[1,4,80,360]{3,2,1,0:T(8,128)(2,1)S(1)}, bf16[1,4,80,360]{3,2,1,0:T(8,128)(2,1)S(1)}, u32[]{:S(2)}, u32[]{:S(2)}) %collective-permute-start.13) | collective-permute-done | bytes 230432 | tf_op jit(solution)/shard_map/ppermute | solution.py:259
  73.7 0.1 fusion.1
  73.9 1.1 %collective-permute-start.15 = (bf16[1,80,360]{2,1,0:T(8,128)(2,1)S(1)}, bf16[1,80,360]{2,1,0:T(8,128)(2,1)S(1)}, u32[]{:S(2)}, u32[]{:S(2)}) collective-permute-start(bf16[1,80,360]{2,1,0:T(8,128)(2,1)S(1)} %get-tuple-element.51), channel_id=1, source_target_pairs={{0,8},{4,12},{8,0},{12,4},{16,24},{20,28},{24,16},{28,20},{1,9},{5... | collective-permute-start | bytes 172808 | tf_op jit(solution)/shard_map/ppermute | solution.py:259
  75.0 1.7 %collective-permute-start.17 = (bf16[1,80,360]{2,1,0:T(8,128)(2,1)S(1)}, bf16[1,80,360]{2,1,0:T(8,128)(2,1)S(1)}, u32[]{:S(2)}, u32[]{:S(2)}) collective-permute-start(bf16[1,80,360]{2,1,0:T(8,128)(2,1)S(1)} %get-tuple-element.52), channel_id=1, source_target_pairs={{0,24},{4,28},{8,16},{12,20},{16,8},{20,12},{24,0},{28,4},{1,25},{... | collective-permute-start | bytes 172808 | tf_op jit(solution)/shard_map/ppermute | solution.py:259
  76.7 0.8 collective-permute-start.16
  77.5 2.7 %collective-permute-start.26 = (bf16[160,320]{1,0:T(8,128)(2,1)S(1)}, bf16[160,320]{1,0:T(8,128)(2,1)S(1)}, u32[]{:S(2)}, u32[]{:S(2)}) collective-permute-start(bf16[160,320]{1,0:T(8,128)(2,1)S(1)} %fusion.5), channel_id=1, source_target_pairs={{0,3},{1,2},{2,1},{3,0},{4,7},{5,6},{6,5},{7,4},{8,11},{9,10},{10,... | collective-permute-start | bytes 307208 | tf_op jit(solution)/shard_map/ppermute | solution.py:259
  80.3 0.8 collective-permute-start.24
  81.1 1.7 %collective-permute-done.16 = bf16[1,80,360]{2,1,0:T(8,128)(2,1)S(1)} collective-permute-done((bf16[1,80,360]{2,1,0:T(8,128)(2,1)S(1)}, bf16[1,80,360]{2,1,0:T(8,128)(2,1)S(1)}, u32[]{:S(2)}, u32[]{:S(2)}) %collective-permute-start.16) | collective-permute-done | bytes 57632 | tf_op jit(solution)/shard_map/ppermute | solution.py:259
  82.8 1.9 %collective-permute-start.20 = (bf16[1,80,360]{2,1,0:T(8,128)(2,1)S(1)}, bf16[1,80,360]{2,1,0:T(8,128)(2,1)S(1)}, u32[]{:S(2)}, u32[]{:S(2)}) collective-permute-start(bf16[1,80,360]{2,1,0:T(8,128)(2,1)S(1)} %fusion.7), channel_id=1, source_target_pairs={{0,3},{1,2},{2,1},{3,0},{4,7},{5,6},{6,5},{7,4},{8,11},{9,10},{10,... | collective-permute-start | bytes 172808 | tf_op jit(solution)/shard_map/ppermute | solution.py:259
  84.7 1.2 %collective-permute-start.19 = (bf16[1,80,360]{2,1,0:T(8,128)(2,1)S(1)}, bf16[1,80,360]{2,1,0:T(8,128)(2,1)S(1)}, u32[]{:S(2)}, u32[]{:S(2)}) collective-permute-start(bf16[1,80,360]{2,1,0:T(8,128)(2,1)S(1)} %fusion.7), channel_id=1, source_target_pairs={{0,2},{1,3},{2,0},{3,1},{4,6},{5,7},{6,4},{7,5},{8,10},{9,11},{10,... | collective-permute-start | bytes 172808 | tf_op jit(solution)/shard_map/ppermute | solution.py:259
  85.9 0.5 collective-permute-start.18
  86.4 0.8 fusion.4
  87.1 1.1 %collective-permute-done.20 = bf16[1,80,360]{2,1,0:T(8,128)(2,1)S(1)} collective-permute-done((bf16[1,80,360]{2,1,0:T(8,128)(2,1)S(1)}, bf16[1,80,360]{2,1,0:T(8,128)(2,1)S(1)}, u32[]{:S(2)}, u32[]{:S(2)}) %collective-permute-start.20) | collective-permute-done | bytes 57632 | tf_op jit(solution)/shard_map/ppermute | solution.py:259
  88.2 0.7 collective-permute-done.19
  88.9 1.2 %collective-permute-done.18 = bf16[1,80,360]{2,1,0:T(8,128)(2,1)S(1)} collective-permute-done((bf16[1,80,360]{2,1,0:T(8,128)(2,1)S(1)}, bf16[1,80,360]{2,1,0:T(8,128)(2,1)S(1)}, u32[]{:S(2)}, u32[]{:S(2)}) %collective-permute-start.18) | collective-permute-done | bytes 57632 | tf_op jit(solution)/shard_map/ppermute | solution.py:259
  90.2 0.8 convert_bitcast_fusion
  (42 shorter events, 0.8 us)
Async XLA Ops:
  1.8 13.1 %collective-permute-start.2 = (bf16[1,80,360]{2,1,0:T(8,128)(2,1)S(1)}, bf16[1,80,360]{2,1,0:T(8,128)(2,1)S(1)}, u32[]{:S(2)}, u32[]{:S(2)}) collective-permute-start(bf16[1,80,360]{2,1,0:T(8,128)(2,1)S(1)} %get-tuple-element.59), channel_id=1, source_target_pairs={{0,24},{4,28},{8,16},{12,20},{16,8},{20,12},{24,0},{28,4},{1,25},{... | collective-permute-start | bytes 172808 | tf_op jit(solution)/shard_map/ppermute | solution.py:259
  6.9 8.0 %collective-permute-start.1 = (bf16[1,80,360]{2,1,0:T(8,128)(2,1)S(1)}, bf16[1,80,360]{2,1,0:T(8,128)(2,1)S(1)}, u32[]{:S(2)}, u32[]{:S(2)}) collective-permute-start(bf16[1,80,360]{2,1,0:T(8,128)(2,1)S(1)} %get-tuple-element.59), channel_id=1, source_target_pairs={{0,16},{4,20},{8,24},{12,28},{16,0},{20,4},{24,8},{28,12},{1,17},{... | collective-permute-start | bytes 172808 | tf_op jit(solution)/shard_map/ppermute | solution.py:259
  6.9 8.0 %collective-permute-start = (bf16[1,80,360]{2,1,0:T(8,128)(2,1)S(1)}, bf16[1,80,360]{2,1,0:T(8,128)(2,1)S(1)}, u32[]{:S(2)}, u32[]{:S(2)}) collective-permute-start(bf16[1,80,360]{2,1,0:T(8,128)(2,1)S(1)} %get-tuple-element.59), channel_id=1, source_target_pairs={{0,8},{4,12},{8,0},{12,4},{16,24},{20,28},{24,16},{28,20},{1,9},{5... | collective-permute-start | bytes 172808 | tf_op jit(solution)/shard_map/ppermute | solution.py:259
  8.5 10.1 %collective-permute-start.6 = (bf16[1,160,320]{2,1,0:T(8,128)(2,1)S(1)}, bf16[1,160,320]{2,1,0:T(8,128)(2,1)S(1)}, u32[]{:S(2)}, u32[]{:S(2)}) collective-permute-start(bf16[1,160,320]{2,1,0:T(8,128)(2,1)S(1)} %get-tuple-element.55), channel_id=1, source_target_pairs={{0,16},{4,20},{8,24},{12,28},{16,0},{20,4},{24,8},{28,12},{1,17},{... | collective-permute-start | bytes 307208 | tf_op jit(solution)/shard_map/ppermute | solution.py:259
  15.0 11.6 %collective-permute-start.5 = (bf16[1,3,80,360]{3,2,1,0:T(8,128)(2,1)S(1)}, bf16[1,3,80,360]{3,2,1,0:T(8,128)(2,1)S(1)}, u32[]{:S(2)}, u32[]{:S(2)}) collective-permute-start(bf16[1,3,80,360]{3,2,1,0:T(8,128)(2,1)S(1)} %get-tuple-element.61), channel_id=1, source_target_pairs={{0,3},{1,2},{2,1},{3,0},{4,7},{5,6},{6,5},{7,4},{8,11},{9,10},{10,... | collective-permute-start | bytes 518408 | tf_op jit(solution)/shard_map/ppermute | solution.py:259
  17.5 9.1 %collective-permute-start.4 = (bf16[1,3,80,360]{3,2,1,0:T(8,128)(2,1)S(1)}, bf16[1,3,80,360]{3,2,1,0:T(8,128)(2,1)S(1)}, u32[]{:S(2)}, u32[]{:S(2)}) collective-permute-start(bf16[1,3,80,360]{3,2,1,0:T(8,128)(2,1)S(1)} %get-tuple-element.61), channel_id=1, source_target_pairs={{0,2},{1,3},{2,0},{3,1},{4,6},{5,7},{6,4},{7,5},{8,10},{9,11},{10,... | collective-permute-start | bytes 518408 | tf_op jit(solution)/shard_map/ppermute | solution.py:259
  18.0 8.6 %collective-permute-start.3 = (bf16[1,3,80,360]{3,2,1,0:T(8,128)(2,1)S(1)}, bf16[1,3,80,360]{3,2,1,0:T(8,128)(2,1)S(1)}, u32[]{:S(2)}, u32[]{:S(2)}) collective-permute-start(bf16[1,3,80,360]{3,2,1,0:T(8,128)(2,1)S(1)} %get-tuple-element.61), channel_id=1, source_target_pairs={{0,1},{1,0},{2,3},{3,2},{4,5},{5,4},{6,7},{7,6},{8,9},{9,8},{10,11... | collective-permute-start | bytes 518408 | tf_op jit(solution)/shard_map/ppermute | solution.py:259
  18.7 8.3 %collective-permute-start.7 = (bf16[1,2,160,320]{3,2,1,0:T(8,128)(2,1)S(1)}, bf16[1,2,160,320]{3,2,1,0:T(8,128)(2,1)S(1)}, u32[]{:S(2)}, u32[]{:S(2)}) collective-permute-start(bf16[1,2,160,320]{3,2,1,0:T(8,128)(2,1)S(1)} %bitcast.108), channel_id=1, source_target_pairs={{0,8},{4,12},{8,0},{12,4},{16,24},{20,28},{24,16},{28,20},{1,9},{5... | collective-permute-start | bytes 614408 | tf_op jit(solution)/shard_map/ppermute | solution.py:259
  26.6 1.2 %copy-start.2 = (s32[1,15]{1,0:T(1,128)S(1)}, s32[1,15]{1,0:T(1,128)}, u32[]{:S(2)}) copy-start(s32[1,15]{1,0:T(1,128)} %param.11) | copy-start | bytes 184
  26.8 3.7 %copy-start = (bf16[15,320,256]{2,1,0:T(8,128)(2,1)S(1)}, bf16[15,320,256]{2,1,0:T(8,128)(2,1)}, u32[]{:S(2)}) copy-start(bf16[15,320,256]{2,1,0:T(8,128)(2,1)} %group_norm.3.normed_ref) | copy-start | bytes 7372804
  26.8 3.7 %copy-start.1 = (s32[1,4]{1,0:T(1,128)S(1)}, s32[1,4]{1,0:T(1,128)}, u32[]{:S(2)}) copy-start(s32[1,4]{1,0:T(1,128)} %counts_ref.1) | copy-start | bytes 52
  27.2 3.3 %collective-permute-start.8 = (bf16[4,4,80,360]{3,2,1,0:T(8,128)(2,1)S(1)}, bf16[4,4,80,360]{3,2,1,0:T(8,128)(2,1)S(1)}, u32[]{:S(2)}, u32[]{:S(2)}) collective-permute-start(bf16[4,4,80,360]{3,2,1,0:T(8,128)(2,1)S(1)} %pad_maximum_fusion.own_ref), channel_id=1, source_target_pairs={{0,4},{4,0},{8,12},{12,8},{16,20},{20,16},{24,28},{28,24},{1,5},{5... | collective-permute-start | bytes 2764808 | tf_op jit(solution)/shard_map/ppermute | solution.py:259
  27.3 3.2 %collective-permute-start.9 = (bf16[4,160,320]{2,1,0:T(8,128)(2,1)S(1)}, bf16[4,160,320]{2,1,0:T(8,128)(2,1)S(1)}, u32[]{:S(2)}, u32[]{:S(2)}) collective-permute-start(bf16[4,160,320]{2,1,0:T(8,128)(2,1)S(1)} %bitcast.98), channel_id=1, source_target_pairs={{0,4},{4,0},{8,12},{12,8},{16,20},{20,16},{24,28},{28,24},{1,5},{5... | collective-permute-start | bytes 1228808 | tf_op jit(solution)/shard_map/ppermute | solution.py:259
  49.1 3.4 %collective-permute-start.10 = (bf16[4,4,80,360]{3,2,1,0:T(8,128)(2,1)S(1)}, bf16[4,4,80,360]{3,2,1,0:T(8,128)(2,1)S(1)}, u32[]{:S(2)}, u32[]{:S(2)}) collective-permute-start(bf16[4,4,80,360]{3,2,1,0:T(8,128)(2,1)S(1)} %get-tuple-element.36), channel_id=1, source_target_pairs={{0,4},{4,0},{8,12},{12,8},{16,20},{20,16},{24,28},{28,24},{1,5},{5... | collective-permute-start | bytes 2764808 | tf_op jit(solution)/shard_map/ppermute | solution.py:259
  49.2 3.1 %collective-permute-start.11 = (bf16[4,160,320]{2,1,0:T(8,128)(2,1)S(1)}, bf16[4,160,320]{2,1,0:T(8,128)(2,1)S(1)}, u32[]{:S(2)}, u32[]{:S(2)}) collective-permute-start(bf16[4,160,320]{2,1,0:T(8,128)(2,1)S(1)} %get-tuple-element.38), channel_id=1, source_target_pairs={{0,4},{4,0},{8,12},{12,8},{16,20},{20,16},{24,28},{28,24},{1,5},{5... | collective-permute-start | bytes 1228808 | tf_op jit(solution)/shard_map/ppermute | solution.py:259
  52.9 14.6 %collective-permute-start.12 = (bf16[1,4,80,360]{3,2,1,0:T(8,128)(2,1)S(1)}, bf16[1,4,80,360]{3,2,1,0:T(8,128)(2,1)S(1)}, u32[]{:S(2)}, u32[]{:S(2)}) collective-permute-start(bf16[1,4,80,360]{3,2,1,0:T(8,128)(2,1)S(1)} %get-tuple-element.41), channel_id=1, source_target_pairs={{0,1},{1,0},{2,3},{3,2},{4,5},{5,4},{6,7},{7,6},{8,9},{9,8},{10,11... | collective-permute-start | bytes 691208 | tf_op jit(solution)/shard_map/ppermute | solution.py:259
  60.7 10.8 %collective-permute-start.14 = (bf16[1,4,80,360]{3,2,1,0:T(8,128)(2,1)S(1)}, bf16[1,4,80,360]{3,2,1,0:T(8,128)(2,1)S(1)}, u32[]{:S(2)}, u32[]{:S(2)}) collective-permute-start(bf16[1,4,80,360]{3,2,1,0:T(8,128)(2,1)S(1)} %get-tuple-element.42), channel_id=1, source_target_pairs={{0,3},{1,2},{2,1},{3,0},{4,7},{5,6},{6,5},{7,4},{8,11},{9,10},{10,... | collective-permute-start | bytes 691208 | tf_op jit(solution)/shard_map/ppermute | solution.py:259
  60.7 13.0 %collective-permute-start.13 = (bf16[1,4,80,360]{3,2,1,0:T(8,128)(2,1)S(1)}, bf16[1,4,80,360]{3,2,1,0:T(8,128)(2,1)S(1)}, u32[]{:S(2)}, u32[]{:S(2)}) collective-permute-start(bf16[1,4,80,360]{3,2,1,0:T(8,128)(2,1)S(1)} %get-tuple-element.43), channel_id=1, source_target_pairs={{0,2},{1,3},{2,0},{3,1},{4,6},{5,7},{6,4},{7,5},{8,10},{9,11},{10,... | collective-permute-start | bytes 691208 | tf_op jit(solution)/shard_map/ppermute | solution.py:259
  62.3 14.4 %collective-permute-start.21 = (bf16[1,160,320]{2,1,0:T(8,128)(2,1)S(1)}, bf16[1,160,320]{2,1,0:T(8,128)(2,1)S(1)}, u32[]{:S(2)}, u32[]{:S(2)}) collective-permute-start(bf16[1,160,320]{2,1,0:T(8,128)(2,1)S(1)} %get-tuple-element.44), channel_id=1, source_target_pairs={{0,8},{4,12},{8,0},{12,4},{16,24},{20,28},{24,16},{28,20},{1,9},{5... | collective-permute-start | bytes 307208 | tf_op jit(solution)/shard_map/ppermute | solution.py:259
  63.4 14.0 %collective-permute-start.23 = (bf16[1,160,320]{2,1,0:T(8,128)(2,1)S(1)}, bf16[1,160,320]{2,1,0:T(8,128)(2,1)S(1)}, u32[]{:S(2)}, u32[]{:S(2)}) collective-permute-start(bf16[1,160,320]{2,1,0:T(8,128)(2,1)S(1)} %get-tuple-element.45), channel_id=1, source_target_pairs={{0,24},{4,28},{8,16},{12,20},{16,8},{20,12},{24,0},{28,4},{1,25},{... | collective-permute-start | bytes 307208 | tf_op jit(solution)/shard_map/ppermute | solution.py:259
  67.4 10.0 %collective-permute-start.22 = (bf16[1,160,320]{2,1,0:T(8,128)(2,1)S(1)}, bf16[1,160,320]{2,1,0:T(8,128)(2,1)S(1)}, u32[]{:S(2)}, u32[]{:S(2)}) collective-permute-start(bf16[1,160,320]{2,1,0:T(8,128)(2,1)S(1)} %get-tuple-element.46), channel_id=1, source_target_pairs={{0,16},{4,20},{8,24},{12,28},{16,0},{20,4},{24,8},{28,12},{1,17},{... | collective-permute-start | bytes 307208 | tf_op jit(solution)/shard_map/ppermute | solution.py:259
  73.9 6.4 %collective-permute-start.15 = (bf16[1,80,360]{2,1,0:T(8,128)(2,1)S(1)}, bf16[1,80,360]{2,1,0:T(8,128)(2,1)S(1)}, u32[]{:S(2)}, u32[]{:S(2)}) collective-permute-start(bf16[1,80,360]{2,1,0:T(8,128)(2,1)S(1)} %get-tuple-element.51), channel_id=1, source_target_pairs={{0,8},{4,12},{8,0},{12,4},{16,24},{20,28},{24,16},{28,20},{1,9},{5... | collective-permute-start | bytes 172808 | tf_op jit(solution)/shard_map/ppermute | solution.py:259
  75.0 6.1 %collective-permute-start.17 = (bf16[1,80,360]{2,1,0:T(8,128)(2,1)S(1)}, bf16[1,80,360]{2,1,0:T(8,128)(2,1)S(1)}, u32[]{:S(2)}, u32[]{:S(2)}) collective-permute-start(bf16[1,80,360]{2,1,0:T(8,128)(2,1)S(1)} %get-tuple-element.52), channel_id=1, source_target_pairs={{0,24},{4,28},{8,16},{12,20},{16,8},{20,12},{24,0},{28,4},{1,25},{... | collective-permute-start | bytes 172808 | tf_op jit(solution)/shard_map/ppermute | solution.py:259
  76.7 6.1 %collective-permute-start.16 = (bf16[1,80,360]{2,1,0:T(8,128)(2,1)S(1)}, bf16[1,80,360]{2,1,0:T(8,128)(2,1)S(1)}, u32[]{:S(2)}, u32[]{:S(2)}) collective-permute-start(bf16[1,80,360]{2,1,0:T(8,128)(2,1)S(1)} %get-tuple-element.53), channel_id=1, source_target_pairs={{0,16},{4,20},{8,24},{12,28},{16,0},{20,4},{24,8},{28,12},{1,17},{... | collective-permute-start | bytes 172808 | tf_op jit(solution)/shard_map/ppermute | solution.py:259
  77.5 8.4 %collective-permute-start.26 = (bf16[160,320]{1,0:T(8,128)(2,1)S(1)}, bf16[160,320]{1,0:T(8,128)(2,1)S(1)}, u32[]{:S(2)}, u32[]{:S(2)}) collective-permute-start(bf16[160,320]{1,0:T(8,128)(2,1)S(1)} %fusion.5), channel_id=1, source_target_pairs={{0,3},{1,2},{2,1},{3,0},{4,7},{5,6},{6,5},{7,4},{8,11},{9,10},{10,... | collective-permute-start | bytes 307208 | tf_op jit(solution)/shard_map/ppermute | solution.py:259
  80.2 6.2 %collective-permute-start.25 = (bf16[160,320]{1,0:T(8,128)(2,1)S(1)}, bf16[160,320]{1,0:T(8,128)(2,1)S(1)}, u32[]{:S(2)}, u32[]{:S(2)}) collective-permute-start(bf16[160,320]{1,0:T(8,128)(2,1)S(1)} %fusion.5), channel_id=1, source_target_pairs={{0,2},{1,3},{2,0},{3,1},{4,6},{5,7},{6,4},{7,5},{8,10},{9,11},{10,... | collective-permute-start | bytes 307208 | tf_op jit(solution)/shard_map/ppermute | solution.py:259
  80.3 6.1 %collective-permute-start.24 = (bf16[160,320]{1,0:T(8,128)(2,1)S(1)}, bf16[160,320]{1,0:T(8,128)(2,1)S(1)}, u32[]{:S(2)}, u32[]{:S(2)}) collective-permute-start(bf16[160,320]{1,0:T(8,128)(2,1)S(1)} %fusion.5), channel_id=1, source_target_pairs={{0,1},{1,0},{2,3},{3,2},{4,5},{5,4},{6,7},{7,6},{8,9},{9,8},{10,11... | collective-permute-start | bytes 307208 | tf_op jit(solution)/shard_map/ppermute | solution.py:259
  82.8 5.4 %collective-permute-start.20 = (bf16[1,80,360]{2,1,0:T(8,128)(2,1)S(1)}, bf16[1,80,360]{2,1,0:T(8,128)(2,1)S(1)}, u32[]{:S(2)}, u32[]{:S(2)}) collective-permute-start(bf16[1,80,360]{2,1,0:T(8,128)(2,1)S(1)} %fusion.7), channel_id=1, source_target_pairs={{0,3},{1,2},{2,1},{3,0},{4,7},{5,6},{6,5},{7,4},{8,11},{9,10},{10,... | collective-permute-start | bytes 172808 | tf_op jit(solution)/shard_map/ppermute | solution.py:259
  84.7 4.2 %collective-permute-start.19 = (bf16[1,80,360]{2,1,0:T(8,128)(2,1)S(1)}, bf16[1,80,360]{2,1,0:T(8,128)(2,1)S(1)}, u32[]{:S(2)}, u32[]{:S(2)}) collective-permute-start(bf16[1,80,360]{2,1,0:T(8,128)(2,1)S(1)} %fusion.7), channel_id=1, source_target_pairs={{0,2},{1,3},{2,0},{3,1},{4,6},{5,7},{6,4},{7,5},{8,10},{9,11},{10,... | collective-permute-start | bytes 172808 | tf_op jit(solution)/shard_map/ppermute | solution.py:259
  85.9 4.2 %collective-permute-start.18 = (bf16[1,80,360]{2,1,0:T(8,128)(2,1)S(1)}, bf16[1,80,360]{2,1,0:T(8,128)(2,1)S(1)}, u32[]{:S(2)}, u32[]{:S(2)}) collective-permute-start(bf16[1,80,360]{2,1,0:T(8,128)(2,1)S(1)} %fusion.7), channel_id=1, source_target_pairs={{0,1},{1,0},{2,3},{3,2},{4,5},{5,4},{6,7},{7,6},{8,9},{9,8},{10,11... | collective-permute-start | bytes 172808 | tf_op jit(solution)/shard_map/ppermute | solution.py:259

commit v9 on v8

--- a/solution.py
+++ b/solution.py
@@ -316,32 +316,45 @@
     shard_bits, peer_bits = bits_of("fsdp"), bits_of("dp")
     rows, outs = conv_master.shape
     time_rows = temb_master.shape[0]
-    part_bits = max(n for n in range(peer_bits + 1) if outs % (16 << n) == 0)
+    part_bits = max(n for n in range(min(peer_bits, 2) + 1) if outs % (16 << n) == 0)
     parts = 1 << part_bits
     part = lax.axis_index("dp") & (parts - 1)
     plane_bits = shard_bits - 1
 
-    master = conv_master.T.astype(bf16).reshape(parts, outs // parts, rows)
-    mine = [lax.dynamic_index_in_dim(master, part ^ m, 0, keepdims=False) for m in range(parts)]
-    time_master, first = lax.optimization_barrier((temb_master, mine[0]))
-    time_master = time_master.astype(bf16)
+    part_rows = outs // parts
+    first = lax.dynamic_slice(conv_master.T, (part * part_rows, 0), (part_rows, rows))
+    first, conv_master, temb_master, tiles_then = lax.optimization_barrier(
+        (first.astype(bf16), conv_master, temb_master, tiles)
+    )
     over_planes = gather_partners(first, "fsdp", 1, plane_bits)
+    time_master = temb_master.astype(bf16)
     near_bits = plane_bits // 2
     far_time = gather_partners(time_master, "fsdp", 1 + near_bits, plane_bits - near_bits, most=1)
+    master = conv_master.T.astype(bf16).reshape(parts, part_rows, rows)
+    mine = [lax.dynamic_index_in_dim(master, part ^ m, 0, keepdims=False) for m in range(parts)]
+    mine = jnp.stack(mine)[:, None]
     steps = number // tiles_per_step(number)
     head = steps // 3
-    tiles_then, first = lax.optimization_barrier((tiles, first))
     normed = group_norm(tiles_then, 0, head) if head else None
-    over_planes, normed, tiles_then = lax.optimization_barrier((over_planes, normed, tiles))
+    over_planes, mine, normed, tiles_then = lax.optimization_barrier(
+        (over_planes, mine, normed, tiles_then)
+    )
+    far = [over_planes[None, 1:]]
+    far += [swap(far[0], "dp", m) for m in range(1, parts)]
     far_time, tiles_then = lax.optimization_barrier((far_time, tiles_then))
-    far = gather_partners(over_planes[1:], "dp", 0, part_bits)
     own_time = gather_partners(far_time, "fsdp", 1, near_bits, most=1)
     own_time = own_time.swapaxes(0, 1).reshape((-1,) + time_master.shape)
     normed = group_norm(tiles_then, head, steps, normed)
-    own = jnp.concatenate([jnp.stack(mine)[:, None], far], axis=1)
-    own, own_time, normed, times = lax.optimization_barrier((own, own_time, normed, timesteps[0]))
+    near = jnp.concatenate([mine[:, 0], over_planes[1:]])
+    normed, near = lax.optimization_barrier((normed, near))
+    other_near = swap(near, "fsdp", 1)
+    own_time, times = lax.optimization_barrier((own_time, timesteps[0]))
+    other_far = [other_near[None, parts:]] + [swap(block, "fsdp", 1) for block in far[1:]]
+    other_mine = other_near[:parts, None]
     features = time_features(jnp.pad(times, (0, LANES - number)), time_rows * shards)
-    other, other_time = swap(own, "fsdp", 1), swap(own_time, "fsdp", 1)
+    own = jnp.concatenate([mine, jnp.concatenate(far)], axis=1)
+    other = jnp.concatenate([other_mine, jnp.concatenate(other_far)], axis=1)
+    other_time = swap(own_time, "fsdp", 1)
 
     predicted, keep, send, keep_time, send_time = conv_both(
         counts, own, other, own_time, other_time, features, normed, tiles, targets

time: 91.3 us -> 91.8 us (level)
  waiting for transfers between devices: 17.5 us -> 13.5 us
  starting transfers between devices: 37.6 us -> 41.1 us
  local copies, waits for them, and re-layouts: 0.32 us -> 1.28 us
    ppermute x27 -> x30, waiting for transfers between devices: 17.5 us -> 13.5 us  [swap(): return lax.ppermute(values, axis, pairs)]
    ppermute x27 -> x30, starting transfers between devices: 37.6 us -> 41.1 us  [swap(): return lax.ppermute(values, axis, pairs)]
  transfers between devices with their start and end apart: 27 -> 30, of which waited for: 9 -> 7; matrix products, arithmetic and copies ran while one was open for 5% -> 6% of each run, Pallas kernels for 11% -> 11%
where the time goes in v9:
time: 91.8 us; the launch traced here: 91.9 us
  starting transfers between devices  41.1 us (45%)
  Pallas kernels  28.4 us (31%)
  waiting for transfers between devices  13.5 us (15%)
  other arithmetic  6.57 us (7%)
  local copies, waits for them, and re-layouts  1.28 us (1%)
  between operations  0.93 us (1%)
    ppermute x30, starting transfers between devices, swap(): return lax.ppermute(values, axis, pairs)  41.1 us
    pallas_call x1, Pallas kernels, conv_both(): pl.pallas_call(functools.partial(conv_kernel, steps), grid_spec=pltpu.Pre...  18.5 us
    ppermute x30, waiting for transfers between devices, swap(): return lax.ppermute(values, axis, pairs)  13.5 us
    pallas_call x2, Pallas kernels, group_norm(): pl.pallas_call(functools.partial(norm_kernel, group_width), grid=(last -...  9.89 us
  transfers between devices with their start and end apart: 30, of which 7 were waited for; matrix products, arithmetic and copies ran while one was open for 6% of the time, Pallas kernels for 11%

profile of v9, /device:TPU:0, one launch (start us, length us, event | category | flops | bytes accessed | tf_op | source)
XLA Modules:
  0.0 91.9 jit_solution(6448320761875969761)
XLA Ops:
  0.6 0.9 fusion.8
  1.6 5.1 %collective-permute-start.2 = (bf16[1,80,360]{2,1,0:T(8,128)(2,1)S(1)}, bf16[1,80,360]{2,1,0:T(8,128)(2,1)S(1)}, u32[]{:S(2)}, u32[]{:S(2)}) collective-permute-start(bf16[1,80,360]{2,1,0:T(8,128)(2,1)S(1)} %bitcast.113), channel_id=1, source_target_pairs={{0,24},{4,28},{8,16},{12,20},{16,8},{20,12},{24,0},{28,4},{1,25},{... | collective-permute-start | bytes 172808 | tf_op jit(solution)/shard_map/ppermute | solution.py:259
  6.7 0.6 collective-permute-start
  7.3 1.0 %convert_bitcast_fusion.2 = (bf16[1,1,160,320]{3,2,1,0:T(8,128)(2,1)S(1)}, bf16[1,160,320]{2,1,0:T(8,128)(2,1)S(1)}) fusion(f32[160,320]{1,0:T(8,128)} %param.13), kind=kLoop, calls=%fused_computation.48 | loop fusion | flops 51200 | bytes 409600 | tf_op jit(solution)/shard_map/stack;broadcast_in_dim | solution.py:275
  8.3 2.4 %collective-permute-start.6 = (bf16[1,160,320]{2,1,0:T(8,128)(2,1)S(1)}, bf16[1,160,320]{2,1,0:T(8,128)(2,1)S(1)}, u32[]{:S(2)}, u32[]{:S(2)}) collective-permute-start(bf16[1,160,320]{2,1,0:T(8,128)(2,1)S(1)} %get-tuple-element.61), channel_id=1, source_target_pairs={{0,16},{4,20},{8,24},{12,28},{16,0},{20,4},{24,8},{28,12},{1,17},{... | collective-permute-start | bytes 307208 | tf_op jit(solution)/shard_map/ppermute | solution.py:259
  10.6 1.1 %convert_element_type.143 = bf16[360,320]{0,1:T(8,128)(2,1)S(1)} convert(f32[360,320]{0,1:T(8,128)} %param.12) | non-fusion elementwise | flops 115200 | bytes 691200 | tf_op jit(solution)/shard_map/convert_element_type | solution.py:333
  11.7 4.0 %group_norm.2.refs_0_ = bf16[15,320,256]{2,1,0:T(8,128)(2,1)} custom-call(bf16[320,320]{1,0:T(8,128)(2,1)} %constant.49.clone.same_ref, bf16[15,320,256]{2,1,0:T(8,128)(2,1)} %bitcast.101), custom_call_target="tpu_custom_call" | custom-call | flops 8192000 | bytes 1638400 | tf_op jit(solution)/shard_map/group_norm/pallas_call | solution.py:62
  16.0 2.5 %collective-permute-start.5 = (bf16[1,3,80,360]{3,2,1,0:T(8,128)(2,1)S(1)}, bf16[1,3,80,360]{3,2,1,0:T(8,128)(2,1)S(1)}, u32[]{:S(2)}, u32[]{:S(2)}) collective-permute-start(bf16[1,3,80,360]{3,2,1,0:T(8,128)(2,1)S(1)} %get-tuple-element.59), channel_id=1, source_target_pairs={{0,3},{1,2},{2,1},{3,0},{4,7},{5,6},{6,5},{7,4},{8,11},{9,10},{10,... | collective-permute-start | bytes 518408 | tf_op jit(solution)/shard_map/ppermute | solution.py:259
  18.5 0.5 collective-permute-start.4
  19.0 0.5 collective-permute-start.3
  19.6 2.1 %collective-permute-start.11 = (bf16[1,2,160,320]{3,2,1,0:T(8,128)(2,1)S(1)}, bf16[1,2,160,320]{3,2,1,0:T(8,128)(2,1)S(1)}, u32[]{:S(2)}, u32[]{:S(2)}) collective-permute-start(bf16[1,2,160,320]{3,2,1,0:T(8,128)(2,1)S(1)} %bitcast.110), channel_id=1, source_target_pairs={{0,8},{4,12},{8,0},{12,4},{16,24},{20,28},{24,16},{28,20},{1,9},{5... | collective-permute-start | bytes 614408 | tf_op jit(solution)/shard_map/ppermute | solution.py:259
  21.7 0.1 pad_maximum_fusion.1
  21.8 5.8 %group_norm.3.normed_ref = bf16[15,320,256]{2,1,0:T(8,128)(2,1)} custom-call(bf16[320,320]{1,0:T(8,128)(2,1)} %constant.49.clone.same_ref, bf16[15,320,256]{2,1,0:T(8,128)(2,1)} %bitcast.102, bf16[15,320,256]{2,1,0:T(8,128)(2,1)} %group_norm.2.refs_0_), custom_call_target="tpu_custom_call", output_to_operand_aliasing={{}: (2, {})} | custom-call | flops 16384000 | bytes 3276800 | tf_op jit(solution)/shard_map/group_norm/pallas_call | solution.py:62
  27.7 0.5 collective-permute-start.10
  28.2 0.4 collective-permute-start.8
  28.7 0.3 maximum_maximum_fusion.own_ref
  28.9 0.1 maximum_bitcast_fusion
  29.2 0.1 collective-permute-start.12
  29.3 1.2 %multiply_cosine_fusion = (f32[640,128]{1,0:T(8,128)S(1)}, f32[640,128]{1,0:T(8,128)S(1)}) fusion(f32[128]{0:T(128)S(1)} %pad_convert_fusion, f32[640]{0:T(1024)S(1)} %multiply_exponential_fusion), kind=kLoop, calls=%fused_computation.12 | loop fusion | flops 81920 | bytes 658432 | tf_op jit(solution)/shard_map/cos | solution.py:308
  30.5 0.2 multiply_convert_fusion.features_ref
  30.8 0.3 maximum_maximum_fusion.1.other_ref
  31.1 18.5 %conv_both.1 = (bf16[15,320,256]{2,1,0:T(8,128)(2,1)}, bf16[4,4,80,360]{3,2,1,0:T(8,128)(2,1)S(1)}, bf16[4,4,80,360]{3,2,1,0:T(8,128)(2,1)S(1)}, bf16[4,160,320]...) custom-call(s32[1,4]{1,0:T(1,128)S(1)} %copy-done.1, bf16[4,4,80,360]{3,2,1,0:T(8,128)(2,1)S(1)} %maximum_maximum_fusion.own_ref, ...), custom_call_target="tpu_custom_call" | custom-call | flops 14155776000 | bytes 9830400 | tf_op jit(solution)/shard_map/conv_both/pallas_call | solution.py:223
  49.6 0.4 collective-permute-start.13
  50.1 2.8 %collective-permute-done.14 = bf16[4,160,320]{2,1,0:T(8,128)(2,1)S(1)} collective-permute-done((bf16[4,160,320]{2,1,0:T(8,128)(2,1)S(1)}, bf16[4,160,320]{2,1,0:T(8,128)(2,1)S(1)}, u32[]{:S(2)}, u32[]{:S(2)}) %collective-permute-start.14) | collective-permute-done | bytes 409632 | tf_op jit(solution)/shard_map/ppermute | solution.py:259
  53.0 0.1 add_convert_fusion.1
  53.1 0.3 add_convert_fusion
  53.4 0.1 slice_bitcast_fusion.2
  53.5 9.3 %collective-permute-start.17 = (bf16[1,4,80,360]{3,2,1,0:T(8,128)(2,1)S(1)}, bf16[1,4,80,360]{3,2,1,0:T(8,128)(2,1)S(1)}, u32[]{:S(2)}, u32[]{:S(2)}) collective-permute-start(bf16[1,4,80,360]{3,2,1,0:T(8,128)(2,1)S(1)} %get-tuple-element.46), channel_id=1, source_target_pairs={{0,3},{1,2},{2,1},{3,0},{4,7},{5,6},{6,5},{7,4},{8,11},{9,10},{10,... | collective-permute-start | bytes 691208 | tf_op jit(solution)/shard_map/ppermute | solution.py:259
  62.9 0.6 collective-permute-start.24
  63.5 1.4 %collective-permute-start.26 = (bf16[1,160,320]{2,1,0:T(8,128)(2,1)S(1)}, bf16[1,160,320]{2,1,0:T(8,128)(2,1)S(1)}, u32[]{:S(2)}, u32[]{:S(2)}) collective-permute-start(bf16[1,160,320]{2,1,0:T(8,128)(2,1)S(1)} %get-tuple-element.49), channel_id=1, source_target_pairs={{0,24},{4,28},{8,16},{12,20},{16,8},{20,12},{24,0},{28,4},{1,25},{... | collective-permute-start | bytes 307208 | tf_op jit(solution)/shard_map/ppermute | solution.py:259
  64.8 3.7 %collective-permute-start.25 = (bf16[1,160,320]{2,1,0:T(8,128)(2,1)S(1)}, bf16[1,160,320]{2,1,0:T(8,128)(2,1)S(1)}, u32[]{:S(2)}, u32[]{:S(2)}) collective-permute-start(bf16[1,160,320]{2,1,0:T(8,128)(2,1)S(1)} %get-tuple-element.50), channel_id=1, source_target_pairs={{0,16},{4,20},{8,24},{12,28},{16,0},{20,4},{24,8},{28,12},{1,17},{... | collective-permute-start | bytes 307208 | tf_op jit(solution)/shard_map/ppermute | solution.py:259
  68.6 5.8 %collective-permute-done.17 = bf16[1,4,80,360]{3,2,1,0:T(8,128)(2,1)S(1)} collective-permute-done((bf16[1,4,80,360]{3,2,1,0:T(8,128)(2,1)S(1)}, bf16[1,4,80,360]{3,2,1,0:T(8,128)(2,1)S(1)}, u32[]{:S(2)}, u32[]{:S(2)}) %collective-permute-start.17) | collective-permute-done | bytes 230432 | tf_op jit(solution)/shard_map/ppermute | solution.py:259
  74.4 1.4 %collective-permute-done.16 = bf16[1,4,80,360]{3,2,1,0:T(8,128)(2,1)S(1)} collective-permute-done((bf16[1,4,80,360]{3,2,1,0:T(8,128)(2,1)S(1)}, bf16[1,4,80,360]{3,2,1,0:T(8,128)(2,1)S(1)}, u32[]{:S(2)}, u32[]{:S(2)}) %collective-permute-start.16) | collective-permute-done | bytes 230432 | tf_op jit(solution)/shard_map/ppermute | solution.py:259
  75.7 0.1 fusion.1
  76.0 1.3 %collective-permute-start.20 = (bf16[1,80,360]{2,1,0:T(8,128)(2,1)S(1)}, bf16[1,80,360]{2,1,0:T(8,128)(2,1)S(1)}, u32[]{:S(2)}, u32[]{:S(2)}) collective-permute-start(bf16[1,80,360]{2,1,0:T(8,128)(2,1)S(1)} %get-tuple-element.56), channel_id=1, source_target_pairs={{0,24},{4,28},{8,16},{12,20},{16,8},{20,12},{24,0},{28,4},{1,25},{... | collective-permute-start | bytes 172808 | tf_op jit(solution)/shard_map/ppermute | solution.py:259
  77.3 2.2 %collective-permute-start.19 = (bf16[1,80,360]{2,1,0:T(8,128)(2,1)S(1)}, bf16[1,80,360]{2,1,0:T(8,128)(2,1)S(1)}, u32[]{:S(2)}, u32[]{:S(2)}) collective-permute-start(bf16[1,80,360]{2,1,0:T(8,128)(2,1)S(1)} %get-tuple-element.57), channel_id=1, source_target_pairs={{0,16},{4,20},{8,24},{12,28},{16,0},{20,4},{24,8},{28,12},{1,17},{... | collective-permute-start | bytes 172808 | tf_op jit(solution)/shard_map/ppermute | solution.py:259
  79.5 0.3 collective-permute-start.29
  79.9 1.5 %collective-permute-start.28 = (bf16[160,320]{1,0:T(8,128)(2,1)S(1)}, bf16[160,320]{1,0:T(8,128)(2,1)S(1)}, u32[]{:S(2)}, u32[]{:S(2)}) collective-permute-start(bf16[160,320]{1,0:T(8,128)(2,1)S(1)} %fusion.5), channel_id=1, source_target_pairs={{0,2},{1,3},{2,0},{3,1},{4,6},{5,7},{6,4},{7,5},{8,10},{9,11},{10,... | collective-permute-start | bytes 307208 | tf_op jit(solution)/shard_map/ppermute | solution.py:259
  81.4 1.7 %collective-permute-start.27 = (bf16[160,320]{1,0:T(8,128)(2,1)S(1)}, bf16[160,320]{1,0:T(8,128)(2,1)S(1)}, u32[]{:S(2)}, u32[]{:S(2)}) collective-permute-start(bf16[160,320]{1,0:T(8,128)(2,1)S(1)} %fusion.5), channel_id=1, source_target_pairs={{0,1},{1,0},{2,3},{3,2},{4,5},{5,4},{6,7},{7,6},{8,9},{9,8},{10,11... | collective-permute-start | bytes 307208 | tf_op jit(solution)/shard_map/ppermute | solution.py:259
  83.1 0.9 collective-permute-done.19
  84.0 1.3 %collective-permute-start.23 = (bf16[1,80,360]{2,1,0:T(8,128)(2,1)S(1)}, bf16[1,80,360]{2,1,0:T(8,128)(2,1)S(1)}, u32[]{:S(2)}, u32[]{:S(2)}) collective-permute-start(bf16[1,80,360]{2,1,0:T(8,128)(2,1)S(1)} %fusion.7), channel_id=1, source_target_pairs={{0,3},{1,2},{2,1},{3,0},{4,7},{5,6},{6,5},{7,4},{8,11},{9,10},{10,... | collective-permute-start | bytes 172808 | tf_op jit(solution)/shard_map/ppermute | solution.py:259
  85.3 1.4 %collective-permute-start.22 = (bf16[1,80,360]{2,1,0:T(8,128)(2,1)S(1)}, bf16[1,80,360]{2,1,0:T(8,128)(2,1)S(1)}, u32[]{:S(2)}, u32[]{:S(2)}) collective-permute-start(bf16[1,80,360]{2,1,0:T(8,128)(2,1)S(1)} %fusion.7), channel_id=1, source_target_pairs={{0,2},{1,3},{2,0},{3,1},{4,6},{5,7},{6,4},{7,5},{8,10},{9,11},{10,... | collective-permute-start | bytes 172808 | tf_op jit(solution)/shard_map/ppermute | solution.py:259
  86.7 0.9 collective-permute-start.21
  87.6 0.8 fusion.4
  88.3 0.9 collective-permute-done.23
  89.2 0.6 collective-permute-done.22
  89.9 1.0 %collective-permute-done.21 = bf16[1,80,360]{2,1,0:T(8,128)(2,1)S(1)} collective-permute-done((bf16[1,80,360]{2,1,0:T(8,128)(2,1)S(1)}, bf16[1,80,360]{2,1,0:T(8,128)(2,1)S(1)}, u32[]{:S(2)}, u32[]{:S(2)}) %collective-permute-start.21) | collective-permute-done | bytes 57632 | tf_op jit(solution)/shard_map/ppermute | solution.py:259
  91.0 0.8 convert_bitcast_fusion
  (52 shorter events, 1.0 us)
Async XLA Ops:
  1.6 14.3 %collective-permute-start.2 = (bf16[1,80,360]{2,1,0:T(8,128)(2,1)S(1)}, bf16[1,80,360]{2,1,0:T(8,128)(2,1)S(1)}, u32[]{:S(2)}, u32[]{:S(2)}) collective-permute-start(bf16[1,80,360]{2,1,0:T(8,128)(2,1)S(1)} %bitcast.113), channel_id=1, source_target_pairs={{0,24},{4,28},{8,16},{12,20},{16,8},{20,12},{24,0},{28,4},{1,25},{... | collective-permute-start | bytes 172808 | tf_op jit(solution)/shard_map/ppermute | solution.py:259
  6.7 9.2 %collective-permute-start.1 = (bf16[1,80,360]{2,1,0:T(8,128)(2,1)S(1)}, bf16[1,80,360]{2,1,0:T(8,128)(2,1)S(1)}, u32[]{:S(2)}, u32[]{:S(2)}) collective-permute-start(bf16[1,80,360]{2,1,0:T(8,128)(2,1)S(1)} %bitcast.114), channel_id=1, source_target_pairs={{0,16},{4,20},{8,24},{12,28},{16,0},{20,4},{24,8},{28,12},{1,17},{... | collective-permute-start | bytes 172808 | tf_op jit(solution)/shard_map/ppermute | solution.py:259
  6.7 9.2 %collective-permute-start = (bf16[1,80,360]{2,1,0:T(8,128)(2,1)S(1)}, bf16[1,80,360]{2,1,0:T(8,128)(2,1)S(1)}, u32[]{:S(2)}, u32[]{:S(2)}) collective-permute-start(bf16[1,80,360]{2,1,0:T(8,128)(2,1)S(1)} %bitcast.115), channel_id=1, source_target_pairs={{0,8},{4,12},{8,0},{12,4},{16,24},{20,28},{24,16},{28,20},{1,9},{5... | collective-permute-start | bytes 172808 | tf_op jit(solution)/shard_map/ppermute | solution.py:259
  8.3 11.3 %collective-permute-start.6 = (bf16[1,160,320]{2,1,0:T(8,128)(2,1)S(1)}, bf16[1,160,320]{2,1,0:T(8,128)(2,1)S(1)}, u32[]{:S(2)}, u32[]{:S(2)}) collective-permute-start(bf16[1,160,320]{2,1,0:T(8,128)(2,1)S(1)} %get-tuple-element.61), channel_id=1, source_target_pairs={{0,16},{4,20},{8,24},{12,28},{16,0},{20,4},{24,8},{28,12},{1,17},{... | collective-permute-start | bytes 307208 | tf_op jit(solution)/shard_map/ppermute | solution.py:259
  16.0 11.6 %collective-permute-start.5 = (bf16[1,3,80,360]{3,2,1,0:T(8,128)(2,1)S(1)}, bf16[1,3,80,360]{3,2,1,0:T(8,128)(2,1)S(1)}, u32[]{:S(2)}, u32[]{:S(2)}) collective-permute-start(bf16[1,3,80,360]{3,2,1,0:T(8,128)(2,1)S(1)} %get-tuple-element.59), channel_id=1, source_target_pairs={{0,3},{1,2},{2,1},{3,0},{4,7},{5,6},{6,5},{7,4},{8,11},{9,10},{10,... | collective-permute-start | bytes 518408 | tf_op jit(solution)/shard_map/ppermute | solution.py:259
  18.5 9.6 %collective-permute-start.4 = (bf16[1,3,80,360]{3,2,1,0:T(8,128)(2,1)S(1)}, bf16[1,3,80,360]{3,2,1,0:T(8,128)(2,1)S(1)}, u32[]{:S(2)}, u32[]{:S(2)}) collective-permute-start(bf16[1,3,80,360]{3,2,1,0:T(8,128)(2,1)S(1)} %get-tuple-element.59), channel_id=1, source_target_pairs={{0,2},{1,3},{2,0},{3,1},{4,6},{5,7},{6,4},{7,5},{8,10},{9,11},{10,... | collective-permute-start | bytes 518408 | tf_op jit(solution)/shard_map/ppermute | solution.py:259
  19.0 9.2 %collective-permute-start.3 = (bf16[1,3,80,360]{3,2,1,0:T(8,128)(2,1)S(1)}, bf16[1,3,80,360]{3,2,1,0:T(8,128)(2,1)S(1)}, u32[]{:S(2)}, u32[]{:S(2)}) collective-permute-start(bf16[1,3,80,360]{3,2,1,0:T(8,128)(2,1)S(1)} %get-tuple-element.59), channel_id=1, source_target_pairs={{0,1},{1,0},{2,3},{3,2},{4,5},{5,4},{6,7},{7,6},{8,9},{9,8},{10,11... | collective-permute-start | bytes 518408 | tf_op jit(solution)/shard_map/ppermute | solution.py:259
  19.6 9.3 %collective-permute-start.11 = (bf16[1,2,160,320]{3,2,1,0:T(8,128)(2,1)S(1)}, bf16[1,2,160,320]{3,2,1,0:T(8,128)(2,1)S(1)}, u32[]{:S(2)}, u32[]{:S(2)}) collective-permute-start(bf16[1,2,160,320]{3,2,1,0:T(8,128)(2,1)S(1)} %bitcast.110), channel_id=1, source_target_pairs={{0,8},{4,12},{8,0},{12,4},{16,24},{20,28},{24,16},{28,20},{1,9},{5... | collective-permute-start | bytes 614408 | tf_op jit(solution)/shard_map/ppermute | solution.py:259
  27.6 1.5 %copy-start.2 = (s32[1,15]{1,0:T(1,128)S(1)}, s32[1,15]{1,0:T(1,128)}, u32[]{:S(2)}) copy-start(s32[1,15]{1,0:T(1,128)} %param.11) | copy-start | bytes 184
  27.6 3.0 %collective-permute-start.7 = (bf16[7,80,360]{2,1,0:T(8,128)(2,1)S(1)}, bf16[7,80,360]{2,1,0:T(8,128)(2,1)S(1)}, u32[]{:S(2)}, u32[]{:S(2)}) collective-permute-start(bf16[7,80,360]{2,1,0:T(8,128)(2,1)S(1)} %pad_maximum_fusion.1), channel_id=1, source_target_pairs={{0,4},{4,0},{8,12},{12,8},{16,20},{20,16},{24,28},{28,24},{1,5},{5... | collective-permute-start | bytes 1209608 | tf_op jit(solution)/shard_map/ppermute | solution.py:259
  27.7 3.1 %collective-permute-start.10 = (bf16[1,3,80,360]{3,2,1,0:T(8,128)(2,1)S(1)}, bf16[1,3,80,360]{3,2,1,0:T(8,128)(2,1)S(1)}, u32[]{:S(2)}, u32[]{:S(2)}) collective-permute-start(bf16[1,3,80,360]{3,2,1,0:T(8,128)(2,1)S(1)} %collective-permute-done.5), channel_id=1, source_target_pairs={{0,4},{4,0},{8,12},{12,8},{16,20},{20,16},{24,28},{28,24},{1,5},{5... | collective-permute-start | bytes 518408 | tf_op jit(solution)/shard_map/ppermute | solution.py:259
  28.2 2.6 %collective-permute-start.9 = (bf16[1,3,80,360]{3,2,1,0:T(8,128)(2,1)S(1)}, bf16[1,3,80,360]{3,2,1,0:T(8,128)(2,1)S(1)}, u32[]{:S(2)}, u32[]{:S(2)}) collective-permute-start(bf16[1,3,80,360]{3,2,1,0:T(8,128)(2,1)S(1)} %collective-permute-done.4), channel_id=1, source_target_pairs={{0,4},{4,0},{8,12},{12,8},{16,20},{20,16},{24,28},{28,24},{1,5},{5... | collective-permute-start | bytes 518408 | tf_op jit(solution)/shard_map/ppermute | solution.py:259
  28.2 2.5 %collective-permute-start.8 = (bf16[1,3,80,360]{3,2,1,0:T(8,128)(2,1)S(1)}, bf16[1,3,80,360]{3,2,1,0:T(8,128)(2,1)S(1)}, u32[]{:S(2)}, u32[]{:S(2)}) collective-permute-start(bf16[1,3,80,360]{3,2,1,0:T(8,128)(2,1)S(1)} %collective-permute-done.3), channel_id=1, source_target_pairs={{0,4},{4,0},{8,12},{12,8},{16,20},{20,16},{24,28},{28,24},{1,5},{5... | collective-permute-start | bytes 518408 | tf_op jit(solution)/shard_map/ppermute | solution.py:259
  29.1 2.0 %copy-start = (bf16[15,320,256]{2,1,0:T(8,128)(2,1)S(1)}, bf16[15,320,256]{2,1,0:T(8,128)(2,1)}, u32[]{:S(2)}) copy-start(bf16[15,320,256]{2,1,0:T(8,128)(2,1)} %group_norm.3.normed_ref) | copy-start | bytes 7372804
  29.1 2.0 %copy-start.1 = (s32[1,4]{1,0:T(1,128)S(1)}, s32[1,4]{1,0:T(1,128)}, u32[]{:S(2)}) copy-start(s32[1,4]{1,0:T(1,128)} %counts_ref.1) | copy-start | bytes 52
  29.2 1.9 %collective-permute-start.12 = (bf16[4,160,320]{2,1,0:T(8,128)(2,1)S(1)}, bf16[4,160,320]{2,1,0:T(8,128)(2,1)S(1)}, u32[]{:S(2)}, u32[]{:S(2)}) collective-permute-start(bf16[4,160,320]{2,1,0:T(8,128)(2,1)S(1)} %bitcast.99), channel_id=1, source_target_pairs={{0,4},{4,0},{8,12},{12,8},{16,20},{20,16},{24,28},{28,24},{1,5},{5... | collective-permute-start | bytes 1228808 | tf_op jit(solution)/shard_map/ppermute | solution.py:259
  49.6 3.5 %collective-permute-start.13 = (bf16[4,4,80,360]{3,2,1,0:T(8,128)(2,1)S(1)}, bf16[4,4,80,360]{3,2,1,0:T(8,128)(2,1)S(1)}, u32[]{:S(2)}, u32[]{:S(2)}) collective-permute-start(bf16[4,4,80,360]{3,2,1,0:T(8,128)(2,1)S(1)} %get-tuple-element.40), channel_id=1, source_target_pairs={{0,4},{4,0},{8,12},{12,8},{16,20},{20,16},{24,28},{28,24},{1,5},{5... | collective-permute-start | bytes 2764808 | tf_op jit(solution)/shard_map/ppermute | solution.py:259
  50.1 2.9 %collective-permute-start.14 = (bf16[4,160,320]{2,1,0:T(8,128)(2,1)S(1)}, bf16[4,160,320]{2,1,0:T(8,128)(2,1)S(1)}, u32[]{:S(2)}, u32[]{:S(2)}) collective-permute-start(bf16[4,160,320]{2,1,0:T(8,128)(2,1)S(1)} %get-tuple-element.42), channel_id=1, source_target_pairs={{0,4},{4,0},{8,12},{12,8},{16,20},{20,16},{24,28},{28,24},{1,5},{5... | collective-permute-start | bytes 1228808 | tf_op jit(solution)/shard_map/ppermute | solution.py:259
  53.5 11.4 %collective-permute-start.15 = (bf16[1,4,80,360]{3,2,1,0:T(8,128)(2,1)S(1)}, bf16[1,4,80,360]{3,2,1,0:T(8,128)(2,1)S(1)}, u32[]{:S(2)}, u32[]{:S(2)}) collective-permute-start(bf16[1,4,80,360]{3,2,1,0:T(8,128)(2,1)S(1)} %get-tuple-element.45), channel_id=1, source_target_pairs={{0,1},{1,0},{2,3},{3,2},{4,5},{5,4},{6,7},{7,6},{8,9},{9,8},{10,11... | collective-permute-start | bytes 691208 | tf_op jit(solution)/shard_map/ppermute | solution.py:259
  53.5 20.8 %collective-permute-start.17 = (bf16[1,4,80,360]{3,2,1,0:T(8,128)(2,1)S(1)}, bf16[1,4,80,360]{3,2,1,0:T(8,128)(2,1)S(1)}, u32[]{:S(2)}, u32[]{:S(2)}) collective-permute-start(bf16[1,4,80,360]{3,2,1,0:T(8,128)(2,1)S(1)} %get-tuple-element.46), channel_id=1, source_target_pairs={{0,3},{1,2},{2,1},{3,0},{4,7},{5,6},{6,5},{7,4},{8,11},{9,10},{10,... | collective-permute-start | bytes 691208 | tf_op jit(solution)/shard_map/ppermute | solution.py:259
  62.8 12.9 %collective-permute-start.16 = (bf16[1,4,80,360]{3,2,1,0:T(8,128)(2,1)S(1)}, bf16[1,4,80,360]{3,2,1,0:T(8,128)(2,1)S(1)}, u32[]{:S(2)}, u32[]{:S(2)}) collective-permute-start(bf16[1,4,80,360]{3,2,1,0:T(8,128)(2,1)S(1)} %get-tuple-element.47), channel_id=1, source_target_pairs={{0,2},{1,3},{2,0},{3,1},{4,6},{5,7},{6,4},{7,5},{8,10},{9,11},{10,... | collective-permute-start | bytes 691208 | tf_op jit(solution)/shard_map/ppermute | solution.py:259
  62.9 14.4 %collective-permute-start.24 = (bf16[1,160,320]{2,1,0:T(8,128)(2,1)S(1)}, bf16[1,160,320]{2,1,0:T(8,128)(2,1)S(1)}, u32[]{:S(2)}, u32[]{:S(2)}) collective-permute-start(bf16[1,160,320]{2,1,0:T(8,128)(2,1)S(1)} %get-tuple-element.48), channel_id=1, source_target_pairs={{0,8},{4,12},{8,0},{12,4},{16,24},{20,28},{24,16},{28,20},{1,9},{5... | collective-permute-start | bytes 307208 | tf_op jit(solution)/shard_map/ppermute | solution.py:259
  63.5 16.0 %collective-permute-start.26 = (bf16[1,160,320]{2,1,0:T(8,128)(2,1)S(1)}, bf16[1,160,320]{2,1,0:T(8,128)(2,1)S(1)}, u32[]{:S(2)}, u32[]{:S(2)}) collective-permute-start(bf16[1,160,320]{2,1,0:T(8,128)(2,1)S(1)} %get-tuple-element.49), channel_id=1, source_target_pairs={{0,24},{4,28},{8,16},{12,20},{16,8},{20,12},{24,0},{28,4},{1,25},{... | collective-permute-start | bytes 307208 | tf_op jit(solution)/shard_map/ppermute | solution.py:259
  64.8 14.6 %collective-permute-start.25 = (bf16[1,160,320]{2,1,0:T(8,128)(2,1)S(1)}, bf16[1,160,320]{2,1,0:T(8,128)(2,1)S(1)}, u32[]{:S(2)}, u32[]{:S(2)}) collective-permute-start(bf16[1,160,320]{2,1,0:T(8,128)(2,1)S(1)} %get-tuple-element.50), channel_id=1, source_target_pairs={{0,16},{4,20},{8,24},{12,28},{16,0},{20,4},{24,8},{28,12},{1,17},{... | collective-permute-start | bytes 307208 | tf_op jit(solution)/shard_map/ppermute | solution.py:259
  75.9 5.5 %collective-permute-start.18 = (bf16[1,80,360]{2,1,0:T(8,128)(2,1)S(1)}, bf16[1,80,360]{2,1,0:T(8,128)(2,1)S(1)}, u32[]{:S(2)}, u32[]{:S(2)}) collective-permute-start(bf16[1,80,360]{2,1,0:T(8,128)(2,1)S(1)} %get-tuple-element.55), channel_id=1, source_target_pairs={{0,8},{4,12},{8,0},{12,4},{16,24},{20,28},{24,16},{28,20},{1,9},{5... | collective-permute-start | bytes 172808 | tf_op jit(solution)/shard_map/ppermute | solution.py:259
  76.0 7.1 %collective-permute-start.20 = (bf16[1,80,360]{2,1,0:T(8,128)(2,1)S(1)}, bf16[1,80,360]{2,1,0:T(8,128)(2,1)S(1)}, u32[]{:S(2)}, u32[]{:S(2)}) collective-permute-start(bf16[1,80,360]{2,1,0:T(8,128)(2,1)S(1)} %get-tuple-element.56), channel_id=1, source_target_pairs={{0,24},{4,28},{8,16},{12,20},{16,8},{20,12},{24,0},{28,4},{1,25},{... | collective-permute-start | bytes 172808 | tf_op jit(solution)/shard_map/ppermute | solution.py:259
  77.3 6.7 %collective-permute-start.19 = (bf16[1,80,360]{2,1,0:T(8,128)(2,1)S(1)}, bf16[1,80,360]{2,1,0:T(8,128)(2,1)S(1)}, u32[]{:S(2)}, u32[]{:S(2)}) collective-permute-start(bf16[1,80,360]{2,1,0:T(8,128)(2,1)S(1)} %get-tuple-element.57), channel_id=1, source_target_pairs={{0,16},{4,20},{8,24},{12,28},{16,0},{20,4},{24,8},{28,12},{1,17},{... | collective-permute-start | bytes 172808 | tf_op jit(solution)/shard_map/ppermute | solution.py:259
  79.5 7.1 %collective-permute-start.29 = (bf16[160,320]{1,0:T(8,128)(2,1)S(1)}, bf16[160,320]{1,0:T(8,128)(2,1)S(1)}, u32[]{:S(2)}, u32[]{:S(2)}) collective-permute-start(bf16[160,320]{1,0:T(8,128)(2,1)S(1)} %fusion.5), channel_id=1, source_target_pairs={{0,3},{1,2},{2,1},{3,0},{4,7},{5,6},{6,5},{7,4},{8,11},{9,10},{10,... | collective-permute-start | bytes 307208 | tf_op jit(solution)/shard_map/ppermute | solution.py:259
  79.9 7.7 %collective-permute-start.28 = (bf16[160,320]{1,0:T(8,128)(2,1)S(1)}, bf16[160,320]{1,0:T(8,128)(2,1)S(1)}, u32[]{:S(2)}, u32[]{:S(2)}) collective-permute-start(bf16[160,320]{1,0:T(8,128)(2,1)S(1)} %fusion.5), channel_id=1, source_target_pairs={{0,2},{1,3},{2,0},{3,1},{4,6},{5,7},{6,4},{7,5},{8,10},{9,11},{10,... | collective-permute-start | bytes 307208 | tf_op jit(solution)/shard_map/ppermute | solution.py:259
  81.4 6.2 %collective-permute-start.27 = (bf16[160,320]{1,0:T(8,128)(2,1)S(1)}, bf16[160,320]{1,0:T(8,128)(2,1)S(1)}, u32[]{:S(2)}, u32[]{:S(2)}) collective-permute-start(bf16[160,320]{1,0:T(8,128)(2,1)S(1)} %fusion.5), channel_id=1, source_target_pairs={{0,1},{1,0},{2,3},{3,2},{4,5},{5,4},{6,7},{7,6},{8,9},{9,8},{10,11... | collective-permute-start | bytes 307208 | tf_op jit(solution)/shard_map/ppermute | solution.py:259
  84.0 5.2 %collective-permute-start.23 = (bf16[1,80,360]{2,1,0:T(8,128)(2,1)S(1)}, bf16[1,80,360]{2,1,0:T(8,128)(2,1)S(1)}, u32[]{:S(2)}, u32[]{:S(2)}) collective-permute-start(bf16[1,80,360]{2,1,0:T(8,128)(2,1)S(1)} %fusion.7), channel_id=1, source_target_pairs={{0,3},{1,2},{2,1},{3,0},{4,7},{5,6},{6,5},{7,4},{8,11},{9,10},{10,... | collective-permute-start | bytes 172808 | tf_op jit(solution)/shard_map/ppermute | solution.py:259
  85.3 4.6 %collective-permute-start.22 = (bf16[1,80,360]{2,1,0:T(8,128)(2,1)S(1)}, bf16[1,80,360]{2,1,0:T(8,128)(2,1)S(1)}, u32[]{:S(2)}, u32[]{:S(2)}) collective-permute-start(bf16[1,80,360]{2,1,0:T(8,128)(2,1)S(1)} %fusion.7), channel_id=1, source_target_pairs={{0,2},{1,3},{2,0},{3,1},{4,6},{5,7},{6,4},{7,5},{8,10},{9,11},{10,... | collective-permute-start | bytes 172808 | tf_op jit(solution)/shard_map/ppermute | solution.py:259
  86.7 4.2 %collective-permute-start.21 = (bf16[1,80,360]{2,1,0:T(8,128)(2,1)S(1)}, bf16[1,80,360]{2,1,0:T(8,128)(2,1)S(1)}, u32[]{:S(2)}, u32[]{:S(2)}) collective-permute-start(bf16[1,80,360]{2,1,0:T(8,128)(2,1)S(1)} %fusion.7), channel_id=1, source_target_pairs={{0,1},{1,0},{2,3},{3,2},{4,5},{5,4},{6,7},{7,6},{8,9},{9,8},{10,11... | collective-permute-start | bytes 172808 | tf_op jit(solution)/shard_map/ppermute | solution.py:259

commit v10 on v9

--- a/solution.py
+++ b/solution.py
@@ -304,8 +304,10 @@
 def time_features(timesteps, emb):
     half_width = emb // 2
     frequency = jnp.exp(-math.log(10000.0) * jnp.arange(half_width, dtype=f32) / half_width)
-    angles = frequency[:, None] * timesteps.astype(f32)[None, :]
-    return jax.nn.silu(jnp.concatenate([jnp.cos(angles), jnp.sin(angles)])).astype(bf16)
+    angles = timesteps.astype(f32)[:, None] * frequency[None, :]
+    waves = jnp.concatenate([jnp.cos(angles), jnp.sin(angles)], axis=1)
+    features = jax.nn.silu(waves).astype(bf16)
+    return jnp.pad(features, ((0, LANES - features.shape[0]), (0, 0))).T
 
 
 def per_device(latents, target_noise, counts, timesteps, conv_master, temb_master):
@@ -322,16 +324,13 @@
     plane_bits = shard_bits - 1
 
     part_rows = outs // parts
-    first = lax.dynamic_slice(conv_master.T, (part * part_rows, 0), (part_rows, rows))
-    first, conv_master, temb_master, tiles_then = lax.optimization_barrier(
-        (first.astype(bf16), conv_master, temb_master, tiles)
-    )
+    master = conv_master.T.astype(bf16).reshape(parts, part_rows, rows)
+    mine = [lax.dynamic_index_in_dim(master, part ^ m, 0, keepdims=False) for m in range(parts)]
+    first, temb_master, tiles_then = lax.optimization_barrier((mine[0], temb_master, tiles))
     over_planes = gather_partners(first, "fsdp", 1, plane_bits)
     time_master = temb_master.astype(bf16)
     near_bits = plane_bits // 2
     far_time = gather_partners(time_master, "fsdp", 1 + near_bits, plane_bits - near_bits, most=1)
-    master = conv_master.T.astype(bf16).reshape(parts, part_rows, rows)
-    mine = [lax.dynamic_index_in_dim(master, part ^ m, 0, keepdims=False) for m in range(parts)]
     mine = jnp.stack(mine)[:, None]
     steps = number // tiles_per_step(number)
     head = steps // 3
@@ -351,7 +350,7 @@
     own_time, times = lax.optimization_barrier((own_time, timesteps[0]))
     other_far = [other_near[None, parts:]] + [swap(block, "fsdp", 1) for block in far[1:]]
     other_mine = other_near[:parts, None]
-    features = time_features(jnp.pad(times, (0, LANES - number)), time_rows * shards)
+    features = time_features(times, time_rows * shards)
     own = jnp.concatenate([mine, jnp.concatenate(far)], axis=1)
     other = jnp.concatenate([other_mine, jnp.concatenate(other_far)], axis=1)
     other_time = swap(own_time, "fsdp", 1)

time: 91.8 us -> 98.7 us (1.075)
  starting transfers between devices: 41.1 us -> 30.8 us
  Pallas kernels: 28.4 us -> 35 us
  waiting for transfers between devices: 13.5 us -> 17.8 us
  other arithmetic: 6.57 us -> 9.61 us
  local copies, waits for them, and re-layouts: 1.28 us -> 4.2 us
    ppermute x30, starting transfers between devices: 41.1 us -> 30.8 us  [swap(): return lax.ppermute(values, axis, pairs)]
    pallas_call x1, Pallas kernels: 18.5 us -> 25.1 us  [conv_both(): pl.pallas_call(functools.partial(conv_kernel, steps), grid_spec=pltpu.Pre...]
    ppermute x30, waiting for transfers between devices: 13.5 us -> 17.8 us  [swap(): return lax.ppermute(values, axis, pairs)]
    concatenate x0 -> x1, local copies, waits for them, and re-layouts: none -> 1.12 us  [time_features(): waves = jnp.concatenate([jnp.cos(angles), jnp.sin(angles)], axis=1)]
    concatenate x1, other arithmetic: 0.25 us -> 1.35 us  [per_device(): own = jnp.concatenate([mine, jnp.concatenate(far)], axis=1)]
    concatenate x1, other arithmetic: 0.26 us -> 1.35 us  [per_device(): other = jnp.concatenate([other_mine, jnp.concatenate(other_far)], axis=1)]
    convert_element_type x2, other arithmetic: 0.19 us -> 1.27 us  [the longest x1 1.27 us: time_features(): features = jax.nn.silu(waves).astype(bf16)]
  transfers between devices with their start and end apart: 30 -> 30, of which waited for: 7 -> 8; matrix products, arithmetic and copies ran while one was open for 6% -> 12% of each run, Pallas kernels for 11% -> 10%
where the time goes in v10:
time: 98.7 us; the launch traced here: 98.3 us
  Pallas kernels  35 us (35%)
  starting transfers between devices  30.8 us (31%)
  waiting for transfers between devices  17.8 us (18%)
  other arithmetic  9.61 us (10%)
  local copies, waits for them, and re-layouts  4.2 us (4%)
    ppermute x30, starting transfers between devices, swap(): return lax.ppermute(values, axis, pairs)  30.8 us
    pallas_call x1, Pallas kernels, conv_both(): pl.pallas_call(functools.partial(conv_kernel, steps), grid_spec=pltpu.Pre...  25.1 us
    ppermute x30, waiting for transfers between devices, swap(): return lax.ppermute(values, axis, pairs)  17.8 us
    pallas_call x2, Pallas kernels, group_norm(): pl.pallas_call(functools.partial(norm_kernel, group_width), grid=(last -...  9.87 us
  transfers between devices with their start and end apart: 30, of which 8 were waited for; matrix products, arithmetic and copies ran while one was open for 12% of the time, Pallas kernels for 10%

profile of v10, /device:TPU:0, one launch (start us, length us, event | category | flops | bytes accessed | tf_op | source)
XLA Modules:
  0.0 98.3 jit_solution(4396068177247156893)
XLA Ops:
  0.6 1.1 %convert_element_type.137 = bf16[360,320]{0,1:T(8,128)(2,1)S(1)} convert(f32[360,320]{0,1:T(8,128)} %param.12) | non-fusion elementwise | flops 115200 | bytes 691200 | tf_op jit(solution)/shard_map/convert_element_type | solution.py:327
  1.8 5.1 %collective-permute-start.2 = (bf16[1,80,360]{2,1,0:T(8,128)(2,1)S(1)}, bf16[1,80,360]{2,1,0:T(8,128)(2,1)S(1)}, u32[]{:S(2)}, u32[]{:S(2)}) collective-permute-start(bf16[1,80,360]{2,1,0:T(8,128)(2,1)S(1)} %get-tuple-element.63), channel_id=1, source_target_pairs={{0,24},{4,28},{8,16},{12,20},{16,8},{20,12},{24,0},{28,4},{1,25},{... | collective-permute-start | bytes 172808 | tf_op jit(solution)/shard_map/ppermute | solution.py:259
  6.9 0.6 collective-permute-start
  7.5 1.0 convert_bitcast_fusion.2
  8.5 2.4 %collective-permute-start.6 = (bf16[1,160,320]{2,1,0:T(8,128)(2,1)S(1)}, bf16[1,160,320]{2,1,0:T(8,128)(2,1)S(1)}, u32[]{:S(2)}, u32[]{:S(2)}) collective-permute-start(bf16[1,160,320]{2,1,0:T(8,128)(2,1)S(1)} %get-tuple-element.59), channel_id=1, source_target_pairs={{0,16},{4,20},{8,24},{12,28},{16,0},{20,4},{24,8},{28,12},{1,17},{... | collective-permute-start | bytes 307208 | tf_op jit(solution)/shard_map/ppermute | solution.py:259
  10.9 4.0 %group_norm.2.refs_0_ = bf16[15,320,256]{2,1,0:T(8,128)(2,1)} custom-call(bf16[320,320]{1,0:T(8,128)(2,1)} %constant.47.clone.same_ref, bf16[15,320,256]{2,1,0:T(8,128)(2,1)} %bitcast.100), custom_call_target="tpu_custom_call" | custom-call | flops 8192000 | bytes 1638400 | tf_op jit(solution)/shard_map/group_norm/pallas_call | solution.py:62
  15.1 2.5 %collective-permute-start.5 = (bf16[1,3,80,360]{3,2,1,0:T(8,128)(2,1)S(1)}, bf16[1,3,80,360]{3,2,1,0:T(8,128)(2,1)}, u32[]{:S(2)}, u32[]{:S(2)}) collective-permute-start(bf16[1,3,80,360]{3,2,1,0:T(8,128)(2,1)S(1)} %get-tuple-element.57), channel_id=1, source_target_pairs={{0,3},{1,2},{2,1},{3,0},{4,7},{5,6},{6,5},{7,4},{8,11},{9,10},{10,... | collective-permute-start | bytes 518408 | tf_op jit(solution)/shard_map/ppermute | solution.py:259
  17.6 0.5 collective-permute-start.4
  18.1 0.5 collective-permute-start.3
  18.7 2.1 %collective-permute-start.11 = (bf16[1,2,160,320]{3,2,1,0:T(8,128)(2,1)S(1)}, bf16[1,2,160,320]{3,2,1,0:T(8,128)(2,1)S(1)}, u32[]{:S(2)}, u32[]{:S(2)}) collective-permute-start(bf16[1,2,160,320]{3,2,1,0:T(8,128)(2,1)S(1)} %bitcast.109), channel_id=1, source_target_pairs={{0,8},{4,12},{8,0},{12,4},{16,24},{20,28},{24,16},{28,20},{1,9},{5... | collective-permute-start | bytes 614408 | tf_op jit(solution)/shard_map/ppermute | solution.py:259
  20.8 0.8 pad_maximum_fusion
  21.6 5.8 %group_norm.3.normed_ref = bf16[15,320,256]{2,1,0:T(8,128)(2,1)} custom-call(bf16[320,320]{1,0:T(8,128)(2,1)} %constant.47.clone.same_ref, bf16[15,320,256]{2,1,0:T(8,128)(2,1)} %bitcast.101, bf16[15,320,256]{2,1,0:T(8,128)(2,1)} %group_norm.2.refs_0_), custom_call_target="tpu_custom_call", output_to_operand_aliasing={{}: (2, {})} | custom-call | flops 16384000 | bytes 3276800 | tf_op jit(solution)/shard_map/group_norm/pallas_call | solution.py:62
  27.5 0.5 collective-permute-start.10
  28.1 0.4 collective-permute-start.8
  28.5 1.3 %maximum_maximum_fusion.own_ref = bf16[4,4,80,360]{3,2,1,0:T(8,128)(2,1)S(1)} fusion(bf16[1,3,80,360]{3,2,1,0:T(8,128)(2,1)} %collective-permute-done.5, bf16[1,3,80,360]{3,2,1,0:T(8,128)(2,1)} %collective-permute-done.4, bf16[1,3,80,360]{3,2,1,0:T(8,128)(2,1)} %collective-permute-done.3, bf16[1,3,80,360]{3,2,1,0:T(8,128)(2,1)S(1)} %get-tuple-element.57, ...), kind=kLoop, calls=%fused_computation.1 | loop fusion | flops 1843200 | bytes 1843200 | tf_op jit(solution)/shard_map/concatenate | solution.py:354
  30.0 0.8 copy.19
  30.9 0.2 multiply_cosine_fusion
  31.1 1.1 %copy.23 = f32[15,1280]{0,1:T(8,128)} copy(f32[15,1280]{1,0:T(8,128)S(1)} %pad_maximum_fusion.2) | data formatting | bytes 153600 | tf_op jit(solution)/shard_map/concatenate | solution.py:308
  32.3 1.3 %multiply_convert_fusion = bf16[15,1280]{0,1:T(8,128)(2,1)S(1)} fusion(f32[15,1280]{0,1:T(8,128)} %copy.23), kind=kLoop, calls=%fused_computation.4 | loop fusion | flops 96000 | bytes 115200 | tf_op jit(solution)/shard_map/convert_element_type | solution.py:309
  33.6 1.0 slice_bitcast_fusion.4
  34.6 0.9 slice_bitcast_fusion.5
  35.6 1.4 %maximum_maximum_fusion.1.other_ref = bf16[4,4,80,360]{3,2,1,0:T(8,128)(2,1)S(1)} fusion(bf16[1,3,80,360]{3,2,1,0:T(8,128)(2,1)} %collective-permute-done.10, bf16[1,3,80,360]{3,2,1,0:T(8,128)(2,1)} %collective-permute-done.9, bf16[1,3,80,360]{3,2,1,0:T(8,128)(2,1)} %collective-permute-done.8, bf16[1,3,80,360]{3,2,1,0:T(8,128)(2,1)S(1)} %slice_bitcast_fusion.5, ...), kind=kLoop, calls=%fused_computation.2 | loop fusion | flops 1843200 | bytes 1843200 | tf_op jit(solution)/shard_map/concatenate | solution.py:355
  37.0 25.1 %conv_both.1 = (bf16[15,320,256]{2,1,0:T(8,128)(2,1)}, bf16[4,4,80,360]{3,2,1,0:T(8,128)(2,1)S(1)}, bf16[4,4,80,360]{3,2,1,0:T(8,128)(2,1)S(1)}, bf16[4,160,320]...) custom-call(s32[1,4]{1,0:T(1,128)S(1)} %copy-done.1, bf16[4,4,80,360]{3,2,1,0:T(8,128)(2,1)S(1)} %maximum_maximum_fusion.own_ref, ...), custom_call_target="tpu_custom_call" | custom-call | flops 14155776000 | bytes 9830400 | tf_op jit(solution)/shard_map/conv_both/pallas_call | solution.py:223
  62.1 0.5 collective-permute-start.14
  62.6 2.8 %collective-permute-done.14 = bf16[4,160,320]{2,1,0:T(8,128)(2,1)S(1)} collective-permute-done((bf16[4,160,320]{2,1,0:T(8,128)(2,1)S(1)}, bf16[4,160,320]{2,1,0:T(8,128)(2,1)S(1)}, u32[]{:S(2)}, u32[]{:S(2)}) %collective-permute-start.14) | collective-permute-done | bytes 409632 | tf_op jit(solution)/shard_map/ppermute | solution.py:259
  65.3 0.1 add_convert_fusion.1
  65.5 0.3 add_convert_fusion
  65.9 3.0 %collective-permute-start.17 = (bf16[1,4,80,360]{3,2,1,0:T(8,128)(2,1)S(1)}, bf16[1,4,80,360]{3,2,1,0:T(8,128)(2,1)S(1)}, u32[]{:S(2)}, u32[]{:S(2)}) collective-permute-start(bf16[1,4,80,360]{3,2,1,0:T(8,128)(2,1)S(1)} %get-tuple-element.44), channel_id=1, source_target_pairs={{0,3},{1,2},{2,1},{3,0},{4,7},{5,6},{6,5},{7,4},{8,11},{9,10},{10,... | collective-permute-start | bytes 691208 | tf_op jit(solution)/shard_map/ppermute | solution.py:259
  68.9 0.4 collective-permute-start.16
  69.5 1.1 %collective-permute-start.26 = (bf16[1,160,320]{2,1,0:T(8,128)(2,1)S(1)}, bf16[1,160,320]{2,1,0:T(8,128)(2,1)S(1)}, u32[]{:S(2)}, u32[]{:S(2)}) collective-permute-start(bf16[1,160,320]{2,1,0:T(8,128)(2,1)S(1)} %get-tuple-element.47), channel_id=1, source_target_pairs={{0,24},{4,28},{8,16},{12,20},{16,8},{20,12},{24,0},{28,4},{1,25},{... | collective-permute-start | bytes 307208 | tf_op jit(solution)/shard_map/ppermute | solution.py:259
  70.6 4.1 %collective-permute-done.15 = bf16[1,4,80,360]{3,2,1,0:T(8,128)(2,1)S(1)} collective-permute-done((bf16[1,4,80,360]{3,2,1,0:T(8,128)(2,1)S(1)}, bf16[1,4,80,360]{3,2,1,0:T(8,128)(2,1)S(1)}, u32[]{:S(2)}, u32[]{:S(2)}) %collective-permute-start.15) | collective-permute-done | bytes 230432 | tf_op jit(solution)/shard_map/ppermute | solution.py:259
  74.7 5.8 %collective-permute-done.17 = bf16[1,4,80,360]{3,2,1,0:T(8,128)(2,1)S(1)} collective-permute-done((bf16[1,4,80,360]{3,2,1,0:T(8,128)(2,1)S(1)}, bf16[1,4,80,360]{3,2,1,0:T(8,128)(2,1)S(1)}, u32[]{:S(2)}, u32[]{:S(2)}) %collective-permute-start.17) | collective-permute-done | bytes 230432 | tf_op jit(solution)/shard_map/ppermute | solution.py:259
  80.5 1.4 %collective-permute-done.16 = bf16[1,4,80,360]{3,2,1,0:T(8,128)(2,1)S(1)} collective-permute-done((bf16[1,4,80,360]{3,2,1,0:T(8,128)(2,1)S(1)}, bf16[1,4,80,360]{3,2,1,0:T(8,128)(2,1)S(1)}, u32[]{:S(2)}, u32[]{:S(2)}) %collective-permute-start.16) | collective-permute-done | bytes 230432 | tf_op jit(solution)/shard_map/ppermute | solution.py:259
  81.9 0.1 fusion.1
  82.1 1.3 %collective-permute-start.20 = (bf16[1,80,360]{2,1,0:T(8,128)(2,1)S(1)}, bf16[1,80,360]{2,1,0:T(8,128)(2,1)S(1)}, u32[]{:S(2)}, u32[]{:S(2)}) collective-permute-start(bf16[1,80,360]{2,1,0:T(8,128)(2,1)S(1)} %get-tuple-element.54), channel_id=1, source_target_pairs={{0,24},{4,28},{8,16},{12,20},{16,8},{20,12},{24,0},{28,4},{1,25},{... | collective-permute-start | bytes 172808 | tf_op jit(solution)/shard_map/ppermute | solution.py:259
  83.4 2.1 %collective-permute-start.19 = (bf16[1,80,360]{2,1,0:T(8,128)(2,1)S(1)}, bf16[1,80,360]{2,1,0:T(8,128)(2,1)S(1)}, u32[]{:S(2)}, u32[]{:S(2)}) collective-permute-start(bf16[1,80,360]{2,1,0:T(8,128)(2,1)S(1)} %get-tuple-element.55), channel_id=1, source_target_pairs={{0,16},{4,20},{8,24},{12,28},{16,0},{20,4},{24,8},{28,12},{1,17},{... | collective-permute-start | bytes 172808 | tf_op jit(solution)/shard_map/ppermute | solution.py:259
  85.7 1.3 %collective-permute-start.29 = (bf16[160,320]{1,0:T(8,128)(2,1)S(1)}, bf16[160,320]{1,0:T(8,128)(2,1)S(1)}, u32[]{:S(2)}, u32[]{:S(2)}) collective-permute-start(bf16[160,320]{1,0:T(8,128)(2,1)S(1)} %fusion.5), channel_id=1, source_target_pairs={{0,3},{1,2},{2,1},{3,0},{4,7},{5,6},{6,5},{7,4},{8,11},{9,10},{10,... | collective-permute-start | bytes 307208 | tf_op jit(solution)/shard_map/ppermute | solution.py:259
  86.9 1.7 %collective-permute-start.28 = (bf16[160,320]{1,0:T(8,128)(2,1)S(1)}, bf16[160,320]{1,0:T(8,128)(2,1)S(1)}, u32[]{:S(2)}, u32[]{:S(2)}) collective-permute-start(bf16[160,320]{1,0:T(8,128)(2,1)S(1)} %fusion.5), channel_id=1, source_target_pairs={{0,2},{1,3},{2,0},{3,1},{4,6},{5,7},{6,4},{7,5},{8,10},{9,11},{10,... | collective-permute-start | bytes 307208 | tf_op jit(solution)/shard_map/ppermute | solution.py:259
  88.7 0.5 collective-permute-start.27
  89.2 0.8 collective-permute-done.19
  90.1 1.6 %collective-permute-start.23 = (bf16[1,80,360]{2,1,0:T(8,128)(2,1)S(1)}, bf16[1,80,360]{2,1,0:T(8,128)(2,1)S(1)}, u32[]{:S(2)}, u32[]{:S(2)}) collective-permute-start(bf16[1,80,360]{2,1,0:T(8,128)(2,1)S(1)} %fusion.7), channel_id=1, source_target_pairs={{0,3},{1,2},{2,1},{3,0},{4,7},{5,6},{6,5},{7,4},{8,11},{9,10},{10,... | collective-permute-start | bytes 172808 | tf_op jit(solution)/shard_map/ppermute | solution.py:259
  91.7 1.4 %collective-permute-start.22 = (bf16[1,80,360]{2,1,0:T(8,128)(2,1)S(1)}, bf16[1,80,360]{2,1,0:T(8,128)(2,1)S(1)}, u32[]{:S(2)}, u32[]{:S(2)}) collective-permute-start(bf16[1,80,360]{2,1,0:T(8,128)(2,1)S(1)} %fusion.7), channel_id=1, source_target_pairs={{0,2},{1,3},{2,0},{3,1},{4,6},{5,7},{6,4},{7,5},{8,10},{9,11},{10,... | collective-permute-start | bytes 172808 | tf_op jit(solution)/shard_map/ppermute | solution.py:259
  93.1 0.5 collective-permute-start.21
  93.7 0.8 fusion.4
  94.5 0.8 collective-permute-done.23
  95.3 0.7 collective-permute-done.22
  96.0 1.4 %collective-permute-done.21 = bf16[1,80,360]{2,1,0:T(8,128)(2,1)S(1)} collective-permute-done((bf16[1,80,360]{2,1,0:T(8,128)(2,1)S(1)}, bf16[1,80,360]{2,1,0:T(8,128)(2,1)S(1)}, u32[]{:S(2)}, u32[]{:S(2)}) %collective-permute-start.21) | collective-permute-done | bytes 57632 | tf_op jit(solution)/shard_map/ppermute | solution.py:259
  97.5 0.8 convert_bitcast_fusion
  (54 shorter events, 1.3 us)
Async XLA Ops:
  1.8 13.2 %collective-permute-start.2 = (bf16[1,80,360]{2,1,0:T(8,128)(2,1)S(1)}, bf16[1,80,360]{2,1,0:T(8,128)(2,1)S(1)}, u32[]{:S(2)}, u32[]{:S(2)}) collective-permute-start(bf16[1,80,360]{2,1,0:T(8,128)(2,1)S(1)} %get-tuple-element.63), channel_id=1, source_target_pairs={{0,24},{4,28},{8,16},{12,20},{16,8},{20,12},{24,0},{28,4},{1,25},{... | collective-permute-start | bytes 172808 | tf_op jit(solution)/shard_map/ppermute | solution.py:259
  6.9 8.1 %collective-permute-start.1 = (bf16[1,80,360]{2,1,0:T(8,128)(2,1)S(1)}, bf16[1,80,360]{2,1,0:T(8,128)(2,1)S(1)}, u32[]{:S(2)}, u32[]{:S(2)}) collective-permute-start(bf16[1,80,360]{2,1,0:T(8,128)(2,1)S(1)} %get-tuple-element.63), channel_id=1, source_target_pairs={{0,16},{4,20},{8,24},{12,28},{16,0},{20,4},{24,8},{28,12},{1,17},{... | collective-permute-start | bytes 172808 | tf_op jit(solution)/shard_map/ppermute | solution.py:259
  6.9 8.1 %collective-permute-start = (bf16[1,80,360]{2,1,0:T(8,128)(2,1)S(1)}, bf16[1,80,360]{2,1,0:T(8,128)(2,1)S(1)}, u32[]{:S(2)}, u32[]{:S(2)}) collective-permute-start(bf16[1,80,360]{2,1,0:T(8,128)(2,1)S(1)} %get-tuple-element.63), channel_id=1, source_target_pairs={{0,8},{4,12},{8,0},{12,4},{16,24},{20,28},{24,16},{28,20},{1,9},{5... | collective-permute-start | bytes 172808 | tf_op jit(solution)/shard_map/ppermute | solution.py:259
  8.5 10.2 %collective-permute-start.6 = (bf16[1,160,320]{2,1,0:T(8,128)(2,1)S(1)}, bf16[1,160,320]{2,1,0:T(8,128)(2,1)S(1)}, u32[]{:S(2)}, u32[]{:S(2)}) collective-permute-start(bf16[1,160,320]{2,1,0:T(8,128)(2,1)S(1)} %get-tuple-element.59), channel_id=1, source_target_pairs={{0,16},{4,20},{8,24},{12,28},{16,0},{20,4},{24,8},{28,12},{1,17},{... | collective-permute-start | bytes 307208 | tf_op jit(solution)/shard_map/ppermute | solution.py:259
  15.1 12.4 %collective-permute-start.5 = (bf16[1,3,80,360]{3,2,1,0:T(8,128)(2,1)S(1)}, bf16[1,3,80,360]{3,2,1,0:T(8,128)(2,1)}, u32[]{:S(2)}, u32[]{:S(2)}) collective-permute-start(bf16[1,3,80,360]{3,2,1,0:T(8,128)(2,1)S(1)} %get-tuple-element.57), channel_id=1, source_target_pairs={{0,3},{1,2},{2,1},{3,0},{4,7},{5,6},{6,5},{7,4},{8,11},{9,10},{10,... | collective-permute-start | bytes 518408 | tf_op jit(solution)/shard_map/ppermute | solution.py:259
  17.6 10.4 %collective-permute-start.4 = (bf16[1,3,80,360]{3,2,1,0:T(8,128)(2,1)S(1)}, bf16[1,3,80,360]{3,2,1,0:T(8,128)(2,1)}, u32[]{:S(2)}, u32[]{:S(2)}) collective-permute-start(bf16[1,3,80,360]{3,2,1,0:T(8,128)(2,1)S(1)} %get-tuple-element.57), channel_id=1, source_target_pairs={{0,2},{1,3},{2,0},{3,1},{4,6},{5,7},{6,4},{7,5},{8,10},{9,11},{10,... | collective-permute-start | bytes 518408 | tf_op jit(solution)/shard_map/ppermute | solution.py:259
  18.1 9.9 %collective-permute-start.3 = (bf16[1,3,80,360]{3,2,1,0:T(8,128)(2,1)S(1)}, bf16[1,3,80,360]{3,2,1,0:T(8,128)(2,1)}, u32[]{:S(2)}, u32[]{:S(2)}) collective-permute-start(bf16[1,3,80,360]{3,2,1,0:T(8,128)(2,1)S(1)} %get-tuple-element.57), channel_id=1, source_target_pairs={{0,1},{1,0},{2,3},{3,2},{4,5},{5,4},{6,7},{7,6},{8,9},{9,8},{10,11... | collective-permute-start | bytes 518408 | tf_op jit(solution)/shard_map/ppermute | solution.py:259
  18.7 11.1 %collective-permute-start.11 = (bf16[1,2,160,320]{3,2,1,0:T(8,128)(2,1)S(1)}, bf16[1,2,160,320]{3,2,1,0:T(8,128)(2,1)S(1)}, u32[]{:S(2)}, u32[]{:S(2)}) collective-permute-start(bf16[1,2,160,320]{3,2,1,0:T(8,128)(2,1)S(1)} %bitcast.109), channel_id=1, source_target_pairs={{0,8},{4,12},{8,0},{12,4},{16,24},{20,28},{24,16},{28,20},{1,9},{5... | collective-permute-start | bytes 614408 | tf_op jit(solution)/shard_map/ppermute | solution.py:259
  27.5 3.3 %copy-start.2 = (s32[1,15]{1,0:T(1,128)S(1)}, s32[1,15]{1,0:T(1,128)}, u32[]{:S(2)}) copy-start(s32[1,15]{1,0:T(1,128)} %param.11) | copy-start | bytes 184
  27.5 6.1 %collective-permute-start.7 = (bf16[7,80,360]{2,1,0:T(8,128)(2,1)}, bf16[7,80,360]{2,1,0:T(8,128)(2,1)}, u32[]{:S(2)}, u32[]{:S(2)}) collective-permute-start(bf16[7,80,360]{2,1,0:T(8,128)(2,1)} %pad_maximum_fusion), channel_id=1, source_target_pairs={{0,4},{4,0},{8,12},{12,8},{16,20},{20,16},{24,28},{28,24},{1,5},{5... | collective-permute-start | bytes 1209608 | tf_op jit(solution)/shard_map/ppermute | solution.py:259
  27.5 8.1 %collective-permute-start.10 = (bf16[1,3,80,360]{3,2,1,0:T(8,128)(2,1)}, bf16[1,3,80,360]{3,2,1,0:T(8,128)(2,1)}, u32[]{:S(2)}, u32[]{:S(2)}) collective-permute-start(bf16[1,3,80,360]{3,2,1,0:T(8,128)(2,1)} %collective-permute-done.5), channel_id=1, source_target_pairs={{0,4},{4,0},{8,12},{12,8},{16,20},{20,16},{24,28},{28,24},{1,5},{5... | collective-permute-start | bytes 518408 | tf_op jit(solution)/shard_map/ppermute | solution.py:259
  28.0 7.6 %collective-permute-start.9 = (bf16[1,3,80,360]{3,2,1,0:T(8,128)(2,1)}, bf16[1,3,80,360]{3,2,1,0:T(8,128)(2,1)}, u32[]{:S(2)}, u32[]{:S(2)}) collective-permute-start(bf16[1,3,80,360]{3,2,1,0:T(8,128)(2,1)} %collective-permute-done.4), channel_id=1, source_target_pairs={{0,4},{4,0},{8,12},{12,8},{16,20},{20,16},{24,28},{28,24},{1,5},{5... | collective-permute-start | bytes 518408 | tf_op jit(solution)/shard_map/ppermute | solution.py:259
  28.1 7.5 %collective-permute-start.8 = (bf16[1,3,80,360]{3,2,1,0:T(8,128)(2,1)}, bf16[1,3,80,360]{3,2,1,0:T(8,128)(2,1)}, u32[]{:S(2)}, u32[]{:S(2)}) collective-permute-start(bf16[1,3,80,360]{3,2,1,0:T(8,128)(2,1)} %collective-permute-done.3), channel_id=1, source_target_pairs={{0,4},{4,0},{8,12},{12,8},{16,20},{20,16},{24,28},{28,24},{1,5},{5... | collective-permute-start | bytes 518408 | tf_op jit(solution)/shard_map/ppermute | solution.py:259
  30.8 6.1 %collective-permute-start.12 = (bf16[4,160,320]{2,1,0:T(8,128)(2,1)}, bf16[4,160,320]{2,1,0:T(8,128)(2,1)}, u32[]{:S(2)}, u32[]{:S(2)}) collective-permute-start(bf16[4,160,320]{2,1,0:T(8,128)(2,1)} %bitcast.27.own_time_ref), channel_id=1, source_target_pairs={{0,4},{4,0},{8,12},{12,8},{16,20},{20,16},{24,28},{28,24},{1,5},{5... | collective-permute-start | bytes 1228808 | tf_op jit(solution)/shard_map/ppermute | solution.py:259
  31.1 5.8 %copy-start = (bf16[15,320,256]{2,1,0:T(8,128)(2,1)S(1)}, bf16[15,320,256]{2,1,0:T(8,128)(2,1)}, u32[]{:S(2)}) copy-start(bf16[15,320,256]{2,1,0:T(8,128)(2,1)} %group_norm.3.normed_ref) | copy-start | bytes 7372804
  31.1 5.8 %copy-start.1 = (s32[1,4]{1,0:T(1,128)S(1)}, s32[1,4]{1,0:T(1,128)}, u32[]{:S(2)}) copy-start(s32[1,4]{1,0:T(1,128)} %counts_ref.1) | copy-start | bytes 52
  62.1 3.4 %collective-permute-start.13 = (bf16[4,4,80,360]{3,2,1,0:T(8,128)(2,1)S(1)}, bf16[4,4,80,360]{3,2,1,0:T(8,128)(2,1)S(1)}, u32[]{:S(2)}, u32[]{:S(2)}) collective-permute-start(bf16[4,4,80,360]{3,2,1,0:T(8,128)(2,1)S(1)} %get-tuple-element.38), channel_id=1, source_target_pairs={{0,4},{4,0},{8,12},{12,8},{16,20},{20,16},{24,28},{28,24},{1,5},{5... | collective-permute-start | bytes 2764808 | tf_op jit(solution)/shard_map/ppermute | solution.py:259
  62.1 3.3 %collective-permute-start.14 = (bf16[4,160,320]{2,1,0:T(8,128)(2,1)S(1)}, bf16[4,160,320]{2,1,0:T(8,128)(2,1)S(1)}, u32[]{:S(2)}, u32[]{:S(2)}) collective-permute-start(bf16[4,160,320]{2,1,0:T(8,128)(2,1)S(1)} %get-tuple-element.40), channel_id=1, source_target_pairs={{0,4},{4,0},{8,12},{12,8},{16,20},{20,16},{24,28},{28,24},{1,5},{5... | collective-permute-start | bytes 1228808 | tf_op jit(solution)/shard_map/ppermute | solution.py:259
  65.8 8.9 %collective-permute-start.15 = (bf16[1,4,80,360]{3,2,1,0:T(8,128)(2,1)S(1)}, bf16[1,4,80,360]{3,2,1,0:T(8,128)(2,1)S(1)}, u32[]{:S(2)}, u32[]{:S(2)}) collective-permute-start(bf16[1,4,80,360]{3,2,1,0:T(8,128)(2,1)S(1)} %get-tuple-element.43), channel_id=1, source_target_pairs={{0,1},{1,0},{2,3},{3,2},{4,5},{5,4},{6,7},{7,6},{8,9},{9,8},{10,11... | collective-permute-start | bytes 691208 | tf_op jit(solution)/shard_map/ppermute | solution.py:259
  65.9 14.6 %collective-permute-start.17 = (bf16[1,4,80,360]{3,2,1,0:T(8,128)(2,1)S(1)}, bf16[1,4,80,360]{3,2,1,0:T(8,128)(2,1)S(1)}, u32[]{:S(2)}, u32[]{:S(2)}) collective-permute-start(bf16[1,4,80,360]{3,2,1,0:T(8,128)(2,1)S(1)} %get-tuple-element.44), channel_id=1, source_target_pairs={{0,3},{1,2},{2,1},{3,0},{4,7},{5,6},{6,5},{7,4},{8,11},{9,10},{10,... | collective-permute-start | bytes 691208 | tf_op jit(solution)/shard_map/ppermute | solution.py:259
  68.9 12.9 %collective-permute-start.16 = (bf16[1,4,80,360]{3,2,1,0:T(8,128)(2,1)S(1)}, bf16[1,4,80,360]{3,2,1,0:T(8,128)(2,1)S(1)}, u32[]{:S(2)}, u32[]{:S(2)}) collective-permute-start(bf16[1,4,80,360]{3,2,1,0:T(8,128)(2,1)S(1)} %get-tuple-element.45), channel_id=1, source_target_pairs={{0,2},{1,3},{2,0},{3,1},{4,6},{5,7},{6,4},{7,5},{8,10},{9,11},{10,... | collective-permute-start | bytes 691208 | tf_op jit(solution)/shard_map/ppermute | solution.py:259
  69.4 14.0 %collective-permute-start.24 = (bf16[1,160,320]{2,1,0:T(8,128)(2,1)S(1)}, bf16[1,160,320]{2,1,0:T(8,128)(2,1)S(1)}, u32[]{:S(2)}, u32[]{:S(2)}) collective-permute-start(bf16[1,160,320]{2,1,0:T(8,128)(2,1)S(1)} %get-tuple-element.46), channel_id=1, source_target_pairs={{0,8},{4,12},{8,0},{12,4},{16,24},{20,28},{24,16},{28,20},{1,9},{5... | collective-permute-start | bytes 307208 | tf_op jit(solution)/shard_map/ppermute | solution.py:259
  69.5 16.1 %collective-permute-start.26 = (bf16[1,160,320]{2,1,0:T(8,128)(2,1)S(1)}, bf16[1,160,320]{2,1,0:T(8,128)(2,1)S(1)}, u32[]{:S(2)}, u32[]{:S(2)}) collective-permute-start(bf16[1,160,320]{2,1,0:T(8,128)(2,1)S(1)} %get-tuple-element.47), channel_id=1, source_target_pairs={{0,24},{4,28},{8,16},{12,20},{16,8},{20,12},{24,0},{28,4},{1,25},{... | collective-permute-start | bytes 307208 | tf_op jit(solution)/shard_map/ppermute | solution.py:259
  74.7 10.9 %collective-permute-start.25 = (bf16[1,160,320]{2,1,0:T(8,128)(2,1)S(1)}, bf16[1,160,320]{2,1,0:T(8,128)(2,1)S(1)}, u32[]{:S(2)}, u32[]{:S(2)}) collective-permute-start(bf16[1,160,320]{2,1,0:T(8,128)(2,1)S(1)} %get-tuple-element.48), channel_id=1, source_target_pairs={{0,16},{4,20},{8,24},{12,28},{16,0},{20,4},{24,8},{28,12},{1,17},{... | collective-permute-start | bytes 307208 | tf_op jit(solution)/shard_map/ppermute | solution.py:259
  82.0 6.7 %collective-permute-start.18 = (bf16[1,80,360]{2,1,0:T(8,128)(2,1)S(1)}, bf16[1,80,360]{2,1,0:T(8,128)(2,1)S(1)}, u32[]{:S(2)}, u32[]{:S(2)}) collective-permute-start(bf16[1,80,360]{2,1,0:T(8,128)(2,1)S(1)} %get-tuple-element.53), channel_id=1, source_target_pairs={{0,8},{4,12},{8,0},{12,4},{16,24},{20,28},{24,16},{28,20},{1,9},{5... | collective-permute-start | bytes 172808 | tf_op jit(solution)/shard_map/ppermute | solution.py:259
  82.1 7.1 %collective-permute-start.20 = (bf16[1,80,360]{2,1,0:T(8,128)(2,1)S(1)}, bf16[1,80,360]{2,1,0:T(8,128)(2,1)S(1)}, u32[]{:S(2)}, u32[]{:S(2)}) collective-permute-start(bf16[1,80,360]{2,1,0:T(8,128)(2,1)S(1)} %get-tuple-element.54), channel_id=1, source_target_pairs={{0,24},{4,28},{8,16},{12,20},{16,8},{20,12},{24,0},{28,4},{1,25},{... | collective-permute-start | bytes 172808 | tf_op jit(solution)/shard_map/ppermute | solution.py:259
  83.4 6.6 %collective-permute-start.19 = (bf16[1,80,360]{2,1,0:T(8,128)(2,1)S(1)}, bf16[1,80,360]{2,1,0:T(8,128)(2,1)S(1)}, u32[]{:S(2)}, u32[]{:S(2)}) collective-permute-start(bf16[1,80,360]{2,1,0:T(8,128)(2,1)S(1)} %get-tuple-element.55), channel_id=1, source_target_pairs={{0,16},{4,20},{8,24},{12,28},{16,0},{20,4},{24,8},{28,12},{1,17},{... | collective-permute-start | bytes 172808 | tf_op jit(solution)/shard_map/ppermute | solution.py:259
  85.7 7.5 %collective-permute-start.29 = (bf16[160,320]{1,0:T(8,128)(2,1)S(1)}, bf16[160,320]{1,0:T(8,128)(2,1)S(1)}, u32[]{:S(2)}, u32[]{:S(2)}) collective-permute-start(bf16[160,320]{1,0:T(8,128)(2,1)S(1)} %fusion.5), channel_id=1, source_target_pairs={{0,3},{1,2},{2,1},{3,0},{4,7},{5,6},{6,5},{7,4},{8,11},{9,10},{10,... | collective-permute-start | bytes 307208 | tf_op jit(solution)/shard_map/ppermute | solution.py:259
  86.9 6.7 %collective-permute-start.28 = (bf16[160,320]{1,0:T(8,128)(2,1)S(1)}, bf16[160,320]{1,0:T(8,128)(2,1)S(1)}, u32[]{:S(2)}, u32[]{:S(2)}) collective-permute-start(bf16[160,320]{1,0:T(8,128)(2,1)S(1)} %fusion.5), channel_id=1, source_target_pairs={{0,2},{1,3},{2,0},{3,1},{4,6},{5,7},{6,4},{7,5},{8,10},{9,11},{10,... | collective-permute-start | bytes 307208 | tf_op jit(solution)/shard_map/ppermute | solution.py:259
  88.7 5.0 %collective-permute-start.27 = (bf16[160,320]{1,0:T(8,128)(2,1)S(1)}, bf16[160,320]{1,0:T(8,128)(2,1)S(1)}, u32[]{:S(2)}, u32[]{:S(2)}) collective-permute-start(bf16[160,320]{1,0:T(8,128)(2,1)S(1)} %fusion.5), channel_id=1, source_target_pairs={{0,1},{1,0},{2,3},{3,2},{4,5},{5,4},{6,7},{7,6},{8,9},{9,8},{10,11... | collective-permute-start | bytes 307208 | tf_op jit(solution)/shard_map/ppermute | solution.py:259
  90.1 5.2 %collective-permute-start.23 = (bf16[1,80,360]{2,1,0:T(8,128)(2,1)S(1)}, bf16[1,80,360]{2,1,0:T(8,128)(2,1)S(1)}, u32[]{:S(2)}, u32[]{:S(2)}) collective-permute-start(bf16[1,80,360]{2,1,0:T(8,128)(2,1)S(1)} %fusion.7), channel_id=1, source_target_pairs={{0,3},{1,2},{2,1},{3,0},{4,7},{5,6},{6,5},{7,4},{8,11},{9,10},{10,... | collective-permute-start | bytes 172808 | tf_op jit(solution)/shard_map/ppermute | solution.py:259
  91.7 4.3 %collective-permute-start.22 = (bf16[1,80,360]{2,1,0:T(8,128)(2,1)S(1)}, bf16[1,80,360]{2,1,0:T(8,128)(2,1)S(1)}, u32[]{:S(2)}, u32[]{:S(2)}) collective-permute-start(bf16[1,80,360]{2,1,0:T(8,128)(2,1)S(1)} %fusion.7), channel_id=1, source_target_pairs={{0,2},{1,3},{2,0},{3,1},{4,6},{5,7},{6,4},{7,5},{8,10},{9,11},{10,... | collective-permute-start | bytes 172808 | tf_op jit(solution)/shard_map/ppermute | solution.py:259
  93.1 4.2 %collective-permute-start.21 = (bf16[1,80,360]{2,1,0:T(8,128)(2,1)S(1)}, bf16[1,80,360]{2,1,0:T(8,128)(2,1)S(1)}, u32[]{:S(2)}, u32[]{:S(2)}) collective-permute-start(bf16[1,80,360]{2,1,0:T(8,128)(2,1)S(1)} %fusion.7), channel_id=1, source_target_pairs={{0,1},{1,0},{2,3},{3,2},{4,5},{5,4},{6,7},{7,6},{8,9},{9,8},{10,11... | collective-permute-start | bytes 172808 | tf_op jit(solution)/shard_map/ppermute | solution.py:259

commit v11 on v10

--- a/solution.py
+++ b/solution.py
@@ -216,20 +216,15 @@
     step = tiles_per_step(number)
     steps = number // step
 
-    def whole(shape):
-        return pl.BlockSpec(shape, lambda i, c: (0,) * len(shape))
-
+    resident = pl.BlockSpec(memory_space=pltpu.VMEM)
     block = pl.BlockSpec((step, channels, pixels), lambda i, c: (i, 0, 0))
     return pl.pallas_call(
         functools.partial(conv_kernel, steps),
         grid_spec=pltpu.PrefetchScalarGridSpec(
             num_scalar_prefetch=1,
             grid=(steps,),
-            in_specs=[whole(own.shape)] * 2
-            + [whole(own_time.shape)] * 2
-            + [whole(features.shape)]
-            + [block] * 3,
-            out_specs=[block] + [whole(own.shape)] * 2 + [whole(own_time.shape)] * 2,
+            in_specs=[resident] * 5 + [block] * 3,
+            out_specs=[block] + [resident] * 4,
             scratch_shapes=[
                 pltpu.VMEM((outs, depth), bf16),
                 pltpu.VMEM((emb, outs), f32),
@@ -246,7 +241,7 @@
             jax.ShapeDtypeStruct(own_time.shape, bf16),
             jax.ShapeDtypeStruct(own_time.shape, bf16),
         ],
-        compiler_params=pltpu.CompilerParams(vmem_limit_bytes=44 * 2**20),
+        compiler_params=pltpu.CompilerParams(vmem_limit_bytes=32 * 2**20),
         cost_estimate=pl.CostEstimate(
             flops=4 * number * pixels * depth * outs, bytes_accessed=8 * tiles.size, transcendentals=0
         ),
@@ -304,10 +299,9 @@
 def time_features(timesteps, emb):
     half_width = emb // 2
     frequency = jnp.exp(-math.log(10000.0) * jnp.arange(half_width, dtype=f32) / half_width)
-    angles = timesteps.astype(f32)[:, None] * frequency[None, :]
-    waves = jnp.concatenate([jnp.cos(angles), jnp.sin(angles)], axis=1)
-    features = jax.nn.silu(waves).astype(bf16)
-    return jnp.pad(features, ((0, LANES - features.shape[0]), (0, 0))).T
+    timesteps = jnp.pad(timesteps, (0, LANES - timesteps.shape[0]))
+    angles = frequency[:, None] * timesteps.astype(f32)[None, :]
+    return jax.nn.silu(jnp.concatenate([jnp.cos(angles), jnp.sin(angles)])).astype(bf16)
 
 
 def per_device(latents, target_noise, counts, timesteps, conv_master, temb_master):

time: 98.7 us -> 90.5 us (0.917)
  starting transfers between devices: 30.8 us -> 39.2 us
  Pallas kernels: 35 us -> 27.1 us
  other arithmetic: 9.61 us -> 6.56 us
  local copies, waits for them, and re-layouts: 4.2 us -> 1.24 us
  waiting for transfers between devices: 17.8 us -> 15.1 us
    ppermute x30, starting transfers between devices: 30.8 us -> 39.2 us  [swap(): return lax.ppermute(values, axis, pairs)]
    pallas_call x1, Pallas kernels: 25.1 us -> 17.2 us  [conv_both(): pl.pallas_call(functools.partial(conv_kernel, steps), grid_spec=pltpu.Pre...]
    ppermute x30, waiting for transfers between devices: 17.8 us -> 15.1 us  [swap(): return lax.ppermute(values, axis, pairs)]
    concatenate x1 -> x0, local copies, waits for them, and re-layouts: 1.12 us -> none  [time_features(): waves = jnp.concatenate([jnp.cos(angles), jnp.sin(angles)], axis=1)]
    concatenate x1, other arithmetic: 1.35 us -> 0.25 us  [per_device(): own = jnp.concatenate([mine, jnp.concatenate(far)], axis=1)]
    concatenate x1, other arithmetic: 1.35 us -> 0.26 us  [per_device(): other = jnp.concatenate([other_mine, jnp.concatenate(other_far)], axis=1)]
    convert_element_type x2, other arithmetic: 1.27 us -> 0.19 us  [the longest x1 0.18 us: time_features(): jax.nn.silu(jnp.concatenate([jnp.cos(angles), jnp.sin(angles)]))]
  transfers between devices with their start and end apart: 30 -> 30, of which waited for: 8 -> 7; matrix products, arithmetic and copies ran while one was open for 12% -> 5% of each run, Pallas kernels for 10% -> 11%
where the time goes in v11:
time: 90.5 us; the launch traced here: 90.2 us
  starting transfers between devices  39.2 us (43%)
  Pallas kernels  27.1 us (30%)
  waiting for transfers between devices  15.1 us (17%)
  other arithmetic  6.56 us (7%)
  local copies, waits for them, and re-layouts  1.24 us (1%)
  between operations  0.95 us (1%)
    ppermute x30, starting transfers between devices, swap(): return lax.ppermute(values, axis, pairs)  39.2 us
    pallas_call x1, Pallas kernels, conv_both(): pl.pallas_call(functools.partial(conv_kernel, steps), grid_spec=pltpu.Pre...  17.2 us
    ppermute x30, waiting for transfers between devices, swap(): return lax.ppermute(values, axis, pairs)  15.1 us
    pallas_call x2, Pallas kernels, group_norm(): pl.pallas_call(functools.partial(norm_kernel, group_width), grid=(last -...  9.88 us
  transfers between devices with their start and end apart: 30, of which 7 were waited for; matrix products, arithmetic and copies ran while one was open for 5% of the time, Pallas kernels for 11%

profile of v11, /device:TPU:0, one launch (start us, length us, event | category | flops | bytes accessed | tf_op | source)
XLA Modules:
  0.0 90.2 jit_solution(9322137769442172090)
XLA Ops:
  0.6 1.1 %convert_element_type.135 = bf16[360,320]{0,1:T(8,128)(2,1)S(1)} convert(f32[360,320]{0,1:T(8,128)} %param.12) | non-fusion elementwise | flops 115200 | bytes 691200 | tf_op jit(solution)/shard_map/convert_element_type | solution.py:321
  1.8 5.1 %collective-permute-start.2 = (bf16[1,80,360]{2,1,0:T(8,128)(2,1)S(1)}, bf16[1,80,360]{2,1,0:T(8,128)(2,1)S(1)}, u32[]{:S(2)}, u32[]{:S(2)}) collective-permute-start(bf16[1,80,360]{2,1,0:T(8,128)(2,1)S(1)} %get-tuple-element.63), channel_id=1, source_target_pairs={{0,24},{4,28},{8,16},{12,20},{16,8},{20,12},{24,0},{28,4},{1,25},{... | collective-permute-start | bytes 172808 | tf_op jit(solution)/shard_map/ppermute | solution.py:254
  6.9 0.6 collective-permute-start
  7.5 1.0 %convert_bitcast_fusion.2 = (bf16[1,1,160,320]{3,2,1,0:T(8,128)(2,1)S(1)}, bf16[1,160,320]{2,1,0:T(8,128)(2,1)S(1)}) fusion(f32[160,320]{1,0:T(8,128)} %param.13), kind=kLoop, calls=%fused_computation.46 | loop fusion | flops 51200 | bytes 409600 | tf_op jit(solution)/shard_map/stack;broadcast_in_dim | solution.py:270
  8.5 2.4 %collective-permute-start.6 = (bf16[1,160,320]{2,1,0:T(8,128)(2,1)S(1)}, bf16[1,160,320]{2,1,0:T(8,128)(2,1)S(1)}, u32[]{:S(2)}, u32[]{:S(2)}) collective-permute-start(bf16[1,160,320]{2,1,0:T(8,128)(2,1)S(1)} %get-tuple-element.59), channel_id=1, source_target_pairs={{0,16},{4,20},{8,24},{12,28},{16,0},{20,4},{24,8},{28,12},{1,17},{... | collective-permute-start | bytes 307208 | tf_op jit(solution)/shard_map/ppermute | solution.py:254
  10.9 4.0 %group_norm.2.refs_0_ = bf16[15,320,256]{2,1,0:T(8,128)(2,1)} custom-call(bf16[320,320]{1,0:T(8,128)(2,1)} %constant.45.clone.same_ref, bf16[15,320,256]{2,1,0:T(8,128)(2,1)} %bitcast.98), custom_call_target="tpu_custom_call" | custom-call | flops 8192000 | bytes 1638400 | tf_op jit(solution)/shard_map/group_norm/pallas_call | solution.py:62
  15.1 2.5 %collective-permute-start.5 = (bf16[1,3,80,360]{3,2,1,0:T(8,128)(2,1)S(1)}, bf16[1,3,80,360]{3,2,1,0:T(8,128)(2,1)S(1)}, u32[]{:S(2)}, u32[]{:S(2)}) collective-permute-start(bf16[1,3,80,360]{3,2,1,0:T(8,128)(2,1)S(1)} %get-tuple-element.57), channel_id=1, source_target_pairs={{0,3},{1,2},{2,1},{3,0},{4,7},{5,6},{6,5},{7,4},{8,11},{9,10},{10,... | collective-permute-start | bytes 518408 | tf_op jit(solution)/shard_map/ppermute | solution.py:254
  17.6 0.5 collective-permute-start.4
  18.1 0.5 collective-permute-start.3
  18.7 2.1 %collective-permute-start.11 = (bf16[1,2,160,320]{3,2,1,0:T(8,128)(2,1)S(1)}, bf16[1,2,160,320]{3,2,1,0:T(8,128)(2,1)S(1)}, u32[]{:S(2)}, u32[]{:S(2)}) collective-permute-start(bf16[1,2,160,320]{3,2,1,0:T(8,128)(2,1)S(1)} %bitcast.110), channel_id=1, source_target_pairs={{0,8},{4,12},{8,0},{12,4},{16,24},{20,28},{24,16},{28,20},{1,9},{5... | collective-permute-start | bytes 614408 | tf_op jit(solution)/shard_map/ppermute | solution.py:254
  20.9 5.8 %group_norm.3.normed_ref = bf16[15,320,256]{2,1,0:T(8,128)(2,1)} custom-call(bf16[320,320]{1,0:T(8,128)(2,1)} %constant.45.clone.same_ref, bf16[15,320,256]{2,1,0:T(8,128)(2,1)} %bitcast.99, bf16[15,320,256]{2,1,0:T(8,128)(2,1)} %group_norm.2.refs_0_), custom_call_target="tpu_custom_call", output_to_operand_aliasing={{}: (2, {})} | custom-call | flops 16384000 | bytes 3276800 | tf_op jit(solution)/shard_map/group_norm/pallas_call | solution.py:62
  26.7 0.5 collective-permute-start.10
  27.3 0.4 collective-permute-start.8
  27.8 0.3 maximum_maximum_fusion.own_ref
  28.0 0.1 maximum_bitcast_fusion
  28.3 0.1 collective-permute-start.12
  28.4 1.2 %multiply_cosine_fusion = (f32[640,128]{1,0:T(8,128)S(1)}, f32[640,128]{1,0:T(8,128)S(1)}) fusion(f32[128]{0:T(128)S(1)} %pad_convert_fusion, f32[640]{0:T(1024)S(1)} %multiply_exponential_fusion), kind=kLoop, calls=%fused_computation.12 | loop fusion | flops 81920 | bytes 658432 | tf_op jit(solution)/shard_map/cos | solution.py:304
  29.6 0.2 multiply_convert_fusion.features_ref
  29.9 0.3 maximum_maximum_fusion.1.other_ref
  30.2 0.1 copy-done.1
  30.3 0.8 copy-done
  31.1 17.2 %conv_both.1 = (bf16[15,320,256]{2,1,0:T(8,128)(2,1)}, bf16[4,4,80,360]{3,2,1,0:T(8,128)(2,1)S(1)}, bf16[4,4,80,360]{3,2,1,0:T(8,128)(2,1)S(1)}, bf16[4,160,320]...) custom-call(s32[1,4]{1,0:T(1,128)S(1)} %copy-done.3, bf16[4,4,80,360]{3,2,1,0:T(8,128)(2,1)S(1)} %maximum_maximum_fusion.own_ref, ...), custom_call_target="tpu_custom_call" | custom-call | flops 14155776000 | bytes 9830400 | tf_op jit(solution)/shard_map/conv_both/pallas_call | solution.py:221
  48.3 0.5 collective-permute-start.14
  48.8 2.8 %collective-permute-done.14 = bf16[4,160,320]{2,1,0:T(8,128)(2,1)S(1)} collective-permute-done((bf16[4,160,320]{2,1,0:T(8,128)(2,1)S(1)}, bf16[4,160,320]{2,1,0:T(8,128)(2,1)S(1)}, u32[]{:S(2)}, u32[]{:S(2)}) %collective-permute-start.14) | collective-permute-done | bytes 409632 | tf_op jit(solution)/shard_map/ppermute | solution.py:254
  51.6 0.1 add_convert_fusion.1
  51.7 0.3 add_convert_fusion
  52.1 8.8 %collective-permute-start.17 = (bf16[1,4,80,360]{3,2,1,0:T(8,128)(2,1)S(1)}, bf16[1,4,80,360]{3,2,1,0:T(8,128)(2,1)S(1)}, u32[]{:S(2)}, u32[]{:S(2)}) collective-permute-start(bf16[1,4,80,360]{3,2,1,0:T(8,128)(2,1)S(1)} %get-tuple-element.44), channel_id=1, source_target_pairs={{0,3},{1,2},{2,1},{3,0},{4,7},{5,6},{6,5},{7,4},{8,11},{9,10},{10,... | collective-permute-start | bytes 691208 | tf_op jit(solution)/shard_map/ppermute | solution.py:254
  61.0 0.5 collective-permute-start.16
  61.6 1.5 %collective-permute-start.26 = (bf16[1,160,320]{2,1,0:T(8,128)(2,1)S(1)}, bf16[1,160,320]{2,1,0:T(8,128)(2,1)S(1)}, u32[]{:S(2)}, u32[]{:S(2)}) collective-permute-start(bf16[1,160,320]{2,1,0:T(8,128)(2,1)S(1)} %get-tuple-element.47), channel_id=1, source_target_pairs={{0,24},{4,28},{8,16},{12,20},{16,8},{20,12},{24,0},{28,4},{1,25},{... | collective-permute-start | bytes 307208 | tf_op jit(solution)/shard_map/ppermute | solution.py:254
  63.0 2.0 %collective-permute-start.25 = (bf16[1,160,320]{2,1,0:T(8,128)(2,1)S(1)}, bf16[1,160,320]{2,1,0:T(8,128)(2,1)S(1)}, u32[]{:S(2)}, u32[]{:S(2)}) collective-permute-start(bf16[1,160,320]{2,1,0:T(8,128)(2,1)S(1)} %get-tuple-element.48), channel_id=1, source_target_pairs={{0,16},{4,20},{8,24},{12,28},{16,0},{20,4},{24,8},{28,12},{1,17},{... | collective-permute-start | bytes 307208 | tf_op jit(solution)/shard_map/ppermute | solution.py:254
  65.0 7.5 %collective-permute-done.17 = bf16[1,4,80,360]{3,2,1,0:T(8,128)(2,1)S(1)} collective-permute-done((bf16[1,4,80,360]{3,2,1,0:T(8,128)(2,1)S(1)}, bf16[1,4,80,360]{3,2,1,0:T(8,128)(2,1)S(1)}, u32[]{:S(2)}, u32[]{:S(2)}) %collective-permute-start.17) | collective-permute-done | bytes 230432 | tf_op jit(solution)/shard_map/ppermute | solution.py:254
  72.5 1.4 %collective-permute-done.16 = bf16[1,4,80,360]{3,2,1,0:T(8,128)(2,1)S(1)} collective-permute-done((bf16[1,4,80,360]{3,2,1,0:T(8,128)(2,1)S(1)}, bf16[1,4,80,360]{3,2,1,0:T(8,128)(2,1)S(1)}, u32[]{:S(2)}, u32[]{:S(2)}) %collective-permute-start.16) | collective-permute-done | bytes 230432 | tf_op jit(solution)/shard_map/ppermute | solution.py:254
  73.9 0.1 fusion.1
  74.1 0.2 collective-permute-start.18
  74.3 1.6 %collective-permute-start.20 = (bf16[1,80,360]{2,1,0:T(8,128)(2,1)S(1)}, bf16[1,80,360]{2,1,0:T(8,128)(2,1)S(1)}, u32[]{:S(2)}, u32[]{:S(2)}) collective-permute-start(bf16[1,80,360]{2,1,0:T(8,128)(2,1)S(1)} %get-tuple-element.54), channel_id=1, source_target_pairs={{0,24},{4,28},{8,16},{12,20},{16,8},{20,12},{24,0},{28,4},{1,25},{... | collective-permute-start | bytes 172808 | tf_op jit(solution)/shard_map/ppermute | solution.py:254
  75.8 1.8 %collective-permute-start.19 = (bf16[1,80,360]{2,1,0:T(8,128)(2,1)S(1)}, bf16[1,80,360]{2,1,0:T(8,128)(2,1)S(1)}, u32[]{:S(2)}, u32[]{:S(2)}) collective-permute-start(bf16[1,80,360]{2,1,0:T(8,128)(2,1)S(1)} %get-tuple-element.55), channel_id=1, source_target_pairs={{0,16},{4,20},{8,24},{12,28},{16,0},{20,4},{24,8},{28,12},{1,17},{... | collective-permute-start | bytes 172808 | tf_op jit(solution)/shard_map/ppermute | solution.py:254
  77.7 1.2 %collective-permute-start.29 = (bf16[160,320]{1,0:T(8,128)(2,1)S(1)}, bf16[160,320]{1,0:T(8,128)(2,1)S(1)}, u32[]{:S(2)}, u32[]{:S(2)}) collective-permute-start(bf16[160,320]{1,0:T(8,128)(2,1)S(1)} %fusion.5), channel_id=1, source_target_pairs={{0,3},{1,2},{2,1},{3,0},{4,7},{5,6},{6,5},{7,4},{8,11},{9,10},{10,... | collective-permute-start | bytes 307208 | tf_op jit(solution)/shard_map/ppermute | solution.py:254
  79.0 2.0 %collective-permute-start.28 = (bf16[160,320]{1,0:T(8,128)(2,1)S(1)}, bf16[160,320]{1,0:T(8,128)(2,1)S(1)}, u32[]{:S(2)}, u32[]{:S(2)}) collective-permute-start(bf16[160,320]{1,0:T(8,128)(2,1)S(1)} %fusion.5), channel_id=1, source_target_pairs={{0,2},{1,3},{2,0},{3,1},{4,6},{5,7},{6,4},{7,5},{8,10},{9,11},{10,... | collective-permute-start | bytes 307208 | tf_op jit(solution)/shard_map/ppermute | solution.py:254
  80.9 0.4 collective-permute-start.27
  81.3 0.9 collective-permute-done.19
  82.2 2.3 %collective-permute-start.23 = (bf16[1,80,360]{2,1,0:T(8,128)(2,1)S(1)}, bf16[1,80,360]{2,1,0:T(8,128)(2,1)S(1)}, u32[]{:S(2)}, u32[]{:S(2)}) collective-permute-start(bf16[1,80,360]{2,1,0:T(8,128)(2,1)S(1)} %fusion.7), channel_id=1, source_target_pairs={{0,3},{1,2},{2,1},{3,0},{4,7},{5,6},{6,5},{7,4},{8,11},{9,10},{10,... | collective-permute-start | bytes 172808 | tf_op jit(solution)/shard_map/ppermute | solution.py:254
  84.5 0.5 collective-permute-start.22
  85.1 1.0 %collective-permute-start.21 = (bf16[1,80,360]{2,1,0:T(8,128)(2,1)S(1)}, bf16[1,80,360]{2,1,0:T(8,128)(2,1)S(1)}, u32[]{:S(2)}, u32[]{:S(2)}) collective-permute-start(bf16[1,80,360]{2,1,0:T(8,128)(2,1)S(1)} %fusion.7), channel_id=1, source_target_pairs={{0,1},{1,0},{2,3},{3,2},{4,5},{5,4},{6,7},{7,6},{8,9},{9,8},{10,11... | collective-permute-start | bytes 172808 | tf_op jit(solution)/shard_map/ppermute | solution.py:254
  86.0 0.8 fusion.4
  86.8 0.7 collective-permute-done.23
  87.5 1.2 %collective-permute-done.22 = bf16[1,80,360]{2,1,0:T(8,128)(2,1)S(1)} collective-permute-done((bf16[1,80,360]{2,1,0:T(8,128)(2,1)S(1)}, bf16[1,80,360]{2,1,0:T(8,128)(2,1)S(1)}, u32[]{:S(2)}, u32[]{:S(2)}) %collective-permute-start.22) | collective-permute-done | bytes 57632 | tf_op jit(solution)/shard_map/ppermute | solution.py:254
  88.8 0.5 collective-permute-done.21
  89.4 0.8 convert_bitcast_fusion
  (55 shorter events, 1.1 us)
Async XLA Ops:
  1.8 13.2 %collective-permute-start.2 = (bf16[1,80,360]{2,1,0:T(8,128)(2,1)S(1)}, bf16[1,80,360]{2,1,0:T(8,128)(2,1)S(1)}, u32[]{:S(2)}, u32[]{:S(2)}) collective-permute-start(bf16[1,80,360]{2,1,0:T(8,128)(2,1)S(1)} %get-tuple-element.63), channel_id=1, source_target_pairs={{0,24},{4,28},{8,16},{12,20},{16,8},{20,12},{24,0},{28,4},{1,25},{... | collective-permute-start | bytes 172808 | tf_op jit(solution)/shard_map/ppermute | solution.py:254
  6.9 8.1 %collective-permute-start.1 = (bf16[1,80,360]{2,1,0:T(8,128)(2,1)S(1)}, bf16[1,80,360]{2,1,0:T(8,128)(2,1)S(1)}, u32[]{:S(2)}, u32[]{:S(2)}) collective-permute-start(bf16[1,80,360]{2,1,0:T(8,128)(2,1)S(1)} %get-tuple-element.63), channel_id=1, source_target_pairs={{0,16},{4,20},{8,24},{12,28},{16,0},{20,4},{24,8},{28,12},{1,17},{... | collective-permute-start | bytes 172808 | tf_op jit(solution)/shard_map/ppermute | solution.py:254
  6.9 8.1 %collective-permute-start = (bf16[1,80,360]{2,1,0:T(8,128)(2,1)S(1)}, bf16[1,80,360]{2,1,0:T(8,128)(2,1)S(1)}, u32[]{:S(2)}, u32[]{:S(2)}) collective-permute-start(bf16[1,80,360]{2,1,0:T(8,128)(2,1)S(1)} %get-tuple-element.63), channel_id=1, source_target_pairs={{0,8},{4,12},{8,0},{12,4},{16,24},{20,28},{24,16},{28,20},{1,9},{5... | collective-permute-start | bytes 172808 | tf_op jit(solution)/shard_map/ppermute | solution.py:254
  8.5 10.2 %collective-permute-start.6 = (bf16[1,160,320]{2,1,0:T(8,128)(2,1)S(1)}, bf16[1,160,320]{2,1,0:T(8,128)(2,1)S(1)}, u32[]{:S(2)}, u32[]{:S(2)}) collective-permute-start(bf16[1,160,320]{2,1,0:T(8,128)(2,1)S(1)} %get-tuple-element.59), channel_id=1, source_target_pairs={{0,16},{4,20},{8,24},{12,28},{16,0},{20,4},{24,8},{28,12},{1,17},{... | collective-permute-start | bytes 307208 | tf_op jit(solution)/shard_map/ppermute | solution.py:254
  15.1 11.6 %collective-permute-start.5 = (bf16[1,3,80,360]{3,2,1,0:T(8,128)(2,1)S(1)}, bf16[1,3,80,360]{3,2,1,0:T(8,128)(2,1)S(1)}, u32[]{:S(2)}, u32[]{:S(2)}) collective-permute-start(bf16[1,3,80,360]{3,2,1,0:T(8,128)(2,1)S(1)} %get-tuple-element.57), channel_id=1, source_target_pairs={{0,3},{1,2},{2,1},{3,0},{4,7},{5,6},{6,5},{7,4},{8,11},{9,10},{10,... | collective-permute-start | bytes 518408 | tf_op jit(solution)/shard_map/ppermute | solution.py:254
  17.6 9.6 %collective-permute-start.4 = (bf16[1,3,80,360]{3,2,1,0:T(8,128)(2,1)S(1)}, bf16[1,3,80,360]{3,2,1,0:T(8,128)(2,1)S(1)}, u32[]{:S(2)}, u32[]{:S(2)}) collective-permute-start(bf16[1,3,80,360]{3,2,1,0:T(8,128)(2,1)S(1)} %get-tuple-element.57), channel_id=1, source_target_pairs={{0,2},{1,3},{2,0},{3,1},{4,6},{5,7},{6,4},{7,5},{8,10},{9,11},{10,... | collective-permute-start | bytes 518408 | tf_op jit(solution)/shard_map/ppermute | solution.py:254
  18.1 9.2 %collective-permute-start.3 = (bf16[1,3,80,360]{3,2,1,0:T(8,128)(2,1)S(1)}, bf16[1,3,80,360]{3,2,1,0:T(8,128)(2,1)S(1)}, u32[]{:S(2)}, u32[]{:S(2)}) collective-permute-start(bf16[1,3,80,360]{3,2,1,0:T(8,128)(2,1)S(1)} %get-tuple-element.57), channel_id=1, source_target_pairs={{0,1},{1,0},{2,3},{3,2},{4,5},{5,4},{6,7},{7,6},{8,9},{9,8},{10,11... | collective-permute-start | bytes 518408 | tf_op jit(solution)/shard_map/ppermute | solution.py:254
  18.7 9.3 %collective-permute-start.11 = (bf16[1,2,160,320]{3,2,1,0:T(8,128)(2,1)S(1)}, bf16[1,2,160,320]{3,2,1,0:T(8,128)(2,1)S(1)}, u32[]{:S(2)}, u32[]{:S(2)}) collective-permute-start(bf16[1,2,160,320]{3,2,1,0:T(8,128)(2,1)S(1)} %bitcast.110), channel_id=1, source_target_pairs={{0,8},{4,12},{8,0},{12,4},{16,24},{20,28},{24,16},{28,20},{1,9},{5... | collective-permute-start | bytes 614408 | tf_op jit(solution)/shard_map/ppermute | solution.py:254
  26.7 1.5 %copy-start.4 = (s32[1,15]{1,0:T(1,128)S(1)}, s32[1,15]{1,0:T(1,128)}, u32[]{:S(2)}) copy-start(s32[1,15]{1,0:T(1,128)} %param.11) | copy-start | bytes 184
  26.7 3.1 %collective-permute-start.7 = (bf16[7,80,360]{2,1,0:T(8,128)(2,1)S(1)}, bf16[7,80,360]{2,1,0:T(8,128)(2,1)S(1)}, u32[]{:S(2)}, u32[]{:S(2)}) collective-permute-start(bf16[7,80,360]{2,1,0:T(8,128)(2,1)S(1)} %pad_maximum_fusion.1), channel_id=1, source_target_pairs={{0,4},{4,0},{8,12},{12,8},{16,20},{20,16},{24,28},{28,24},{1,5},{5... | collective-permute-start | bytes 1209608 | tf_op jit(solution)/shard_map/ppermute | solution.py:254
  26.7 3.1 %collective-permute-start.10 = (bf16[1,3,80,360]{3,2,1,0:T(8,128)(2,1)S(1)}, bf16[1,3,80,360]{3,2,1,0:T(8,128)(2,1)S(1)}, u32[]{:S(2)}, u32[]{:S(2)}) collective-permute-start(bf16[1,3,80,360]{3,2,1,0:T(8,128)(2,1)S(1)} %collective-permute-done.5), channel_id=1, source_target_pairs={{0,4},{4,0},{8,12},{12,8},{16,20},{20,16},{24,28},{28,24},{1,5},{5... | collective-permute-start | bytes 518408 | tf_op jit(solution)/shard_map/ppermute | solution.py:254
  27.3 2.6 %collective-permute-start.9 = (bf16[1,3,80,360]{3,2,1,0:T(8,128)(2,1)S(1)}, bf16[1,3,80,360]{3,2,1,0:T(8,128)(2,1)S(1)}, u32[]{:S(2)}, u32[]{:S(2)}) collective-permute-start(bf16[1,3,80,360]{3,2,1,0:T(8,128)(2,1)S(1)} %collective-permute-done.4), channel_id=1, source_target_pairs={{0,4},{4,0},{8,12},{12,8},{16,20},{20,16},{24,28},{28,24},{1,5},{5... | collective-permute-start | bytes 518408 | tf_op jit(solution)/shard_map/ppermute | solution.py:254
  27.3 2.6 %collective-permute-start.8 = (bf16[1,3,80,360]{3,2,1,0:T(8,128)(2,1)S(1)}, bf16[1,3,80,360]{3,2,1,0:T(8,128)(2,1)S(1)}, u32[]{:S(2)}, u32[]{:S(2)}) collective-permute-start(bf16[1,3,80,360]{3,2,1,0:T(8,128)(2,1)S(1)} %collective-permute-done.3), channel_id=1, source_target_pairs={{0,4},{4,0},{8,12},{12,8},{16,20},{20,16},{24,28},{28,24},{1,5},{5... | collective-permute-start | bytes 518408 | tf_op jit(solution)/shard_map/ppermute | solution.py:254
  27.8 2.4 %copy-start.2 = (bf16[1,15,256,320]{2,3,1,0:T(8,128)(2,1)S(1)}, bf16[1,15,256,320]{2,3,1,0:T(8,128)(2,1)}, u32[]{:S(2)}) copy-start(bf16[1,15,256,320]{2,3,1,0:T(8,128)(2,1)} %param.9) | copy-start | bytes 7372804
  28.1 2.2 %copy-start.1 = (bf16[15,320,256]{2,1,0:T(8,128)(2,1)S(1)}, bf16[15,320,256]{2,1,0:T(8,128)(2,1)}, u32[]{:S(2)}) copy-start(bf16[15,320,256]{2,1,0:T(8,128)(2,1)} %group_norm.3.normed_ref) | copy-start | bytes 7372804
  28.2 2.8 %copy-start = (bf16[1,15,256,320]{2,3,1,0:T(8,128)(2,1)S(1)}, bf16[1,15,256,320]{2,3,1,0:T(8,128)(2,1)}, u32[]{:S(2)}) copy-start(bf16[1,15,256,320]{2,3,1,0:T(8,128)(2,1)} %param.8) | copy-start | bytes 7372804
  28.2 2.8 %copy-start.3 = (s32[1,4]{1,0:T(1,128)S(1)}, s32[1,4]{1,0:T(1,128)}, u32[]{:S(2)}) copy-start(s32[1,4]{1,0:T(1,128)} %counts_ref.1) | copy-start | bytes 52
  28.3 1.9 %collective-permute-start.12 = (bf16[4,160,320]{2,1,0:T(8,128)(2,1)S(1)}, bf16[4,160,320]{2,1,0:T(8,128)(2,1)S(1)}, u32[]{:S(2)}, u32[]{:S(2)}) collective-permute-start(bf16[4,160,320]{2,1,0:T(8,128)(2,1)S(1)} %bitcast.101), channel_id=1, source_target_pairs={{0,4},{4,0},{8,12},{12,8},{16,20},{20,16},{24,28},{28,24},{1,5},{5... | collective-permute-start | bytes 1228808 | tf_op jit(solution)/shard_map/ppermute | solution.py:254
  48.3 3.4 %collective-permute-start.13 = (bf16[4,4,80,360]{3,2,1,0:T(8,128)(2,1)S(1)}, bf16[4,4,80,360]{3,2,1,0:T(8,128)(2,1)S(1)}, u32[]{:S(2)}, u32[]{:S(2)}) collective-permute-start(bf16[4,4,80,360]{3,2,1,0:T(8,128)(2,1)S(1)} %get-tuple-element.38), channel_id=1, source_target_pairs={{0,4},{4,0},{8,12},{12,8},{16,20},{20,16},{24,28},{28,24},{1,5},{5... | collective-permute-start | bytes 2764808 | tf_op jit(solution)/shard_map/ppermute | solution.py:254
  48.3 3.3 %collective-permute-start.14 = (bf16[4,160,320]{2,1,0:T(8,128)(2,1)S(1)}, bf16[4,160,320]{2,1,0:T(8,128)(2,1)S(1)}, u32[]{:S(2)}, u32[]{:S(2)}) collective-permute-start(bf16[4,160,320]{2,1,0:T(8,128)(2,1)S(1)} %get-tuple-element.40), channel_id=1, source_target_pairs={{0,4},{4,0},{8,12},{12,8},{16,20},{20,16},{24,28},{28,24},{1,5},{5... | collective-permute-start | bytes 1228808 | tf_op jit(solution)/shard_map/ppermute | solution.py:254
  52.0 11.0 %collective-permute-start.15 = (bf16[1,4,80,360]{3,2,1,0:T(8,128)(2,1)S(1)}, bf16[1,4,80,360]{3,2,1,0:T(8,128)(2,1)S(1)}, u32[]{:S(2)}, u32[]{:S(2)}) collective-permute-start(bf16[1,4,80,360]{3,2,1,0:T(8,128)(2,1)S(1)} %get-tuple-element.43), channel_id=1, source_target_pairs={{0,1},{1,0},{2,3},{3,2},{4,5},{5,4},{6,7},{7,6},{8,9},{9,8},{10,11... | collective-permute-start | bytes 691208 | tf_op jit(solution)/shard_map/ppermute | solution.py:254
  52.1 20.4 %collective-permute-start.17 = (bf16[1,4,80,360]{3,2,1,0:T(8,128)(2,1)S(1)}, bf16[1,4,80,360]{3,2,1,0:T(8,128)(2,1)S(1)}, u32[]{:S(2)}, u32[]{:S(2)}) collective-permute-start(bf16[1,4,80,360]{3,2,1,0:T(8,128)(2,1)S(1)} %get-tuple-element.44), channel_id=1, source_target_pairs={{0,3},{1,2},{2,1},{3,0},{4,7},{5,6},{6,5},{7,4},{8,11},{9,10},{10,... | collective-permute-start | bytes 691208 | tf_op jit(solution)/shard_map/ppermute | solution.py:254
  61.0 13.0 %collective-permute-start.16 = (bf16[1,4,80,360]{3,2,1,0:T(8,128)(2,1)S(1)}, bf16[1,4,80,360]{3,2,1,0:T(8,128)(2,1)S(1)}, u32[]{:S(2)}, u32[]{:S(2)}) collective-permute-start(bf16[1,4,80,360]{3,2,1,0:T(8,128)(2,1)S(1)} %get-tuple-element.45), channel_id=1, source_target_pairs={{0,2},{1,3},{2,0},{3,1},{4,6},{5,7},{6,4},{7,5},{8,10},{9,11},{10,... | collective-permute-start | bytes 691208 | tf_op jit(solution)/shard_map/ppermute | solution.py:254
  61.5 14.4 %collective-permute-start.24 = (bf16[1,160,320]{2,1,0:T(8,128)(2,1)S(1)}, bf16[1,160,320]{2,1,0:T(8,128)(2,1)S(1)}, u32[]{:S(2)}, u32[]{:S(2)}) collective-permute-start(bf16[1,160,320]{2,1,0:T(8,128)(2,1)S(1)} %get-tuple-element.46), channel_id=1, source_target_pairs={{0,8},{4,12},{8,0},{12,4},{16,24},{20,28},{24,16},{28,20},{1,9},{5... | collective-permute-start | bytes 307208 | tf_op jit(solution)/shard_map/ppermute | solution.py:254
  61.6 16.1 %collective-permute-start.26 = (bf16[1,160,320]{2,1,0:T(8,128)(2,1)S(1)}, bf16[1,160,320]{2,1,0:T(8,128)(2,1)S(1)}, u32[]{:S(2)}, u32[]{:S(2)}) collective-permute-start(bf16[1,160,320]{2,1,0:T(8,128)(2,1)S(1)} %get-tuple-element.47), channel_id=1, source_target_pairs={{0,24},{4,28},{8,16},{12,20},{16,8},{20,12},{24,0},{28,4},{1,25},{... | collective-permute-start | bytes 307208 | tf_op jit(solution)/shard_map/ppermute | solution.py:254
  63.0 14.6 %collective-permute-start.25 = (bf16[1,160,320]{2,1,0:T(8,128)(2,1)S(1)}, bf16[1,160,320]{2,1,0:T(8,128)(2,1)S(1)}, u32[]{:S(2)}, u32[]{:S(2)}) collective-permute-start(bf16[1,160,320]{2,1,0:T(8,128)(2,1)S(1)} %get-tuple-element.48), channel_id=1, source_target_pairs={{0,16},{4,20},{8,24},{12,28},{16,0},{20,4},{24,8},{28,12},{1,17},{... | collective-permute-start | bytes 307208 | tf_op jit(solution)/shard_map/ppermute | solution.py:254
  74.1 6.8 %collective-permute-start.18 = (bf16[1,80,360]{2,1,0:T(8,128)(2,1)S(1)}, bf16[1,80,360]{2,1,0:T(8,128)(2,1)S(1)}, u32[]{:S(2)}, u32[]{:S(2)}) collective-permute-start(bf16[1,80,360]{2,1,0:T(8,128)(2,1)S(1)} %get-tuple-element.53), channel_id=1, source_target_pairs={{0,8},{4,12},{8,0},{12,4},{16,24},{20,28},{24,16},{28,20},{1,9},{5... | collective-permute-start | bytes 172808 | tf_op jit(solution)/shard_map/ppermute | solution.py:254
  74.3 7.0 %collective-permute-start.20 = (bf16[1,80,360]{2,1,0:T(8,128)(2,1)S(1)}, bf16[1,80,360]{2,1,0:T(8,128)(2,1)S(1)}, u32[]{:S(2)}, u32[]{:S(2)}) collective-permute-start(bf16[1,80,360]{2,1,0:T(8,128)(2,1)S(1)} %get-tuple-element.54), channel_id=1, source_target_pairs={{0,24},{4,28},{8,16},{12,20},{16,8},{20,12},{24,0},{28,4},{1,25},{... | collective-permute-start | bytes 172808 | tf_op jit(solution)/shard_map/ppermute | solution.py:254
  75.8 6.4 %collective-permute-start.19 = (bf16[1,80,360]{2,1,0:T(8,128)(2,1)S(1)}, bf16[1,80,360]{2,1,0:T(8,128)(2,1)S(1)}, u32[]{:S(2)}, u32[]{:S(2)}) collective-permute-start(bf16[1,80,360]{2,1,0:T(8,128)(2,1)S(1)} %get-tuple-element.55), channel_id=1, source_target_pairs={{0,16},{4,20},{8,24},{12,28},{16,0},{20,4},{24,8},{28,12},{1,17},{... | collective-permute-start | bytes 172808 | tf_op jit(solution)/shard_map/ppermute | solution.py:254
  77.7 7.3 %collective-permute-start.29 = (bf16[160,320]{1,0:T(8,128)(2,1)S(1)}, bf16[160,320]{1,0:T(8,128)(2,1)S(1)}, u32[]{:S(2)}, u32[]{:S(2)}) collective-permute-start(bf16[160,320]{1,0:T(8,128)(2,1)S(1)} %fusion.5), channel_id=1, source_target_pairs={{0,3},{1,2},{2,1},{3,0},{4,7},{5,6},{6,5},{7,4},{8,11},{9,10},{10,... | collective-permute-start | bytes 307208 | tf_op jit(solution)/shard_map/ppermute | solution.py:254
  79.0 7.0 %collective-permute-start.28 = (bf16[160,320]{1,0:T(8,128)(2,1)S(1)}, bf16[160,320]{1,0:T(8,128)(2,1)S(1)}, u32[]{:S(2)}, u32[]{:S(2)}) collective-permute-start(bf16[160,320]{1,0:T(8,128)(2,1)S(1)} %fusion.5), channel_id=1, source_target_pairs={{0,2},{1,3},{2,0},{3,1},{4,6},{5,7},{6,4},{7,5},{8,10},{9,11},{10,... | collective-permute-start | bytes 307208 | tf_op jit(solution)/shard_map/ppermute | solution.py:254
  80.9 5.1 %collective-permute-start.27 = (bf16[160,320]{1,0:T(8,128)(2,1)S(1)}, bf16[160,320]{1,0:T(8,128)(2,1)S(1)}, u32[]{:S(2)}, u32[]{:S(2)}) collective-permute-start(bf16[160,320]{1,0:T(8,128)(2,1)S(1)} %fusion.5), channel_id=1, source_target_pairs={{0,1},{1,0},{2,3},{3,2},{4,5},{5,4},{6,7},{7,6},{8,9},{9,8},{10,11... | collective-permute-start | bytes 307208 | tf_op jit(solution)/shard_map/ppermute | solution.py:254
  82.2 5.3 %collective-permute-start.23 = (bf16[1,80,360]{2,1,0:T(8,128)(2,1)S(1)}, bf16[1,80,360]{2,1,0:T(8,128)(2,1)S(1)}, u32[]{:S(2)}, u32[]{:S(2)}) collective-permute-start(bf16[1,80,360]{2,1,0:T(8,128)(2,1)S(1)} %fusion.7), channel_id=1, source_target_pairs={{0,3},{1,2},{2,1},{3,0},{4,7},{5,6},{6,5},{7,4},{8,11},{9,10},{10,... | collective-permute-start | bytes 172808 | tf_op jit(solution)/shard_map/ppermute | solution.py:254
  84.5 4.2 %collective-permute-start.22 = (bf16[1,80,360]{2,1,0:T(8,128)(2,1)S(1)}, bf16[1,80,360]{2,1,0:T(8,128)(2,1)S(1)}, u32[]{:S(2)}, u32[]{:S(2)}) collective-permute-start(bf16[1,80,360]{2,1,0:T(8,128)(2,1)S(1)} %fusion.7), channel_id=1, source_target_pairs={{0,2},{1,3},{2,0},{3,1},{4,6},{5,7},{6,4},{7,5},{8,10},{9,11},{10,... | collective-permute-start | bytes 172808 | tf_op jit(solution)/shard_map/ppermute | solution.py:254
  85.1 4.2 %collective-permute-start.21 = (bf16[1,80,360]{2,1,0:T(8,128)(2,1)S(1)}, bf16[1,80,360]{2,1,0:T(8,128)(2,1)S(1)}, u32[]{:S(2)}, u32[]{:S(2)}) collective-permute-start(bf16[1,80,360]{2,1,0:T(8,128)(2,1)S(1)} %fusion.7), channel_id=1, source_target_pairs={{0,1},{1,0},{2,3},{3,2},{4,5},{5,4},{6,7},{7,6},{8,9},{9,8},{10,11... | collective-permute-start | bytes 172808 | tf_op jit(solution)/shard_map/ppermute | solution.py:254

commit v12 on v11

--- a/solution.py
+++ b/solution.py
@@ -110,17 +110,12 @@
     tiles_ref,
     target_ref,
     predicted_ref,
-    keep_ref,
-    send_ref,
     keep_time_ref,
     send_time_ref,
-    weight,
-    time_weight,
-    bias,
-    sums,
-    columns,
-    total,
+    *refs,
 ):
+    keep_refs, send_refs = refs[: len(refs) // 2 - 3], refs[len(refs) // 2 - 3 : -6]
+    weight, time_weight, bias, sums, columns, total = refs[-6:]
     i = pl.program_id(0)
     parts, planes, part_rows, rows = own_ref.shape
     step, channels, pixels = normed_ref.shape
@@ -196,15 +191,15 @@
         )
         for c in range(2):
             for f in range(shards):
-                into = keep_ref if f % 2 == c else send_ref
                 time_into = keep_time_ref if f % 2 == c else send_time_ref
 
                 @pl.when(core == c)
                 def _():
                     at = (f // 2) ^ plane
-                    for q in range(parts):
-                        here = slice(q * part_rows, (q + 1) * part_rows)
-                        into[q ^ part, at] = total[here, f * rows : (f + 1) * rows].astype(bf16)
+                    for k in range(parts):
+                        into = (keep_refs if f % 2 == c else send_refs)[k]
+                        here = pl.ds(pl.multiple_of((k ^ part) * part_rows, part_rows), part_rows)
+                        into[at] = total[here, f * rows : (f + 1) * rows].astype(bf16)
                     time_into[at] = time_total[f * time_rows : (f + 1) * time_rows].astype(bf16)
 
 
@@ -224,7 +219,7 @@
             num_scalar_prefetch=1,
             grid=(steps,),
             in_specs=[resident] * 5 + [block] * 3,
-            out_specs=[block] + [resident] * 4,
+            out_specs=[block] + [resident] * (2 + 2 * parts),
             scratch_shapes=[
                 pltpu.VMEM((outs, depth), bf16),
                 pltpu.VMEM((emb, outs), f32),
@@ -236,11 +231,10 @@
         ),
         out_shape=[
             jax.ShapeDtypeStruct(tiles.shape, bf16),
-            jax.ShapeDtypeStruct(own.shape, bf16),
-            jax.ShapeDtypeStruct(own.shape, bf16),
             jax.ShapeDtypeStruct(own_time.shape, bf16),
             jax.ShapeDtypeStruct(own_time.shape, bf16),
-        ],
+        ]
+        + [jax.ShapeDtypeStruct(own.shape[1:], bf16)] * (2 * parts),
         compiler_params=pltpu.CompilerParams(vmem_limit_bytes=32 * 2**20),
         cost_estimate=pl.CostEstimate(
             flops=4 * number * pixels * depth * outs, bytes_accessed=8 * tiles.size, transcendentals=0
@@ -349,14 +343,16 @@
     other = jnp.concatenate([other_mine, jnp.concatenate(other_far)], axis=1)
     other_time = swap(own_time, "fsdp", 1)
 
-    predicted, keep, send, keep_time, send_time = conv_both(
+    predicted, keep_time, send_time, *blocks = conv_both(
         counts, own, other, own_time, other_time, features, normed, tiles, targets
     )
 
-    grad = add_up([keep, swap(send, "fsdp", 1)])
+    keep, send = blocks[:parts], blocks[parts:]
+    blocks = [swap(send[k], "fsdp", 1) for k in [*range(1, parts), 0]]
+    blocks = [add_up([keep[k], blocks[k - 1]]) for k in range(parts)]
     time_grad = add_up([keep_time, swap(send_time, "fsdp", 1)])
-    grad, time_grad = lax.optimization_barrier((grad, time_grad))
-    grad = scatter_partners(grad, "dp", 0, part_bits)
+    blocks[-1], time_grad = lax.optimization_barrier((blocks[-1], time_grad))
+    grad = add_up(blocks[:1] + [swap(blocks[k], "dp", k) for k in range(1, parts)])
     for bit in range(part_bits, peer_bits):
         grad = sum_partners(grad, "dp", bit, 1)
     time_grad = scatter_partners(time_grad, "fsdp", 1, plane_bits)

time: 90.5 us -> 88.5 us (0.978); the launches traced: 90.2 us -> 89.9 us
  starting transfers between devices: 39.2 us -> 30.1 us
  Pallas kernels: 27.1 us -> 33.4 us
  waiting for transfers between devices: 15.1 us -> 17.7 us
    ppermute x30 -> x33, starting transfers between devices: 39.2 us -> 30.1 us  [swap(): return lax.ppermute(values, axis, pairs)]
    pallas_call x1, Pallas kernels: 17.2 us -> 23.5 us  [conv_both(): pl.pallas_call(functools.partial(conv_kernel, steps), grid_spec=pltpu.Pre...]
    ppermute x30 -> x33, waiting for transfers between devices: 15.1 us -> 17.7 us  [swap(): return lax.ppermute(values, axis, pairs)]
  transfers between devices with their start and end apart: 30 -> 33, of which waited for: 7 -> 9; matrix products, arithmetic and copies ran while one was open for 5% -> 5% of each run, Pallas kernels for 11% -> 11%
where the time goes in v12:
time: 88.5 us; the launch traced here: 89.9 us
  Pallas kernels  33.4 us (38%)
  starting transfers between devices  30.1 us (34%)
  waiting for transfers between devices  17.7 us (20%)
  other arithmetic  6.52 us (7%)
  local copies, waits for them, and re-layouts  1.17 us (1%)
  between operations  0.99 us (1%)
    ppermute x33, starting transfers between devices, swap(): return lax.ppermute(values, axis, pairs)  30.1 us
    pallas_call x1, Pallas kernels, conv_both(): pl.pallas_call(functools.partial(conv_kernel, steps), grid_spec=pltpu.Pre...  23.5 us
    ppermute x33, waiting for transfers between devices, swap(): return lax.ppermute(values, axis, pairs)  17.7 us
    pallas_call x2, Pallas kernels, group_norm(): pl.pallas_call(functools.partial(norm_kernel, group_width), grid=(last -...  9.88 us
  transfers between devices with their start and end apart: 33, of which 9 were waited for; matrix products, arithmetic and copies ran while one was open for 5% of the time, Pallas kernels for 11%

profile of v12, /device:TPU:0, one launch (start us, length us, event | category | flops | bytes accessed | tf_op | source)
XLA Modules:
  0.0 89.9 jit_solution(11074597807362851425)
XLA Ops:
  0.6 1.1 %convert_element_type.151 = bf16[360,320]{0,1:T(8,128)(2,1)S(1)} convert(f32[360,320]{0,1:T(8,128)} %param.12) | non-fusion elementwise | flops 115200 | bytes 691200 | tf_op jit(solution)/shard_map/convert_element_type | solution.py:315
  1.8 5.1 %collective-permute-start.2 = (bf16[1,80,360]{2,1,0:T(8,128)(2,1)S(1)}, bf16[1,80,360]{2,1,0:T(8,128)(2,1)S(1)}, u32[]{:S(2)}, u32[]{:S(2)}) collective-permute-start(bf16[1,80,360]{2,1,0:T(8,128)(2,1)S(1)} %get-tuple-element.72), channel_id=1, source_target_pairs={{0,24},{4,28},{8,16},{12,20},{16,8},{20,12},{24,0},{28,4},{1,25},{... | collective-permute-start | bytes 172808 | tf_op jit(solution)/shard_map/ppermute | solution.py:248
  6.9 0.6 collective-permute-start
  7.5 1.0 %convert_bitcast_fusion.2 = (bf16[1,1,160,320]{3,2,1,0:T(8,128)(2,1)S(1)}, bf16[1,160,320]{2,1,0:T(8,128)(2,1)S(1)}) fusion(f32[160,320]{1,0:T(8,128)} %param.13), kind=kLoop, calls=%fused_computation.44 | loop fusion | flops 51200 | bytes 409600 | tf_op jit(solution)/shard_map/stack;broadcast_in_dim | solution.py:264
  8.5 2.4 %collective-permute-start.6 = (bf16[1,160,320]{2,1,0:T(8,128)(2,1)S(1)}, bf16[1,160,320]{2,1,0:T(8,128)(2,1)S(1)}, u32[]{:S(2)}, u32[]{:S(2)}) collective-permute-start(bf16[1,160,320]{2,1,0:T(8,128)(2,1)S(1)} %get-tuple-element.68), channel_id=1, source_target_pairs={{0,16},{4,20},{8,24},{12,28},{16,0},{20,4},{24,8},{28,12},{1,17},{... | collective-permute-start | bytes 307208 | tf_op jit(solution)/shard_map/ppermute | solution.py:248
  10.9 4.0 %group_norm.2.refs_0_ = bf16[15,320,256]{2,1,0:T(8,128)(2,1)} custom-call(bf16[320,320]{1,0:T(8,128)(2,1)} %constant.45.clone.same_ref, bf16[15,320,256]{2,1,0:T(8,128)(2,1)} %bitcast.88), custom_call_target="tpu_custom_call" | custom-call | flops 8192000 | bytes 1638400 | tf_op jit(solution)/shard_map/group_norm/pallas_call | solution.py:62
  15.1 2.5 %collective-permute-start.5 = (bf16[1,3,80,360]{3,2,1,0:T(8,128)(2,1)S(1)}, bf16[1,3,80,360]{3,2,1,0:T(8,128)(2,1)S(1)}, u32[]{:S(2)}, u32[]{:S(2)}) collective-permute-start(bf16[1,3,80,360]{3,2,1,0:T(8,128)(2,1)S(1)} %get-tuple-element.66), channel_id=1, source_target_pairs={{0,3},{1,2},{2,1},{3,0},{4,7},{5,6},{6,5},{7,4},{8,11},{9,10},{10,... | collective-permute-start | bytes 518408 | tf_op jit(solution)/shard_map/ppermute | solution.py:248
  17.6 0.5 collective-permute-start.4
  18.1 0.5 collective-permute-start.3
  18.7 2.1 %collective-permute-start.11 = (bf16[1,2,160,320]{3,2,1,0:T(8,128)(2,1)S(1)}, bf16[1,2,160,320]{3,2,1,0:T(8,128)(2,1)S(1)}, u32[]{:S(2)}, u32[]{:S(2)}) collective-permute-start(bf16[1,2,160,320]{3,2,1,0:T(8,128)(2,1)S(1)} %bitcast.98), channel_id=1, source_target_pairs={{0,8},{4,12},{8,0},{12,4},{16,24},{20,28},{24,16},{28,20},{1,9},{5... | collective-permute-start | bytes 614408 | tf_op jit(solution)/shard_map/ppermute | solution.py:248
  20.8 0.1 pad_maximum_fusion.1
  20.9 5.8 %group_norm.3.normed_ref = bf16[15,320,256]{2,1,0:T(8,128)(2,1)} custom-call(bf16[320,320]{1,0:T(8,128)(2,1)} %constant.45.clone.same_ref, bf16[15,320,256]{2,1,0:T(8,128)(2,1)} %bitcast.89, bf16[15,320,256]{2,1,0:T(8,128)(2,1)} %group_norm.2.refs_0_), custom_call_target="tpu_custom_call", output_to_operand_aliasing={{}: (2, {})} | custom-call | flops 16384000 | bytes 3276800 | tf_op jit(solution)/shard_map/group_norm/pallas_call | solution.py:62
  26.7 0.5 collective-permute-start.10
  27.3 0.4 collective-permute-start.8
  27.8 0.3 maximum_maximum_fusion.own_ref
  28.0 0.1 maximum_bitcast_fusion
  28.3 0.1 collective-permute-start.12
  28.4 1.2 %multiply_cosine_fusion = (f32[640,128]{1,0:T(8,128)S(1)}, f32[640,128]{1,0:T(8,128)S(1)}) fusion(f32[128]{0:T(128)S(1)} %pad_convert_fusion, f32[640]{0:T(1024)S(1)} %multiply_exponential_fusion), kind=kLoop, calls=%fused_computation.13 | loop fusion | flops 81920 | bytes 658432 | tf_op jit(solution)/shard_map/cos | solution.py:298
  29.6 0.2 multiply_convert_fusion.features_ref
  29.9 0.3 maximum_maximum_fusion.1.other_ref
  30.2 0.1 copy-done.1
  30.3 0.8 copy-done
  31.1 23.5 %conv_both.1 = (bf16[15,320,256]{2,1,0:T(8,128)(2,1)}, bf16[4,160,320]{2,1,0:T(8,128)(2,1)S(1)}, bf16[4,160,320]{2,1,0:T(8,128)(2,1)S(1)}, bf16[4,80,360]{2,1,0:...) custom-call(s32[1,4]{1,0:T(1,128)S(1)} %copy-done.3, ...), custom_call_target="tpu_custom_call" | custom-call | flops 14155776000 | bytes 9830400 | tf_op jit(solution)/shard_map/conv_both/pallas_call | solution.py:216
  54.6 0.5 collective-permute-start.13
  55.1 0.5 collective-permute-start.18
  55.6 0.4 collective-permute-done.14
  56.2 0.6 collective-permute-done.16
  56.8 2.5 %collective-permute-start.17 = (bf16[4,80,360]{2,1,0:T(8,128)(2,1)S(1)}, bf16[4,80,360]{2,1,0:T(8,128)(2,1)S(1)}, u32[]{:S(2)}, u32[]{:S(2)}) collective-permute-start(bf16[4,80,360]{2,1,0:T(8,128)(2,1)S(1)} %add_convert_fusion.3), channel_id=1, source_target_pairs={{0,2},{1,3},{2,0},{3,1},{4,6},{5,7},{6,4},{7,5},{8,10},{9,11},{10,... | collective-permute-start | bytes 691208 | tf_op jit(solution)/shard_map/ppermute | solution.py:248
  59.4 0.1 add_convert_fusion
  59.6 0.9 %collective-permute-start.20 = (bf16[4,80,360]{2,1,0:T(8,128)(2,1)S(1)}, bf16[4,80,360]{2,1,0:T(8,128)(2,1)S(1)}, u32[]{:S(2)}, u32[]{:S(2)}) collective-permute-start(bf16[4,80,360]{2,1,0:T(8,128)(2,1)S(1)} %add_convert_fusion.2), channel_id=1, source_target_pairs={{0,3},{1,2},{2,1},{3,0},{4,7},{5,6},{6,5},{7,4},{8,11},{9,10},{10,... | collective-permute-start | bytes 691208 | tf_op jit(solution)/shard_map/ppermute | solution.py:248
  60.6 1.2 %collective-permute-start.29 = (bf16[1,160,320]{2,1,0:T(8,128)(2,1)S(1)}, bf16[1,160,320]{2,1,0:T(8,128)(2,1)S(1)}, u32[]{:S(2)}, u32[]{:S(2)}) collective-permute-start(bf16[1,160,320]{2,1,0:T(8,128)(2,1)S(1)} %get-tuple-element.56), channel_id=1, source_target_pairs={{0,24},{4,28},{8,16},{12,20},{16,8},{20,12},{24,0},{28,4},{1,25},{... | collective-permute-start | bytes 307208 | tf_op jit(solution)/shard_map/ppermute | solution.py:248
  61.8 3.2 %collective-permute-done.15 = bf16[4,80,360]{2,1,0:T(8,128)(2,1)S(1)} collective-permute-done((bf16[4,80,360]{2,1,0:T(8,128)(2,1)S(1)}, bf16[4,80,360]{2,1,0:T(8,128)(2,1)S(1)}, u32[]{:S(2)}, u32[]{:S(2)}) %collective-permute-start.15) | collective-permute-done | bytes 230432 | tf_op jit(solution)/shard_map/ppermute | solution.py:248
  65.0 5.6 %collective-permute-done.17 = bf16[4,80,360]{2,1,0:T(8,128)(2,1)S(1)} collective-permute-done((bf16[4,80,360]{2,1,0:T(8,128)(2,1)S(1)}, bf16[4,80,360]{2,1,0:T(8,128)(2,1)S(1)}, u32[]{:S(2)}, u32[]{:S(2)}) %collective-permute-start.17) | collective-permute-done | bytes 230432 | tf_op jit(solution)/shard_map/ppermute | solution.py:248
  70.6 0.2 fusion
  70.8 0.1 collective-permute-start.21
  70.9 1.7 %collective-permute-start.23 = (bf16[1,80,360]{2,1,0:T(8,128)(2,1)S(1)}, bf16[1,80,360]{2,1,0:T(8,128)(2,1)S(1)}, u32[]{:S(2)}, u32[]{:S(2)}) collective-permute-start(bf16[1,80,360]{2,1,0:T(8,128)(2,1)S(1)} %get-tuple-element.63), channel_id=1, source_target_pairs={{0,24},{4,28},{8,16},{12,20},{16,8},{20,12},{24,0},{28,4},{1,25},{... | collective-permute-start | bytes 172808 | tf_op jit(solution)/shard_map/ppermute | solution.py:248
  72.6 1.8 %collective-permute-start.22 = (bf16[1,80,360]{2,1,0:T(8,128)(2,1)S(1)}, bf16[1,80,360]{2,1,0:T(8,128)(2,1)S(1)}, u32[]{:S(2)}, u32[]{:S(2)}) collective-permute-start(bf16[1,80,360]{2,1,0:T(8,128)(2,1)S(1)} %get-tuple-element.64), channel_id=1, source_target_pairs={{0,16},{4,20},{8,24},{12,28},{16,0},{20,4},{24,8},{28,12},{1,17},{... | collective-permute-start | bytes 172808 | tf_op jit(solution)/shard_map/ppermute | solution.py:248
  74.3 3.9 %collective-permute-done.28 = bf16[1,160,320]{2,1,0:T(8,128)(2,1)S(1)} collective-permute-done((bf16[1,160,320]{2,1,0:T(8,128)(2,1)S(1)}, bf16[1,160,320]{2,1,0:T(8,128)(2,1)S(1)}, u32[]{:S(2)}, u32[]{:S(2)}) %collective-permute-start.28) | collective-permute-done | bytes 102432 | tf_op jit(solution)/shard_map/ppermute | solution.py:248
  78.5 3.4 %collective-permute-start.30 = (bf16[160,320]{1,0:T(8,128)(2,1)S(1)}, bf16[160,320]{1,0:T(8,128)(2,1)S(1)}, u32[]{:S(2)}, u32[]{:S(2)}) collective-permute-start(bf16[160,320]{1,0:T(8,128)(2,1)S(1)} %fusion.4), channel_id=1, source_target_pairs={{0,1},{1,0},{2,3},{3,2},{4,5},{5,4},{6,7},{7,6},{8,9},{9,8},{10,11... | collective-permute-start | bytes 307208 | tf_op jit(solution)/shard_map/ppermute | solution.py:248
  81.9 0.1 collective-permute-start.26
  82.1 1.4 %collective-permute-start.25 = (bf16[1,80,360]{2,1,0:T(8,128)(2,1)S(1)}, bf16[1,80,360]{2,1,0:T(8,128)(2,1)S(1)}, u32[]{:S(2)}, u32[]{:S(2)}) collective-permute-start(bf16[1,80,360]{2,1,0:T(8,128)(2,1)S(1)} %fusion.6), channel_id=1, source_target_pairs={{0,2},{1,3},{2,0},{3,1},{4,6},{5,7},{6,4},{7,5},{8,10},{9,11},{10,... | collective-permute-start | bytes 172808 | tf_op jit(solution)/shard_map/ppermute | solution.py:248
  83.5 1.2 %collective-permute-done.32 = bf16[160,320]{1,0:T(8,128)(2,1)S(1)} collective-permute-done((bf16[160,320]{1,0:T(8,128)(2,1)S(1)}, bf16[160,320]{1,0:T(8,128)(2,1)S(1)}, u32[]{:S(2)}, u32[]{:S(2)}) %collective-permute-start.32) | collective-permute-done | bytes 102432 | tf_op jit(solution)/shard_map/ppermute | solution.py:248
  84.7 0.8 collective-permute-start.24
  85.5 0.4 collective-permute-done.31
  85.9 0.8 fusion.3
  86.7 0.6 collective-permute-done.26
  87.3 1.6 %collective-permute-done.24 = bf16[1,80,360]{2,1,0:T(8,128)(2,1)S(1)} collective-permute-done((bf16[1,80,360]{2,1,0:T(8,128)(2,1)S(1)}, bf16[1,80,360]{2,1,0:T(8,128)(2,1)S(1)}, u32[]{:S(2)}, u32[]{:S(2)}) %collective-permute-start.24) | collective-permute-done | bytes 57632 | tf_op jit(solution)/shard_map/ppermute | solution.py:248
  89.0 0.8 convert_bitcast_fusion
  (62 shorter events, 1.5 us)
Async XLA Ops:
  1.8 13.2 %collective-permute-start.2 = (bf16[1,80,360]{2,1,0:T(8,128)(2,1)S(1)}, bf16[1,80,360]{2,1,0:T(8,128)(2,1)S(1)}, u32[]{:S(2)}, u32[]{:S(2)}) collective-permute-start(bf16[1,80,360]{2,1,0:T(8,128)(2,1)S(1)} %get-tuple-element.72), channel_id=1, source_target_pairs={{0,24},{4,28},{8,16},{12,20},{16,8},{20,12},{24,0},{28,4},{1,25},{... | collective-permute-start | bytes 172808 | tf_op jit(solution)/shard_map/ppermute | solution.py:248
  6.9 8.1 %collective-permute-start.1 = (bf16[1,80,360]{2,1,0:T(8,128)(2,1)S(1)}, bf16[1,80,360]{2,1,0:T(8,128)(2,1)S(1)}, u32[]{:S(2)}, u32[]{:S(2)}) collective-permute-start(bf16[1,80,360]{2,1,0:T(8,128)(2,1)S(1)} %get-tuple-element.72), channel_id=1, source_target_pairs={{0,16},{4,20},{8,24},{12,28},{16,0},{20,4},{24,8},{28,12},{1,17},{... | collective-permute-start | bytes 172808 | tf_op jit(solution)/shard_map/ppermute | solution.py:248
  6.9 8.1 %collective-permute-start = (bf16[1,80,360]{2,1,0:T(8,128)(2,1)S(1)}, bf16[1,80,360]{2,1,0:T(8,128)(2,1)S(1)}, u32[]{:S(2)}, u32[]{:S(2)}) collective-permute-start(bf16[1,80,360]{2,1,0:T(8,128)(2,1)S(1)} %get-tuple-element.72), channel_id=1, source_target_pairs={{0,8},{4,12},{8,0},{12,4},{16,24},{20,28},{24,16},{28,20},{1,9},{5... | collective-permute-start | bytes 172808 | tf_op jit(solution)/shard_map/ppermute | solution.py:248
  8.5 10.2 %collective-permute-start.6 = (bf16[1,160,320]{2,1,0:T(8,128)(2,1)S(1)}, bf16[1,160,320]{2,1,0:T(8,128)(2,1)S(1)}, u32[]{:S(2)}, u32[]{:S(2)}) collective-permute-start(bf16[1,160,320]{2,1,0:T(8,128)(2,1)S(1)} %get-tuple-element.68), channel_id=1, source_target_pairs={{0,16},{4,20},{8,24},{12,28},{16,0},{20,4},{24,8},{28,12},{1,17},{... | collective-permute-start | bytes 307208 | tf_op jit(solution)/shard_map/ppermute | solution.py:248
  15.1 11.6 %collective-permute-start.5 = (bf16[1,3,80,360]{3,2,1,0:T(8,128)(2,1)S(1)}, bf16[1,3,80,360]{3,2,1,0:T(8,128)(2,1)S(1)}, u32[]{:S(2)}, u32[]{:S(2)}) collective-permute-start(bf16[1,3,80,360]{3,2,1,0:T(8,128)(2,1)S(1)} %get-tuple-element.66), channel_id=1, source_target_pairs={{0,3},{1,2},{2,1},{3,0},{4,7},{5,6},{6,5},{7,4},{8,11},{9,10},{10,... | collective-permute-start | bytes 518408 | tf_op jit(solution)/shard_map/ppermute | solution.py:248
  17.6 9.6 %collective-permute-start.4 = (bf16[1,3,80,360]{3,2,1,0:T(8,128)(2,1)S(1)}, bf16[1,3,80,360]{3,2,1,0:T(8,128)(2,1)S(1)}, u32[]{:S(2)}, u32[]{:S(2)}) collective-permute-start(bf16[1,3,80,360]{3,2,1,0:T(8,128)(2,1)S(1)} %get-tuple-element.66), channel_id=1, source_target_pairs={{0,2},{1,3},{2,0},{3,1},{4,6},{5,7},{6,4},{7,5},{8,10},{9,11},{10,... | collective-permute-start | bytes 518408 | tf_op jit(solution)/shard_map/ppermute | solution.py:248
  18.1 9.2 %collective-permute-start.3 = (bf16[1,3,80,360]{3,2,1,0:T(8,128)(2,1)S(1)}, bf16[1,3,80,360]{3,2,1,0:T(8,128)(2,1)S(1)}, u32[]{:S(2)}, u32[]{:S(2)}) collective-permute-start(bf16[1,3,80,360]{3,2,1,0:T(8,128)(2,1)S(1)} %get-tuple-element.66), channel_id=1, source_target_pairs={{0,1},{1,0},{2,3},{3,2},{4,5},{5,4},{6,7},{7,6},{8,9},{9,8},{10,11... | collective-permute-start | bytes 518408 | tf_op jit(solution)/shard_map/ppermute | solution.py:248
  18.7 9.3 %collective-permute-start.11 = (bf16[1,2,160,320]{3,2,1,0:T(8,128)(2,1)S(1)}, bf16[1,2,160,320]{3,2,1,0:T(8,128)(2,1)S(1)}, u32[]{:S(2)}, u32[]{:S(2)}) collective-permute-start(bf16[1,2,160,320]{3,2,1,0:T(8,128)(2,1)S(1)} %bitcast.98), channel_id=1, source_target_pairs={{0,8},{4,12},{8,0},{12,4},{16,24},{20,28},{24,16},{28,20},{1,9},{5... | collective-permute-start | bytes 614408 | tf_op jit(solution)/shard_map/ppermute | solution.py:248
  26.7 1.5 %copy-start.4 = (s32[1,15]{1,0:T(1,128)S(1)}, s32[1,15]{1,0:T(1,128)}, u32[]{:S(2)}) copy-start(s32[1,15]{1,0:T(1,128)} %param.11) | copy-start | bytes 184
  26.7 3.1 %collective-permute-start.7 = (bf16[7,80,360]{2,1,0:T(8,128)(2,1)S(1)}, bf16[7,80,360]{2,1,0:T(8,128)(2,1)S(1)}, u32[]{:S(2)}, u32[]{:S(2)}) collective-permute-start(bf16[7,80,360]{2,1,0:T(8,128)(2,1)S(1)} %pad_maximum_fusion.1), channel_id=1, source_target_pairs={{0,4},{4,0},{8,12},{12,8},{16,20},{20,16},{24,28},{28,24},{1,5},{5... | collective-permute-start | bytes 1209608 | tf_op jit(solution)/shard_map/ppermute | solution.py:248
  26.7 3.1 %collective-permute-start.10 = (bf16[1,3,80,360]{3,2,1,0:T(8,128)(2,1)S(1)}, bf16[1,3,80,360]{3,2,1,0:T(8,128)(2,1)S(1)}, u32[]{:S(2)}, u32[]{:S(2)}) collective-permute-start(bf16[1,3,80,360]{3,2,1,0:T(8,128)(2,1)S(1)} %collective-permute-done.5), channel_id=1, source_target_pairs={{0,4},{4,0},{8,12},{12,8},{16,20},{20,16},{24,28},{28,24},{1,5},{5... | collective-permute-start | bytes 518408 | tf_op jit(solution)/shard_map/ppermute | solution.py:248
  27.3 2.6 %collective-permute-start.9 = (bf16[1,3,80,360]{3,2,1,0:T(8,128)(2,1)S(1)}, bf16[1,3,80,360]{3,2,1,0:T(8,128)(2,1)S(1)}, u32[]{:S(2)}, u32[]{:S(2)}) collective-permute-start(bf16[1,3,80,360]{3,2,1,0:T(8,128)(2,1)S(1)} %collective-permute-done.4), channel_id=1, source_target_pairs={{0,4},{4,0},{8,12},{12,8},{16,20},{20,16},{24,28},{28,24},{1,5},{5... | collective-permute-start | bytes 518408 | tf_op jit(solution)/shard_map/ppermute | solution.py:248
  27.3 2.6 %collective-permute-start.8 = (bf16[1,3,80,360]{3,2,1,0:T(8,128)(2,1)S(1)}, bf16[1,3,80,360]{3,2,1,0:T(8,128)(2,1)S(1)}, u32[]{:S(2)}, u32[]{:S(2)}) collective-permute-start(bf16[1,3,80,360]{3,2,1,0:T(8,128)(2,1)S(1)} %collective-permute-done.3), channel_id=1, source_target_pairs={{0,4},{4,0},{8,12},{12,8},{16,20},{20,16},{24,28},{28,24},{1,5},{5... | collective-permute-start | bytes 518408 | tf_op jit(solution)/shard_map/ppermute | solution.py:248
  27.8 2.4 %copy-start.2 = (bf16[1,15,256,320]{2,3,1,0:T(8,128)(2,1)S(1)}, bf16[1,15,256,320]{2,3,1,0:T(8,128)(2,1)}, u32[]{:S(2)}) copy-start(bf16[1,15,256,320]{2,3,1,0:T(8,128)(2,1)} %param.9) | copy-start | bytes 7372804
  28.1 2.2 %copy-start.1 = (bf16[15,320,256]{2,1,0:T(8,128)(2,1)S(1)}, bf16[15,320,256]{2,1,0:T(8,128)(2,1)}, u32[]{:S(2)}) copy-start(bf16[15,320,256]{2,1,0:T(8,128)(2,1)} %group_norm.3.normed_ref) | copy-start | bytes 7372804
  28.2 2.8 %copy-start = (bf16[1,15,256,320]{2,3,1,0:T(8,128)(2,1)S(1)}, bf16[1,15,256,320]{2,3,1,0:T(8,128)(2,1)}, u32[]{:S(2)}) copy-start(bf16[1,15,256,320]{2,3,1,0:T(8,128)(2,1)} %param.8) | copy-start | bytes 7372804
  28.2 2.8 %copy-start.3 = (s32[1,4]{1,0:T(1,128)S(1)}, s32[1,4]{1,0:T(1,128)}, u32[]{:S(2)}) copy-start(s32[1,4]{1,0:T(1,128)} %counts_ref.1) | copy-start | bytes 52
  28.3 1.9 %collective-permute-start.12 = (bf16[4,160,320]{2,1,0:T(8,128)(2,1)S(1)}, bf16[4,160,320]{2,1,0:T(8,128)(2,1)S(1)}, u32[]{:S(2)}, u32[]{:S(2)}) collective-permute-start(bf16[4,160,320]{2,1,0:T(8,128)(2,1)S(1)} %bitcast.91), channel_id=1, source_target_pairs={{0,4},{4,0},{8,12},{12,8},{16,20},{20,16},{24,28},{28,24},{1,5},{5... | collective-permute-start | bytes 1228808 | tf_op jit(solution)/shard_map/ppermute | solution.py:248
  54.6 1.5 %collective-permute-start.14 = (bf16[4,80,360]{2,1,0:T(8,128)(2,1)S(1)}, bf16[4,80,360]{2,1,0:T(8,128)(2,1)S(1)}, u32[]{:S(2)}, u32[]{:S(2)}) collective-permute-start(bf16[4,80,360]{2,1,0:T(8,128)(2,1)S(1)} %get-tuple-element.46), channel_id=1, source_target_pairs={{0,4},{4,0},{8,12},{12,8},{16,20},{20,16},{24,28},{28,24},{1,5},{5... | collective-permute-start | bytes 691208 | tf_op jit(solution)/shard_map/ppermute | solution.py:248
  54.6 6.0 %collective-permute-start.13 = (bf16[4,80,360]{2,1,0:T(8,128)(2,1)S(1)}, bf16[4,80,360]{2,1,0:T(8,128)(2,1)S(1)}, u32[]{:S(2)}, u32[]{:S(2)}) collective-permute-start(bf16[4,80,360]{2,1,0:T(8,128)(2,1)S(1)} %get-tuple-element.44), channel_id=1, source_target_pairs={{0,4},{4,0},{8,12},{12,8},{16,20},{20,16},{24,28},{28,24},{1,5},{5... | collective-permute-start | bytes 691208 | tf_op jit(solution)/shard_map/ppermute | solution.py:248
  55.1 1.7 %collective-permute-start.16 = (bf16[4,80,360]{2,1,0:T(8,128)(2,1)S(1)}, bf16[4,80,360]{2,1,0:T(8,128)(2,1)S(1)}, u32[]{:S(2)}, u32[]{:S(2)}) collective-permute-start(bf16[4,80,360]{2,1,0:T(8,128)(2,1)S(1)} %get-tuple-element.48), channel_id=1, source_target_pairs={{0,4},{4,0},{8,12},{12,8},{16,20},{20,16},{24,28},{28,24},{1,5},{5... | collective-permute-start | bytes 691208 | tf_op jit(solution)/shard_map/ppermute | solution.py:248
  55.1 4.2 %collective-permute-start.18 = (bf16[4,80,360]{2,1,0:T(8,128)(2,1)S(1)}, bf16[4,80,360]{2,1,0:T(8,128)(2,1)S(1)}, u32[]{:S(2)}, u32[]{:S(2)}) collective-permute-start(bf16[4,80,360]{2,1,0:T(8,128)(2,1)S(1)} %get-tuple-element.50), channel_id=1, source_target_pairs={{0,4},{4,0},{8,12},{12,8},{16,20},{20,16},{24,28},{28,24},{1,5},{5... | collective-permute-start | bytes 691208 | tf_op jit(solution)/shard_map/ppermute | solution.py:248
  55.6 3.8 %collective-permute-start.19 = (bf16[4,160,320]{2,1,0:T(8,128)(2,1)S(1)}, bf16[4,160,320]{2,1,0:T(8,128)(2,1)S(1)}, u32[]{:S(2)}, u32[]{:S(2)}) collective-permute-start(bf16[4,160,320]{2,1,0:T(8,128)(2,1)S(1)} %get-tuple-element.52), channel_id=1, source_target_pairs={{0,4},{4,0},{8,12},{12,8},{16,20},{20,16},{24,28},{28,24},{1,5},{5... | collective-permute-start | bytes 1228808 | tf_op jit(solution)/shard_map/ppermute | solution.py:248
  56.1 8.9 %collective-permute-start.15 = (bf16[4,80,360]{2,1,0:T(8,128)(2,1)S(1)}, bf16[4,80,360]{2,1,0:T(8,128)(2,1)S(1)}, u32[]{:S(2)}, u32[]{:S(2)}) collective-permute-start(bf16[4,80,360]{2,1,0:T(8,128)(2,1)S(1)} %add_convert_fusion.4), channel_id=1, source_target_pairs={{0,1},{1,0},{2,3},{3,2},{4,5},{5,4},{6,7},{7,6},{8,9},{9,8},{10,11... | collective-permute-start | bytes 691208 | tf_op jit(solution)/shard_map/ppermute | solution.py:248
  56.8 13.8 %collective-permute-start.17 = (bf16[4,80,360]{2,1,0:T(8,128)(2,1)S(1)}, bf16[4,80,360]{2,1,0:T(8,128)(2,1)S(1)}, u32[]{:S(2)}, u32[]{:S(2)}) collective-permute-start(bf16[4,80,360]{2,1,0:T(8,128)(2,1)S(1)} %add_convert_fusion.3), channel_id=1, source_target_pairs={{0,2},{1,3},{2,0},{3,1},{4,6},{5,7},{6,4},{7,5},{8,10},{9,11},{10,... | collective-permute-start | bytes 691208 | tf_op jit(solution)/shard_map/ppermute | solution.py:248
  59.6 11.0 %collective-permute-start.20 = (bf16[4,80,360]{2,1,0:T(8,128)(2,1)S(1)}, bf16[4,80,360]{2,1,0:T(8,128)(2,1)S(1)}, u32[]{:S(2)}, u32[]{:S(2)}) collective-permute-start(bf16[4,80,360]{2,1,0:T(8,128)(2,1)S(1)} %add_convert_fusion.2), channel_id=1, source_target_pairs={{0,3},{1,2},{2,1},{3,0},{4,7},{5,6},{6,5},{7,4},{8,11},{9,10},{10,... | collective-permute-start | bytes 691208 | tf_op jit(solution)/shard_map/ppermute | solution.py:248
  60.5 12.1 %collective-permute-start.27 = (bf16[1,160,320]{2,1,0:T(8,128)(2,1)S(1)}, bf16[1,160,320]{2,1,0:T(8,128)(2,1)S(1)}, u32[]{:S(2)}, u32[]{:S(2)}) collective-permute-start(bf16[1,160,320]{2,1,0:T(8,128)(2,1)S(1)} %get-tuple-element.55), channel_id=1, source_target_pairs={{0,8},{4,12},{8,0},{12,4},{16,24},{20,28},{24,16},{28,20},{1,9},{5... | collective-permute-start | bytes 307208 | tf_op jit(solution)/shard_map/ppermute | solution.py:248
  60.6 13.7 %collective-permute-start.29 = (bf16[1,160,320]{2,1,0:T(8,128)(2,1)S(1)}, bf16[1,160,320]{2,1,0:T(8,128)(2,1)S(1)}, u32[]{:S(2)}, u32[]{:S(2)}) collective-permute-start(bf16[1,160,320]{2,1,0:T(8,128)(2,1)S(1)} %get-tuple-element.56), channel_id=1, source_target_pairs={{0,24},{4,28},{8,16},{12,20},{16,8},{20,12},{24,0},{28,4},{1,25},{... | collective-permute-start | bytes 307208 | tf_op jit(solution)/shard_map/ppermute | solution.py:248
  65.0 13.3 %collective-permute-start.28 = (bf16[1,160,320]{2,1,0:T(8,128)(2,1)S(1)}, bf16[1,160,320]{2,1,0:T(8,128)(2,1)S(1)}, u32[]{:S(2)}, u32[]{:S(2)}) collective-permute-start(bf16[1,160,320]{2,1,0:T(8,128)(2,1)S(1)} %get-tuple-element.57), channel_id=1, source_target_pairs={{0,16},{4,20},{8,24},{12,28},{16,0},{20,4},{24,8},{28,12},{1,17},{... | collective-permute-start | bytes 307208 | tf_op jit(solution)/shard_map/ppermute | solution.py:248
  70.8 7.7 %collective-permute-start.21 = (bf16[1,80,360]{2,1,0:T(8,128)(2,1)S(1)}, bf16[1,80,360]{2,1,0:T(8,128)(2,1)S(1)}, u32[]{:S(2)}, u32[]{:S(2)}) collective-permute-start(bf16[1,80,360]{2,1,0:T(8,128)(2,1)S(1)} %get-tuple-element.62), channel_id=1, source_target_pairs={{0,8},{4,12},{8,0},{12,4},{16,24},{20,28},{24,16},{28,20},{1,9},{5... | collective-permute-start | bytes 172808 | tf_op jit(solution)/shard_map/ppermute | solution.py:248
  70.9 11.0 %collective-permute-start.23 = (bf16[1,80,360]{2,1,0:T(8,128)(2,1)S(1)}, bf16[1,80,360]{2,1,0:T(8,128)(2,1)S(1)}, u32[]{:S(2)}, u32[]{:S(2)}) collective-permute-start(bf16[1,80,360]{2,1,0:T(8,128)(2,1)S(1)} %get-tuple-element.63), channel_id=1, source_target_pairs={{0,24},{4,28},{8,16},{12,20},{16,8},{20,12},{24,0},{28,4},{1,25},{... | collective-permute-start | bytes 172808 | tf_op jit(solution)/shard_map/ppermute | solution.py:248
  72.6 9.3 %collective-permute-start.22 = (bf16[1,80,360]{2,1,0:T(8,128)(2,1)S(1)}, bf16[1,80,360]{2,1,0:T(8,128)(2,1)S(1)}, u32[]{:S(2)}, u32[]{:S(2)}) collective-permute-start(bf16[1,80,360]{2,1,0:T(8,128)(2,1)S(1)} %get-tuple-element.64), channel_id=1, source_target_pairs={{0,16},{4,20},{8,24},{12,28},{16,0},{20,4},{24,8},{28,12},{1,17},{... | collective-permute-start | bytes 172808 | tf_op jit(solution)/shard_map/ppermute | solution.py:248
  78.3 6.4 %collective-permute-start.32 = (bf16[160,320]{1,0:T(8,128)(2,1)S(1)}, bf16[160,320]{1,0:T(8,128)(2,1)S(1)}, u32[]{:S(2)}, u32[]{:S(2)}) collective-permute-start(bf16[160,320]{1,0:T(8,128)(2,1)S(1)} %fusion.4), channel_id=1, source_target_pairs={{0,3},{1,2},{2,1},{3,0},{4,7},{5,6},{6,5},{7,4},{8,11},{9,10},{10,... | collective-permute-start | bytes 307208 | tf_op jit(solution)/shard_map/ppermute | solution.py:248
  78.4 7.5 %collective-permute-start.31 = (bf16[160,320]{1,0:T(8,128)(2,1)S(1)}, bf16[160,320]{1,0:T(8,128)(2,1)S(1)}, u32[]{:S(2)}, u32[]{:S(2)}) collective-permute-start(bf16[160,320]{1,0:T(8,128)(2,1)S(1)} %fusion.4), channel_id=1, source_target_pairs={{0,2},{1,3},{2,0},{3,1},{4,6},{5,7},{6,4},{7,5},{8,10},{9,11},{10,... | collective-permute-start | bytes 307208 | tf_op jit(solution)/shard_map/ppermute | solution.py:248
  78.5 7.4 %collective-permute-start.30 = (bf16[160,320]{1,0:T(8,128)(2,1)S(1)}, bf16[160,320]{1,0:T(8,128)(2,1)S(1)}, u32[]{:S(2)}, u32[]{:S(2)}) collective-permute-start(bf16[160,320]{1,0:T(8,128)(2,1)S(1)} %fusion.4), channel_id=1, source_target_pairs={{0,1},{1,0},{2,3},{3,2},{4,5},{5,4},{6,7},{7,6},{8,9},{9,8},{10,11... | collective-permute-start | bytes 307208 | tf_op jit(solution)/shard_map/ppermute | solution.py:248
  81.9 5.4 %collective-permute-start.26 = (bf16[1,80,360]{2,1,0:T(8,128)(2,1)S(1)}, bf16[1,80,360]{2,1,0:T(8,128)(2,1)S(1)}, u32[]{:S(2)}, u32[]{:S(2)}) collective-permute-start(bf16[1,80,360]{2,1,0:T(8,128)(2,1)S(1)} %fusion.6), channel_id=1, source_target_pairs={{0,3},{1,2},{2,1},{3,0},{4,7},{5,6},{6,5},{7,4},{8,11},{9,10},{10,... | collective-permute-start | bytes 172808 | tf_op jit(solution)/shard_map/ppermute | solution.py:248
  82.1 5.2 %collective-permute-start.25 = (bf16[1,80,360]{2,1,0:T(8,128)(2,1)S(1)}, bf16[1,80,360]{2,1,0:T(8,128)(2,1)S(1)}, u32[]{:S(2)}, u32[]{:S(2)}) collective-permute-start(bf16[1,80,360]{2,1,0:T(8,128)(2,1)S(1)} %fusion.6), channel_id=1, source_target_pairs={{0,2},{1,3},{2,0},{3,1},{4,6},{5,7},{6,4},{7,5},{8,10},{9,11},{10,... | collective-permute-start | bytes 172808 | tf_op jit(solution)/shard_map/ppermute | solution.py:248
  84.7 4.2 %collective-permute-start.24 = (bf16[1,80,360]{2,1,0:T(8,128)(2,1)S(1)}, bf16[1,80,360]{2,1,0:T(8,128)(2,1)S(1)}, u32[]{:S(2)}, u32[]{:S(2)}) collective-permute-start(bf16[1,80,360]{2,1,0:T(8,128)(2,1)S(1)} %fusion.6), channel_id=1, source_target_pairs={{0,1},{1,0},{2,3},{3,2},{4,5},{5,4},{6,7},{7,6},{8,9},{9,8},{10,11... | collective-permute-start | bytes 172808 | tf_op jit(solution)/shard_map/ppermute | solution.py:248

commit v13 on v12

--- a/solution.py
+++ b/solution.py
@@ -66,7 +66,7 @@
         out_specs=block,
         out_shape=jax.ShapeDtypeStruct(tiles.shape, bf16),
         input_output_aliases={} if into is None else {2: 0},
-        compiler_params=pltpu.CompilerParams(vmem_limit_bytes=60 * 2**20),
+        compiler_params=pltpu.CompilerParams(vmem_limit_bytes=24 * 2**20),
         cost_estimate=pl.CostEstimate(
             flops=20 * size, bytes_accessed=4 * size, transcendentals=size
         ),

time: 88.5 us -> 86.2 us (0.974); the launches traced: 89.9 us -> 85.8 us
  waiting for transfers between devices: 17.7 us -> 13.2 us
  Pallas kernels: 33.4 us -> 29.2 us
  starting transfers between devices: 30.1 us -> 32.5 us
  local copies, waits for them, and re-layouts: 1.17 us -> 3.34 us
    ppermute x33, waiting for transfers between devices: 17.7 us -> 13.2 us  [swap(): return lax.ppermute(values, axis, pairs)]
    pallas_call x2, Pallas kernels: 9.88 us -> 5.65 us  [group_norm(): pl.pallas_call(functools.partial(norm_kernel, group_width), grid=(last -...]
    ppermute x33, starting transfers between devices: 30.1 us -> 32.5 us  [swap(): return lax.ppermute(values, axis, pairs)]
    unnamed x10 -> x12, local copies, waits for them, and re-layouts: 0.89 us -> 3.06 us
  transfers between devices with their start and end apart: 33 -> 33, of which waited for: 9 -> 14; matrix products, arithmetic and copies ran while one was open for 5% -> 6% of each run, Pallas kernels for 11% -> 7%
where the time goes in v13:
time: 86.2 us; the launch traced here: 85.8 us
  starting transfers between devices  32.5 us (38%)
  Pallas kernels  29.2 us (34%)
  waiting for transfers between devices  13.2 us (15%)
  other arithmetic  6.52 us (8%)
  local copies, waits for them, and re-layouts  3.34 us (4%)
  between operations  0.98 us (1%)
    ppermute x33, starting transfers between devices, swap(): return lax.ppermute(values, axis, pairs)  32.5 us
    pallas_call x1, Pallas kernels, conv_both(): pl.pallas_call(functools.partial(conv_kernel, steps), grid_spec=pltpu.Pre...  23.6 us
    ppermute x33, waiting for transfers between devices, swap(): return lax.ppermute(values, axis, pairs)  13.2 us
    pallas_call x2, Pallas kernels, group_norm(): pl.pallas_call(functools.partial(norm_kernel, group_width), grid=(last -...  5.65 us
    unnamed x12, local copies, waits for them, and re-layouts  3.06 us
  transfers between devices with their start and end apart: 33, of which 14 were waited for; matrix products, arithmetic and copies ran while one was open for 6% of the time, Pallas kernels for 7%

profile of v13, /device:TPU:0, one launch (start us, length us, event | category | flops | bytes accessed | tf_op | source)
XLA Modules:
  0.0 85.8 jit_solution(16272742378658904627)
XLA Ops:
  0.6 1.1 %convert_element_type.151 = bf16[360,320]{0,1:T(8,128)(2,1)S(1)} convert(f32[360,320]{0,1:T(8,128)} %param.12) | non-fusion elementwise | flops 115200 | bytes 691200 | tf_op jit(solution)/shard_map/convert_element_type | solution.py:315
  1.8 5.1 %collective-permute-start.2 = (bf16[1,80,360]{2,1,0:T(8,128)(2,1)S(1)}, bf16[1,80,360]{2,1,0:T(8,128)(2,1)S(1)}, u32[]{:S(2)}, u32[]{:S(2)}) collective-permute-start(bf16[1,80,360]{2,1,0:T(8,128)(2,1)S(1)} %get-tuple-element.72), channel_id=1, source_target_pairs={{0,24},{4,28},{8,16},{12,20},{16,8},{20,12},{24,0},{28,4},{1,25},{... | collective-permute-start | bytes 172808 | tf_op jit(solution)/shard_map/ppermute | solution.py:248
  6.9 0.6 collective-permute-start
  7.5 1.0 %convert_bitcast_fusion.2 = (bf16[1,1,160,320]{3,2,1,0:T(8,128)(2,1)S(1)}, bf16[1,160,320]{2,1,0:T(8,128)(2,1)S(1)}) fusion(f32[160,320]{1,0:T(8,128)} %param.13), kind=kLoop, calls=%fused_computation.44 | loop fusion | flops 51200 | bytes 409600 | tf_op jit(solution)/shard_map/stack;broadcast_in_dim | solution.py:264
  8.5 2.4 %collective-permute-start.6 = (bf16[1,160,320]{2,1,0:T(8,128)(2,1)S(1)}, bf16[1,160,320]{2,1,0:T(8,128)(2,1)S(1)}, u32[]{:S(2)}, u32[]{:S(2)}) collective-permute-start(bf16[1,160,320]{2,1,0:T(8,128)(2,1)S(1)} %get-tuple-element.68), channel_id=1, source_target_pairs={{0,16},{4,20},{8,24},{12,28},{16,0},{20,4},{24,8},{28,12},{1,17},{... | collective-permute-start | bytes 307208 | tf_op jit(solution)/shard_map/ppermute | solution.py:248
  10.9 1.7 %copy-done = bf16[1,15,256,320]{2,3,1,0:T(8,128)(2,1)S(1)} copy-done((bf16[1,15,256,320]{2,3,1,0:T(8,128)(2,1)S(1)}, bf16[1,15,256,320]{2,3,1,0:T(8,128)(2,1)}, u32[]{:S(2)}) %copy-start) | copy-done | bytes 2457624
  12.5 0.9 %copy-done.2 = bf16[320,320]{1,0:T(8,128)(2,1)S(1)} copy-done((bf16[320,320]{1,0:T(8,128)(2,1)S(1)}, bf16[320,320]{1,0:T(8,128)(2,1)}, u32[]{:S(2)}) %copy-start.2) | copy-done | bytes 204824
  13.5 1.9 %group_norm.2.refs_0_ = bf16[15,320,256]{2,1,0:T(8,128)(2,1)S(1)} custom-call(bf16[320,320]{1,0:T(8,128)(2,1)S(1)} %copy-done.2, bf16[15,320,256]{2,1,0:T(8,128)(2,1)S(1)} %bitcast.88), custom_call_target="tpu_custom_call" | custom-call | flops 8192000 | bytes 1638400 | tf_op jit(solution)/shard_map/group_norm/pallas_call | solution.py:62
  15.6 2.5 %collective-permute-start.5 = (bf16[1,3,80,360]{3,2,1,0:T(8,128)(2,1)S(1)}, bf16[1,3,80,360]{3,2,1,0:T(8,128)(2,1)S(1)}, u32[]{:S(2)}, u32[]{:S(2)}) collective-permute-start(bf16[1,3,80,360]{3,2,1,0:T(8,128)(2,1)S(1)} %get-tuple-element.66), channel_id=1, source_target_pairs={{0,3},{1,2},{2,1},{3,0},{4,7},{5,6},{6,5},{7,4},{8,11},{9,10},{10,... | collective-permute-start | bytes 518408 | tf_op jit(solution)/shard_map/ppermute | solution.py:248
  18.1 0.5 collective-permute-start.4
  18.6 0.5 collective-permute-start.3
  19.2 2.1 %collective-permute-start.11 = (bf16[1,2,160,320]{3,2,1,0:T(8,128)(2,1)S(1)}, bf16[1,2,160,320]{3,2,1,0:T(8,128)(2,1)S(1)}, u32[]{:S(2)}, u32[]{:S(2)}) collective-permute-start(bf16[1,2,160,320]{3,2,1,0:T(8,128)(2,1)S(1)} %bitcast.98), channel_id=1, source_target_pairs={{0,8},{4,12},{8,0},{12,4},{16,24},{20,28},{24,16},{28,20},{1,9},{5... | collective-permute-start | bytes 614408 | tf_op jit(solution)/shard_map/ppermute | solution.py:248
  21.4 3.8 %group_norm.3.normed_ref = bf16[15,320,256]{2,1,0:T(8,128)(2,1)S(1)} custom-call(bf16[320,320]{1,0:T(8,128)(2,1)S(1)} %copy-done.2, bf16[15,320,256]{2,1,0:T(8,128)(2,1)S(1)} %bitcast.89, bf16[15,320,256]{2,1,0:T(8,128)(2,1)S(1)} %group_norm.2.refs_0_), custom_call_target="tpu_custom_call", output_to_operand_aliasing={{}: (2, {})} | custom-call | flops 16384000 | bytes 3276800 | tf_op jit(solution)/shard_map/group_norm/pallas_call | solution.py:62
  25.3 0.5 collective-permute-start.10
  25.8 0.3 collective-permute-done.4
  26.1 0.4 collective-permute-start.8
  27.2 1.2 %multiply_cosine_fusion = (f32[640,128]{1,0:T(8,128)S(1)}, f32[640,128]{1,0:T(8,128)S(1)}) fusion(f32[128]{0:T(128)S(1)} %pad_convert_fusion, f32[640]{0:T(1024)S(1)} %multiply_exponential_fusion), kind=kLoop, calls=%fused_computation.13 | loop fusion | flops 81920 | bytes 658432 | tf_op jit(solution)/shard_map/cos | solution.py:298
  29.0 0.4 copy-done.1
  29.4 23.6 %conv_both.1 = (bf16[15,320,256]{2,1,0:T(8,128)(2,1)}, bf16[4,160,320]{2,1,0:T(8,128)(2,1)S(1)}, bf16[4,160,320]{2,1,0:T(8,128)(2,1)S(1)}, bf16[4,80,360]{2,1,0:...) custom-call(s32[1,4]{1,0:T(1,128)S(1)} %copy-done.4, ...), custom_call_target="tpu_custom_call" | custom-call | flops 14155776000 | bytes 9830400 | tf_op jit(solution)/shard_map/conv_both/pallas_call | solution.py:216
  53.0 0.5 collective-permute-start.13
  53.5 0.5 collective-permute-start.18
  54.0 0.5 collective-permute-done.14
  54.6 0.6 collective-permute-done.16
  55.2 1.3 %collective-permute-start.17 = (bf16[4,80,360]{2,1,0:T(8,128)(2,1)S(1)}, bf16[4,80,360]{2,1,0:T(8,128)(2,1)S(1)}, u32[]{:S(2)}, u32[]{:S(2)}) collective-permute-start(bf16[4,80,360]{2,1,0:T(8,128)(2,1)S(1)} %add_convert_fusion.3), channel_id=1, source_target_pairs={{0,2},{1,3},{2,0},{3,1},{4,6},{5,7},{6,4},{7,5},{8,10},{9,11},{10,... | collective-permute-start | bytes 691208 | tf_op jit(solution)/shard_map/ppermute | solution.py:248
  56.7 1.8 %collective-permute-start.20 = (bf16[4,80,360]{2,1,0:T(8,128)(2,1)S(1)}, bf16[4,80,360]{2,1,0:T(8,128)(2,1)S(1)}, u32[]{:S(2)}, u32[]{:S(2)}) collective-permute-start(bf16[4,80,360]{2,1,0:T(8,128)(2,1)S(1)} %add_convert_fusion.2), channel_id=1, source_target_pairs={{0,3},{1,2},{2,1},{3,0},{4,7},{5,6},{6,5},{7,4},{8,11},{9,10},{10,... | collective-permute-start | bytes 691208 | tf_op jit(solution)/shard_map/ppermute | solution.py:248
  58.5 1.3 %collective-permute-start.27 = (bf16[1,160,320]{2,1,0:T(8,128)(2,1)S(1)}, bf16[1,160,320]{2,1,0:T(8,128)(2,1)S(1)}, u32[]{:S(2)}, u32[]{:S(2)}) collective-permute-start(bf16[1,160,320]{2,1,0:T(8,128)(2,1)S(1)} %get-tuple-element.55), channel_id=1, source_target_pairs={{0,8},{4,12},{8,0},{12,4},{16,24},{20,28},{24,16},{28,20},{1,9},{5... | collective-permute-start | bytes 307208 | tf_op jit(solution)/shard_map/ppermute | solution.py:248
  59.9 0.9 collective-permute-start.29
  60.7 2.7 %collective-permute-done.15 = bf16[4,80,360]{2,1,0:T(8,128)(2,1)S(1)} collective-permute-done((bf16[4,80,360]{2,1,0:T(8,128)(2,1)S(1)}, bf16[4,80,360]{2,1,0:T(8,128)(2,1)S(1)}, u32[]{:S(2)}, u32[]{:S(2)}) %collective-permute-start.15) | collective-permute-done | bytes 230432 | tf_op jit(solution)/shard_map/ppermute | solution.py:248
  63.4 0.6 collective-permute-start.28
  64.0 3.5 %collective-permute-done.17 = bf16[4,80,360]{2,1,0:T(8,128)(2,1)S(1)} collective-permute-done((bf16[4,80,360]{2,1,0:T(8,128)(2,1)S(1)}, bf16[4,80,360]{2,1,0:T(8,128)(2,1)S(1)}, u32[]{:S(2)}, u32[]{:S(2)}) %collective-permute-start.17) | collective-permute-done | bytes 230432 | tf_op jit(solution)/shard_map/ppermute | solution.py:248
  67.6 1.2 %collective-permute-done.20 = bf16[4,80,360]{2,1,0:T(8,128)(2,1)S(1)} collective-permute-done((bf16[4,80,360]{2,1,0:T(8,128)(2,1)S(1)}, bf16[4,80,360]{2,1,0:T(8,128)(2,1)S(1)}, u32[]{:S(2)}, u32[]{:S(2)}) %collective-permute-start.20) | collective-permute-done | bytes 230432 | tf_op jit(solution)/shard_map/ppermute | solution.py:248
  68.9 1.9 %collective-permute-start.21 = (bf16[1,80,360]{2,1,0:T(8,128)(2,1)S(1)}, bf16[1,80,360]{2,1,0:T(8,128)(2,1)S(1)}, u32[]{:S(2)}, u32[]{:S(2)}) collective-permute-start(bf16[1,80,360]{2,1,0:T(8,128)(2,1)S(1)} %get-tuple-element.62), channel_id=1, source_target_pairs={{0,8},{4,12},{8,0},{12,4},{16,24},{20,28},{24,16},{28,20},{1,9},{5... | collective-permute-start | bytes 172808 | tf_op jit(solution)/shard_map/ppermute | solution.py:248
  70.8 0.7 collective-permute-start.23
  71.5 0.9 %collective-permute-start.22 = (bf16[1,80,360]{2,1,0:T(8,128)(2,1)S(1)}, bf16[1,80,360]{2,1,0:T(8,128)(2,1)S(1)}, u32[]{:S(2)}, u32[]{:S(2)}) collective-permute-start(bf16[1,80,360]{2,1,0:T(8,128)(2,1)S(1)} %get-tuple-element.64), channel_id=1, source_target_pairs={{0,16},{4,20},{8,24},{12,28},{16,0},{20,4},{24,8},{28,12},{1,17},{... | collective-permute-start | bytes 172808 | tf_op jit(solution)/shard_map/ppermute | solution.py:248
  72.5 0.8 collective-permute-done.28
  73.3 1.2 %collective-permute-start.32 = (bf16[160,320]{1,0:T(8,128)(2,1)S(1)}, bf16[160,320]{1,0:T(8,128)(2,1)S(1)}, u32[]{:S(2)}, u32[]{:S(2)}) collective-permute-start(bf16[160,320]{1,0:T(8,128)(2,1)S(1)} %fusion.4), channel_id=1, source_target_pairs={{0,3},{1,2},{2,1},{3,0},{4,7},{5,6},{6,5},{7,4},{8,11},{9,10},{10,... | collective-permute-start | bytes 307208 | tf_op jit(solution)/shard_map/ppermute | solution.py:248
  74.5 1.3 %collective-permute-start.31 = (bf16[160,320]{1,0:T(8,128)(2,1)S(1)}, bf16[160,320]{1,0:T(8,128)(2,1)S(1)}, u32[]{:S(2)}, u32[]{:S(2)}) collective-permute-start(bf16[160,320]{1,0:T(8,128)(2,1)S(1)} %fusion.4), channel_id=1, source_target_pairs={{0,2},{1,3},{2,0},{3,1},{4,6},{5,7},{6,4},{7,5},{8,10},{9,11},{10,... | collective-permute-start | bytes 307208 | tf_op jit(solution)/shard_map/ppermute | solution.py:248
  75.9 1.0 %collective-permute-start.30 = (bf16[160,320]{1,0:T(8,128)(2,1)S(1)}, bf16[160,320]{1,0:T(8,128)(2,1)S(1)}, u32[]{:S(2)}, u32[]{:S(2)}) collective-permute-start(bf16[160,320]{1,0:T(8,128)(2,1)S(1)} %fusion.4), channel_id=1, source_target_pairs={{0,1},{1,0},{2,3},{3,2},{4,5},{5,4},{6,7},{7,6},{8,9},{9,8},{10,11... | collective-permute-start | bytes 307208 | tf_op jit(solution)/shard_map/ppermute | solution.py:248
  76.9 1.4 %collective-permute-done.22 = bf16[1,80,360]{2,1,0:T(8,128)(2,1)S(1)} collective-permute-done((bf16[1,80,360]{2,1,0:T(8,128)(2,1)S(1)}, bf16[1,80,360]{2,1,0:T(8,128)(2,1)S(1)}, u32[]{:S(2)}, u32[]{:S(2)}) %collective-permute-start.22) | collective-permute-done | bytes 57632 | tf_op jit(solution)/shard_map/ppermute | solution.py:248
  78.4 1.5 %collective-permute-start.26 = (bf16[1,80,360]{2,1,0:T(8,128)(2,1)S(1)}, bf16[1,80,360]{2,1,0:T(8,128)(2,1)S(1)}, u32[]{:S(2)}, u32[]{:S(2)}) collective-permute-start(bf16[1,80,360]{2,1,0:T(8,128)(2,1)S(1)} %fusion.6), channel_id=1, source_target_pairs={{0,3},{1,2},{2,1},{3,0},{4,7},{5,6},{6,5},{7,4},{8,11},{9,10},{10,... | collective-permute-start | bytes 172808 | tf_op jit(solution)/shard_map/ppermute | solution.py:248
  79.8 0.8 collective-permute-start.25
  80.6 1.3 %collective-permute-start.24 = (bf16[1,80,360]{2,1,0:T(8,128)(2,1)S(1)}, bf16[1,80,360]{2,1,0:T(8,128)(2,1)S(1)}, u32[]{:S(2)}, u32[]{:S(2)}) collective-permute-start(bf16[1,80,360]{2,1,0:T(8,128)(2,1)S(1)} %fusion.6), channel_id=1, source_target_pairs={{0,1},{1,0},{2,3},{3,2},{4,5},{5,4},{6,7},{7,6},{8,9},{9,8},{10,11... | collective-permute-start | bytes 172808 | tf_op jit(solution)/shard_map/ppermute | solution.py:248
  81.9 0.7 collective-permute-done.30
  82.6 0.8 fusion.3
  83.4 0.5 collective-permute-done.26
  83.8 0.6 collective-permute-done.25
  84.5 0.4 collective-permute-done.24
  85.0 0.8 convert_bitcast_fusion
  (64 shorter events, 2.5 us)
Async XLA Ops:
  1.8 13.7 %collective-permute-start.2 = (bf16[1,80,360]{2,1,0:T(8,128)(2,1)S(1)}, bf16[1,80,360]{2,1,0:T(8,128)(2,1)S(1)}, u32[]{:S(2)}, u32[]{:S(2)}) collective-permute-start(bf16[1,80,360]{2,1,0:T(8,128)(2,1)S(1)} %get-tuple-element.72), channel_id=1, source_target_pairs={{0,24},{4,28},{8,16},{12,20},{16,8},{20,12},{24,0},{28,4},{1,25},{... | collective-permute-start | bytes 172808 | tf_op jit(solution)/shard_map/ppermute | solution.py:248
  6.9 8.6 %collective-permute-start.1 = (bf16[1,80,360]{2,1,0:T(8,128)(2,1)S(1)}, bf16[1,80,360]{2,1,0:T(8,128)(2,1)S(1)}, u32[]{:S(2)}, u32[]{:S(2)}) collective-permute-start(bf16[1,80,360]{2,1,0:T(8,128)(2,1)S(1)} %get-tuple-element.72), channel_id=1, source_target_pairs={{0,16},{4,20},{8,24},{12,28},{16,0},{20,4},{24,8},{28,12},{1,17},{... | collective-permute-start | bytes 172808 | tf_op jit(solution)/shard_map/ppermute | solution.py:248
  6.9 8.6 %collective-permute-start = (bf16[1,80,360]{2,1,0:T(8,128)(2,1)S(1)}, bf16[1,80,360]{2,1,0:T(8,128)(2,1)S(1)}, u32[]{:S(2)}, u32[]{:S(2)}) collective-permute-start(bf16[1,80,360]{2,1,0:T(8,128)(2,1)S(1)} %get-tuple-element.72), channel_id=1, source_target_pairs={{0,8},{4,12},{8,0},{12,4},{16,24},{20,28},{24,16},{28,20},{1,9},{5... | collective-permute-start | bytes 172808 | tf_op jit(solution)/shard_map/ppermute | solution.py:248
  8.5 10.6 %collective-permute-start.6 = (bf16[1,160,320]{2,1,0:T(8,128)(2,1)S(1)}, bf16[1,160,320]{2,1,0:T(8,128)(2,1)S(1)}, u32[]{:S(2)}, u32[]{:S(2)}) collective-permute-start(bf16[1,160,320]{2,1,0:T(8,128)(2,1)S(1)} %get-tuple-element.68), channel_id=1, source_target_pairs={{0,16},{4,20},{8,24},{12,28},{16,0},{20,4},{24,8},{28,12},{1,17},{... | collective-permute-start | bytes 307208 | tf_op jit(solution)/shard_map/ppermute | solution.py:248
  10.9 1.7 %copy-start = (bf16[1,15,256,320]{2,3,1,0:T(8,128)(2,1)S(1)}, bf16[1,15,256,320]{2,3,1,0:T(8,128)(2,1)}, u32[]{:S(2)}) copy-start(bf16[1,15,256,320]{2,3,1,0:T(8,128)(2,1)} %param.8) | copy-start | bytes 7372804
  12.5 0.9 %copy-start.2 = (bf16[320,320]{1,0:T(8,128)(2,1)S(1)}, bf16[320,320]{1,0:T(8,128)(2,1)}, u32[]{:S(2)}) copy-start(bf16[320,320]{1,0:T(8,128)(2,1)} %constant.45.clone.same_ref) | copy-start | bytes 614404
  15.6 9.7 %collective-permute-start.5 = (bf16[1,3,80,360]{3,2,1,0:T(8,128)(2,1)S(1)}, bf16[1,3,80,360]{3,2,1,0:T(8,128)(2,1)S(1)}, u32[]{:S(2)}, u32[]{:S(2)}) collective-permute-start(bf16[1,3,80,360]{3,2,1,0:T(8,128)(2,1)S(1)} %get-tuple-element.66), channel_id=1, source_target_pairs={{0,3},{1,2},{2,1},{3,0},{4,7},{5,6},{6,5},{7,4},{8,11},{9,10},{10,... | collective-permute-start | bytes 518408 | tf_op jit(solution)/shard_map/ppermute | solution.py:248
  18.1 7.9 %collective-permute-start.4 = (bf16[1,3,80,360]{3,2,1,0:T(8,128)(2,1)S(1)}, bf16[1,3,80,360]{3,2,1,0:T(8,128)(2,1)S(1)}, u32[]{:S(2)}, u32[]{:S(2)}) collective-permute-start(bf16[1,3,80,360]{3,2,1,0:T(8,128)(2,1)S(1)} %get-tuple-element.66), channel_id=1, source_target_pairs={{0,2},{1,3},{2,0},{3,1},{4,6},{5,7},{6,4},{7,5},{8,10},{9,11},{10,... | collective-permute-start | bytes 518408 | tf_op jit(solution)/shard_map/ppermute | solution.py:248
  18.6 7.5 %collective-permute-start.3 = (bf16[1,3,80,360]{3,2,1,0:T(8,128)(2,1)S(1)}, bf16[1,3,80,360]{3,2,1,0:T(8,128)(2,1)S(1)}, u32[]{:S(2)}, u32[]{:S(2)}) collective-permute-start(bf16[1,3,80,360]{3,2,1,0:T(8,128)(2,1)S(1)} %get-tuple-element.66), channel_id=1, source_target_pairs={{0,1},{1,0},{2,3},{3,2},{4,5},{5,4},{6,7},{7,6},{8,9},{9,8},{10,11... | collective-permute-start | bytes 518408 | tf_op jit(solution)/shard_map/ppermute | solution.py:248
  19.2 7.6 %collective-permute-start.11 = (bf16[1,2,160,320]{3,2,1,0:T(8,128)(2,1)S(1)}, bf16[1,2,160,320]{3,2,1,0:T(8,128)(2,1)S(1)}, u32[]{:S(2)}, u32[]{:S(2)}) collective-permute-start(bf16[1,2,160,320]{3,2,1,0:T(8,128)(2,1)S(1)} %bitcast.98), channel_id=1, source_target_pairs={{0,8},{4,12},{8,0},{12,4},{16,24},{20,28},{24,16},{28,20},{1,9},{5... | collective-permute-start | bytes 614408 | tf_op jit(solution)/shard_map/ppermute | solution.py:248
  25.2 1.9 %copy-start.5 = (s32[1,15]{1,0:T(1,128)S(1)}, s32[1,15]{1,0:T(1,128)}, u32[]{:S(2)}) copy-start(s32[1,15]{1,0:T(1,128)} %param.11) | copy-start | bytes 184
  25.2 3.4 %collective-permute-start.7 = (bf16[7,80,360]{2,1,0:T(8,128)(2,1)S(1)}, bf16[7,80,360]{2,1,0:T(8,128)(2,1)S(1)}, u32[]{:S(2)}, u32[]{:S(2)}) collective-permute-start(bf16[7,80,360]{2,1,0:T(8,128)(2,1)S(1)} %pad_maximum_fusion.1), channel_id=1, source_target_pairs={{0,4},{4,0},{8,12},{12,8},{16,20},{20,16},{24,28},{28,24},{1,5},{5... | collective-permute-start | bytes 1209608 | tf_op jit(solution)/shard_map/ppermute | solution.py:248
  25.3 3.4 %collective-permute-start.10 = (bf16[1,3,80,360]{3,2,1,0:T(8,128)(2,1)S(1)}, bf16[1,3,80,360]{3,2,1,0:T(8,128)(2,1)S(1)}, u32[]{:S(2)}, u32[]{:S(2)}) collective-permute-start(bf16[1,3,80,360]{3,2,1,0:T(8,128)(2,1)S(1)} %collective-permute-done.5), channel_id=1, source_target_pairs={{0,4},{4,0},{8,12},{12,8},{16,20},{20,16},{24,28},{28,24},{1,5},{5... | collective-permute-start | bytes 518408 | tf_op jit(solution)/shard_map/ppermute | solution.py:248
  26.0 2.6 %collective-permute-start.9 = (bf16[1,3,80,360]{3,2,1,0:T(8,128)(2,1)S(1)}, bf16[1,3,80,360]{3,2,1,0:T(8,128)(2,1)S(1)}, u32[]{:S(2)}, u32[]{:S(2)}) collective-permute-start(bf16[1,3,80,360]{3,2,1,0:T(8,128)(2,1)S(1)} %collective-permute-done.4), channel_id=1, source_target_pairs={{0,4},{4,0},{8,12},{12,8},{16,20},{20,16},{24,28},{28,24},{1,5},{5... | collective-permute-start | bytes 518408 | tf_op jit(solution)/shard_map/ppermute | solution.py:248
  26.1 2.6 %collective-permute-start.8 = (bf16[1,3,80,360]{3,2,1,0:T(8,128)(2,1)S(1)}, bf16[1,3,80,360]{3,2,1,0:T(8,128)(2,1)S(1)}, u32[]{:S(2)}, u32[]{:S(2)}) collective-permute-start(bf16[1,3,80,360]{3,2,1,0:T(8,128)(2,1)S(1)} %collective-permute-done.3), channel_id=1, source_target_pairs={{0,4},{4,0},{8,12},{12,8},{16,20},{20,16},{24,28},{28,24},{1,5},{5... | collective-permute-start | bytes 518408 | tf_op jit(solution)/shard_map/ppermute | solution.py:248
  26.9 2.0 %copy-start.3 = (bf16[1,15,256,320]{2,3,1,0:T(8,128)(2,1)S(1)}, bf16[1,15,256,320]{2,3,1,0:T(8,128)(2,1)}, u32[]{:S(2)}) copy-start(bf16[1,15,256,320]{2,3,1,0:T(8,128)(2,1)} %param.9) | copy-start | bytes 7372804
  27.0 2.4 %copy-start.1 = (bf16[1,15,256,320]{2,3,1,0:T(8,128)(2,1)S(1)}, bf16[1,15,256,320]{2,3,1,0:T(8,128)(2,1)}, u32[]{:S(2)}) copy-start(bf16[1,15,256,320]{2,3,1,0:T(8,128)(2,1)} %param.8) | copy-start | bytes 7372804
  27.0 2.4 %copy-start.4 = (s32[1,4]{1,0:T(1,128)S(1)}, s32[1,4]{1,0:T(1,128)}, u32[]{:S(2)}) copy-start(s32[1,4]{1,0:T(1,128)} %counts_ref.1) | copy-start | bytes 52
  27.0 1.9 %collective-permute-start.12 = (bf16[4,160,320]{2,1,0:T(8,128)(2,1)S(1)}, bf16[4,160,320]{2,1,0:T(8,128)(2,1)S(1)}, u32[]{:S(2)}, u32[]{:S(2)}) collective-permute-start(bf16[4,160,320]{2,1,0:T(8,128)(2,1)S(1)} %bitcast.91), channel_id=1, source_target_pairs={{0,4},{4,0},{8,12},{12,8},{16,20},{20,16},{24,28},{28,24},{1,5},{5... | collective-permute-start | bytes 1228808 | tf_op jit(solution)/shard_map/ppermute | solution.py:248
  53.0 1.5 %collective-permute-start.14 = (bf16[4,80,360]{2,1,0:T(8,128)(2,1)S(1)}, bf16[4,80,360]{2,1,0:T(8,128)(2,1)S(1)}, u32[]{:S(2)}, u32[]{:S(2)}) collective-permute-start(bf16[4,80,360]{2,1,0:T(8,128)(2,1)S(1)} %get-tuple-element.46), channel_id=1, source_target_pairs={{0,4},{4,0},{8,12},{12,8},{16,20},{20,16},{24,28},{28,24},{1,5},{5... | collective-permute-start | bytes 691208 | tf_op jit(solution)/shard_map/ppermute | solution.py:248
  53.0 6.9 %collective-permute-start.13 = (bf16[4,80,360]{2,1,0:T(8,128)(2,1)S(1)}, bf16[4,80,360]{2,1,0:T(8,128)(2,1)S(1)}, u32[]{:S(2)}, u32[]{:S(2)}) collective-permute-start(bf16[4,80,360]{2,1,0:T(8,128)(2,1)S(1)} %get-tuple-element.44), channel_id=1, source_target_pairs={{0,4},{4,0},{8,12},{12,8},{16,20},{20,16},{24,28},{28,24},{1,5},{5... | collective-permute-start | bytes 691208 | tf_op jit(solution)/shard_map/ppermute | solution.py:248
  53.5 1.7 %collective-permute-start.16 = (bf16[4,80,360]{2,1,0:T(8,128)(2,1)S(1)}, bf16[4,80,360]{2,1,0:T(8,128)(2,1)S(1)}, u32[]{:S(2)}, u32[]{:S(2)}) collective-permute-start(bf16[4,80,360]{2,1,0:T(8,128)(2,1)S(1)} %get-tuple-element.48), channel_id=1, source_target_pairs={{0,4},{4,0},{8,12},{12,8},{16,20},{20,16},{24,28},{28,24},{1,5},{5... | collective-permute-start | bytes 691208 | tf_op jit(solution)/shard_map/ppermute | solution.py:248
  53.5 3.1 %collective-permute-start.18 = (bf16[4,80,360]{2,1,0:T(8,128)(2,1)S(1)}, bf16[4,80,360]{2,1,0:T(8,128)(2,1)S(1)}, u32[]{:S(2)}, u32[]{:S(2)}) collective-permute-start(bf16[4,80,360]{2,1,0:T(8,128)(2,1)S(1)} %get-tuple-element.50), channel_id=1, source_target_pairs={{0,4},{4,0},{8,12},{12,8},{16,20},{20,16},{24,28},{28,24},{1,5},{5... | collective-permute-start | bytes 691208 | tf_op jit(solution)/shard_map/ppermute | solution.py:248
  54.0 2.6 %collective-permute-start.19 = (bf16[4,160,320]{2,1,0:T(8,128)(2,1)S(1)}, bf16[4,160,320]{2,1,0:T(8,128)(2,1)S(1)}, u32[]{:S(2)}, u32[]{:S(2)}) collective-permute-start(bf16[4,160,320]{2,1,0:T(8,128)(2,1)S(1)} %get-tuple-element.52), channel_id=1, source_target_pairs={{0,4},{4,0},{8,12},{12,8},{16,20},{20,16},{24,28},{28,24},{1,5},{5... | collective-permute-start | bytes 1228808 | tf_op jit(solution)/shard_map/ppermute | solution.py:248
  54.5 8.9 %collective-permute-start.15 = (bf16[4,80,360]{2,1,0:T(8,128)(2,1)S(1)}, bf16[4,80,360]{2,1,0:T(8,128)(2,1)S(1)}, u32[]{:S(2)}, u32[]{:S(2)}) collective-permute-start(bf16[4,80,360]{2,1,0:T(8,128)(2,1)S(1)} %add_convert_fusion.4), channel_id=1, source_target_pairs={{0,1},{1,0},{2,3},{3,2},{4,5},{5,4},{6,7},{7,6},{8,9},{9,8},{10,11... | collective-permute-start | bytes 691208 | tf_op jit(solution)/shard_map/ppermute | solution.py:248
  55.2 12.3 %collective-permute-start.17 = (bf16[4,80,360]{2,1,0:T(8,128)(2,1)S(1)}, bf16[4,80,360]{2,1,0:T(8,128)(2,1)S(1)}, u32[]{:S(2)}, u32[]{:S(2)}) collective-permute-start(bf16[4,80,360]{2,1,0:T(8,128)(2,1)S(1)} %add_convert_fusion.3), channel_id=1, source_target_pairs={{0,2},{1,3},{2,0},{3,1},{4,6},{5,7},{6,4},{7,5},{8,10},{9,11},{10,... | collective-permute-start | bytes 691208 | tf_op jit(solution)/shard_map/ppermute | solution.py:248
  56.7 12.0 %collective-permute-start.20 = (bf16[4,80,360]{2,1,0:T(8,128)(2,1)S(1)}, bf16[4,80,360]{2,1,0:T(8,128)(2,1)S(1)}, u32[]{:S(2)}, u32[]{:S(2)}) collective-permute-start(bf16[4,80,360]{2,1,0:T(8,128)(2,1)S(1)} %add_convert_fusion.2), channel_id=1, source_target_pairs={{0,3},{1,2},{2,1},{3,0},{4,7},{5,6},{6,5},{7,4},{8,11},{9,10},{10,... | collective-permute-start | bytes 691208 | tf_op jit(solution)/shard_map/ppermute | solution.py:248
  58.5 13.0 %collective-permute-start.27 = (bf16[1,160,320]{2,1,0:T(8,128)(2,1)S(1)}, bf16[1,160,320]{2,1,0:T(8,128)(2,1)S(1)}, u32[]{:S(2)}, u32[]{:S(2)}) collective-permute-start(bf16[1,160,320]{2,1,0:T(8,128)(2,1)S(1)} %get-tuple-element.55), channel_id=1, source_target_pairs={{0,8},{4,12},{8,0},{12,4},{16,24},{20,28},{24,16},{28,20},{1,9},{5... | collective-permute-start | bytes 307208 | tf_op jit(solution)/shard_map/ppermute | solution.py:248
  59.9 12.6 %collective-permute-start.29 = (bf16[1,160,320]{2,1,0:T(8,128)(2,1)S(1)}, bf16[1,160,320]{2,1,0:T(8,128)(2,1)S(1)}, u32[]{:S(2)}, u32[]{:S(2)}) collective-permute-start(bf16[1,160,320]{2,1,0:T(8,128)(2,1)S(1)} %get-tuple-element.56), channel_id=1, source_target_pairs={{0,24},{4,28},{8,16},{12,20},{16,8},{20,12},{24,0},{28,4},{1,25},{... | collective-permute-start | bytes 307208 | tf_op jit(solution)/shard_map/ppermute | solution.py:248
  63.4 9.8 %collective-permute-start.28 = (bf16[1,160,320]{2,1,0:T(8,128)(2,1)S(1)}, bf16[1,160,320]{2,1,0:T(8,128)(2,1)S(1)}, u32[]{:S(2)}, u32[]{:S(2)}) collective-permute-start(bf16[1,160,320]{2,1,0:T(8,128)(2,1)S(1)} %get-tuple-element.57), channel_id=1, source_target_pairs={{0,16},{4,20},{8,24},{12,28},{16,0},{20,4},{24,8},{28,12},{1,17},{... | collective-permute-start | bytes 307208 | tf_op jit(solution)/shard_map/ppermute | solution.py:248
  68.9 6.9 %collective-permute-start.21 = (bf16[1,80,360]{2,1,0:T(8,128)(2,1)S(1)}, bf16[1,80,360]{2,1,0:T(8,128)(2,1)S(1)}, u32[]{:S(2)}, u32[]{:S(2)}) collective-permute-start(bf16[1,80,360]{2,1,0:T(8,128)(2,1)S(1)} %get-tuple-element.62), channel_id=1, source_target_pairs={{0,8},{4,12},{8,0},{12,4},{16,24},{20,28},{24,16},{28,20},{1,9},{5... | collective-permute-start | bytes 172808 | tf_op jit(solution)/shard_map/ppermute | solution.py:248
  70.8 6.1 %collective-permute-start.23 = (bf16[1,80,360]{2,1,0:T(8,128)(2,1)S(1)}, bf16[1,80,360]{2,1,0:T(8,128)(2,1)S(1)}, u32[]{:S(2)}, u32[]{:S(2)}) collective-permute-start(bf16[1,80,360]{2,1,0:T(8,128)(2,1)S(1)} %get-tuple-element.63), channel_id=1, source_target_pairs={{0,24},{4,28},{8,16},{12,20},{16,8},{20,12},{24,0},{28,4},{1,25},{... | collective-permute-start | bytes 172808 | tf_op jit(solution)/shard_map/ppermute | solution.py:248
  71.5 6.8 %collective-permute-start.22 = (bf16[1,80,360]{2,1,0:T(8,128)(2,1)S(1)}, bf16[1,80,360]{2,1,0:T(8,128)(2,1)S(1)}, u32[]{:S(2)}, u32[]{:S(2)}) collective-permute-start(bf16[1,80,360]{2,1,0:T(8,128)(2,1)S(1)} %get-tuple-element.64), channel_id=1, source_target_pairs={{0,16},{4,20},{8,24},{12,28},{16,0},{20,4},{24,8},{28,12},{1,17},{... | collective-permute-start | bytes 172808 | tf_op jit(solution)/shard_map/ppermute | solution.py:248
  73.3 7.3 %collective-permute-start.32 = (bf16[160,320]{1,0:T(8,128)(2,1)S(1)}, bf16[160,320]{1,0:T(8,128)(2,1)S(1)}, u32[]{:S(2)}, u32[]{:S(2)}) collective-permute-start(bf16[160,320]{1,0:T(8,128)(2,1)S(1)} %fusion.4), channel_id=1, source_target_pairs={{0,3},{1,2},{2,1},{3,0},{4,7},{5,6},{6,5},{7,4},{8,11},{9,10},{10,... | collective-permute-start | bytes 307208 | tf_op jit(solution)/shard_map/ppermute | solution.py:248
  74.5 7.4 %collective-permute-start.31 = (bf16[160,320]{1,0:T(8,128)(2,1)S(1)}, bf16[160,320]{1,0:T(8,128)(2,1)S(1)}, u32[]{:S(2)}, u32[]{:S(2)}) collective-permute-start(bf16[160,320]{1,0:T(8,128)(2,1)S(1)} %fusion.4), channel_id=1, source_target_pairs={{0,2},{1,3},{2,0},{3,1},{4,6},{5,7},{6,4},{7,5},{8,10},{9,11},{10,... | collective-permute-start | bytes 307208 | tf_op jit(solution)/shard_map/ppermute | solution.py:248
  75.9 6.8 %collective-permute-start.30 = (bf16[160,320]{1,0:T(8,128)(2,1)S(1)}, bf16[160,320]{1,0:T(8,128)(2,1)S(1)}, u32[]{:S(2)}, u32[]{:S(2)}) collective-permute-start(bf16[160,320]{1,0:T(8,128)(2,1)S(1)} %fusion.4), channel_id=1, source_target_pairs={{0,1},{1,0},{2,3},{3,2},{4,5},{5,4},{6,7},{7,6},{8,9},{9,8},{10,11... | collective-permute-start | bytes 307208 | tf_op jit(solution)/shard_map/ppermute | solution.py:248
  78.4 5.5 %collective-permute-start.26 = (bf16[1,80,360]{2,1,0:T(8,128)(2,1)S(1)}, bf16[1,80,360]{2,1,0:T(8,128)(2,1)S(1)}, u32[]{:S(2)}, u32[]{:S(2)}) collective-permute-start(bf16[1,80,360]{2,1,0:T(8,128)(2,1)S(1)} %fusion.6), channel_id=1, source_target_pairs={{0,3},{1,2},{2,1},{3,0},{4,7},{5,6},{6,5},{7,4},{8,11},{9,10},{10,... | collective-permute-start | bytes 172808 | tf_op jit(solution)/shard_map/ppermute | solution.py:248
  79.8 4.6 %collective-permute-start.25 = (bf16[1,80,360]{2,1,0:T(8,128)(2,1)S(1)}, bf16[1,80,360]{2,1,0:T(8,128)(2,1)S(1)}, u32[]{:S(2)}, u32[]{:S(2)}) collective-permute-start(bf16[1,80,360]{2,1,0:T(8,128)(2,1)S(1)} %fusion.6), channel_id=1, source_target_pairs={{0,2},{1,3},{2,0},{3,1},{4,6},{5,7},{6,4},{7,5},{8,10},{9,11},{10,... | collective-permute-start | bytes 172808 | tf_op jit(solution)/shard_map/ppermute | solution.py:248
  80.6 4.2 %collective-permute-start.24 = (bf16[1,80,360]{2,1,0:T(8,128)(2,1)S(1)}, bf16[1,80,360]{2,1,0:T(8,128)(2,1)S(1)}, u32[]{:S(2)}, u32[]{:S(2)}) collective-permute-start(bf16[1,80,360]{2,1,0:T(8,128)(2,1)S(1)} %fusion.6), channel_id=1, source_target_pairs={{0,1},{1,0},{2,3},{3,2},{4,5},{5,4},{6,7},{7,6},{8,9},{9,8},{10,11... | collective-permute-start | bytes 172808 | tf_op jit(solution)/shard_map/ppermute | solution.py:248

commit v14 on v13

--- a/solution.py
+++ b/solution.py
@@ -3,7 +3,6 @@
 
 import jax
 import jax.numpy as jnp
-import numpy as np
 from jax import lax
 from jax.experimental import pallas as pl
 from jax.experimental.pallas import tpu as pltpu
@@ -21,10 +20,15 @@
     return max(size for size in range(1, 6) if number % size == 0)
 
 
-def norm_kernel(group_width, same_ref, tiles_ref, *refs):
+def norm_kernel(group_width, tiles_ref, *refs):
     out_ref = refs[-1]
-    same_group = same_ref[...]
     number, channels, pixels = tiles_ref.shape
+
+    def group_of(shape, axis):
+        channel = lax.broadcasted_iota(jnp.int32, shape, axis).astype(f32)
+        return jnp.floor((channel + 0.5) * (1.0 / group_width))
+
+    same_group = (group_of((channels, channels), 0) == group_of((channels, channels), 1)).astype(bf16)
     scale = 1.0 / (group_width * pixels)
     lane = lax.broadcasted_iota(jnp.int32, (channels, LANES), 1)
 
@@ -52,11 +56,9 @@
     number, channels, pixels = tiles.shape
     step = tiles_per_step(number)
     group_width = channels // GROUPS
-    group = np.arange(channels) // group_width
-    same_group = jnp.asarray(group[:, None] == group[None, :], bf16)
     block = pl.BlockSpec((step, channels, pixels), lambda i: (i + first, 0, 0))
     size = (last - first) * step * channels * pixels
-    operands, specs = [same_group, tiles], [pl.BlockSpec((channels, channels), lambda i: (0, 0)), block]
+    operands, specs = [tiles], [block]
     if into is not None:
         operands, specs = operands + [into], specs + [pl.BlockSpec(memory_space=pl.ANY)]
     return pl.pallas_call(
@@ -65,7 +67,7 @@
         in_specs=specs,
         out_specs=block,
         out_shape=jax.ShapeDtypeStruct(tiles.shape, bf16),
-        input_output_aliases={} if into is None else {2: 0},
+        input_output_aliases={} if into is None else {1: 0},
         compiler_params=pltpu.CompilerParams(vmem_limit_bytes=24 * 2**20),
         cost_estimate=pl.CostEstimate(
             flops=20 * size, bytes_accessed=4 * size, transcendentals=size

time: 86.2 us -> 85.9 us (level)
  starting transfers between devices: 32.5 us -> 40.3 us
  Pallas kernels: 29.2 us -> 22.8 us
  local copies, waits for them, and re-layouts: 3.34 us -> 2.4 us
    ppermute x33, starting transfers between devices: 32.5 us -> 40.3 us  [swap(): return lax.ppermute(values, axis, pairs)]
    pallas_call x1, Pallas kernels: 23.6 us -> 17.2 us  [conv_both(): pl.pallas_call(functools.partial(conv_kernel, steps), grid_spec=pltpu.Pre...]
    unnamed x12 -> x10, local copies, waits for them, and re-layouts: 3.06 us -> 2.12 us
  transfers between devices with their start and end apart: 33 -> 33, of which waited for: 14 -> 13; matrix products, arithmetic and copies ran while one was open for 6% -> 6% of each run, Pallas kernels for 7% -> 7%
where the time goes in v14:
time: 85.9 us; the launch traced here: 85.6 us
  starting transfers between devices  40.3 us (47%)
  Pallas kernels  22.8 us (27%)
  waiting for transfers between devices  12.5 us (15%)
  other arithmetic  6.52 us (8%)
  local copies, waits for them, and re-layouts  2.4 us (3%)
  between operations  0.98 us (1%)
    ppermute x33, starting transfers between devices, swap(): return lax.ppermute(values, axis, pairs)  40.3 us
    pallas_call x1, Pallas kernels, conv_both(): pl.pallas_call(functools.partial(conv_kernel, steps), grid_spec=pltpu.Pre...  17.2 us
    ppermute x33, waiting for transfers between devices, swap(): return lax.ppermute(values, axis, pairs)  12.5 us
    pallas_call x2, Pallas kernels, group_norm(): pl.pallas_call(functools.partial(norm_kernel, group_width), grid=(last -...  5.61 us
    unnamed x10, local copies, waits for them, and re-layouts  2.12 us
  transfers between devices with their start and end apart: 33, of which 13 were waited for; matrix products, arithmetic and copies ran while one was open for 6% of the time, Pallas kernels for 7%

profile of v14, /device:TPU:0, one launch (start us, length us, event | category | flops | bytes accessed | tf_op | source)
XLA Modules:
  0.0 85.6 jit_solution(12146782688794306383)
XLA Ops:
  0.6 1.1 %convert_element_type.151 = bf16[360,320]{0,1:T(8,128)(2,1)S(1)} convert(f32[360,320]{0,1:T(8,128)} %param.10) | non-fusion elementwise | flops 115200 | bytes 691200 | tf_op jit(solution)/shard_map/convert_element_type | solution.py:317
  1.8 5.1 %collective-permute-start.2 = (bf16[1,80,360]{2,1,0:T(8,128)(2,1)S(1)}, bf16[1,80,360]{2,1,0:T(8,128)(2,1)S(1)}, u32[]{:S(2)}, u32[]{:S(2)}) collective-permute-start(bf16[1,80,360]{2,1,0:T(8,128)(2,1)S(1)} %get-tuple-element.72), channel_id=1, source_target_pairs={{0,24},{4,28},{8,16},{12,20},{16,8},{20,12},{24,0},{28,4},{1,25},{... | collective-permute-start | bytes 172808 | tf_op jit(solution)/shard_map/ppermute | solution.py:250
  6.9 0.6 collective-permute-start
  7.5 1.0 %convert_bitcast_fusion.2 = (bf16[1,1,160,320]{3,2,1,0:T(8,128)(2,1)S(1)}, bf16[1,160,320]{2,1,0:T(8,128)(2,1)S(1)}) fusion(f32[160,320]{1,0:T(8,128)} %param.11), kind=kLoop, calls=%fused_computation.44 | loop fusion | flops 51200 | bytes 409600 | tf_op jit(solution)/shard_map/stack;broadcast_in_dim | solution.py:266
  8.5 2.4 %collective-permute-start.6 = (bf16[1,160,320]{2,1,0:T(8,128)(2,1)S(1)}, bf16[1,160,320]{2,1,0:T(8,128)(2,1)S(1)}, u32[]{:S(2)}, u32[]{:S(2)}) collective-permute-start(bf16[1,160,320]{2,1,0:T(8,128)(2,1)S(1)} %get-tuple-element.68), channel_id=1, source_target_pairs={{0,16},{4,20},{8,24},{12,28},{16,0},{20,4},{24,8},{28,12},{1,17},{... | collective-permute-start | bytes 307208 | tf_op jit(solution)/shard_map/ppermute | solution.py:250
  10.9 1.7 %copy-done = bf16[1,15,256,320]{2,3,1,0:T(8,128)(2,1)S(1)} copy-done((bf16[1,15,256,320]{2,3,1,0:T(8,128)(2,1)S(1)}, bf16[1,15,256,320]{2,3,1,0:T(8,128)(2,1)}, u32[]{:S(2)}) %copy-start) | copy-done | bytes 2457624
  12.5 1.9 %group_norm.2.refs_0_ = bf16[15,320,256]{2,1,0:T(8,128)(2,1)S(1)} custom-call(bf16[15,320,256]{2,1,0:T(8,128)(2,1)S(1)} %bitcast.88), custom_call_target="tpu_custom_call" | custom-call | flops 8192000 | bytes 1638400 | tf_op jit(solution)/shard_map/group_norm/pallas_call | solution.py:64
  14.6 2.5 %collective-permute-start.5 = (bf16[1,3,80,360]{3,2,1,0:T(8,128)(2,1)S(1)}, bf16[1,3,80,360]{3,2,1,0:T(8,128)(2,1)S(1)}, u32[]{:S(2)}, u32[]{:S(2)}) collective-permute-start(bf16[1,3,80,360]{3,2,1,0:T(8,128)(2,1)S(1)} %get-tuple-element.66), channel_id=1, source_target_pairs={{0,3},{1,2},{2,1},{3,0},{4,7},{5,6},{6,5},{7,4},{8,11},{9,10},{10,... | collective-permute-start | bytes 518408 | tf_op jit(solution)/shard_map/ppermute | solution.py:250
  17.1 0.5 collective-permute-start.4
  17.7 0.5 collective-permute-start.3
  18.2 2.1 %collective-permute-start.11 = (bf16[1,2,160,320]{3,2,1,0:T(8,128)(2,1)S(1)}, bf16[1,2,160,320]{3,2,1,0:T(8,128)(2,1)S(1)}, u32[]{:S(2)}, u32[]{:S(2)}) collective-permute-start(bf16[1,2,160,320]{3,2,1,0:T(8,128)(2,1)S(1)} %bitcast.98), channel_id=1, source_target_pairs={{0,8},{4,12},{8,0},{12,4},{16,24},{20,28},{24,16},{28,20},{1,9},{5... | collective-permute-start | bytes 614408 | tf_op jit(solution)/shard_map/ppermute | solution.py:250
  20.4 3.8 %group_norm.3.normed_ref = bf16[15,320,256]{2,1,0:T(8,128)(2,1)S(1)} custom-call(bf16[15,320,256]{2,1,0:T(8,128)(2,1)S(1)} %bitcast.89, bf16[15,320,256]{2,1,0:T(8,128)(2,1)S(1)} %group_norm.2.refs_0_), custom_call_target="tpu_custom_call", output_to_operand_aliasing={{}: (1, {})} | custom-call | flops 16384000 | bytes 3276800 | tf_op jit(solution)/shard_map/group_norm/pallas_call | solution.py:64
  24.3 0.5 collective-permute-start.10
  24.8 0.3 collective-permute-done.4
  25.2 0.4 collective-permute-start.8
  25.6 0.3 maximum_maximum_fusion.own_ref
  26.2 1.2 %multiply_cosine_fusion = (f32[640,128]{1,0:T(8,128)S(1)}, f32[640,128]{1,0:T(8,128)S(1)}) fusion(f32[128]{0:T(128)S(1)} %pad_convert_fusion, f32[640]{0:T(1024)S(1)} %multiply_exponential_fusion), kind=kLoop, calls=%fused_computation.13 | loop fusion | flops 81920 | bytes 658432 | tf_op jit(solution)/shard_map/cos | solution.py:300
  28.0 0.4 copy-done.1
  28.4 17.2 %conv_both.1 = (bf16[15,320,256]{2,1,0:T(8,128)(2,1)}, bf16[4,160,320]{2,1,0:T(8,128)(2,1)S(1)}, bf16[4,160,320]{2,1,0:T(8,128)(2,1)S(1)}, bf16[4,80,360]{2,1,0:...) custom-call(s32[1,4]{1,0:T(1,128)S(1)} %copy-done.3, ...), custom_call_target="tpu_custom_call" | custom-call | flops 14155776000 | bytes 9830400 | tf_op jit(solution)/shard_map/conv_both/pallas_call | solution.py:218
  45.7 6.4 %collective-permute-start.14 = (bf16[4,80,360]{2,1,0:T(8,128)(2,1)S(1)}, bf16[4,80,360]{2,1,0:T(8,128)(2,1)S(1)}, u32[]{:S(2)}, u32[]{:S(2)}) collective-permute-start(bf16[4,80,360]{2,1,0:T(8,128)(2,1)S(1)} %get-tuple-element.46), channel_id=1, source_target_pairs={{0,4},{4,0},{8,12},{12,8},{16,20},{20,16},{24,28},{28,24},{1,5},{5... | collective-permute-start | bytes 691208 | tf_op jit(solution)/shard_map/ppermute | solution.py:250
  52.1 0.5 collective-permute-start.16
  52.6 0.5 collective-permute-start.19
  53.4 0.6 collective-permute-done.16
  54.0 2.5 %collective-permute-start.17 = (bf16[4,80,360]{2,1,0:T(8,128)(2,1)S(1)}, bf16[4,80,360]{2,1,0:T(8,128)(2,1)S(1)}, u32[]{:S(2)}, u32[]{:S(2)}) collective-permute-start(bf16[4,80,360]{2,1,0:T(8,128)(2,1)S(1)} %add_convert_fusion.3), channel_id=1, source_target_pairs={{0,2},{1,3},{2,0},{3,1},{4,6},{5,7},{6,4},{7,5},{8,10},{9,11},{10,... | collective-permute-start | bytes 691208 | tf_op jit(solution)/shard_map/ppermute | solution.py:250
  56.7 0.9 %collective-permute-start.20 = (bf16[4,80,360]{2,1,0:T(8,128)(2,1)S(1)}, bf16[4,80,360]{2,1,0:T(8,128)(2,1)S(1)}, u32[]{:S(2)}, u32[]{:S(2)}) collective-permute-start(bf16[4,80,360]{2,1,0:T(8,128)(2,1)S(1)} %add_convert_fusion.2), channel_id=1, source_target_pairs={{0,3},{1,2},{2,1},{3,0},{4,7},{5,6},{6,5},{7,4},{8,11},{9,10},{10,... | collective-permute-start | bytes 691208 | tf_op jit(solution)/shard_map/ppermute | solution.py:250
  57.6 1.8 %collective-permute-start.27 = (bf16[1,160,320]{2,1,0:T(8,128)(2,1)S(1)}, bf16[1,160,320]{2,1,0:T(8,128)(2,1)S(1)}, u32[]{:S(2)}, u32[]{:S(2)}) collective-permute-start(bf16[1,160,320]{2,1,0:T(8,128)(2,1)S(1)} %get-tuple-element.55), channel_id=1, source_target_pairs={{0,8},{4,12},{8,0},{12,4},{16,24},{20,28},{24,16},{28,20},{1,9},{5... | collective-permute-start | bytes 307208 | tf_op jit(solution)/shard_map/ppermute | solution.py:250
  59.4 1.1 %collective-permute-start.29 = (bf16[1,160,320]{2,1,0:T(8,128)(2,1)S(1)}, bf16[1,160,320]{2,1,0:T(8,128)(2,1)S(1)}, u32[]{:S(2)}, u32[]{:S(2)}) collective-permute-start(bf16[1,160,320]{2,1,0:T(8,128)(2,1)S(1)} %get-tuple-element.56), channel_id=1, source_target_pairs={{0,24},{4,28},{8,16},{12,20},{16,8},{20,12},{24,0},{28,4},{1,25},{... | collective-permute-start | bytes 307208 | tf_op jit(solution)/shard_map/ppermute | solution.py:250
  60.5 1.6 %collective-permute-done.15 = bf16[4,80,360]{2,1,0:T(8,128)(2,1)S(1)} collective-permute-done((bf16[4,80,360]{2,1,0:T(8,128)(2,1)S(1)}, bf16[4,80,360]{2,1,0:T(8,128)(2,1)S(1)}, u32[]{:S(2)}, u32[]{:S(2)}) %collective-permute-start.15) | collective-permute-done | bytes 230432 | tf_op jit(solution)/shard_map/ppermute | solution.py:250
  62.1 0.7 collective-permute-start.28
  62.9 4.8 %collective-permute-done.17 = bf16[4,80,360]{2,1,0:T(8,128)(2,1)S(1)} collective-permute-done((bf16[4,80,360]{2,1,0:T(8,128)(2,1)S(1)}, bf16[4,80,360]{2,1,0:T(8,128)(2,1)S(1)}, u32[]{:S(2)}, u32[]{:S(2)}) %collective-permute-start.17) | collective-permute-done | bytes 230432 | tf_op jit(solution)/shard_map/ppermute | solution.py:250
  67.9 2.3 %collective-permute-start.21 = (bf16[1,80,360]{2,1,0:T(8,128)(2,1)S(1)}, bf16[1,80,360]{2,1,0:T(8,128)(2,1)S(1)}, u32[]{:S(2)}, u32[]{:S(2)}) collective-permute-start(bf16[1,80,360]{2,1,0:T(8,128)(2,1)S(1)} %get-tuple-element.62), channel_id=1, source_target_pairs={{0,8},{4,12},{8,0},{12,4},{16,24},{20,28},{24,16},{28,20},{1,9},{5... | collective-permute-start | bytes 172808 | tf_op jit(solution)/shard_map/ppermute | solution.py:250
  70.2 0.7 collective-permute-start.23
  71.0 0.8 collective-permute-start.22
  71.8 0.5 collective-permute-done.28
  72.3 1.9 %collective-permute-start.32 = (bf16[160,320]{1,0:T(8,128)(2,1)S(1)}, bf16[160,320]{1,0:T(8,128)(2,1)S(1)}, u32[]{:S(2)}, u32[]{:S(2)}) collective-permute-start(bf16[160,320]{1,0:T(8,128)(2,1)S(1)} %fusion.4), channel_id=1, source_target_pairs={{0,3},{1,2},{2,1},{3,0},{4,7},{5,6},{6,5},{7,4},{8,11},{9,10},{10,... | collective-permute-start | bytes 307208 | tf_op jit(solution)/shard_map/ppermute | solution.py:250
  74.3 1.2 %collective-permute-start.31 = (bf16[160,320]{1,0:T(8,128)(2,1)S(1)}, bf16[160,320]{1,0:T(8,128)(2,1)S(1)}, u32[]{:S(2)}, u32[]{:S(2)}) collective-permute-start(bf16[160,320]{1,0:T(8,128)(2,1)S(1)} %fusion.4), channel_id=1, source_target_pairs={{0,2},{1,3},{2,0},{3,1},{4,6},{5,7},{6,4},{7,5},{8,10},{9,11},{10,... | collective-permute-start | bytes 307208 | tf_op jit(solution)/shard_map/ppermute | solution.py:250
  75.5 0.4 collective-permute-start.30
  75.9 0.5 collective-permute-done.23
  76.4 1.3 %collective-permute-done.22 = bf16[1,80,360]{2,1,0:T(8,128)(2,1)S(1)} collective-permute-done((bf16[1,80,360]{2,1,0:T(8,128)(2,1)S(1)}, bf16[1,80,360]{2,1,0:T(8,128)(2,1)S(1)}, u32[]{:S(2)}, u32[]{:S(2)}) %collective-permute-start.22) | collective-permute-done | bytes 57632 | tf_op jit(solution)/shard_map/ppermute | solution.py:250
  77.7 1.4 %collective-permute-start.26 = (bf16[1,80,360]{2,1,0:T(8,128)(2,1)S(1)}, bf16[1,80,360]{2,1,0:T(8,128)(2,1)S(1)}, u32[]{:S(2)}, u32[]{:S(2)}) collective-permute-start(bf16[1,80,360]{2,1,0:T(8,128)(2,1)S(1)} %fusion.6), channel_id=1, source_target_pairs={{0,3},{1,2},{2,1},{3,0},{4,7},{5,6},{6,5},{7,4},{8,11},{9,10},{10,... | collective-permute-start | bytes 172808 | tf_op jit(solution)/shard_map/ppermute | solution.py:250
  79.2 1.3 %collective-permute-start.25 = (bf16[1,80,360]{2,1,0:T(8,128)(2,1)S(1)}, bf16[1,80,360]{2,1,0:T(8,128)(2,1)S(1)}, u32[]{:S(2)}, u32[]{:S(2)}) collective-permute-start(bf16[1,80,360]{2,1,0:T(8,128)(2,1)S(1)} %fusion.6), channel_id=1, source_target_pairs={{0,2},{1,3},{2,0},{3,1},{4,6},{5,7},{6,4},{7,5},{8,10},{9,11},{10,... | collective-permute-start | bytes 172808 | tf_op jit(solution)/shard_map/ppermute | solution.py:250
  80.5 0.9 collective-permute-start.24
  81.3 0.6 collective-permute-done.31
  81.9 0.8 fusion.3
  82.7 0.3 collective-permute-done.26
  82.9 0.6 collective-permute-done.25
  83.6 1.1 %collective-permute-done.24 = bf16[1,80,360]{2,1,0:T(8,128)(2,1)S(1)} collective-permute-done((bf16[1,80,360]{2,1,0:T(8,128)(2,1)S(1)}, bf16[1,80,360]{2,1,0:T(8,128)(2,1)S(1)}, u32[]{:S(2)}, u32[]{:S(2)}) %collective-permute-start.24) | collective-permute-done | bytes 57632 | tf_op jit(solution)/shard_map/ppermute | solution.py:250
  84.8 0.8 convert_bitcast_fusion
  (62 shorter events, 2.3 us)
Async XLA Ops:
  1.8 12.7 %collective-permute-start.2 = (bf16[1,80,360]{2,1,0:T(8,128)(2,1)S(1)}, bf16[1,80,360]{2,1,0:T(8,128)(2,1)S(1)}, u32[]{:S(2)}, u32[]{:S(2)}) collective-permute-start(bf16[1,80,360]{2,1,0:T(8,128)(2,1)S(1)} %get-tuple-element.72), channel_id=1, source_target_pairs={{0,24},{4,28},{8,16},{12,20},{16,8},{20,12},{24,0},{28,4},{1,25},{... | collective-permute-start | bytes 172808 | tf_op jit(solution)/shard_map/ppermute | solution.py:250
  6.9 7.6 %collective-permute-start.1 = (bf16[1,80,360]{2,1,0:T(8,128)(2,1)S(1)}, bf16[1,80,360]{2,1,0:T(8,128)(2,1)S(1)}, u32[]{:S(2)}, u32[]{:S(2)}) collective-permute-start(bf16[1,80,360]{2,1,0:T(8,128)(2,1)S(1)} %get-tuple-element.72), channel_id=1, source_target_pairs={{0,16},{4,20},{8,24},{12,28},{16,0},{20,4},{24,8},{28,12},{1,17},{... | collective-permute-start | bytes 172808 | tf_op jit(solution)/shard_map/ppermute | solution.py:250
  6.9 7.6 %collective-permute-start = (bf16[1,80,360]{2,1,0:T(8,128)(2,1)S(1)}, bf16[1,80,360]{2,1,0:T(8,128)(2,1)S(1)}, u32[]{:S(2)}, u32[]{:S(2)}) collective-permute-start(bf16[1,80,360]{2,1,0:T(8,128)(2,1)S(1)} %get-tuple-element.72), channel_id=1, source_target_pairs={{0,8},{4,12},{8,0},{12,4},{16,24},{20,28},{24,16},{28,20},{1,9},{5... | collective-permute-start | bytes 172808 | tf_op jit(solution)/shard_map/ppermute | solution.py:250
  8.5 9.7 %collective-permute-start.6 = (bf16[1,160,320]{2,1,0:T(8,128)(2,1)S(1)}, bf16[1,160,320]{2,1,0:T(8,128)(2,1)S(1)}, u32[]{:S(2)}, u32[]{:S(2)}) collective-permute-start(bf16[1,160,320]{2,1,0:T(8,128)(2,1)S(1)} %get-tuple-element.68), channel_id=1, source_target_pairs={{0,16},{4,20},{8,24},{12,28},{16,0},{20,4},{24,8},{28,12},{1,17},{... | collective-permute-start | bytes 307208 | tf_op jit(solution)/shard_map/ppermute | solution.py:250
  10.9 1.7 %copy-start = (bf16[1,15,256,320]{2,3,1,0:T(8,128)(2,1)S(1)}, bf16[1,15,256,320]{2,3,1,0:T(8,128)(2,1)}, u32[]{:S(2)}) copy-start(bf16[1,15,256,320]{2,3,1,0:T(8,128)(2,1)} %param.6) | copy-start | bytes 7372804
  14.6 9.6 %collective-permute-start.5 = (bf16[1,3,80,360]{3,2,1,0:T(8,128)(2,1)S(1)}, bf16[1,3,80,360]{3,2,1,0:T(8,128)(2,1)S(1)}, u32[]{:S(2)}, u32[]{:S(2)}) collective-permute-start(bf16[1,3,80,360]{3,2,1,0:T(8,128)(2,1)S(1)} %get-tuple-element.66), channel_id=1, source_target_pairs={{0,3},{1,2},{2,1},{3,0},{4,7},{5,6},{6,5},{7,4},{8,11},{9,10},{10,... | collective-permute-start | bytes 518408 | tf_op jit(solution)/shard_map/ppermute | solution.py:250
  17.1 7.9 %collective-permute-start.4 = (bf16[1,3,80,360]{3,2,1,0:T(8,128)(2,1)S(1)}, bf16[1,3,80,360]{3,2,1,0:T(8,128)(2,1)S(1)}, u32[]{:S(2)}, u32[]{:S(2)}) collective-permute-start(bf16[1,3,80,360]{3,2,1,0:T(8,128)(2,1)S(1)} %get-tuple-element.66), channel_id=1, source_target_pairs={{0,2},{1,3},{2,0},{3,1},{4,6},{5,7},{6,4},{7,5},{8,10},{9,11},{10,... | collective-permute-start | bytes 518408 | tf_op jit(solution)/shard_map/ppermute | solution.py:250
  17.7 7.5 %collective-permute-start.3 = (bf16[1,3,80,360]{3,2,1,0:T(8,128)(2,1)S(1)}, bf16[1,3,80,360]{3,2,1,0:T(8,128)(2,1)S(1)}, u32[]{:S(2)}, u32[]{:S(2)}) collective-permute-start(bf16[1,3,80,360]{3,2,1,0:T(8,128)(2,1)S(1)} %get-tuple-element.66), channel_id=1, source_target_pairs={{0,1},{1,0},{2,3},{3,2},{4,5},{5,4},{6,7},{7,6},{8,9},{9,8},{10,11... | collective-permute-start | bytes 518408 | tf_op jit(solution)/shard_map/ppermute | solution.py:250
  18.2 7.6 %collective-permute-start.11 = (bf16[1,2,160,320]{3,2,1,0:T(8,128)(2,1)S(1)}, bf16[1,2,160,320]{3,2,1,0:T(8,128)(2,1)S(1)}, u32[]{:S(2)}, u32[]{:S(2)}) collective-permute-start(bf16[1,2,160,320]{3,2,1,0:T(8,128)(2,1)S(1)} %bitcast.98), channel_id=1, source_target_pairs={{0,8},{4,12},{8,0},{12,4},{16,24},{20,28},{24,16},{28,20},{1,9},{5... | collective-permute-start | bytes 614408 | tf_op jit(solution)/shard_map/ppermute | solution.py:250
  24.2 1.9 %copy-start.4 = (s32[1,15]{1,0:T(1,128)S(1)}, s32[1,15]{1,0:T(1,128)}, u32[]{:S(2)}) copy-start(s32[1,15]{1,0:T(1,128)} %param.9) | copy-start | bytes 184
  24.2 3.4 %collective-permute-start.7 = (bf16[7,80,360]{2,1,0:T(8,128)(2,1)S(1)}, bf16[7,80,360]{2,1,0:T(8,128)(2,1)S(1)}, u32[]{:S(2)}, u32[]{:S(2)}) collective-permute-start(bf16[7,80,360]{2,1,0:T(8,128)(2,1)S(1)} %pad_maximum_fusion.1), channel_id=1, source_target_pairs={{0,4},{4,0},{8,12},{12,8},{16,20},{20,16},{24,28},{28,24},{1,5},{5... | collective-permute-start | bytes 1209608 | tf_op jit(solution)/shard_map/ppermute | solution.py:250
  24.3 3.4 %collective-permute-start.10 = (bf16[1,3,80,360]{3,2,1,0:T(8,128)(2,1)S(1)}, bf16[1,3,80,360]{3,2,1,0:T(8,128)(2,1)S(1)}, u32[]{:S(2)}, u32[]{:S(2)}) collective-permute-start(bf16[1,3,80,360]{3,2,1,0:T(8,128)(2,1)S(1)} %collective-permute-done.5), channel_id=1, source_target_pairs={{0,4},{4,0},{8,12},{12,8},{16,20},{20,16},{24,28},{28,24},{1,5},{5... | collective-permute-start | bytes 518408 | tf_op jit(solution)/shard_map/ppermute | solution.py:250
  25.1 2.6 %collective-permute-start.9 = (bf16[1,3,80,360]{3,2,1,0:T(8,128)(2,1)S(1)}, bf16[1,3,80,360]{3,2,1,0:T(8,128)(2,1)S(1)}, u32[]{:S(2)}, u32[]{:S(2)}) collective-permute-start(bf16[1,3,80,360]{3,2,1,0:T(8,128)(2,1)S(1)} %collective-permute-done.4), channel_id=1, source_target_pairs={{0,4},{4,0},{8,12},{12,8},{16,20},{20,16},{24,28},{28,24},{1,5},{5... | collective-permute-start | bytes 518408 | tf_op jit(solution)/shard_map/ppermute | solution.py:250
  25.2 2.6 %collective-permute-start.8 = (bf16[1,3,80,360]{3,2,1,0:T(8,128)(2,1)S(1)}, bf16[1,3,80,360]{3,2,1,0:T(8,128)(2,1)S(1)}, u32[]{:S(2)}, u32[]{:S(2)}) collective-permute-start(bf16[1,3,80,360]{3,2,1,0:T(8,128)(2,1)S(1)} %collective-permute-done.3), channel_id=1, source_target_pairs={{0,4},{4,0},{8,12},{12,8},{16,20},{20,16},{24,28},{28,24},{1,5},{5... | collective-permute-start | bytes 518408 | tf_op jit(solution)/shard_map/ppermute | solution.py:250
  26.0 2.0 %copy-start.2 = (bf16[1,15,256,320]{2,3,1,0:T(8,128)(2,1)S(1)}, bf16[1,15,256,320]{2,3,1,0:T(8,128)(2,1)}, u32[]{:S(2)}) copy-start(bf16[1,15,256,320]{2,3,1,0:T(8,128)(2,1)} %param.7) | copy-start | bytes 7372804
  26.0 2.4 %copy-start.1 = (bf16[1,15,256,320]{2,3,1,0:T(8,128)(2,1)S(1)}, bf16[1,15,256,320]{2,3,1,0:T(8,128)(2,1)}, u32[]{:S(2)}) copy-start(bf16[1,15,256,320]{2,3,1,0:T(8,128)(2,1)} %param.6) | copy-start | bytes 7372804
  26.1 2.4 %copy-start.3 = (s32[1,4]{1,0:T(1,128)S(1)}, s32[1,4]{1,0:T(1,128)}, u32[]{:S(2)}) copy-start(s32[1,4]{1,0:T(1,128)} %counts_ref.1) | copy-start | bytes 52
  26.1 1.9 %collective-permute-start.12 = (bf16[4,160,320]{2,1,0:T(8,128)(2,1)S(1)}, bf16[4,160,320]{2,1,0:T(8,128)(2,1)S(1)}, u32[]{:S(2)}, u32[]{:S(2)}) collective-permute-start(bf16[4,160,320]{2,1,0:T(8,128)(2,1)S(1)} %bitcast.91), channel_id=1, source_target_pairs={{0,4},{4,0},{8,12},{12,8},{16,20},{20,16},{24,28},{28,24},{1,5},{5... | collective-permute-start | bytes 1228808 | tf_op jit(solution)/shard_map/ppermute | solution.py:250
  45.7 7.6 %collective-permute-start.14 = (bf16[4,80,360]{2,1,0:T(8,128)(2,1)S(1)}, bf16[4,80,360]{2,1,0:T(8,128)(2,1)S(1)}, u32[]{:S(2)}, u32[]{:S(2)}) collective-permute-start(bf16[4,80,360]{2,1,0:T(8,128)(2,1)S(1)} %get-tuple-element.46), channel_id=1, source_target_pairs={{0,4},{4,0},{8,12},{12,8},{16,20},{20,16},{24,28},{28,24},{1,5},{5... | collective-permute-start | bytes 691208 | tf_op jit(solution)/shard_map/ppermute | solution.py:250
  52.1 7.3 %collective-permute-start.13 = (bf16[4,80,360]{2,1,0:T(8,128)(2,1)S(1)}, bf16[4,80,360]{2,1,0:T(8,128)(2,1)S(1)}, u32[]{:S(2)}, u32[]{:S(2)}) collective-permute-start(bf16[4,80,360]{2,1,0:T(8,128)(2,1)S(1)} %get-tuple-element.44), channel_id=1, source_target_pairs={{0,4},{4,0},{8,12},{12,8},{16,20},{20,16},{24,28},{28,24},{1,5},{5... | collective-permute-start | bytes 691208 | tf_op jit(solution)/shard_map/ppermute | solution.py:250
  52.1 1.9 %collective-permute-start.16 = (bf16[4,80,360]{2,1,0:T(8,128)(2,1)S(1)}, bf16[4,80,360]{2,1,0:T(8,128)(2,1)S(1)}, u32[]{:S(2)}, u32[]{:S(2)}) collective-permute-start(bf16[4,80,360]{2,1,0:T(8,128)(2,1)S(1)} %get-tuple-element.48), channel_id=1, source_target_pairs={{0,4},{4,0},{8,12},{12,8},{16,20},{20,16},{24,28},{28,24},{1,5},{5... | collective-permute-start | bytes 691208 | tf_op jit(solution)/shard_map/ppermute | solution.py:250
  52.6 3.9 %collective-permute-start.18 = (bf16[4,80,360]{2,1,0:T(8,128)(2,1)S(1)}, bf16[4,80,360]{2,1,0:T(8,128)(2,1)S(1)}, u32[]{:S(2)}, u32[]{:S(2)}) collective-permute-start(bf16[4,80,360]{2,1,0:T(8,128)(2,1)S(1)} %get-tuple-element.50), channel_id=1, source_target_pairs={{0,4},{4,0},{8,12},{12,8},{16,20},{20,16},{24,28},{28,24},{1,5},{5... | collective-permute-start | bytes 691208 | tf_op jit(solution)/shard_map/ppermute | solution.py:250
  52.6 4.0 %collective-permute-start.19 = (bf16[4,160,320]{2,1,0:T(8,128)(2,1)S(1)}, bf16[4,160,320]{2,1,0:T(8,128)(2,1)S(1)}, u32[]{:S(2)}, u32[]{:S(2)}) collective-permute-start(bf16[4,160,320]{2,1,0:T(8,128)(2,1)S(1)} %get-tuple-element.52), channel_id=1, source_target_pairs={{0,4},{4,0},{8,12},{12,8},{16,20},{20,16},{24,28},{28,24},{1,5},{5... | collective-permute-start | bytes 1228808 | tf_op jit(solution)/shard_map/ppermute | solution.py:250
  53.3 8.9 %collective-permute-start.15 = (bf16[4,80,360]{2,1,0:T(8,128)(2,1)S(1)}, bf16[4,80,360]{2,1,0:T(8,128)(2,1)S(1)}, u32[]{:S(2)}, u32[]{:S(2)}) collective-permute-start(bf16[4,80,360]{2,1,0:T(8,128)(2,1)S(1)} %add_convert_fusion.4), channel_id=1, source_target_pairs={{0,1},{1,0},{2,3},{3,2},{4,5},{5,4},{6,7},{7,6},{8,9},{9,8},{10,11... | collective-permute-start | bytes 691208 | tf_op jit(solution)/shard_map/ppermute | solution.py:250
  54.0 13.7 %collective-permute-start.17 = (bf16[4,80,360]{2,1,0:T(8,128)(2,1)S(1)}, bf16[4,80,360]{2,1,0:T(8,128)(2,1)S(1)}, u32[]{:S(2)}, u32[]{:S(2)}) collective-permute-start(bf16[4,80,360]{2,1,0:T(8,128)(2,1)S(1)} %add_convert_fusion.3), channel_id=1, source_target_pairs={{0,2},{1,3},{2,0},{3,1},{4,6},{5,7},{6,4},{7,5},{8,10},{9,11},{10,... | collective-permute-start | bytes 691208 | tf_op jit(solution)/shard_map/ppermute | solution.py:250
  56.7 11.0 %collective-permute-start.20 = (bf16[4,80,360]{2,1,0:T(8,128)(2,1)S(1)}, bf16[4,80,360]{2,1,0:T(8,128)(2,1)S(1)}, u32[]{:S(2)}, u32[]{:S(2)}) collective-permute-start(bf16[4,80,360]{2,1,0:T(8,128)(2,1)S(1)} %add_convert_fusion.2), channel_id=1, source_target_pairs={{0,3},{1,2},{2,1},{3,0},{4,7},{5,6},{6,5},{7,4},{8,11},{9,10},{10,... | collective-permute-start | bytes 691208 | tf_op jit(solution)/shard_map/ppermute | solution.py:250
  57.6 13.3 %collective-permute-start.27 = (bf16[1,160,320]{2,1,0:T(8,128)(2,1)S(1)}, bf16[1,160,320]{2,1,0:T(8,128)(2,1)S(1)}, u32[]{:S(2)}, u32[]{:S(2)}) collective-permute-start(bf16[1,160,320]{2,1,0:T(8,128)(2,1)S(1)} %get-tuple-element.55), channel_id=1, source_target_pairs={{0,8},{4,12},{8,0},{12,4},{16,24},{20,28},{24,16},{28,20},{1,9},{5... | collective-permute-start | bytes 307208 | tf_op jit(solution)/shard_map/ppermute | solution.py:250
  59.4 12.4 %collective-permute-start.29 = (bf16[1,160,320]{2,1,0:T(8,128)(2,1)S(1)}, bf16[1,160,320]{2,1,0:T(8,128)(2,1)S(1)}, u32[]{:S(2)}, u32[]{:S(2)}) collective-permute-start(bf16[1,160,320]{2,1,0:T(8,128)(2,1)S(1)} %get-tuple-element.56), channel_id=1, source_target_pairs={{0,24},{4,28},{8,16},{12,20},{16,8},{20,12},{24,0},{28,4},{1,25},{... | collective-permute-start | bytes 307208 | tf_op jit(solution)/shard_map/ppermute | solution.py:250
  62.1 10.1 %collective-permute-start.28 = (bf16[1,160,320]{2,1,0:T(8,128)(2,1)S(1)}, bf16[1,160,320]{2,1,0:T(8,128)(2,1)S(1)}, u32[]{:S(2)}, u32[]{:S(2)}) collective-permute-start(bf16[1,160,320]{2,1,0:T(8,128)(2,1)S(1)} %get-tuple-element.57), channel_id=1, source_target_pairs={{0,16},{4,20},{8,24},{12,28},{16,0},{20,4},{24,8},{28,12},{1,17},{... | collective-permute-start | bytes 307208 | tf_op jit(solution)/shard_map/ppermute | solution.py:250
  67.9 7.6 %collective-permute-start.21 = (bf16[1,80,360]{2,1,0:T(8,128)(2,1)S(1)}, bf16[1,80,360]{2,1,0:T(8,128)(2,1)S(1)}, u32[]{:S(2)}, u32[]{:S(2)}) collective-permute-start(bf16[1,80,360]{2,1,0:T(8,128)(2,1)S(1)} %get-tuple-element.62), channel_id=1, source_target_pairs={{0,8},{4,12},{8,0},{12,4},{16,24},{20,28},{24,16},{28,20},{1,9},{5... | collective-permute-start | bytes 172808 | tf_op jit(solution)/shard_map/ppermute | solution.py:250
  70.2 6.1 %collective-permute-start.23 = (bf16[1,80,360]{2,1,0:T(8,128)(2,1)S(1)}, bf16[1,80,360]{2,1,0:T(8,128)(2,1)S(1)}, u32[]{:S(2)}, u32[]{:S(2)}) collective-permute-start(bf16[1,80,360]{2,1,0:T(8,128)(2,1)S(1)} %get-tuple-element.63), channel_id=1, source_target_pairs={{0,24},{4,28},{8,16},{12,20},{16,8},{20,12},{24,0},{28,4},{1,25},{... | collective-permute-start | bytes 172808 | tf_op jit(solution)/shard_map/ppermute | solution.py:250
  71.0 6.7 %collective-permute-start.22 = (bf16[1,80,360]{2,1,0:T(8,128)(2,1)S(1)}, bf16[1,80,360]{2,1,0:T(8,128)(2,1)S(1)}, u32[]{:S(2)}, u32[]{:S(2)}) collective-permute-start(bf16[1,80,360]{2,1,0:T(8,128)(2,1)S(1)} %get-tuple-element.64), channel_id=1, source_target_pairs={{0,16},{4,20},{8,24},{12,28},{16,0},{20,4},{24,8},{28,12},{1,17},{... | collective-permute-start | bytes 172808 | tf_op jit(solution)/shard_map/ppermute | solution.py:250
  72.3 8.1 %collective-permute-start.32 = (bf16[160,320]{1,0:T(8,128)(2,1)S(1)}, bf16[160,320]{1,0:T(8,128)(2,1)S(1)}, u32[]{:S(2)}, u32[]{:S(2)}) collective-permute-start(bf16[160,320]{1,0:T(8,128)(2,1)S(1)} %fusion.4), channel_id=1, source_target_pairs={{0,3},{1,2},{2,1},{3,0},{4,7},{5,6},{6,5},{7,4},{8,11},{9,10},{10,... | collective-permute-start | bytes 307208 | tf_op jit(solution)/shard_map/ppermute | solution.py:250
  74.3 7.6 %collective-permute-start.31 = (bf16[160,320]{1,0:T(8,128)(2,1)S(1)}, bf16[160,320]{1,0:T(8,128)(2,1)S(1)}, u32[]{:S(2)}, u32[]{:S(2)}) collective-permute-start(bf16[160,320]{1,0:T(8,128)(2,1)S(1)} %fusion.4), channel_id=1, source_target_pairs={{0,2},{1,3},{2,0},{3,1},{4,6},{5,7},{6,4},{7,5},{8,10},{9,11},{10,... | collective-permute-start | bytes 307208 | tf_op jit(solution)/shard_map/ppermute | solution.py:250
  75.5 6.4 %collective-permute-start.30 = (bf16[160,320]{1,0:T(8,128)(2,1)S(1)}, bf16[160,320]{1,0:T(8,128)(2,1)S(1)}, u32[]{:S(2)}, u32[]{:S(2)}) collective-permute-start(bf16[160,320]{1,0:T(8,128)(2,1)S(1)} %fusion.4), channel_id=1, source_target_pairs={{0,1},{1,0},{2,3},{3,2},{4,5},{5,4},{6,7},{7,6},{8,9},{9,8},{10,11... | collective-permute-start | bytes 307208 | tf_op jit(solution)/shard_map/ppermute | solution.py:250
  77.7 5.2 %collective-permute-start.26 = (bf16[1,80,360]{2,1,0:T(8,128)(2,1)S(1)}, bf16[1,80,360]{2,1,0:T(8,128)(2,1)S(1)}, u32[]{:S(2)}, u32[]{:S(2)}) collective-permute-start(bf16[1,80,360]{2,1,0:T(8,128)(2,1)S(1)} %fusion.6), channel_id=1, source_target_pairs={{0,3},{1,2},{2,1},{3,0},{4,7},{5,6},{6,5},{7,4},{8,11},{9,10},{10,... | collective-permute-start | bytes 172808 | tf_op jit(solution)/shard_map/ppermute | solution.py:250
  79.2 4.4 %collective-permute-start.25 = (bf16[1,80,360]{2,1,0:T(8,128)(2,1)S(1)}, bf16[1,80,360]{2,1,0:T(8,128)(2,1)S(1)}, u32[]{:S(2)}, u32[]{:S(2)}) collective-permute-start(bf16[1,80,360]{2,1,0:T(8,128)(2,1)S(1)} %fusion.6), channel_id=1, source_target_pairs={{0,2},{1,3},{2,0},{3,1},{4,6},{5,7},{6,4},{7,5},{8,10},{9,11},{10,... | collective-permute-start | bytes 172808 | tf_op jit(solution)/shard_map/ppermute | solution.py:250
  80.5 4.2 %collective-permute-start.24 = (bf16[1,80,360]{2,1,0:T(8,128)(2,1)S(1)}, bf16[1,80,360]{2,1,0:T(8,128)(2,1)S(1)}, u32[]{:S(2)}, u32[]{:S(2)}) collective-permute-start(bf16[1,80,360]{2,1,0:T(8,128)(2,1)S(1)} %fusion.6), channel_id=1, source_target_pairs={{0,1},{1,0},{2,3},{3,2},{4,5},{5,4},{6,7},{7,6},{8,9},{9,8},{10,11... | collective-permute-start | bytes 172808 | tf_op jit(solution)/shard_map/ppermute | solution.py:250
